TPU v7x, 32 devices: a whole 2x2x4 slice. The times are simulated.
32 devices in a mesh: cell: 4 (over x, core), spot: 2 (over y), gene: 4 (over z).
Axes of the slice: x: 2, y: 2, z: 4, core: 2. Of those that a mesh axis runs over, the one named last changes fastest.
Arguments:
- logits: bfloat16 [45056, 1024], P(('cell', 'gene'), 'spot'), may hold values from -8 to 8
- expression: bfloat16 [45056, 2048], P(('cell', 'spot'), 'gene'), may hold values from 5e-05 to 12, as said below
- spatial: bfloat16 [1024, 2048], P('spot', 'gene'), may hold values from 5e-05 to 12, as said below
- slide_ids: int32 [1024], P('spot'), may hold values from 0 to 2, never falling along the last dimension, each value on 1 to 512 neighbouring positions
- spot_mask: int32 [1024], P('spot'), may hold values 0 or 1
- densities: float32 [45056], P(('cell', 'gene')), may hold values from 0.2 to 5
Outputs:
- loss_terms: float32 [5], replicated
- grad_logits: float32 [45056, 1024], P(('cell', 'gene'), 'spot')
Inputs may be any that keep to these rules, and one draw needn't show every extreme that they name: `slide_ids`: spots are ordered by slide: the ids never fall, every slide has at least one spot, and the largest slide has exactly 512 spots. Positive expression levels. `spatial`: positive expression levels.
All inputs are finite; a program needn't handle non-finite values. No bound on the sum of `spot_mask` on one device may be relied on, other than what follows from the above.
Results may differ from a plain program's by a relative error of at most 0.0003.
Values may be sent and summed in bfloat16 or wider, within the bound.
No kernel may reach another device: no remote copies, remote signals or barrier semaphores. Data moves between devices by JAX's collectives and lax.ppermute only.
A program may use at most 128 MiB of HBM per device.

v0:
```python
import jax
import jax.numpy as jnp
from jax import lax
from jax.sharding import PartitionSpec as P

SLIDES = 3


def contract_cells(left_block, right_block):
    return lax.dot_general(
        left_block, right_block, (((0,), (0,)), ((), ())), preferred_element_type=jnp.float32
    )


def contract_genes(left_block, right_block):
    return lax.dot_general(
        left_block, right_block, (((1,), (1,)), ((), ())), preferred_element_type=jnp.float32
    )


def per_device(logits, expression, spatial, slide_ids, spot_mask, densities):
    highest = lax.Precision.HIGHEST
    logit_vals = logits.astype(jnp.float32)
    spots_all = logits.shape[1] * lax.axis_size("spot")
    genes_all = spatial.shape[1] * lax.axis_size("gene")
    local_max = jnp.max(logit_vals, axis=0)
    dens_local = jnp.sum(densities)
    col_max = lax.pmax(local_max, ("cell", "gene"))
    expo_vals = jnp.exp(logit_vals - col_max)
    col_total, dens_total = lax.psum((jnp.sum(expo_vals, axis=0), dens_local), ("cell", "gene"))
    prob_vals = expo_vals / col_total
    prob_low = prob_vals.astype(jnp.bfloat16)
    prob_block = lax.all_gather(prob_low, "gene", axis=0, tiled=True)
    expr_block = lax.all_gather(expression, "spot", axis=0, tiled=True)
    partial_pred = contract_cells(prob_block, expr_block)
    predicted = lax.psum(partial_pred, "cell")
    target = spatial.astype(jnp.float32)
    valid_spots = spot_mask.astype(jnp.float32)
    member = jnp.where(
        (slide_ids[None, :] == jnp.arange(SLIDES, dtype=jnp.int32)[:, None])
        & (spot_mask[None, :] == 1),
        1.0,
        0.0,
    ).astype(jnp.float32)
    gene_parts = jnp.stack(
        [
            jnp.dot(member, predicted * target, precision=highest),
            jnp.dot(member, predicted * predicted, precision=highest),
            jnp.dot(member, target * target, precision=highest),
        ]
    )
    slide_stats, mass_sum, valid_sum = lax.psum(
        (gene_parts, jnp.sum(prob_vals, axis=1), jnp.sum(valid_spots)), "spot"
    )
    spot_parts = jnp.stack(
        [
            jnp.sum(predicted * target, axis=1),
            jnp.sum(predicted * predicted, axis=1),
            jnp.sum(target * target, axis=1),
        ]
    )
    spot_sums = lax.psum(spot_parts, "gene")
    valid_total = jnp.maximum(valid_sum, 1.0)
    pred_floor = jnp.maximum(slide_stats[1], 1.0)
    target_floor = jnp.maximum(slide_stats[2], 1.0)
    root_gene = jnp.sqrt(pred_floor * target_floor)
    cos_gene = slide_stats[0] / root_gene
    gene_scale = -1.0 / (SLIDES * genes_all)
    weight_target = gene_scale / root_gene
    weight_pred = jnp.where(slide_stats[1] > 1.0, -gene_scale * cos_gene / pred_floor, 0.0)
    spot_pred = spot_sums[1] + 1e-06
    spot_target = spot_sums[2] + 1e-06
    root_spot = jnp.sqrt(spot_pred * spot_target)
    cos_spot = spot_sums[0] / root_spot
    spot_coef = -valid_spots / valid_total
    grad_pred = jnp.dot(member.T, weight_target, precision=highest) * target
    grad_pred = grad_pred + jnp.dot(member.T, weight_pred, precision=highest) * predicted
    grad_pred = grad_pred + (spot_coef / root_spot)[:, None] * target
    grad_pred = grad_pred - (spot_coef * cos_spot / spot_pred)[:, None] * predicted
    grad_low = grad_pred.astype(jnp.bfloat16)
    grad_probs = lax.psum_scatter(
        contract_genes(expr_block, grad_low), "gene", scatter_dimension=0, tiled=True
    )
    cell_mass = mass_sum / spots_all
    target_share = densities / dens_total
    grad_probs = grad_probs - (target_share / (cell_mass * spots_all))[:, None]
    col_inner = lax.psum(jnp.sum(prob_vals * grad_probs, axis=0), ("cell", "gene"))
    grad_logits = prob_vals * (grad_probs - col_inner)
    log_prob = logit_vals - col_max - jnp.log(col_total)
    cell_first = jnp.where(lax.axis_index("cell") == 0, 1.0, 0.0)
    spot_first = jnp.where(lax.axis_index("spot") == 0, 1.0, 0.0)
    gene_first = jnp.where(lax.axis_index("gene") == 0, 1.0, 0.0)
    gene_local = jnp.sum(cos_gene) * cell_first * spot_first
    spot_local = jnp.sum(valid_spots * cos_spot) * cell_first * gene_first
    kl_local = jnp.sum(target_share * (jnp.log(target_share) - jnp.log(cell_mass))) * spot_first
    entropy_local = -jnp.sum(prob_vals * log_prob)
    loss_totals = lax.psum(
        jnp.stack([gene_local, spot_local, kl_local, entropy_local]), ("cell", "spot", "gene")
    )
    gene_term = loss_totals[0] / (SLIDES * genes_all)
    spot_term = loss_totals[1] / valid_total
    divergence = loss_totals[2]
    entropy = loss_totals[3] / spots_all
    total = -gene_term - spot_term + divergence
    loss_terms = jnp.stack([total, gene_term, spot_term, divergence, entropy])
    return (loss_terms, grad_logits)


def solution(mesh):
    return jax.shard_map(
        per_device,
        mesh=mesh,
        in_specs=(
            P(("cell", "gene"), "spot"),
            P(("cell", "spot"), "gene"),
            P("spot", "gene"),
            P("spot"),
            P("spot"),
            P(("cell", "gene")),
        ),
        out_specs=(P(), P(("cell", "gene"), "spot")),
        check_vma=False,
    )
```

profile of v0, /device:TPU:0, one launch (start us, length us, event | category | flops | bytes accessed | tf_op | source)
XLA Modules:
  0.0 935.2 jit_solution(4013603901567317538)
XLA Ops:
  7.2 0.0 all-gather.5.cloned.1.call-start
  7.2 0.7 all-gather.5.cloned.1.call-update
  7.9 0.0 copy-start.2
  7.9 0.0 all-gather.3.cloned.1.call-start
  8.0 3.1 copy.8
  11.1 2.3 reduce_max.14
  13.3 0.0 copy-done.2
  13.3 0.6 reduce_sum.114
  14.0 35.1 %pmax.7 = f32[512]{0:T(512)S(1)} all-reduce(bf16[512]{0:T(512)(128)(2,1)S(1)} %reduce_max.14), channel_id=1, replica_groups=mesh['cell'=4,'spot'=2,'gene'=4] {'cell','gene'}, use_global_device_ids=true, to_apply=%region_1.0 | all-reduce | flops 512 | bytes 3072 | tf_op jit(solution)/shard_map/pmax | solution.py:28
  49.1 1.1 fusion.2
  50.1 30.3 %all-reduce = (f32[512]{0:T(512)S(1)}, f32[]{:T(128)}) all-reduce(f32[512]{0:T(512)S(1)} %fusion.2, f32[]{:T(128)} %reduce_sum.114), channel_id=1, replica_groups=mesh['cell'=4,'spot'=2,'gene'=4] {'cell','gene'}, use_global_device_ids=true, to_apply=%region_3.0 | all-reduce | flops 513 | bytes 4104 | tf_op jit(solution)/shard_map/psum | solution.py:30
  80.4 2.8 fusion.60
  83.2 0.0 all-gather.3.cloned.1.call-update
  83.2 0.0 copy-start.3
  83.2 0.0 copy-start
  83.3 0.0 copy-start.1
  83.3 0.0 all-reduce.4.cloned.1.call-start
  83.3 70.0 %all-gather.5.cloned.1.call-done = bf16[11264,512]{1,0:T(8,128)(2,1)} async-done(((bf16[5632,512]{1,0:T(8,128)(2,1)}), bf16[11264,512]{1,0:T(8,128)(2,1)}) %all-gather.5.cloned.1.call-update) | async-done | bytes 11534352 | tf_op jit(solution)/shard_map/all_gather | solution.py:34
  153.3 203.2 %all-gather.3.cloned.1.call-done = bf16[11264,512]{0,1:T(8,128)(2,1)} async-done(((bf16[2816,512]{0,1:T(8,128)(2,1)}), bf16[11264,512]{0,1:T(8,128)(2,1)}) %all-gather.3.cloned.1.call-update) | async-done | bytes 11534352 | tf_op jit(solution)/shard_map/all_gather | solution.py:33
  356.5 13.1 %fusion.65 = f32[512,512]{1,0:T(8,128)} fusion(bf16[11264,512]{0,1:T(8,128)(2,1)} %all-gather.3.cloned.1.call-done, bf16[11264,512]{1,0:T(8,128)(2,1)} %all-gather.5.cloned.1.call-done), kind=kOutput, calls=%fused_computation.90 | convolution fusion | flops 5905580032 | bytes 24117248 | tf_op jit(solution)/shard_map/dot_general | solution.py:10
  369.6 0.0 all-reduce.4.cloned.1.call-update
  369.6 0.0 reduce-scatter.2.cloned.1.call-start
  369.7 0.0 copy-done.3
  369.7 0.0 copy-done
  369.7 0.0 copy-done.1
  369.7 0.7 fusion.9
  370.4 33.7 %all-reduce.4.cloned.1.call-done = f32[512,512]{1,0:T(8,128)} async-done(((f32[512,512]{1,0:T(8,128)}), f32[512,512]{1,0:T(8,128)}) %all-reduce.4.cloned.1.call-update) | async-done | bytes 1048592 | tf_op jit(solution)/shard_map/psum | solution.py:36
  404.1 1.6 fusion.11
  405.7 11.8 %psum.66 = f32[3,512]{1,0:T(4,128)S(1)} all-reduce(f32[3,512]{1,0:T(4,128)S(1)} %pad_maximum_fusion.1), channel_id=1, replica_groups=mesh['cell'=4,'spot'=2,'gene'=4] {'gene'}, use_global_device_ids=true, to_apply=%region_10.11 | all-reduce | flops 1536 | bytes 12288 | tf_op jit(solution)/shard_map/psum | solution.py:62
  417.6 0.6 convert_reduce_fusion
  418.2 1.9 convolution_bitcast_fusion.2
  420.1 1.9 convolution_bitcast_fusion.1
  422.0 9.6 %all-reduce.1 = (f32[3,3,512]{2,1,0:T(4,128)S(1)}, f32[]{:T(128)}, f32[2816]{0:T(1024)S(1)}) all-reduce(f32[3,3,512]{2,1,0:T(4,128)S(1)} %pad_maximum_fusion, f32[]{:T(128)} %get-tuple-element.9, f32[2816]{0:T(1024)S(1)} %get-tuple-element.18), channel_id=1, replica_groups=mesh['cell'=4,'spot'=2,'gene'=4] {'spot'}, use_global_device_ids=true, to_apply=%region_5.0 | all-reduce | flops 7425 | bytes 59400 | tf_op jit(solution)/shard_map/psum | solution.py:52
  431.6 2.0 convert_multiply_fusion.1
  433.6 0.6 fusion.62
  434.9 2.8 fusion.6
  437.7 19.1 %convolution_bitcast_fusion = f32[11264,512]{0,1:T(8,128)} fusion(bf16[512,512]{1,0:T(8,128)(2,1)S(1)} %fusion.6, bf16[11264,512]{1,0:T(8,128)(2,1)} %all-gather.5.cloned.1.call-done), kind=kOutput, calls=%fused_computation | convolution fusion | flops 5905580032 | bytes 35127296 | tf_op jit(solution)/shard_map/dot_general | solution.py:16
  456.8 0.0 reduce-scatter.2.cloned.1.call-update
  456.9 1.3 multiply_reduce_fusion.3
  460.0 374.4 %reduce-scatter.2.cloned.1.call-done = f32[2816,512]{0,1:T(8,128)} async-done(((f32[11264,512]{0,1:T(8,128)}), f32[2816,512]{0,1:T(8,128)}) %reduce-scatter.2.cloned.1.call-update) | async-done | bytes 5767184 | tf_op jit(solution)/shard_map/reduce_scatter | solution.py:81
  834.4 6.0 multiply_reduce_fusion
  840.4 34.1 %psum.71 = f32[512]{0:T(512)S(1)} all-reduce(f32[512]{0:T(512)S(1)} %get-tuple-element.4), channel_id=1, replica_groups=mesh['cell'=4,'spot'=2,'gene'=4] {'cell','gene'}, use_global_device_ids=true, to_apply=%region_23.24 | all-reduce | flops 512 | bytes 4096 | tf_op jit(solution)/shard_map/psum | solution.py:87
  875.2 0.1 pad_maximum_fusion.2
  875.3 5.5 subtract_multiply_fusion
  880.8 6.2 copy.9
  887.0 37.1 %psum.69 = f32[4]{0:T(128)S(1)} all-reduce(f32[4]{0:T(128)S(1)} %pad_maximum_fusion.2), channel_id=1, replica_groups=mesh['cell'=4,'spot'=2,'gene'=4] {'cell','spot','gene'}, use_global_device_ids=true, to_apply=%region_18.19 | all-reduce | flops 4 | bytes 32 | tf_op jit(solution)/shard_map/psum | solution.py:97
  924.1 0.7 fusion.64
  927.4 1.3 stack.65
  (6 shorter events, 0.1 us)
Async XLA Ops:
  7.2 146.1 %all-gather.5.cloned.1.call-start = ((), (), s32[]{:S(2)}) async-start(), calls=%async_computation.2 | async-start | bytes 17301504 | tf_op jit(solution)/shard_map/all_gather | solution.py:34
  7.9 5.5 copy-start.2
  7.9 348.6 %all-gather.3.cloned.1.call-start = ((), (), s32[]{:S(2)}) async-start(), calls=%async_computation.1 | async-start | bytes 14417920 | tf_op jit(solution)/shard_map/all_gather | solution.py:33
  83.2 286.5 %copy-start.3 = (s32[512]{0:T(512)S(1)}, s32[512]{0:T(512)}, u32[]{:S(2)}) copy-start(s32[512]{0:T(512)} %param.10) | copy-start | bytes 6148
  83.2 286.5 %copy-start = (bf16[512,512]{1,0:T(8,128)(2,1)S(1)}, bf16[512,512]{1,0:T(8,128)(2,1)}, u32[]{:S(2)}) copy-start(bf16[512,512]{1,0:T(8,128)(2,1)} %param.8) | copy-start | bytes 1572868
  83.3 286.5 %copy-start.1 = (s32[512]{0:T(512)S(1)}, s32[512]{0:T(512)}, u32[]{:S(2)}) copy-start(s32[512]{0:T(512)} %param.9) | copy-start | bytes 6148
  83.3 320.8 %all-reduce.4.cloned.1.call-start = ((), (), s32[]{:S(2)}) async-start(), calls=%async_computation.3 | async-start | bytes 2097152 | tf_op jit(solution)/shard_map/psum | solution.py:36
  369.6 464.8 %reduce-scatter.2.cloned.1.call-start = ((), (), s32[]{:S(2)}) async-start(), calls=%async_computation.4 | async-start | bytes 28835840 | tf_op jit(solution)/shard_map/reduce_scatter | solution.py:81
Sparse Core Ops, SparseCore 0:
  9.6 143.7 all-gather.4
  155.4 201.0 all-gather.2
  369.8 34.2 all-reduce.3
  456.9 377.4 reduce-scatter.1
where the time goes:
time: 936 us; the launch traced here: 935 us
  waiting for transfers between devices  682 us (73%)
  blocking collectives  158 us (17%)
  matrix products  41.4 us (4%)
  other arithmetic  22.4 us (2%)
  between operations  19.7 us (2%)
  local copies, waits for them, and re-layouts  11.3 us (1%)
    reduce_scatter x1, waiting for transfers between devices, per_device(): lax.psum_scatter(contract_genes(expr_block, grad_low), 'gene', scatter_di...  374 us
    all_gather x1, waiting for transfers between devices, per_device(): prob_block = lax.all_gather(prob_low, 'gene', axis=0, tiled=True)  203 us
    all_gather x1, waiting for transfers between devices, per_device(): expr_block = lax.all_gather(expression, 'spot', axis=0, tiled=True)  70 us
    psum x1, blocking collectives, per_device(): lax.psum(jnp.stack([gene_local, spot_local, kl_local, entropy_local]), ('...  37.1 us
    pmax x1, blocking collectives, per_device(): col_max = lax.pmax(local_max, ('cell', 'gene'))  35.1 us
    psum x1, blocking collectives, per_device(): lax.psum(jnp.sum(prob_vals * grad_probs, axis=0), ('cell', 'gene'))  34.1 us
    psum x1, waiting for transfers between devices, per_device(): predicted = lax.psum(partial_pred, 'cell')  33.7 us
    psum x1, blocking collectives, per_device(): lax.psum((jnp.sum(expo_vals, axis=0), dens_local), ('cell', 'gene'))  30.3 us
  transfers between devices with their start and end apart: 4, of which 4 were waited for; matrix products, arithmetic and copies ran while one was open for 1% of the time, Pallas kernels for 0%

commit v1 on v0

v1 whole, which is shorter than its diff:
```python
import functools
import jax
import jax.numpy as jnp
from jax import lax
from jax.experimental import pallas as pl
from jax.experimental.pallas import tpu as pltpu
from jax.sharding import PartitionSpec as P

SLIDES = 3
LANES = 128
ANY = pl.BlockSpec(memory_space=pl.ANY)
BF = jnp.bfloat16
F32 = jnp.float32
VMEM_BYTES = 56 * 1024 * 1024
WIDTHS = (256, 128, 128)
ORDER = (
    "Y0 Y1 t0 e0",
    "Z0 L0 e1 Y2",
    "Z1 L1 t1 S0",
    "Z2 L2 e2 t2",
    "S1 e3 F0 m0",
    "P0 S2 Q0 F1",
    "P1 R0 Q1 G0",
    "R1 H0 F2 P2",
    "Q2 T0 R2 G1",
    "H1 T1 G2 H2",
    "T2",
)


def sds(shape, dtype):
    return jax.ShapeDtypeStruct(shape, dtype)


def whole(shape):
    zeros = (0,) * len(shape)
    return pl.BlockSpec(shape, lambda *_: zeros)


def xor_pairs(size, step):
    return [(n, n ^ step) for n in range(size)]


class Chain:
    def __init__(self, flags):
        self.flags = flags
        self.token = jnp.zeros((8, LANES), F32)

    def run(self, name, body, ins=(), outs=(), through=(), grid=(1,), scratch=()):
        n_in, n_out, n_thr = len(ins), len(outs), len(through) + 1

        def kernel(flags, *refs):
            in_refs = refs[:n_in]
            out_refs = refs[n_in + n_thr : n_in + n_thr + n_out]
            scratch_refs = refs[n_in + 2 * n_thr + n_out :]
            if body is not None:
                body(flags, in_refs, out_refs, *scratch_refs)

        carried = (*through, self.token)
        results = pl.pallas_call(
            kernel,
            out_shape=[s for s, _ in outs] + [sds(a.shape, a.dtype) for a in carried],
            grid_spec=pltpu.PrefetchScalarGridSpec(
                num_scalar_prefetch=1,
                grid=grid,
                in_specs=[s for _, s in ins] + [ANY] * n_thr,
                out_specs=[s for _, s in outs] + [ANY] * n_thr,
                scratch_shapes=list(scratch),
            ),
            input_output_aliases={1 + n_in + j: n_out + j for j in range(n_thr)},
            compiler_params=pltpu.CompilerParams(vmem_limit_bytes=VMEM_BYTES),
            name=name,
        )(self.flags, *[a for a, _ in ins], *carried)
        self.token = results[-1]
        return results[:-1]


def copy_all(copies, sems):
    made = [(c, pltpu.make_async_copy(s, d, sems.at[n])) for n, (c, s, d) in enumerate(copies)]
    for act in ("start", "wait"):
        for cond, copy in made:
            if cond is None:
                getattr(copy, act)()
            else:
                pl.when(cond)(getattr(copy, act))


def column(row):
    return jnp.transpose(jnp.broadcast_to(row, (LANES, row.shape[1])))


def per_device(sizes, logits, expression, spatial, slide_ids, spot_mask, densities):
    spot_size = sizes["spot"]
    rows, spots = logits.shape
    genes = spatial.shape[1]
    spots_all = spots * spot_size
    genes_all = genes * sizes["gene"]
    slots = sizes["gene"]
    quarter = spots // sizes["cell"]
    half = rows // 2
    cell, spot, gene = (lax.axis_index(a) for a in ("cell", "spot", "gene"))
    home = (gene // 2 == spot).astype(jnp.int32)
    side = (gene % 2).astype(jnp.int32)
    chain = Chain(jnp.stack([home, side, cell.astype(jnp.int32)]))
    run = chain.run
    offsets = [sum(WIDTHS[:n]) for n in range(len(WIDTHS))]
    chunks = range(len(WIDTHS))

    def over_core(v):
        return lax.ppermute(v, "cell", xor_pairs(4, 1))

    def over_x(v):
        return lax.ppermute(v, "cell", xor_pairs(4, 2))

    def over_gene(v, step):
        return lax.ppermute(v, "gene", xor_pairs(4, step))

    def over_spot(v, step=1):
        return lax.ppermute(v, "spot", xor_pairs(spot_size, step))

    def sum_spot(v):
        step = 1
        while step < spot_size:
            v = v + over_spot(v, step)
            step *= 2
        return v

    mask_f = spot_mask.astype(F32)
    order = cell ^ jnp.arange(sizes["cell"])

    def ordered(v):
        return v.reshape(sizes["cell"], quarter)[order].reshape(spots)

    lanes = jnp.arange(LANES)[None, :]
    ids_o, mask_o = ordered(slide_ids)[:, None], ordered(spot_mask)[:, None]
    member = jnp.where((lanes < SLIDES) & (lanes == ids_o) & (mask_o == 1), 1.0, 0.0)
    member = jnp.where(lanes == SLIDES, mask_o.astype(F32), member).astype(F32)
    dens_row = densities.reshape(1, rows)

    expr = expression.reshape(2, half * 2, genes) if spot_size == 2 else None
    st = {}

    def start_swap(c):
        w, o = WIDTHS[c], offsets[c] // WIDTHS[c]
        blk = (1, half, w)

        def body(fl, i, out):
            out[0][...] = i[0][...]
            out[1][...] = i[1][...]

        spec_a = pl.BlockSpec(
            blk, lambda g, f: (jnp.where(f[0] == 1, f[1], g), jnp.where(f[0] == 1, g, 0), o)
        )
        spec_b = pl.BlockSpec(blk, lambda g, f: (1 - f[1], g, o))
        out_spec = pl.BlockSpec(blk, lambda g, f: (g, 0, 0))
        ya, yb = run(
            f"swap{c}", body, [(expr, spec_a), (expr, spec_b)], [(sds((2, half, w), BF), out_spec)] * 2, grid=(2,)
        )
        st["y", c] = lax.ppermute(ya, "spot", xor_pairs(2, 1))
        st["n", c] = lax.ppermute(yb, ("spot", "gene"), [(0, 1), (1, 0), (6, 7), (7, 6)])

    def start_far(c):
        w, o = WIDTHS[c], offsets[c] // WIDTHS[c]
        blk = (1, half, w)

        def body(fl, i, out):
            @pl.when(fl[0] == 1)
            def _():
                out[0][...] = i[0][0]
                out[1][...] = i[1][0]

            @pl.when(fl[0] == 0)
            def _():
                out[0][...] = i[2][0]
                out[1][...] = i[3][0]

        specs = [
            pl.BlockSpec(blk, lambda g, f: (f[1], 0, 0)),
            pl.BlockSpec(blk, lambda g, f: (1 - f[1], 0, 0)),
            pl.BlockSpec(blk, lambda g, f: (f[1], 1, o)),
            pl.BlockSpec(blk, lambda g, f: (1 - f[1], 1, o)),
        ]
        y = st["y", c]
        a, b = run(
            f"far{c}", body, list(zip([y, y, expr, expr], specs)), [(sds((half, w), BF), whole((half, w)))] * 2
        )
        st["f2", c], st["f3", c] = over_gene(a, 2), over_gene(b, 3)

    def start_near(c):
        (st["n", c],) = run(f"near{c}", None, through=[st["n", c]])
        st["l", c] = lax.ppermute(st["n", c], ("spot", "gene"), [(0, 4), (1, 5), (6, 2), (7, 3)])

    def start_back(c):
        st["f2", c], st["f3", c] = run(f"back{c}", None, through=[st["f2", c], st["f3", c]])
        st["s2", c], st["s3", c] = over_spot(st["f2", c]), over_spot(st["f3", c])

    def totals(n):
        if n == 0:

            def body(fl, i, out):
                out[0][...] = jnp.zeros((8, spots), F32)
                out[0][0:1, :] = jnp.sum(jnp.exp(i[0][...].astype(F32)), axis=0, keepdims=True)
                out[0][1:2, :] = jnp.broadcast_to(jnp.sum(i[1][...]), (1, spots))

            (v,) = run(
                "totals", body, [(logits, whole(logits.shape)), (dens_row, whole(dens_row.shape))],
                [(sds((8, spots), F32), whole((8, spots)))],
            )
            st["tot"] = (v, over_core(v))
        elif n in (1, 2):

            def body(fl, i, out):
                out[0][...] = i[0][...] + i[1][...]

            sp = whole((8, spots))
            (v,) = run(f"totals{n}", body, [(a, sp) for a in st["tot"]], [(sds((8, spots), F32), sp)])
            st["tot"] = (v, over_x(v)) if n == 1 else (v, *[over_gene(v, s) for s in (1, 2, 3)])
        else:
            blk = LANES

            def body(fl, i, out):
                tot = (i[1][...] + i[2][...]) + (i[3][...] + i[4][...])
                out[3][...] = tot
                inv = 1.0 / tot[0:1, :]
                log_tot = jnp.log(tot[0:1, :])
                vals = i[0][...].astype(F32)
                prob = jnp.exp(vals) * inv
                ent = -jnp.sum(prob * (vals - log_tot))
                prob_t = jnp.transpose(prob)
                out[1][...] = jnp.broadcast_to(jnp.sum(prob_t, axis=0, keepdims=True), (8, blk))
                for q in range(sizes["cell"]):
                    at = pl.multiple_of((fl[2] ^ q) * quarter, quarter)
                    out[0][pl.ds(at, quarter), :] = prob_t[q * quarter : (q + 1) * quarter].astype(BF)

                @pl.when(pl.program_id(0) == 0)
                def _():
                    out[2][...] = jnp.zeros((8, LANES), F32)

                out[2][...] += ent

            sp = whole((8, spots))
            pt, mass, ent, tot = run(
                "prob", body,
                [(logits, pl.BlockSpec((blk, spots), lambda g, f: (g, 0)))] + [(a, sp) for a in st["tot"]],
                [
                    (sds((spots, rows), BF), pl.BlockSpec((spots, blk), lambda g, f: (0, g))),
                    (sds((8, rows), F32), pl.BlockSpec((8, blk), lambda g, f: (0, g))),
                    (sds((8, LANES), F32), whole((8, LANES))),
                    (sds((8, spots), F32), sp),
                ],
                grid=(rows // blk,),
            )
            st["pt"], st["ent"], st["tot"] = pt, ent, tot
            st["mass"] = [mass, over_spot(mass)] if spot_size == 2 else [sum_spot(mass)]

    def shares(_):
        masses = st["mass"]

        def body(fl, i, out):
            mass = i[2][0:1, :]
            for extra in i[3:]:
                mass = mass + extra[0:1, :]
            share = i[0][...] / i[1][1:2, 0:1]
            out[0][...] = jnp.broadcast_to(share / mass, (8, rows))
            kl = jnp.sum(share * (jnp.log(share) - jnp.log(mass / spots_all)))
            out[1][...] = jnp.broadcast_to(kl, (8, LANES))

        st["sm"], st["kl"] = run(
            "shares", body,
            [(dens_row, whole(dens_row.shape)), (st["tot"], whole((8, spots)))]
            + [(m, whole((8, rows))) for m in masses],
            [(sds((8, rows), F32), whole((8, rows))), (sds((8, LANES), F32), whole((8, LANES)))],
        )

    def target(n):
        blk = (quarter, genes)
        if n == 0:

            def body(fl, i, out):
                out[0][...] = i[0][...]

            (v,) = run(
                "target", body, [(spatial, pl.BlockSpec(blk, lambda g, f: (f[2], 0)))], [(sds(blk, BF), whole(blk))]
            )
            st["t"] = [v] + [over_gene(v, s) for s in (1, 2, 3)]
        elif n == 1:
            shape = (slots, *blk)

            def body(fl, i, out):
                for s in range(slots):
                    out[0][s] = i[s][...]

            (v,) = run("target1", body, [(a, whole(blk)) for a in st["t"]], [(sds(shape, BF), whole(shape))])
            st["t"] = [v, over_core(v), over_x(v)]
        else:
            (v,) = run("target2", None, through=[st["t"][2]])
            st["t"] = [st["t"][0], st["t"][1], v, over_core(v)]

    def forward(c):
        w = WIDTHS[c]
        wide = slots * w
        shape = (2, quarter, wide)
        outs = [
            (sds((rows, wide), BF), whole((rows, wide))),
            (sds(shape, F32), whole(shape)),
            (sds(shape, F32), whole(shape)),
        ]

        def product(pt, ef, keep, send):
            tile = 256

            @pl.loop(0, wide // tile)
            def _(n):
                at = pl.ds(pl.multiple_of(n * tile, tile), tile)
                acc = jnp.dot(pt[...], ef[:, at], preferred_element_type=F32)
                for q, ref in enumerate((keep, send, keep, send)):
                    ref[q // 2, :, at] = acc[q * quarter : (q + 1) * quarter]

        if spot_size == 2:
            col = pl.ds(offsets[c], w)

            def body(fl, i, out, sems):
                pt, e, y, n, l, f2, f3, s2, s3 = i
                ef = out[0]
                at_home, away = fl[0] == 1, fl[0] == 0
                top, low = pl.ds(0, half), pl.ds(half, half)
                copies = [
                    (at_home, e.at[fl[1], :, col], ef.at[:, pl.ds(0, w)]),
                    (away, y.at[0], ef.at[top, pl.ds(0, w)]),
                    (away, y.at[1], ef.at[low, pl.ds(0, w)]),
                ]
                for part, at in ((0, top), (1, low)):
                    copies += [
                        (at_home, n.at[part], ef.at[at, pl.ds(w, w)]),
                        (away, l.at[part], ef.at[at, pl.ds(w, w)]),
                    ]
                for s, direct, swapped in ((2, f2, s2), (3, f3, s3)):
                    cols = pl.ds(s * w, w)
                    copies += [
                        (at_home, direct, ef.at[low, cols]),
                        (at_home, swapped, ef.at[top, cols]),
                        (away, direct, ef.at[top, cols]),
                        (away, swapped, ef.at[low, cols]),
                    ]
                copy_all(copies, sems)
                product(pt, ef, out[1], out[2])

            names = ("y", "n", "l", "f2", "f3", "s2", "s3")
            ins = [(st["pt"], whole((spots, rows))), (expr, ANY)] + [(st[k, c], ANY) for k in names]
            scratch = [pltpu.SemaphoreType.DMA((16,))]
        else:

            def body(fl, i, out):
                for s in range(slots):
                    out[0][:, s * w : (s + 1) * w] = i[1 + s][...]
                product(i[0], *out)

            o = offsets[c] // w
            ins = [(st["pt"], whole((spots, rows)))] + [
                (a, pl.BlockSpec((rows, w), lambda *_: (0, o))) for a in st["pieces"]
            ]
            scratch = []
        st["e", c], keep, send = run(f"forward{c}", body, ins, outs, scratch=scratch)
        st["r", c] = (keep, over_core(send))

    def reduce_core(c):
        wide = slots * WIDTHS[c]
        shape, one = (2, quarter, wide), (quarter, wide)

        def body(fl, i, out):
            out[0][...] = i[0][0] + i[1][0]
            out[1][...] = i[0][1] + i[1][1]

        a, b = run(
            f"core{c}", body, [(v, whole(shape)) for v in st["r", c]], [(sds(one, F32), whole(one))] * 2
        )
        st["r", c] = (a, over_x(b))

    def reduce_x(c):
        w = WIDTHS[c]
        one, part = (quarter, slots * w), (quarter, w)

        def body(fl, i, out):
            for s in range(slots):
                at = slice(s * w, (s + 1) * w)
                out[s][...] = i[0][:, at] + i[1][:, at]

        parts = run(
            f"x{c}", body, [(v, whole(one)) for v in st["r", c]], [(sds(part, F32), whole(part))] * slots
        )
        st["r", c] = [parts[0]] + [over_gene(parts[s], s) for s in (1, 2, 3)]

    def reduce_gene(c):
        part = (quarter, WIDTHS[c])

        def body(fl, i, out):
            out[0][...] = (i[0][...] + i[1][...]) + (i[2][...] + i[3][...])

        (v,) = run(
            f"gene{c}", body, [(a, whole(part)) for a in st["r", c]], [(sds(part, F32), whole(part))]
        )
        st["r", c] = [v] + [over_gene(v, s) for s in (1, 2, 3)]

    def gather_x(c):
        w = WIDTHS[c]
        one, part = (quarter, slots * w), (quarter, w)

        def body(fl, i, out):
            for s in range(slots):
                out[0][:, s * w : (s + 1) * w] = i[s][...]

        (v,) = run(
            f"gather{c}", body, [(a, whole(part)) for a in st["r", c]], [(sds(one, F32), whole(one))]
        )
        st["p", c] = [v, over_core(v), over_x(v)]

    def gather_core(c):
        (v,) = run(f"gathercore{c}", None, through=[st["p", c][2]])
        st["p", c] = [st["p", c][0], st["p", c][1], v, over_core(v)]

    def stats(c):
        w = WIDTHS[c]
        wide, o = slots * w, offsets[c] // w
        n_blk = len(st["t"])
        first = c == 0

        def body(fl, i, out):
            preds, targets, memb = i[:n_blk], i[n_blk : 2 * n_blk], i[2 * n_blk]
            lane = lax.broadcasted_iota(jnp.int32, (quarter, LANES), 1)
            valid = jnp.sum(memb[:, SLIDES : SLIDES + 1])
            out[0][9:16, :] = jnp.broadcast_to(valid, (7, wide))
            for s in range(slots):
                at = slice(s * w, (s + 1) * w)
                rows_k = [jnp.zeros((1, w), F32) for _ in range(9)]
                for b in range(n_blk):
                    pr, ta = preds[b][:, at], targets[b][s].astype(F32)
                    prods = (pr * ta, pr * pr, ta * ta)
                    mb = slice(b * quarter, (b + 1) * quarter)
                    spot_vals = [jnp.sum(v, axis=1, keepdims=True) for v in prods]
                    new = jnp.where(lane == 0, spot_vals[0], 0.0)
                    new = jnp.where(lane == 1, spot_vals[1], new)
                    new = jnp.where(lane == 2, spot_vals[2], new)
                    if s > 0:
                        new = new + out[1][mb, :]
                    elif not first:
                        new = new + i[2 * n_blk + 1][mb, :]
                    out[1][mb, :] = new
                    for k in range(SLIDES):
                        col = memb[mb, k : k + 1]
                        for j, v in enumerate(prods):
                            rows_k[3 * j + k] += jnp.sum(col * v, axis=0, keepdims=True)
                for n, v in enumerate(rows_k):
                    out[0][n : n + 1, at] = v

        ins = [(a, whole((quarter, wide))) for a in st["p", c]]
        ins += [(a, pl.BlockSpec((slots, quarter, w), lambda *_: (0, 0, o))) for a in st["t"]]
        ins += [(member, whole((spots, LANES)))]
        if not first:
            ins += [(st["sp"], whole((spots, LANES)))]
        gs, st["sp"] = run(
            f"stats{c}", body, ins,
            [(sds((16, wide), F32), whole((16, wide))), (sds((spots, LANES), F32), whole((spots, LANES)))],
        )
        st["gs", c] = [gs, over_spot(gs)] if spot_size == 2 else [sum_spot(gs)]

    steps = {
        "Y": start_swap, "Z": start_far, "L": start_near, "S": start_back, "e": totals, "m": shares, "t": target,
        "F": forward, "P": reduce_core, "Q": reduce_x, "R": reduce_gene, "G": gather_x, "H": gather_core, "T": stats,
    }
    if spot_size != 2:
        full = lax.all_gather(expression, "spot", axis=0, tiled=True).reshape(slots, rows, genes)
        pieces = [lax.dynamic_index_in_dim(full, gene ^ s, 0, False) for s in range(slots)]
        st["pieces"] = [pieces[0]] + [over_gene(pieces[s], s) for s in (1, 2, 3)]
    for word in " ".join(ORDER).split():
        if spot_size == 2 or word[0] not in "YZLS":
            steps[word[0]](int(word[1]))

    row_blk = rows // 2
    n_blk = sizes["cell"]
    n_ch = len(WIDTHS)
    n_gs = len(st["gs", 0])

    def backward_body(fl, i, out, *grads):
        i = list(i)
        lg, tot, sm, memb, sp = i[:5]
        efs = i[5 : 5 + n_ch]
        gss = i[5 + n_ch : 5 + n_ch + n_ch * n_gs]
        preds = i[5 + n_ch + n_ch * n_gs : 5 + n_ch + n_ch * n_gs + n_ch * n_blk]
        targets = i[5 + n_ch + n_ch * n_gs + n_ch * n_blk :]

        @pl.when(pl.program_id(0) == 0)
        def _():
            scale = -1.0 / (SLIDES * genes_all)
            gene_sum = jnp.zeros((), F32)
            gene_rows = []
            for c in range(n_ch):
                g_all = gss[c * n_gs][...]
                for extra in gss[c * n_gs + 1 : (c + 1) * n_gs]:
                    g_all = g_all + extra[...]
                num, psq, tsq = g_all[0:3], g_all[3:6], g_all[6:9]
                p_floor, t_floor = jnp.maximum(psq, 1.0), jnp.maximum(tsq, 1.0)
                root = jnp.sqrt(p_floor * t_floor)
                cosine = num / root
                w_t = scale / root
                w_p = jnp.where(psq > 1.0, -scale * cosine / p_floor, 0.0)
                gene_rows.append((w_t, w_p))
                gene_sum += jnp.sum(cosine[:, 0 : WIDTHS[c]])
                if c == 0:
                    valid_total = jnp.maximum(g_all[9, 0], 1.0)
            spot_sum = jnp.zeros((), F32)
            for b in range(n_blk):
                mb = slice(b * quarter, (b + 1) * quarter)
                s_num = sp[mb, 0:1]
                s_p, s_t = sp[mb, 1:2] + 1e-06, sp[mb, 2:3] + 1e-06
                root = jnp.sqrt(s_p * s_t)
                cos_spot = s_num / root
                valid = memb[mb, SLIDES : SLIDES + 1]
                coef = -valid / valid_total
                spot_sum += jnp.sum(valid * cos_spot)
                c_t, c_p = coef / root, -coef * cos_spot / s_p
                cols = [memb[mb, k : k + 1] for k in range(SLIDES)]
                to = pl.ds(pl.multiple_of((fl[2] ^ b) * quarter, quarter), quarter)
                for c in range(n_ch):
                    w = WIDTHS[c]
                    w_t, w_p = gene_rows[c]
                    for s in range(slots):
                        at = slice(s * w, (s + 1) * w)
                        f_t, f_p = c_t, c_p
                        for k in range(SLIDES):
                            f_t = f_t + cols[k] * w_t[k : k + 1, at]
                            f_p = f_p + cols[k] * w_p[k : k + 1, at]
                        ta = targets[b][s, :, offsets[c] : offsets[c] + w].astype(F32)
                        pr = preds[c * n_blk + b][:, at]
                        grads[c][to, at] = (f_t * ta + f_p * pr).astype(BF)
            out[1][...] = jnp.zeros((8, spots), F32)
            lane = lax.broadcasted_iota(jnp.int32, (1, spots), 1)
            out[1][1:2, :] = jnp.where(lane == 0, gene_sum, jnp.where(lane == 1, spot_sum, 0.0))

        acc = jnp.zeros((row_blk, spots), F32)
        for c in range(n_ch):
            acc += lax.dot_general(
                efs[c][...], grads[c][...], (((1,), (1,)), ((), ())), preferred_element_type=F32
            )
        acc = acc - column(sm[0:1, :])[:, 0:1]
        out[0][...] = acc
        prob = jnp.exp(lg[...].astype(F32)) * (1.0 / tot[0:1, :])
        out[1][0:1, :] += jnp.sum(prob * acc, axis=0, keepdims=True)

    ins = [
        (logits, pl.BlockSpec((row_blk, spots), lambda g, f: (g, 0))),
        (st["tot"], whole((8, spots))),
        (st["sm"], pl.BlockSpec((8, row_blk), lambda g, f: (0, g))),
        (member, whole((spots, LANES))),
        (st["sp"], whole((spots, LANES))),
    ]
    ins += [(st["e", c], pl.BlockSpec((row_blk, slots * WIDTHS[c]), lambda g, f: (g, 0))) for c in chunks]
    ins += [(a, whole(a.shape)) for c in chunks for a in st["gs", c]]
    ins += [(a, whole(a.shape)) for c in chunks for a in st["p", c]]
    ins += [(a, whole(a.shape)) for a in st["t"]]
    grad_probs, part = run(
        "backward", backward_body, ins,
        [
            (sds((rows, spots), F32), pl.BlockSpec((row_blk, spots), lambda g, f: (g, 0))),
            (sds((8, spots), F32), whole((8, spots))),
        ],
        grid=(rows // row_blk,),
        scratch=[pltpu.VMEM((spots, slots * w), BF) for w in WIDTHS],
    )

    firsts = [jnp.where(a == 0, 1.0, 0.0) for a in (cell, spot, gene)]
    terms = jnp.stack(
        [
            part[1, 0] * firsts[0] * firsts[1],
            part[1, 1] * firsts[0] * firsts[2],
            st["kl"][0, 0] * firsts[1],
            st["ent"][0, 0],
        ]
    )
    v = jnp.concatenate([part[0], terms, jnp.zeros((4,), F32)])
    v = v + over_core(v)
    v = v + over_x(v)
    v = (v + over_gene(v, 1)) + (over_gene(v, 2) + over_gene(v, 3))
    inner = jnp.broadcast_to(v[None, :spots], (8, spots))

    def final_body(fl, i, out):
        prob = jnp.exp(i[0][...].astype(F32)) * (1.0 / i[1][0:1, :])
        out[0][...] = prob * (i[2][...] - i[3][0:1, :])

    blk = pl.BlockSpec((row_blk, spots), lambda g, f: (g, 0))
    (grad_logits,) = run(
        "final", final_body,
        [(logits, blk), (st["tot"], whole((8, spots))), (grad_probs, blk), (inner, whole((8, spots)))],
        [(sds((rows, spots), F32), blk)], grid=(rows // row_blk,),
    )
    sums = sum_spot(v[spots : spots + 4])
    valid_total = jnp.maximum(sum_spot(jnp.sum(mask_f)), 1.0)
    gene_term = sums[0] / (SLIDES * genes_all)
    spot_term = sums[1] / valid_total
    divergence = sums[2]
    entropy = sums[3] / spots_all
    loss_terms = jnp.stack([divergence - gene_term - spot_term, gene_term, spot_term, divergence, entropy])
    return (loss_terms, grad_logits)


def solution(mesh):
    return jax.shard_map(
        functools.partial(per_device, dict(mesh.shape)),
        mesh=mesh,
        in_specs=(
            P(("cell", "gene"), "spot"),
            P(("cell", "spot"), "gene"),
            P("spot", "gene"),
            P("spot"),
            P("spot"),
            P(("cell", "gene")),
        ),
        out_specs=(P(), P(("cell", "gene"), "spot")),
        check_vma=False,
    )
```

time: 936 us -> 473 us (0.51)
  waiting for transfers between devices: 682 us -> 169 us
  blocking collectives: 158 us -> 0 us
  Pallas kernels: 0 us -> 155 us
  starting transfers between devices: 0.16 us -> 108 us
  matrix products: 41.4 us -> 0 us
  other arithmetic: 22.4 us -> 2.28 us
  local copies, waits for them, and re-layouts: 11.3 us -> 29 us
  between operations: 19.7 us -> 7.54 us
    reduce_scatter x1 -> x0, waiting for transfers between devices: 374 us -> none  [per_device(): lax.psum_scatter(contract_genes(expr_block, grad_low), 'gene', scatter_di...]
    all_gather x2 -> x0, waiting for transfers between devices: 273 us -> none  [the longest x1 203 us: per_device(): prob_block = lax.all_gather(prob_low, 'gene', axis=0, tiled=True)]
    ppermute x0 -> x76, waiting for transfers between devices: none -> 169 us  [the longest x33 82.8 us: over_gene(): return lax.ppermute(v, 'gene', xor_pairs(4, step))]
    pallas_call x0 -> x43, Pallas kernels: none -> 155 us  [run(): pl.pallas_call(kernel, out_shape=[s for s, _ in outs] + [sds(a.shape, a.d...]
    psum x5 -> x0, blocking collectives: 123 us -> none  [the longest x1 37.1 us: per_device(): lax.psum(jnp.stack([gene_local, spot_local, kl_local, entropy_local]), ('...]
    ppermute x0 -> x76, starting transfers between devices: none -> 108 us  [the longest x33 60.5 us: over_gene(): return lax.ppermute(v, 'gene', xor_pairs(4, step))]
    dot_general x7 -> x0, matrix products: 41.4 us -> none  [the longest x1 19.1 us: contract_genes(): lax.dot_general(left_block, right_block, (((1,), (1,)), ((), ())), prefer...]
    pmax x1 -> x0, blocking collectives: 35.1 us -> none  [per_device(): col_max = lax.pmax(local_max, ('cell', 'gene'))]
  transfers between devices with their start and end apart: 4 -> 76, of which waited for: 4 -> 24; matrix products, arithmetic and copies ran while one was open for 1% -> 1% of each run, Pallas kernels for 0% -> 21%
where the time goes in v1:
time: 473 us; the launch traced here: 471 us
  waiting for transfers between devices  169 us (36%)
  Pallas kernels  155 us (33%)
  starting transfers between devices  108 us (23%)
  local copies, waits for them, and re-layouts  29 us (6%)
  between operations  7.54 us (2%)
    pallas_call x43, Pallas kernels, run(): pl.pallas_call(kernel, out_shape=[s for s, _ in outs] + [sds(a.shape, a.d...  155 us
    ppermute x33, waiting for transfers between devices, over_gene(): return lax.ppermute(v, 'gene', xor_pairs(4, step))  82.8 us
    ppermute x33, starting transfers between devices, over_gene(): return lax.ppermute(v, 'gene', xor_pairs(4, step))  60.5 us
    ppermute x3, waiting for transfers between devices, start_swap(): st['y', c] = lax.ppermute(ya, 'spot', xor_pairs(2, 1))  35.8 us
    ppermute x12, waiting for transfers between devices, over_spot(): return lax.ppermute(v, 'spot', xor_pairs(spot_size, step))  24.5 us
    ppermute x9, waiting for transfers between devices, over_x(): return lax.ppermute(v, 'cell', xor_pairs(4, 2))  23.8 us
    unnamed x178, local copies, waits for them, and re-layouts  19 us
    ppermute x12, starting transfers between devices, over_spot(): return lax.ppermute(v, 'spot', xor_pairs(spot_size, step))  14.4 us
  transfers between devices with their start and end apart: 76, of which 24 were waited for; matrix products, arithmetic and copies ran while one was open for 1% of the time, Pallas kernels for 21%

profile of v1, /device:TPU:0, one launch (start us, length us, event | category | flops | bytes accessed | tf_op | source)
XLA Modules:
  0.0 470.7 jit_solution(17083283931403461536)
XLA Ops:
  1.9 3.7 swap0.1
  5.6 3.0 collective-permute-start.2
  8.6 3.5 collective-permute-start.1
  12.1 3.2 swap1.1
  21.8 3.9 totals.1
  25.7 15.5 %collective-permute-done.2.refs_0_.refs_1_.refs_2_ = bf16[2,1408,256]{2,1,0:T(8,128)(2,1)S(1)} collective-permute-done((bf16[2,1408,256]{2,1,0:T(8,128)(2,1)}, bf16[2,1408,256]{2,1,0:T(8,128)(2,1)S(1)}, u32[]{:S(2)}, u32[]{:S(2)}) %collective-permute-start.2) | collective-permute-done | bytes 1441824 | tf_op jit(solution)/shard_map/ppermute | solution.py:159
  42.3 3.8 far0.1
  46.1 3.1 collective-permute-start.6
  49.2 13.5 %collective-permute-done.10.refs_3_ = bf16[128,512]{1,0:T(8,128)(2,1)S(1)} collective-permute-done((bf16[128,512]{1,0:T(8,128)(2,1)}, bf16[128,512]{1,0:T(8,128)(2,1)S(1)}, u32[]{:S(2)}, u32[]{:S(2)}) %collective-permute-start.10) | collective-permute-done | bytes 131104 | tf_op jit(solution)/shard_map/ppermute | solution.py:116
  62.7 18.5 %collective-permute-done.8.refs_1_ = bf16[128,512]{1,0:T(8,128)(2,1)S(1)} collective-permute-done((bf16[128,512]{1,0:T(8,128)(2,1)S(1)}, bf16[128,512]{1,0:T(8,128)(2,1)S(1)}, u32[]{:S(2)}, u32[]{:S(2)}) %collective-permute-start.8) | collective-permute-done | bytes 131104 | tf_op jit(solution)/shard_map/ppermute | solution.py:116
  81.3 3.9 collective-permute-start.7
  85.8 18.6 %collective-permute-done.9.refs_2_ = bf16[128,512]{1,0:T(8,128)(2,1)S(1)} collective-permute-done((bf16[128,512]{1,0:T(8,128)(2,1)S(1)}, bf16[128,512]{1,0:T(8,128)(2,1)S(1)}, u32[]{:S(2)}, u32[]{:S(2)}) %collective-permute-start.9) | collective-permute-done | bytes 131104 | tf_op jit(solution)/shard_map/ppermute | solution.py:116
  104.4 5.2 %collective-permute-start.20 = (bf16[2,1408,256]{2,1,0:T(8,128)(2,1)}, bf16[2,1408,256]{2,1,0:T(8,128)(2,1)S(1)}, u32[]{:S(2)}, u32[]{:S(2)}) collective-permute-start(bf16[2,1408,256]{2,1,0:T(8,128)(2,1)} %get-tuple-element.157.refs_3_), channel_id=1, source_target_pairs={{0,4},{1,5},{6,2},{7,3},{8,12},{9,13},{14,10},{15,11},{16,20},{17,... | collective-permute-start | bytes 4325384 | tf_op jit(solution)/shard_map/ppermute | solution.py:191
  111.6 3.0 swap2.1
  116.7 3.0 far1.1
  125.4 4.7 collective-permute-start.21
  130.1 7.0 %collective-permute-done.16.refs_0_ = bf16[1408,128]{1,0:T(8,128)(2,1)S(1)} collective-permute-done((bf16[1408,128]{1,0:T(8,128)(2,1)}, bf16[1408,128]{1,0:T(8,128)(2,1)S(1)}, u32[]{:S(2)}, u32[]{:S(2)}) %collective-permute-start.16) | collective-permute-done | bytes 360480 | tf_op jit(solution)/shard_map/ppermute | solution.py:116
  137.1 20.2 %collective-permute-done.5.refs_0_.refs_1_.refs_2_ = bf16[2,1408,128]{2,1,0:T(8,128)(2,1)S(1)} collective-permute-done((bf16[2,1408,128]{2,1,0:T(8,128)(2,1)}, bf16[2,1408,128]{2,1,0:T(8,128)(2,1)S(1)}, u32[]{:S(2)}, u32[]{:S(2)}) %collective-permute-start.5) | collective-permute-done | bytes 720928 | tf_op jit(solution)/shard_map/ppermute | solution.py:159
  158.8 4.5 collective-permute-start.17
  163.3 2.9 far2.1
  169.3 4.2 collective-permute-start.14
  173.5 3.4 collective-permute-start.15
  179.9 15.6 %prob.1 = (bf16[512,2816]{1,0:T(8,128)(2,1)}, f32[8,2816]{1,0:T(8,128)}, f32[8,128]{1,0:T(8,128)}, f32[8,512]{1,0:T(8,128)}, f32[8,128]{1,0:T(8,128)}) custom-call(s32[3]{0:T(128)} %pad_add_fusion.flags, bf16[2816,512]{1,0:T(8,128)(2,1)} %refs_0_.9, f32[8,512]{1,0:T(8,128)} %get-tuple-element.147.refs_1_, ...), custom_call_target="tpu_custom_call", output_to_operand_aliasing={{4}: (6, {})} | custom-call | tf_op jit(solution)/shard_map/prob/pallas_call | solution.py:60
  197.1 11.4 %forward0.1 = (bf16[2816,1024]{1,0:T(8,128)(2,1)}, f32[2,128,1024]{2,1,0:T(8,128)}, f32[2,128,1024]{2,1,0:T(8,128)}, f32[8,128]{1,0:T(8,128)}) custom-call(s32[3]{0:T(128)} %pad_add_fusion.flags, bf16[512,2816]{1,0:T(8,128)(2,1)} %get-tuple-element.156.refs_0_, bf16[2,2816,512]{2,1,0:T(8,128)(2,1)} %bitcast.38, ...), custom_call_target="tpu_custom_call", output_to_operand_aliasing={{3}: (10, {})} | custom-call | tf_op jit(solution)/shard_map/forward0/pallas_call | solution.py:60
  208.8 3.2 collective-permute-start.33
  212.1 17.8 %collective-permute-done.19.refs_3_ = f32[8,2816]{1,0:T(8,128)S(1)} collective-permute-done((f32[8,2816]{1,0:T(8,128)S(1)}, f32[8,2816]{1,0:T(8,128)S(1)}, u32[]{:S(2)}, u32[]{:S(2)}) %collective-permute-start.19) | collective-permute-done | bytes 90144 | tf_op jit(solution)/shard_map/ppermute | solution.py:119
  234.0 3.2 core0.1
  237.8 4.5 collective-permute-start.25
  244.4 5.9 %collective-permute-done.25.refs_1_ = bf16[1408,128]{1,0:T(8,128)(2,1)S(1)} collective-permute-done((bf16[1408,128]{1,0:T(8,128)(2,1)S(1)}, bf16[1408,128]{1,0:T(8,128)(2,1)S(1)}, u32[]{:S(2)}, u32[]{:S(2)}) %collective-permute-start.25) | collective-permute-done | bytes 360480 | tf_op jit(solution)/shard_map/ppermute | solution.py:116
  255.2 4.2 collective-permute-done.35.refs_8_
  260.2 7.3 %forward1.1 = (bf16[2816,512]{1,0:T(8,128)(2,1)}, f32[2,128,512]{2,1,0:T(8,128)}, f32[2,128,512]{2,1,0:T(8,128)}, f32[8,128]{1,0:T(8,128)}) custom-call(s32[3]{0:T(128)} %pad_add_fusion.flags, bf16[512,2816]{1,0:T(8,128)(2,1)} %get-tuple-element.156.refs_0_, bf16[2,2816,512]{2,1,0:T(8,128)(2,1)} %bitcast.39, ...), custom_call_target="tpu_custom_call", output_to_operand_aliasing={{3}: (10, {})} | custom-call | tf_op jit(solution)/shard_map/forward1/pallas_call | solution.py:60
  267.6 3.4 collective-permute-start.30
  274.5 2.7 core1.1
  278.6 3.8 collective-permute-start.23
  295.3 6.9 %collective-permute-done.38.refs_2_ = f32[128,256]{1,0:T(8,128)S(1)} collective-permute-done((f32[128,256]{1,0:T(8,128)}, f32[128,256]{1,0:T(8,128)S(1)}, u32[]{:S(2)}, u32[]{:S(2)}) %collective-permute-start.38) | collective-permute-done | bytes 131104 | tf_op jit(solution)/shard_map/ppermute | solution.py:116
  313.5 3.0 collective-permute-start.43
  321.3 4.0 collective-permute-done.44.refs_3_
  330.8 7.5 %forward2.1 = (bf16[2816,512]{1,0:T(8,128)(2,1)}, f32[2,128,512]{2,1,0:T(8,128)}, f32[2,128,512]{2,1,0:T(8,128)}, f32[8,128]{1,0:T(8,128)}) custom-call(s32[3]{0:T(128)} %pad_add_fusion.flags, bf16[512,2816]{1,0:T(8,128)(2,1)} %get-tuple-element.156.refs_0_, bf16[2,2816,512]{2,1,0:T(8,128)(2,1)} %bitcast.40, ...), custom_call_target="tpu_custom_call", output_to_operand_aliasing={{3}: (10, {})} | custom-call | tf_op jit(solution)/shard_map/forward2/pallas_call | solution.py:60
  340.6 2.7 core2.1
  344.5 7.4 %collective-permute-done.46.refs_1_ = f32[128,512]{1,0:T(8,128)S(1)} collective-permute-done((f32[128,512]{1,0:T(8,128)}, f32[128,512]{1,0:T(8,128)S(1)}, u32[]{:S(2)}, u32[]{:S(2)}) %collective-permute-start.46) | collective-permute-done | bytes 262176 | tf_op jit(solution)/shard_map/ppermute | solution.py:113
  364.1 6.0 %stats0.1 = (f32[16,1024]{1,0:T(8,128)}, f32[512,128]{1,0:T(8,128)}, f32[8,128]{1,0:T(8,128)}) custom-call(s32[3]{0:T(128)} %pad_add_fusion.flags, f32[128,1024]{1,0:T(8,128)} %get-tuple-element.192.refs_0_.refs_14_, f32[128,1024]{1,0:T(8,128)} %collective-permute-done.50.refs_1_.refs_15_, ...), custom_call_target="tpu_custom_call", output_to_operand_aliasing={{2}: (10, {})} | custom-call | tf_op jit(solution)/shard_map/stats0/pallas_call | solution.py:60
  376.5 6.0 %collective-permute-done.61.refs_0_ = f32[128,512]{1,0:T(8,128)S(1)} collective-permute-done((f32[128,512]{1,0:T(8,128)}, f32[128,512]{1,0:T(8,128)S(1)}, u32[]{:S(2)}, u32[]{:S(2)}) %collective-permute-start.61) | collective-permute-done | bytes 262176 | tf_op jit(solution)/shard_map/ppermute | solution.py:113
  389.3 5.0 %stats1.1 = (f32[16,512]{1,0:T(8,128)}, f32[512,128]{1,0:T(8,128)}, f32[8,128]{1,0:T(8,128)}) custom-call(s32[3]{0:T(128)} %pad_add_fusion.flags, f32[128,512]{1,0:T(8,128)} %get-tuple-element.217.refs_0_.refs_18_, f32[128,512]{1,0:T(8,128)} %copy-done.30, f32[128,512]{1,0:T(8,128)} %get-tuple-element.219.refs_2_.refs_20_, ...), custom_call_target="tpu_custom_call", output_to_operand_aliasing={{2}: (11, {})} | custom-call | tf_op jit(solution)/shard_map/stats1/pallas_call | solution.py:60
  398.2 7.3 %collective-permute-done.64.refs_0_ = f32[128,512]{1,0:T(8,128)S(1)} collective-permute-done((f32[128,512]{1,0:T(8,128)}, f32[128,512]{1,0:T(8,128)S(1)}, u32[]{:S(2)}, u32[]{:S(2)}) %collective-permute-start.64) | collective-permute-done | bytes 262176 | tf_op jit(solution)/shard_map/ppermute | solution.py:113
  409.9 4.9 %stats2.1 = (f32[16,512]{1,0:T(8,128)}, f32[512,128]{1,0:T(8,128)}, f32[8,128]{1,0:T(8,128)}) custom-call(s32[3]{0:T(128)} %pad_add_fusion.flags, f32[128,512]{1,0:T(8,128)} %get-tuple-element.223.refs_0_.refs_22_, f32[128,512]{1,0:T(8,128)} %copy-done.32, f32[128,512]{1,0:T(8,128)} %get-tuple-element.225.refs_2_.refs_24_, ...), custom_call_target="tpu_custom_call", output_to_operand_aliasing={{2}: (11, {})} | custom-call | tf_op jit(solution)/shard_map/stats2/pallas_call | solution.py:60
  419.8 19.4 %backward.1 = (f32[2816,512]{1,0:T(8,128)}, f32[8,512]{1,0:T(8,128)}, f32[8,128]{1,0:T(8,128)}) custom-call(s32[3]{0:T(128)} %pad_add_fusion.flags, bf16[2816,512]{1,0:T(8,128)(2,1)} %refs_0_.9, f32[8,512]{1,0:T(8,128)} %get-tuple-element.154.refs_1_, f32[8,2816]{1,0:T(8,128)} %get-tuple-element.162.refs_2_, ...), custom_call_target="tpu_custom_call", output_to_operand_aliasing={{2}: (31, {})} | custom-call | tf_op jit(solution)/shard_map/backward/pallas_call | solution.py:60
  444.9 3.1 collective-permute-done.70
  459.7 6.4 %final.1 = (f32[2816,512]{1,0:T(8,128)}, f32[8,128]{1,0:T(8,128)}) custom-call(s32[3]{0:T(128)} %pad_add_fusion.flags, bf16[2816,512]{1,0:T(8,128)(2,1)} %refs_0_.9, f32[8,512]{1,0:T(8,128)} %get-tuple-element.154.refs_1_, f32[2816,512]{1,0:T(8,128)} %get-tuple-element.239.refs_2_, ...), custom_call_target="tpu_custom_call", output_to_operand_aliasing={{1}: (5, {})} | custom-call | tf_op jit(solution)/shard_map/final/pallas_call | solution.py:60
  (352 shorter events, 138.3 us)
Async XLA Ops:
  5.6 35.6 %collective-permute-start.2 = (bf16[2,1408,256]{2,1,0:T(8,128)(2,1)}, bf16[2,1408,256]{2,1,0:T(8,128)(2,1)S(1)}, u32[]{:S(2)}, u32[]{:S(2)}) collective-permute-start(bf16[2,1408,256]{2,1,0:T(8,128)(2,1)} %get-tuple-element.127), channel_id=1, source_target_pairs={{0,4},{4,0},{1,5},{5,1},{2,6},{6,2},{3,7},{7,3},{8,12},{12,8},{9,1... | collective-permute-start | bytes 4325384 | tf_op jit(solution)/shard_map/ppermute | solution.py:159
  8.6 72.7 %collective-permute-start.1 = (bf16[2,1408,256]{2,1,0:T(8,128)(2,1)}, bf16[2,1408,256]{2,1,0:T(8,128)(2,1)S(1)}, u32[]{:S(2)}, u32[]{:S(2)}) collective-permute-start(bf16[2,1408,256]{2,1,0:T(8,128)(2,1)} %get-tuple-element.126), channel_id=1, source_target_pairs={{0,1},{1,0},{6,7},{7,6},{8,9},{9,8},{14,15},{15,14},{16,17},{17,16... | collective-permute-start | bytes 4325384 | tf_op jit(solution)/shard_map/ppermute | solution.py:160
  15.3 99.4 %collective-permute-start.12 = (bf16[2,1408,128]{2,1,0:T(8,128)(2,1)}, bf16[2,1408,128]{2,1,0:T(8,128)(2,1)S(1)}, u32[]{:S(2)}, u32[]{:S(2)}) collective-permute-start(bf16[2,1408,128]{2,1,0:T(8,128)(2,1)} %get-tuple-element.139), channel_id=1, source_target_pairs={{0,4},{4,0},{1,5},{5,1},{2,6},{6,2},{3,7},{7,3},{8,12},{12,8},{9,1... | collective-permute-start | bytes 2162696 | tf_op jit(solution)/shard_map/ppermute | solution.py:159
  15.3 99.4 %collective-permute-start.11 = (bf16[2,1408,128]{2,1,0:T(8,128)(2,1)}, bf16[2,1408,128]{2,1,0:T(8,128)(2,1)S(1)}, u32[]{:S(2)}, u32[]{:S(2)}) collective-permute-start(bf16[2,1408,128]{2,1,0:T(8,128)(2,1)} %get-tuple-element.138), channel_id=1, source_target_pairs={{0,1},{1,0},{6,7},{7,6},{8,9},{9,8},{14,15},{15,14},{16,17},{17,16... | collective-permute-start | bytes 2162696 | tf_op jit(solution)/shard_map/ppermute | solution.py:160
  19.8 42.9 %collective-permute-start.10 = (bf16[128,512]{1,0:T(8,128)(2,1)}, bf16[128,512]{1,0:T(8,128)(2,1)S(1)}, u32[]{:S(2)}, u32[]{:S(2)}) collective-permute-start(bf16[128,512]{1,0:T(8,128)(2,1)} %get-tuple-element.137.refs_0_), channel_id=1, source_target_pairs={{0,3},{1,2},{2,1},{3,0},{4,7},{5,6},{6,5},{7,4},{8,11},{9,10},{10,... | collective-permute-start | bytes 393224 | tf_op jit(solution)/shard_map/ppermute | solution.py:116
  46.1 73.7 %collective-permute-start.6 = (bf16[1408,256]{1,0:T(8,128)(2,1)}, bf16[1408,256]{1,0:T(8,128)(2,1)S(1)}, u32[]{:S(2)}, u32[]{:S(2)}) collective-permute-start(bf16[1408,256]{1,0:T(8,128)(2,1)} %get-tuple-element.135), channel_id=1, source_target_pairs={{0,2},{1,3},{2,0},{3,1},{4,6},{5,7},{6,4},{7,5},{8,10},{9,11},{10,... | collective-permute-start | bytes 2162696 | tf_op jit(solution)/shard_map/ppermute | solution.py:116
  62.7 18.5 %collective-permute-start.8 = (bf16[128,512]{1,0:T(8,128)(2,1)S(1)}, bf16[128,512]{1,0:T(8,128)(2,1)S(1)}, u32[]{:S(2)}, u32[]{:S(2)}) collective-permute-start(bf16[128,512]{1,0:T(8,128)(2,1)S(1)} %copy-done.48), channel_id=1, source_target_pairs={{0,1},{1,0},{2,3},{3,2},{4,5},{5,4},{6,7},{7,6},{8,9},{9,8},{10,11... | collective-permute-start | bytes 393224 | tf_op jit(solution)/shard_map/ppermute | solution.py:116
  81.2 23.1 %collective-permute-start.9 = (bf16[128,512]{1,0:T(8,128)(2,1)S(1)}, bf16[128,512]{1,0:T(8,128)(2,1)S(1)}, u32[]{:S(2)}, u32[]{:S(2)}) collective-permute-start(bf16[128,512]{1,0:T(8,128)(2,1)S(1)} %copy-done.48), channel_id=1, source_target_pairs={{0,2},{1,3},{2,0},{3,1},{4,6},{5,7},{6,4},{7,5},{8,10},{9,11},{10,... | collective-permute-start | bytes 393224 | tf_op jit(solution)/shard_map/ppermute | solution.py:116
  81.3 38.6 %collective-permute-start.7 = (bf16[1408,256]{1,0:T(8,128)(2,1)}, bf16[1408,256]{1,0:T(8,128)(2,1)S(1)}, u32[]{:S(2)}, u32[]{:S(2)}) collective-permute-start(bf16[1408,256]{1,0:T(8,128)(2,1)} %get-tuple-element.136), channel_id=1, source_target_pairs={{0,3},{1,2},{2,1},{3,0},{4,7},{5,6},{6,5},{7,4},{8,11},{9,10},{10,... | collective-permute-start | bytes 2162696 | tf_op jit(solution)/shard_map/ppermute | solution.py:116
  104.4 91.1 %collective-permute-start.20 = (bf16[2,1408,256]{2,1,0:T(8,128)(2,1)}, bf16[2,1408,256]{2,1,0:T(8,128)(2,1)S(1)}, u32[]{:S(2)}, u32[]{:S(2)}) collective-permute-start(bf16[2,1408,256]{2,1,0:T(8,128)(2,1)} %get-tuple-element.157.refs_3_), channel_id=1, source_target_pairs={{0,4},{1,5},{6,2},{7,3},{8,12},{9,13},{14,10},{15,11},{16,20},{17,... | collective-permute-start | bytes 4325384 | tf_op jit(solution)/shard_map/ppermute | solution.py:191
  114.6 42.7 %collective-permute-start.5 = (bf16[2,1408,128]{2,1,0:T(8,128)(2,1)}, bf16[2,1408,128]{2,1,0:T(8,128)(2,1)S(1)}, u32[]{:S(2)}, u32[]{:S(2)}) collective-permute-start(bf16[2,1408,128]{2,1,0:T(8,128)(2,1)} %get-tuple-element.134), channel_id=1, source_target_pairs={{0,4},{4,0},{1,5},{5,1},{2,6},{6,2},{3,7},{7,3},{8,12},{12,8},{9,1... | collective-permute-start | bytes 2162696 | tf_op jit(solution)/shard_map/ppermute | solution.py:159
  114.7 44.1 %collective-permute-start.4 = (bf16[2,1408,128]{2,1,0:T(8,128)(2,1)}, bf16[2,1408,128]{2,1,0:T(8,128)(2,1)S(1)}, u32[]{:S(2)}, u32[]{:S(2)}) collective-permute-start(bf16[2,1408,128]{2,1,0:T(8,128)(2,1)} %get-tuple-element.133), channel_id=1, source_target_pairs={{0,1},{1,0},{6,7},{7,6},{8,9},{9,8},{14,15},{15,14},{16,17},{17,16... | collective-permute-start | bytes 2162696 | tf_op jit(solution)/shard_map/ppermute | solution.py:160
  119.8 17.3 %collective-permute-start.16 = (bf16[1408,128]{1,0:T(8,128)(2,1)}, bf16[1408,128]{1,0:T(8,128)(2,1)S(1)}, u32[]{:S(2)}, u32[]{:S(2)}) collective-permute-start(bf16[1408,128]{1,0:T(8,128)(2,1)} %get-tuple-element.148), channel_id=1, source_target_pairs={{0,2},{1,3},{2,0},{3,1},{4,6},{5,7},{6,4},{7,5},{8,10},{9,11},{10,... | collective-permute-start | bytes 1081352 | tf_op jit(solution)/shard_map/ppermute | solution.py:116
  125.4 70.1 %collective-permute-start.21 = (bf16[1408,256]{1,0:T(8,128)(2,1)}, bf16[1408,256]{1,0:T(8,128)(2,1)S(1)}, u32[]{:S(2)}, u32[]{:S(2)}) collective-permute-start(bf16[1408,256]{1,0:T(8,128)(2,1)} %get-tuple-element.158.refs_5_), channel_id=1, source_target_pairs={{0,4},{4,0},{1,5},{5,1},{2,6},{6,2},{3,7},{7,3},{8,12},{12,8},{9,1... | collective-permute-start | bytes 2162696 | tf_op jit(solution)/shard_map/ppermute | solution.py:119
  137.1 58.4 %collective-permute-start.22 = (bf16[1408,256]{1,0:T(8,128)(2,1)}, bf16[1408,256]{1,0:T(8,128)(2,1)S(1)}, u32[]{:S(2)}, u32[]{:S(2)}) collective-permute-start(bf16[1408,256]{1,0:T(8,128)(2,1)} %get-tuple-element.159.refs_6_), channel_id=1, source_target_pairs={{0,4},{4,0},{1,5},{5,1},{2,6},{6,2},{3,7},{7,3},{8,12},{12,8},{9,1... | collective-permute-start | bytes 2162696 | tf_op jit(solution)/shard_map/ppermute | solution.py:119
  157.3 12.0 %collective-permute-start.18 = (bf16[4,128,512]{2,1,0:T(8,128)(2,1)}, bf16[4,128,512]{2,1,0:T(8,128)(2,1)S(1)}, u32[]{:S(2)}, u32[]{:S(2)}) collective-permute-start(bf16[4,128,512]{2,1,0:T(8,128)(2,1)} %get-tuple-element.150.refs_4_.refs_26_), channel_id=1, source_target_pairs={{0,16},{8,24},{16,0},{24,8},{1,17},{9,25},{17,1},{25,9},{2,18},{10... | collective-permute-start | bytes 1572872 | tf_op jit(solution)/shard_map/ppermute | solution.py:113
  158.8 10.5 %collective-permute-start.17 = (bf16[1408,128]{1,0:T(8,128)(2,1)}, bf16[1408,128]{1,0:T(8,128)(2,1)S(1)}, u32[]{:S(2)}, u32[]{:S(2)}) collective-permute-start(bf16[1408,128]{1,0:T(8,128)(2,1)} %get-tuple-element.149), channel_id=1, source_target_pairs={{0,3},{1,2},{2,1},{3,0},{4,7},{5,6},{6,5},{7,4},{8,11},{9,10},{10,... | collective-permute-start | bytes 1081352 | tf_op jit(solution)/shard_map/ppermute | solution.py:116
  208.6 24.4 %collective-permute-start.26 = (f32[2,128,1024]{2,1,0:T(8,128)}, f32[2,128,1024]{2,1,0:T(8,128)S(1)}, u32[]{:S(2)}, u32[]{:S(2)}) collective-permute-start(f32[2,128,1024]{2,1,0:T(8,128)} %get-tuple-element.167), channel_id=1, source_target_pairs={{0,8},{8,0},{16,24},{24,16},{1,9},{9,1},{17,25},{25,17},{2,10},{10... | collective-permute-start | bytes 3145736 | tf_op jit(solution)/shard_map/ppermute | solution.py:110
  208.6 33.7 %collective-permute-start.24 = (bf16[1408,128]{1,0:T(8,128)(2,1)S(1)}, bf16[1408,128]{1,0:T(8,128)(2,1)S(1)}, u32[]{:S(2)}, u32[]{:S(2)}) collective-permute-start(bf16[1408,128]{1,0:T(8,128)(2,1)S(1)} %copy-done.85), channel_id=1, source_target_pairs={{0,2},{1,3},{2,0},{3,1},{4,6},{5,7},{6,4},{7,5},{8,10},{9,11},{10,... | collective-permute-start | bytes 1081352 | tf_op jit(solution)/shard_map/ppermute | solution.py:116
  208.8 46.4 %collective-permute-start.33 = (bf16[2,1408,128]{2,1,0:T(8,128)(2,1)S(1)}, bf16[2,1408,128]{2,1,0:T(8,128)(2,1)S(1)}, u32[]{:S(2)}, u32[]{:S(2)}) collective-permute-start(bf16[2,1408,128]{2,1,0:T(8,128)(2,1)S(1)} %copy-done.13), channel_id=1, source_target_pairs={{0,4},{1,5},{6,2},{7,3},{8,12},{9,13},{14,10},{15,11},{16,20},{17,... | collective-permute-start | bytes 2162696 | tf_op jit(solution)/shard_map/ppermute | solution.py:191
  212.1 17.8 %collective-permute-start.19 = (f32[8,2816]{1,0:T(8,128)S(1)}, f32[8,2816]{1,0:T(8,128)S(1)}, u32[]{:S(2)}, u32[]{:S(2)}) collective-permute-start(f32[8,2816]{1,0:T(8,128)S(1)} %copy-done.58), channel_id=1, source_target_pairs={{0,4},{4,0},{1,5},{5,1},{2,6},{6,2},{3,7},{7,3},{8,12},{12,8},{9,1... | collective-permute-start | bytes 270344 | tf_op jit(solution)/shard_map/ppermute | solution.py:119
  237.2 14.5 %collective-permute-start.29 = (f32[128,1024]{1,0:T(8,128)}, f32[128,1024]{1,0:T(8,128)S(1)}, u32[]{:S(2)}, u32[]{:S(2)}) collective-permute-start(f32[128,1024]{1,0:T(8,128)} %get-tuple-element.173), channel_id=1, source_target_pairs={{0,16},{8,24},{16,0},{24,8},{1,17},{9,25},{17,1},{25,9},{2,18},{10... | collective-permute-start | bytes 1572872 | tf_op jit(solution)/shard_map/ppermute | solution.py:113
  237.8 12.6 %collective-permute-start.25 = (bf16[1408,128]{1,0:T(8,128)(2,1)S(1)}, bf16[1408,128]{1,0:T(8,128)(2,1)S(1)}, u32[]{:S(2)}, u32[]{:S(2)}) collective-permute-start(bf16[1408,128]{1,0:T(8,128)(2,1)S(1)} %copy-done.84), channel_id=1, source_target_pairs={{0,3},{1,2},{2,1},{3,0},{4,7},{5,6},{6,5},{7,4},{8,11},{9,10},{10,... | collective-permute-start | bytes 1081352 | tf_op jit(solution)/shard_map/ppermute | solution.py:116
  242.3 12.9 %collective-permute-start.34 = (bf16[1408,128]{1,0:T(8,128)(2,1)S(1)}, bf16[1408,128]{1,0:T(8,128)(2,1)S(1)}, u32[]{:S(2)}, u32[]{:S(2)}) collective-permute-start(bf16[1408,128]{1,0:T(8,128)(2,1)S(1)} %copy-done.22), channel_id=1, source_target_pairs={{0,4},{4,0},{1,5},{5,1},{2,6},{6,2},{3,7},{7,3},{8,12},{12,8},{9,1... | collective-permute-start | bytes 1081352 | tf_op jit(solution)/shard_map/ppermute | solution.py:119
  242.3 17.1 %collective-permute-start.35 = (bf16[1408,128]{1,0:T(8,128)(2,1)S(1)}, bf16[1408,128]{1,0:T(8,128)(2,1)S(1)}, u32[]{:S(2)}, u32[]{:S(2)}) collective-permute-start(bf16[1408,128]{1,0:T(8,128)(2,1)S(1)} %copy-done.26), channel_id=1, source_target_pairs={{0,4},{4,0},{1,5},{5,1},{2,6},{6,2},{3,7},{7,3},{8,12},{12,8},{9,1... | collective-permute-start | bytes 1081352 | tf_op jit(solution)/shard_map/ppermute | solution.py:119
  267.6 14.8 %collective-permute-start.30 = (f32[128,256]{1,0:T(8,128)S(1)}, f32[128,256]{1,0:T(8,128)S(1)}, u32[]{:S(2)}, u32[]{:S(2)}) collective-permute-start(f32[128,256]{1,0:T(8,128)S(1)} %copy-done.88), channel_id=1, source_target_pairs={{0,1},{1,0},{2,3},{3,2},{4,5},{5,4},{6,7},{7,6},{8,9},{9,8},{10,11... | collective-permute-start | bytes 393224 | tf_op jit(solution)/shard_map/ppermute | solution.py:116
  271.0 12.9 %collective-permute-start.31 = (f32[128,256]{1,0:T(8,128)S(1)}, f32[128,256]{1,0:T(8,128)S(1)}, u32[]{:S(2)}, u32[]{:S(2)}) collective-permute-start(f32[128,256]{1,0:T(8,128)S(1)} %copy-done.87), channel_id=1, source_target_pairs={{0,2},{1,3},{2,0},{3,1},{4,6},{5,7},{6,4},{7,5},{8,10},{9,11},{10,... | collective-permute-start | bytes 393224 | tf_op jit(solution)/shard_map/ppermute | solution.py:116
  272.2 11.7 %collective-permute-start.32 = (f32[128,256]{1,0:T(8,128)S(1)}, f32[128,256]{1,0:T(8,128)S(1)}, u32[]{:S(2)}, u32[]{:S(2)}) collective-permute-start(f32[128,256]{1,0:T(8,128)S(1)} %copy-done.86), channel_id=1, source_target_pairs={{0,3},{1,2},{2,1},{3,0},{4,7},{5,6},{6,5},{7,4},{8,11},{9,10},{10,... | collective-permute-start | bytes 393224 | tf_op jit(solution)/shard_map/ppermute | solution.py:116
  277.1 15.0 %collective-permute-start.40 = (f32[128,512]{1,0:T(8,128)}, f32[128,512]{1,0:T(8,128)S(1)}, u32[]{:S(2)}, u32[]{:S(2)}) collective-permute-start(f32[128,512]{1,0:T(8,128)} %get-tuple-element.189), channel_id=1, source_target_pairs={{0,16},{8,24},{16,0},{24,8},{1,17},{9,25},{17,1},{25,9},{2,18},{10... | collective-permute-start | bytes 786440 | tf_op jit(solution)/shard_map/ppermute | solution.py:113
  278.6 51.0 %collective-permute-start.23 = (bf16[2,1408,128]{2,1,0:T(8,128)(2,1)S(1)}, bf16[2,1408,128]{2,1,0:T(8,128)(2,1)S(1)}, u32[]{:S(2)}, u32[]{:S(2)}) collective-permute-start(bf16[2,1408,128]{2,1,0:T(8,128)(2,1)S(1)} %copy-done.15), channel_id=1, source_target_pairs={{0,4},{1,5},{6,2},{7,3},{8,12},{9,13},{14,10},{15,11},{16,20},{17,... | collective-permute-start | bytes 2162696 | tf_op jit(solution)/shard_map/ppermute | solution.py:191
  289.6 12.6 %collective-permute-start.38 = (f32[128,256]{1,0:T(8,128)}, f32[128,256]{1,0:T(8,128)S(1)}, u32[]{:S(2)}, u32[]{:S(2)}) collective-permute-start(f32[128,256]{1,0:T(8,128)} %get-tuple-element.187.refs_0_), channel_id=1, source_target_pairs={{0,2},{1,3},{2,0},{3,1},{4,6},{5,7},{6,4},{7,5},{8,10},{9,11},{10,... | collective-permute-start | bytes 393224 | tf_op jit(solution)/shard_map/ppermute | solution.py:116
  290.7 11.5 %collective-permute-start.39 = (f32[128,256]{1,0:T(8,128)}, f32[128,256]{1,0:T(8,128)S(1)}, u32[]{:S(2)}, u32[]{:S(2)}) collective-permute-start(f32[128,256]{1,0:T(8,128)} %get-tuple-element.187.refs_0_), channel_id=1, source_target_pairs={{0,3},{1,2},{2,1},{3,0},{4,7},{5,6},{6,5},{7,4},{8,11},{9,10},{10,... | collective-permute-start | bytes 393224 | tf_op jit(solution)/shard_map/ppermute | solution.py:116
  305.5 22.7 %collective-permute-start.41 = (f32[128,1024]{1,0:T(8,128)}, f32[128,1024]{1,0:T(8,128)S(1)}, u32[]{:S(2)}, u32[]{:S(2)}) collective-permute-start(f32[128,1024]{1,0:T(8,128)} %get-tuple-element.192.refs_0_.refs_14_), channel_id=1, source_target_pairs={{0,16},{8,24},{16,0},{24,8},{1,17},{9,25},{17,1},{25,9},{2,18},{10... | collective-permute-start | bytes 1572872 | tf_op jit(solution)/shard_map/ppermute | solution.py:113
  306.9 22.7 %collective-permute-start.27 = (bf16[1408,128]{1,0:T(8,128)(2,1)S(1)}, bf16[1408,128]{1,0:T(8,128)(2,1)S(1)}, u32[]{:S(2)}, u32[]{:S(2)}) collective-permute-start(bf16[1408,128]{1,0:T(8,128)(2,1)S(1)} %copy-done.24), channel_id=1, source_target_pairs={{0,4},{4,0},{1,5},{5,1},{2,6},{6,2},{3,7},{7,3},{8,12},{12,8},{9,1... | collective-permute-start | bytes 1081352 | tf_op jit(solution)/shard_map/ppermute | solution.py:119
  308.2 21.4 %collective-permute-start.28 = (bf16[1408,128]{1,0:T(8,128)(2,1)S(1)}, bf16[1408,128]{1,0:T(8,128)(2,1)S(1)}, u32[]{:S(2)}, u32[]{:S(2)}) collective-permute-start(bf16[1408,128]{1,0:T(8,128)(2,1)S(1)} %copy-done.28), channel_id=1, source_target_pairs={{0,4},{4,0},{1,5},{5,1},{2,6},{6,2},{3,7},{7,3},{8,12},{12,8},{9,1... | collective-permute-start | bytes 1081352 | tf_op jit(solution)/shard_map/ppermute | solution.py:119
  339.0 16.8 %collective-permute-start.52 = (bf16[4,128,512]{2,1,0:T(8,128)(2,1)S(1)}, bf16[4,128,512]{2,1,0:T(8,128)(2,1)S(1)}, u32[]{:S(2)}, u32[]{:S(2)}) collective-permute-start(bf16[4,128,512]{2,1,0:T(8,128)(2,1)S(1)} %copy-done.4), channel_id=1, source_target_pairs={{0,8},{8,0},{16,24},{24,16},{1,9},{9,1},{17,25},{25,17},{2,10},{10... | collective-permute-start | bytes 1572872 | tf_op jit(solution)/shard_map/ppermute | solution.py:110
  339.5 17.6 %collective-permute-start.53 = (bf16[4,128,512]{2,1,0:T(8,128)(2,1)S(1)}, bf16[4,128,512]{2,1,0:T(8,128)(2,1)S(1)}, u32[]{:S(2)}, u32[]{:S(2)}) collective-permute-start(bf16[4,128,512]{2,1,0:T(8,128)(2,1)S(1)} %copy-done.2), channel_id=1, source_target_pairs={{0,8},{8,0},{16,24},{24,16},{1,9},{9,1},{17,25},{25,17},{2,10},{10... | collective-permute-start | bytes 1572872 | tf_op jit(solution)/shard_map/ppermute | solution.py:110
  339.6 19.5 %collective-permute-start.50 = (f32[128,1024]{1,0:T(8,128)S(1)}, f32[128,1024]{1,0:T(8,128)}, u32[]{:S(2)}, u32[]{:S(2)}) collective-permute-start(f32[128,1024]{1,0:T(8,128)S(1)} %copy-done.20), channel_id=1, source_target_pairs={{0,8},{8,0},{16,24},{24,16},{1,9},{9,1},{17,25},{25,17},{2,10},{10... | collective-permute-start | bytes 1572872 | tf_op jit(solution)/shard_map/ppermute | solution.py:110
  340.1 20.2 %collective-permute-start.51 = (f32[128,1024]{1,0:T(8,128)S(1)}, f32[128,1024]{1,0:T(8,128)}, u32[]{:S(2)}, u32[]{:S(2)}) collective-permute-start(f32[128,1024]{1,0:T(8,128)S(1)} %copy-done.11), channel_id=1, source_target_pairs={{0,8},{8,0},{16,24},{24,16},{1,9},{9,1},{17,25},{25,17},{2,10},{10... | collective-permute-start | bytes 1572872 | tf_op jit(solution)/shard_map/ppermute | solution.py:110
  355.8 17.1 %collective-permute-start.57 = (f32[128,128]{1,0:T(8,128)S(1)}, f32[128,128]{1,0:T(8,128)S(1)}, u32[]{:S(2)}, u32[]{:S(2)}) collective-permute-start(f32[128,128]{1,0:T(8,128)S(1)} %copy-done.62), channel_id=1, source_target_pairs={{0,1},{1,0},{2,3},{3,2},{4,5},{5,4},{6,7},{7,6},{8,9},{9,8},{10,11... | collective-permute-start | bytes 196616 | tf_op jit(solution)/shard_map/ppermute | solution.py:116
  357.1 15.8 %collective-permute-start.58 = (f32[128,128]{1,0:T(8,128)S(1)}, f32[128,128]{1,0:T(8,128)S(1)}, u32[]{:S(2)}, u32[]{:S(2)}) collective-permute-start(f32[128,128]{1,0:T(8,128)S(1)} %copy-done.62), channel_id=1, source_target_pairs={{0,2},{1,3},{2,0},{3,1},{4,6},{5,7},{6,4},{7,5},{8,10},{9,11},{10,... | collective-permute-start | bytes 196616 | tf_op jit(solution)/shard_map/ppermute | solution.py:116
  359.2 13.8 %collective-permute-start.59 = (f32[128,128]{1,0:T(8,128)S(1)}, f32[128,128]{1,0:T(8,128)S(1)}, u32[]{:S(2)}, u32[]{:S(2)}) collective-permute-start(f32[128,128]{1,0:T(8,128)S(1)} %copy-done.62), channel_id=1, source_target_pairs={{0,3},{1,2},{2,1},{3,0},{4,7},{5,6},{6,5},{7,4},{8,11},{9,10},{10,... | collective-permute-start | bytes 196616 | tf_op jit(solution)/shard_map/ppermute | solution.py:116
  376.5 11.9 %collective-permute-start.60 = (f32[128,512]{1,0:T(8,128)}, f32[128,512]{1,0:T(8,128)S(1)}, u32[]{:S(2)}, u32[]{:S(2)}) collective-permute-start(f32[128,512]{1,0:T(8,128)} %get-tuple-element.217.refs_0_.refs_18_), channel_id=1, source_target_pairs={{0,8},{8,0},{16,24},{24,16},{1,9},{9,1},{17,25},{25,17},{2,10},{10... | collective-permute-start | bytes 786440 | tf_op jit(solution)/shard_map/ppermute | solution.py:110
  384.0 10.2 %collective-permute-start.54 = (f32[128,128]{1,0:T(8,128)}, f32[128,128]{1,0:T(8,128)S(1)}, u32[]{:S(2)}, u32[]{:S(2)}) collective-permute-start(f32[128,128]{1,0:T(8,128)} %get-tuple-element.214.refs_0_), channel_id=1, source_target_pairs={{0,1},{1,0},{2,3},{3,2},{4,5},{5,4},{6,7},{7,6},{8,9},{9,8},{10,11... | collective-permute-start | bytes 196616 | tf_op jit(solution)/shard_map/ppermute | solution.py:116
  398.2 10.9 %collective-permute-start.63 = (f32[128,512]{1,0:T(8,128)}, f32[128,512]{1,0:T(8,128)S(1)}, u32[]{:S(2)}, u32[]{:S(2)}) collective-permute-start(f32[128,512]{1,0:T(8,128)} %get-tuple-element.223.refs_0_.refs_22_), channel_id=1, source_target_pairs={{0,8},{8,0},{16,24},{24,16},{1,9},{9,1},{17,25},{25,17},{2,10},{10... | collective-permute-start | bytes 786440 | tf_op jit(solution)/shard_map/ppermute | solution.py:110
  407.0 12.2 %collective-permute-start.66 = (f32[16,1024]{1,0:T(8,128)S(1)}, f32[16,1024]{1,0:T(8,128)S(1)}, u32[]{:S(2)}, u32[]{:S(2)}) collective-permute-start(f32[16,1024]{1,0:T(8,128)S(1)} %copy-done.60), channel_id=1, source_target_pairs={{0,4},{4,0},{1,5},{5,1},{2,6},{6,2},{3,7},{7,3},{8,12},{12,8},{9,1... | collective-permute-start | bytes 196616 | tf_op jit(solution)/shard_map/ppermute | solution.py:119
  408.3 10.8 %collective-permute-start.67 = (f32[16,512]{1,0:T(8,128)}, f32[16,512]{1,0:T(8,128)S(1)}, u32[]{:S(2)}, u32[]{:S(2)}) collective-permute-start(f32[16,512]{1,0:T(8,128)} %get-tuple-element.233.refs_10_), channel_id=1, source_target_pairs={{0,4},{4,0},{1,5},{5,1},{2,6},{6,2},{3,7},{7,3},{8,12},{12,8},{9,1... | collective-permute-start | bytes 98312 | tf_op jit(solution)/shard_map/ppermute | solution.py:119
  448.0 10.0 %collective-permute-start.71 = (f32[520]{0:T(1024)S(1)}, f32[520]{0:T(1024)S(1)}, u32[]{:S(2)}, u32[]{:S(2)}) collective-permute-start(f32[520]{0:T(1024)S(1)} %add.40), channel_id=1, source_target_pairs={{0,1},{1,0},{2,3},{3,2},{4,5},{5,4},{6,7},{7,6},{8,9},{9,8},{10,11... | collective-permute-start | bytes 6248 | tf_op jit(solution)/shard_map/ppermute | solution.py:116
  (117 other events, 1368.2 us)

commit v2 on v1

v2 whole, which is shorter than its diff:
```python
import functools
import jax
import jax.numpy as jnp
from jax import lax
from jax.experimental import pallas as pl
from jax.experimental.pallas import tpu as pltpu
from jax.sharding import PartitionSpec as P

SLIDES = 3
LANES = 128
ANY = pl.BlockSpec(memory_space=pl.ANY)
BF = jnp.bfloat16
F32 = jnp.float32
VMEM_BYTES = 64 * 1024 * 1024
WIDTHS = (128, 128, 128, 128)
GROUPS = ((0, 1), (2, 3))
ORDER = (
    "Y0 e0 Y1 w:ez1+ez2+ez3",
    "Y2 A0 a0 e3",
    "b0 A1 Y3 w:f20+f30+n0",
    "a1 A2 w:f21+f31+n1 a2",
    "S0 A3 w:f22+f32+n2 a3",
    "S1 w:s0 S2 w:s1",
    "F0 w:f23+f33+n3 S3 f0",
    "t0 P0 w:s2 t1",
    "Q0 w:s3 F1 f1",
    "P1 R0 t2 Q1",
    "W0 R1 H0 W1",
    "T0 H1 m0 T1",
)


def sds(shape, dtype):
    return jax.ShapeDtypeStruct(shape, dtype)


def whole(shape):
    zeros = (0,) * len(shape)
    return pl.BlockSpec(shape, lambda *_: zeros)


def xor_pairs(size, step):
    return [(n, n ^ step) for n in range(size)]


class Chain:
    def __init__(self, flags):
        self.flags = flags
        self.token = jnp.zeros((8, LANES), F32)

    def run(self, name, body, ins=(), outs=(), after=(), through=(), grid=(1,), scratch=()):
        ins = [*ins, *((a, ANY) for a in after)]
        carried = (*through, self.token)
        n_in, n_out, n_thr = len(ins), len(outs), len(carried)

        def kernel(flags, *refs):
            in_refs = refs[:n_in]
            out_refs = refs[n_in + n_thr : n_in + n_thr + n_out]
            scratch_refs = refs[n_in + 2 * n_thr + n_out :]
            if body is not None:
                body(flags, in_refs, out_refs, *scratch_refs)

        results = pl.pallas_call(
            kernel,
            out_shape=[s for s, _ in outs] + [sds(a.shape, a.dtype) for a in carried],
            grid_spec=pltpu.PrefetchScalarGridSpec(
                num_scalar_prefetch=1,
                grid=grid,
                in_specs=[s for _, s in ins] + [ANY] * n_thr,
                out_specs=[s for _, s in outs] + [ANY] * n_thr,
                scratch_shapes=list(scratch),
            ),
            input_output_aliases={1 + n_in + j: n_out + j for j in range(n_thr)},
            compiler_params=pltpu.CompilerParams(vmem_limit_bytes=VMEM_BYTES),
            cost_estimate=pl.CostEstimate(flops=0, bytes_accessed=0, transcendentals=0),
            name=name,
        )(self.flags, *[a for a, _ in ins], *carried)
        self.token = results[-1]
        return results[:-1]


def copy_all(copies, sems):
    made = [(c, pltpu.make_async_copy(s, d, sems.at[n])) for n, (c, s, d) in enumerate(copies)]
    for act in ("start", "wait"):
        for cond, copy in made:
            if cond is None:
                getattr(copy, act)()
            else:
                pl.when(cond)(getattr(copy, act))


def column(row):
    return jnp.transpose(jnp.broadcast_to(row, (LANES, row.shape[1])))


def per_device(sizes, logits, expression, spatial, slide_ids, spot_mask, densities):
    spot_size = sizes["spot"]
    rows, spots = logits.shape
    genes = spatial.shape[1]
    spots_all = spots * spot_size
    genes_all = genes * sizes["gene"]
    slots = sizes["gene"]
    quarter = spots // sizes["cell"]
    half = rows // 2
    cell, spot, gene = (lax.axis_index(a) for a in ("cell", "spot", "gene"))
    home = (gene // 2 == spot).astype(jnp.int32)
    side = (gene % 2).astype(jnp.int32)
    chain = Chain(jnp.stack([home, side, cell, gene, spot]).astype(jnp.int32))
    run = chain.run
    offsets = [sum(WIDTHS[:n]) for n in range(len(WIDTHS))]
    chunks = range(len(WIDTHS))
    group_width = [sum(WIDTHS[c] for c in g) for g in GROUPS]

    def over_core(v):
        return lax.ppermute(v, "cell", xor_pairs(4, 1))

    def over_x(v):
        return lax.ppermute(v, "cell", xor_pairs(4, 2))

    def over_gene(v, step):
        return lax.ppermute(v, "gene", xor_pairs(4, step))

    def over_spot(v, step=1):
        return lax.ppermute(v, "spot", xor_pairs(spot_size, step))

    def sum_spot(v):
        step = 1
        while step < spot_size:
            v = v + over_spot(v, step)
            step *= 2
        return v

    ids_row, mask_row = slide_ids.reshape(1, spots), spot_mask.reshape(1, spots)
    dens_row = densities.reshape(1, rows)

    expr = expression.reshape(2, half * 2, genes) if spot_size == 2 else None
    st, sent = {}, {}

    def start_swap(c):
        w, o = WIDTHS[c], offsets[c] // WIDTHS[c]

        def body(fl, i, out):
            out[0][...] = i[0][...]

        (v,) = run(
            f"swap{c}", body, [(expr, pl.BlockSpec((1, rows, w), lambda g, f: (g, 0, o)))],
            [(sds((2, rows, w), BF), pl.BlockSpec((1, rows, w), lambda g, f: (g, 0, 0)))], grid=(2,),
        )
        sent[f"y{c}"] = over_spot(v)

    def start_along(c):
        w, o = WIDTHS[c], offsets[c] // WIDTHS[c]
        blk, one = (1, half, w), (half, w)

        def body(fl, i, out):
            @pl.when(fl[0] == 1)
            def _():
                out[0][...] = i[0][0]
                out[1][...] = i[1][0]
                out[2][0] = i[2][0]
                out[2][1] = i[3][0]

            @pl.when(fl[0] == 0)
            def _():
                out[0][...] = i[4][0]
                out[1][...] = i[5][0]
                out[2][0] = i[6][0]
                out[2][1] = i[7][0]

        def at(same, part, col):
            return pl.BlockSpec(blk, lambda g, f: (f[1] if same else 1 - f[1], part, col))

        y = sent[f"y{c}"]
        ins = [(y, at(True, 0, 0)), (y, at(False, 0, 0)), (expr, at(False, 0, o)), (expr, at(False, 1, o))]
        ins += [(expr, at(True, 1, o)), (expr, at(False, 1, o)), (y, at(False, 0, 0)), (y, at(False, 1, 0))]
        outs = [(sds(one, BF), whole(one))] * 2 + [(sds((2, half, w), BF), whole((2, half, w)))]
        st["along", c] = run(f"along{c}", body, ins, outs)

    def along_send(c):
        a, b, n = run(f"alongsend{c}", None, through=st["along", c])
        sent[f"f2{c}"], sent[f"f3{c}"], sent[f"n{c}"] = over_gene(a, 2), over_gene(b, 3), over_gene(n, 1)

    def start_back(c):
        w = WIDTHS[c]

        def body(fl, i, out):
            out[0][0] = i[0][...]
            out[0][1] = i[1][...]

        one = whole((half, w))
        (st["f", c],) = run(
            f"back{c}", body, [(sent[f"f2{c}"], one), (sent[f"f3{c}"], one)], [(sds((2, half, w), BF), whole((2, half, w)))]
        )
        sent[f"s{c}"] = over_spot(st["f", c])

    def wait_for(name):
        run("wait", None, after=[sent[n] for n in name.split("+")])

    def members_of(_):
        def body(fl, i, out):
            ids, valid = column(i[0][...].astype(F32)), column(i[1][...].astype(F32))
            lane = lax.broadcasted_iota(jnp.int32, (spots, LANES), 1)
            inside = (lane < SLIDES) & (lane.astype(F32) == ids) & (valid == 1.0)
            value = jnp.where(inside, 1.0, jnp.where(lane == SLIDES, valid, 0.0))
            for q in range(sizes["cell"]):
                at = pl.multiple_of((fl[2] ^ q) * quarter, quarter)
                out[0][pl.ds(at, quarter), :] = value[q * quarter : (q + 1) * quarter]

        row, tall = whole((1, spots)), whole((spots, LANES))
        (st["member"],) = run("member", body, [(ids_row, row), (mask_row, row)], [(sds((spots, LANES), F32), tall)])

    def totals(n):
        sp = whole((8, spots))
        if n == 0:

            def body(fl, i, out):
                out[0][...] = jnp.zeros((8, spots), F32)
                out[0][0:1, :] = jnp.sum(jnp.exp(i[0][...].astype(F32)), axis=0, keepdims=True)
                out[0][1:2, :] = jnp.broadcast_to(jnp.sum(i[1][...]), (1, spots))

            ins = [(logits, whole(logits.shape)), (dens_row, whole(dens_row.shape))]
            (v,) = run("totals", body, ins, [(sds((8, spots), F32), sp)])
            st["tot"] = lax.psum(v, "cell")
            for s in (1, 2, 3):
                sent[f"ez{s}"] = over_gene(st["tot"], s)
        else:
            blk = 2 * LANES

            def body(fl, i, out):
                tot = (i[1][...] + i[2][...]) + (i[3][...] + i[4][...])
                out[3][...] = tot
                inv = 1.0 / tot[0:1, :]
                log_tot = jnp.log(tot[0:1, :])
                vals = i[0][...].astype(F32)
                prob = jnp.exp(vals) * inv
                prob_t = jnp.transpose(prob.astype(BF))
                for q in range(sizes["cell"]):
                    at = pl.multiple_of((fl[2] ^ q) * quarter, quarter)
                    out[0][pl.ds(at, quarter), :] = prob_t[q * quarter : (q + 1) * quarter]
                folded = sum(prob[:, n : n + LANES] for n in range(0, spots, LANES))
                row_sums = jnp.sum(jnp.transpose(folded), axis=0, keepdims=True)
                out[1][...] = jnp.broadcast_to(row_sums, (8, blk))

                @pl.when(pl.program_id(0) == 0)
                def _():
                    out[2][...] = jnp.zeros((8, spots), F32)

                out[2][0:1, :] -= jnp.sum(prob * (vals - log_tot), axis=0, keepdims=True)

            parts = [st["tot"]] + [sent[f"ez{s}"] for s in (1, 2, 3)]
            pt, mass, ent, st["tot"] = run(
                "prob", body,
                [(logits, pl.BlockSpec((blk, spots), lambda g, f: (g, 0)))] + [(a, sp) for a in parts],
                [
                    (sds((spots, rows), BF), pl.BlockSpec((spots, blk), lambda g, f: (0, g))),
                    (sds((8, rows), F32), pl.BlockSpec((8, blk), lambda g, f: (0, g))),
                    (sds((8, spots), F32), sp),
                    (sds((8, spots), F32), sp),
                ],
                grid=(rows // blk,),
            )
            st["pt"], st["ent"] = pt, ent
            st["mass"] = mass if spot_size == 2 else sum_spot(mass)
            if spot_size == 2:
                sent["my"] = over_spot(mass)

    def shares(_):
        masses = [st["mass"]] + ([sent["my"]] if spot_size == 2 else [])

        def body(fl, i, out):
            mass = i[2][0:1, :]
            for extra in i[3:]:
                mass = mass + extra[0:1, :]
            share = i[0][...] / i[1][1:2, 0:1]
            out[0][...] = column(share / mass)
            kl = jnp.sum(share * (jnp.log(share) - jnp.log(mass / spots_all)))
            out[1][...] = jnp.broadcast_to(kl, (8, LANES))

        st["sm"], st["kl"] = run(
            "shares", body,
            [(dens_row, whole(dens_row.shape)), (st["tot"], whole((8, spots)))]
            + [(m, whole((8, rows))) for m in masses],
            [(sds((rows, LANES), F32), whole((rows, LANES))), (sds((8, LANES), F32), whole((8, LANES)))],
        )

    def target(n):
        blk = (quarter, genes)
        if n == 0:

            def body(fl, i, out):
                out[0][...] = i[0][...]

            (v,) = run(
                "target", body, [(spatial, pl.BlockSpec(blk, lambda g, f: (f[2], 0)))], [(sds(blk, BF), whole(blk))]
            )
            st["t"] = v
            for s in (1, 2, 3):
                sent[f"tz{s}"] = over_gene(v, s)
        elif n == 1:
            shape = (slots, *blk)

            def body(fl, i, out):
                for s in range(slots):
                    out[0][s] = i[s][...]

            parts = [st["t"]] + [sent[f"tz{s}"] for s in (1, 2, 3)]
            (v,) = run("target1", body, [(a, whole(blk)) for a in parts], [(sds(shape, BF), whole(shape))])
            st["t"], sent["tc"], sent["tx"] = v, over_core(v), over_x(v)
        else:
            run("target2", None, after=[sent["tx"]])
            sent["tc2"] = over_core(sent["tx"])

    def forward(g):
        members, wide_all = GROUPS[g], group_width[g] * slots
        shape = (2, quarter, wide_all)
        outs = [(sds((rows, slots * WIDTHS[c]), BF), whole((rows, slots * WIDTHS[c]))) for c in members]
        outs += [(sds(shape, F32), whole(shape))] * 2

        def product(pt, efs, keep, send):
            done = 0
            for c, ef in zip(members, efs):
                w = WIDTHS[c]
                acc = jnp.dot(pt[...], ef[...], preferred_element_type=F32)
                for q, ref in enumerate((keep, send, keep, send)):
                    rows_q = acc[q * quarter : (q + 1) * quarter]
                    for s in range(slots):
                        base = s * group_width[g] + done
                        ref[q // 2, :, base : base + w] = rows_q[:, s * w : (s + 1) * w]
                done += w

        if spot_size == 2:

            def body(fl, i, out, sems):
                pt, e = i[:2]
                at_home, away = fl[0] == 1, fl[0] == 0
                top, low = pl.ds(0, half), pl.ds(half, half)
                copies = []
                for m, c in enumerate(members):
                    w, ef = WIDTHS[c], out[m]
                    y, n, f, s = i[2 + 4 * m : 6 + 4 * m]
                    copies += [
                        (at_home, e.at[fl[1], :, pl.ds(offsets[c], w)], ef.at[:, pl.ds(0, w)]),
                        (away, y.at[fl[1]], ef.at[:, pl.ds(0, w)]),
                        (None, n.at[0], ef.at[top, pl.ds(w, w)]),
                        (None, n.at[1], ef.at[low, pl.ds(w, w)]),
                    ]
                    for part in (0, 1):
                        cols = pl.ds((2 + part) * w, w)
                        copies += [
                            (at_home, f.at[part], ef.at[low, cols]),
                            (at_home, s.at[part], ef.at[top, cols]),
                            (away, f.at[part], ef.at[top, cols]),
                            (away, s.at[part], ef.at[low, cols]),
                        ]
                copy_all(copies, sems)
                product(pt, out[: len(members)], *out[len(members) :])

            ins = [(st["pt"], whole((spots, rows))), (expr, ANY)]
            ins += [
                (a, ANY)
                for c in members
                for a in (sent[f"y{c}"], sent[f"n{c}"], st["f", c], sent[f"s{c}"])
            ]
            scratch = [pltpu.SemaphoreType.DMA((12 * len(members),))]
        else:

            def body(fl, i, out):
                for m, c in enumerate(members):
                    w = WIDTHS[c]
                    for s in range(slots):
                        out[m][:, s * w : (s + 1) * w] = i[1 + m * slots + s][...]
                product(i[0], out[: len(members)], *out[len(members) :])

            def at_chunk(c):
                return pl.BlockSpec((rows, WIDTHS[c]), lambda *_: (0, offsets[c] // WIDTHS[c]))

            ins = [(st["pt"], whole((spots, rows)))] + [(a, at_chunk(c)) for c in members for a in st["pieces"]]
            scratch = []
        *efs, keep, send = run(f"forward{g}", body, ins, outs, scratch=scratch)
        for c, ef in zip(members, efs):
            st["e", c] = ef
        st["r", g], st["send", g] = keep, send

    def forward_send(g):
        (send,) = run(f"send{g}", None, through=[st["send", g]])
        sent[f"rc{g}"] = over_core(send)

    def reduce_core(g):
        wide = slots * group_width[g]
        shape, one = (2, quarter, wide), (quarter, wide)

        def body(fl, i, out):
            out[0][...] = i[0][0] + i[1][0]
            out[1][...] = i[0][1] + i[1][1]

        ins = [(st["r", g], whole(shape)), (sent[f"rc{g}"], whole(shape))]
        st["r", g], b = run(f"core{g}", body, ins, [(sds(one, F32), whole(one))] * 2)
        sent[f"rx{g}"] = over_x(b)

    def reduce_x(g):
        w = group_width[g]
        one, part = (quarter, slots * w), (quarter, w)

        def body(fl, i, out):
            for s in range(slots):
                at = slice(s * w, (s + 1) * w)
                out[s][...] = i[0][:, at] + i[1][:, at]

        ins = [(st["r", g], whole(one)), (sent[f"rx{g}"], whole(one))]
        st["r", g], *parts = run(f"x{g}", body, ins, [(sds(part, F32), whole(part))] * slots)
        for s in (1, 2, 3):
            sent[f"rz{s}{g}"] = over_gene(parts[s - 1], s)

    def reduce_gene(g):
        part = (quarter, group_width[g])

        def body(fl, i, out):
            out[0][...] = (i[0][...] + i[1][...]) + (i[2][...] + i[3][...])

        parts = [st["r", g]] + [sent[f"rz{s}{g}"] for s in (1, 2, 3)]
        (v,) = run(f"gene{g}", body, [(a, whole(part)) for a in parts], [(sds(part, F32), whole(part))])
        st["r", g] = v
        for s in (1, 2, 3):
            sent[f"gz{s}{g}"] = over_gene(v, s)

    def gather_x(g):
        w = group_width[g]
        one, part = (quarter, slots * w), (quarter, w)

        def body(fl, i, out):
            for s in range(slots):
                out[0][:, s * w : (s + 1) * w] = i[s][...]

        parts = [st["r", g]] + [sent[f"gz{s}{g}"] for s in (1, 2, 3)]
        (v,) = run(f"gather{g}", body, [(a, whole(part)) for a in parts], [(sds(one, F32), whole(one))])
        st["p", g], sent[f"gc{g}"], sent[f"gx{g}"] = v, over_core(v), over_x(v)

    def gather_core(g):
        v = sent[f"gx{g}"]
        run(f"gathercore{g}", None, after=[v])
        sent[f"gd{g}"] = over_core(v)

    def blocks_of(g):
        return [st["p", g], sent[f"gc{g}"], sent[f"gx{g}"], sent[f"gd{g}"]]

    def blocks_of_target():
        return [st["t"], sent["tc"], sent["tx"], sent["tc2"]]

    def stats(c):
        w = group_width[c]
        wide, o = slots * w, offsets[GROUPS[c][0]] // w
        n_blk = sizes["cell"]
        first = c == 0

        def body(fl, i, out):
            preds, targets, memb = i[:n_blk], i[n_blk : 2 * n_blk], i[2 * n_blk]
            lane = lax.broadcasted_iota(jnp.int32, (quarter, LANES), 1)
            valid = jnp.sum(memb[:, SLIDES : SLIDES + 1])
            out[0][9:16, :] = jnp.broadcast_to(valid, (7, wide))
            for s in range(slots):
                at = slice(s * w, (s + 1) * w)
                rows_k = [jnp.zeros((1, w), F32) for _ in range(9)]
                for b in range(n_blk):
                    pr, ta = preds[b][:, at], targets[b][s].astype(F32)
                    prods = (pr * ta, pr * pr, ta * ta)
                    mb = slice(b * quarter, (b + 1) * quarter)
                    spot_vals = [jnp.sum(v, axis=1, keepdims=True) for v in prods]
                    new = jnp.where(lane == 0, spot_vals[0], 0.0)
                    new = jnp.where(lane == 1, spot_vals[1], new)
                    new = jnp.where(lane == 2, spot_vals[2], new)
                    if s > 0:
                        new = new + out[1][mb, :]
                    elif not first:
                        new = new + i[2 * n_blk + 1][mb, :]
                    out[1][mb, :] = new
                    for k in range(SLIDES):
                        col = memb[mb, k : k + 1]
                        for j, v in enumerate(prods):
                            rows_k[3 * j + k] += jnp.sum(col * v, axis=0, keepdims=True)
                for n, v in enumerate(rows_k):
                    out[0][n : n + 1, at] = v

        ins = [(a, whole((quarter, wide))) for a in blocks_of(c)]
        ins += [(a, pl.BlockSpec((slots, quarter, w), lambda *_: (0, 0, o))) for a in blocks_of_target()]
        ins += [(st["member"], whole((spots, LANES)))]
        if not first:
            ins += [(st["sp"], whole((spots, LANES)))]
        gs, st["sp"] = run(
            f"stats{c}", body, ins,
            [(sds((16, wide), F32), whole((16, wide))), (sds((spots, LANES), F32), whole((spots, LANES)))],
        )
        if spot_size == 2:
            sent[f"gs{c}"] = over_spot(gs)
        st["gs", c] = [gs, sent[f"gs{c}"]] if spot_size == 2 else [sum_spot(gs)]

    steps = {
        "Y": start_swap, "A": start_along, "a": along_send, "S": start_back,
        "e": totals, "m": shares, "t": target, "F": forward, "f": forward_send, "b": members_of, "P": reduce_core, "Q": reduce_x, "R": reduce_gene,
        "W": gather_x, "H": gather_core, "T": stats,
    }
    if spot_size != 2:
        full = lax.all_gather(expression, "spot", axis=0, tiled=True).reshape(slots, rows, genes)
        pieces = [lax.dynamic_index_in_dim(full, gene ^ s, 0, False) for s in range(slots)]
        st["pieces"] = [pieces[0]] + [over_gene(pieces[s], s) for s in (1, 2, 3)]
    for word in " ".join(ORDER).split():
        if word[:2] == "w:":
            if spot_size == 2 or word == "w:ez1+ez2+ez3":
                wait_for(word[2:])
        elif spot_size == 2 or word[0] not in "YAaS":
            steps[word[0]](int(word[1]))

    n_blk = sizes["cell"]
    n_ch, n_gr = len(WIDTHS), len(GROUPS)
    n_gs = len(st["gs", 0])

    def grads_body(fl, i, out, coef_t, coef_p):
        i = list(i)
        memb, sp, kl, ent = i[:4]
        i = i[4:]
        gss, i = i[: n_gr * n_gs], i[n_gr * n_gs :]
        preds, targets = i[: n_gr * n_blk], i[n_gr * n_blk :]
        scale = -1.0 / (SLIDES * genes_all)
        sums, weights = [], []
        for g in range(n_gr):
            sums.append(sum(ref[...] for ref in gss[g * n_gs : (g + 1) * n_gs]))
            num, psq, tsq = sums[g][0:3], sums[g][3:6], sums[g][6:9]
            p_floor, t_floor = jnp.maximum(psq, 1.0), jnp.maximum(tsq, 1.0)
            root = jnp.sqrt(p_floor * t_floor)
            cosine = num / root
            weights.append((scale / root, jnp.where(psq > 1.0, -scale * cosine / p_floor, 0.0), cosine))

        @pl.when(pl.program_id(0) == 0)
        def _():
            valid_total = jnp.maximum(sums[0][9, 0], 1.0)
            s_num = sp[:, 0:1]
            s_p, s_t = sp[:, 1:2] + 1e-06, sp[:, 2:3] + 1e-06
            root = jnp.sqrt(s_p * s_t)
            cos_spot = s_num / root
            valid = memb[:, SLIDES : SLIDES + 1]
            coef = -valid / valid_total
            coef_t[...] = jnp.broadcast_to(coef / root, (spots, LANES))
            coef_p[...] = jnp.broadcast_to(-coef * cos_spot / s_p, (spots, LANES))
            first = [(fl[n] == 0).astype(F32) for n in (2, 4, 3)]
            terms = [
                sum(jnp.sum(w[2]) for w in weights) * first[0] * first[1],
                jnp.sum(valid * cos_spot) * first[0] * first[2],
                kl[0, 0] * first[1],
                jnp.sum(ent[0:1, :]),
                valid_total * first[0] * first[1] * first[2],
            ]
            lane = lax.broadcasted_iota(jnp.int32, (8, spots), 1)
            value = jnp.zeros((8, spots), F32)
            for n, term in enumerate(terms):
                value = jnp.where(lane == n, term, value)
            out[n_ch][...] = value

        for b in range(n_blk):
            mb = slice(b * quarter, (b + 1) * quarter)
            cols = [jnp.broadcast_to(memb[mb, k : k + 1], (quarter, LANES)) for k in range(SLIDES)]
            to = pl.ds(pl.multiple_of((fl[2] ^ b) * quarter, quarter), quarter)
            for g in range(n_gr):
                w_t, w_p, _ = weights[g]
                base = 0
                for c in GROUPS[g]:
                    for o in range(0, WIDTHS[c], LANES):
                        at = slice(base + o, base + o + LANES)
                        f_t, f_p = coef_t[mb, :], coef_p[mb, :]
                        for k in range(SLIDES):
                            f_t = f_t + cols[k] * w_t[k : k + 1, at]
                            f_p = f_p + cols[k] * w_p[k : k + 1, at]
                        start = offsets[c] + o
                        ta = targets[b][0, :, start : start + LANES].astype(F32)
                        pr = preds[g * n_blk + b][:, at]
                        out[c][to, o : o + LANES] = (f_t * ta + f_p * pr).astype(BF)
                    base += WIDTHS[c]

    def by_slot(rows_in, g):
        return pl.BlockSpec((rows_in, group_width[g]), lambda s, f: (0, s))

    tall, row8, flat = whole((spots, LANES)), whole((8, spots)), whole((8, LANES))
    ins = [(st["member"], tall), (st["sp"], tall), (st["kl"], flat), (st["ent"], row8)]
    ins += [(a, by_slot(16, g)) for g in range(n_gr) for a in st["gs", g]]
    ins += [(a, by_slot(quarter, g)) for g in range(n_gr) for a in blocks_of(g)]
    ins += [(a, pl.BlockSpec((1, quarter, genes), lambda s, f: (s, 0, 0))) for a in blocks_of_target()]
    outs = [(sds((spots, slots * w), BF), pl.BlockSpec((spots, w), lambda s, f: (0, s))) for w in WIDTHS]
    outs += [(sds((8, spots), F32), row8)]
    *grads, terms = run(
        "grads", grads_body, ins, outs, grid=(slots,), scratch=[pltpu.VMEM((spots, LANES), F32)] * 2
    )

    row_blk = rows // 4

    def backward_body(fl, i, out):
        lg, tot, sm, terms = i[:4]
        efs, gs = i[4 : 4 + n_ch], i[4 + n_ch :]

        @pl.when(pl.program_id(0) == 0)
        def _():
            row = lax.broadcasted_iota(jnp.int32, (8, spots), 0)
            out[1][...] = jnp.where(row == 0, 0.0, terms[...])

        acc = -jnp.broadcast_to(sm[:, 0:1], (row_blk, spots))
        for ef, grad in zip(efs, gs):
            acc += lax.dot_general(ef[...], grad[...], (((1,), (1,)), ((), ())), preferred_element_type=F32)
        out[0][...] = acc
        prob = jnp.exp(lg[...].astype(F32)) * (1.0 / tot[0:1, :])
        out[1][0:1, :] += jnp.sum(prob * acc, axis=0, keepdims=True)

    def by_rows(width, size=row_blk):
        return pl.BlockSpec((size, width), lambda g, f: (g, 0))

    ins = [(logits, by_rows(spots)), (st["tot"], row8), (st["sm"], by_rows(LANES)), (terms, row8)]
    ins += [(st["e", c], by_rows(slots * WIDTHS[c])) for c in chunks]
    ins += [(a, whole(a.shape)) for a in grads]
    grad_probs, v = run(
        "backward", backward_body, ins,
        [(sds((rows, spots), F32), by_rows(spots)), (sds((8, spots), F32), row8)],
        grid=(rows // row_blk,),
    )

    v = v + over_core(v)
    v = v + over_x(v)
    v = (v + over_gene(v, 1)) + (over_gene(v, 2) + over_gene(v, 3))
    sums = sum_spot(v)[1, :5]

    def final_body(fl, i, out):
        prob = jnp.exp(i[0][...].astype(F32)) * (1.0 / i[1][0:1, :])
        out[0][...] = prob * (i[2][...] - i[3][0:1, :])

    last_blk = rows // 2
    blk = by_rows(spots, last_blk)
    (grad_logits,) = run(
        "final", final_body, [(logits, blk), (st["tot"], row8), (grad_probs, blk), (v, row8)],
        [(sds((rows, spots), F32), blk)], grid=(rows // last_blk,),
    )
    gene_term = sums[0] / (SLIDES * genes_all)
    spot_term = sums[1] / sums[4]
    divergence = sums[2]
    entropy = sums[3] / spots_all
    loss_terms = jnp.stack([divergence - gene_term - spot_term, gene_term, spot_term, divergence, entropy])
    return (loss_terms, grad_logits)


def solution(mesh):
    return jax.shard_map(
        functools.partial(per_device, dict(mesh.shape)),
        mesh=mesh,
        in_specs=(
            P(("cell", "gene"), "spot"),
            P(("cell", "spot"), "gene"),
            P("spot", "gene"),
            P("spot"),
            P("spot"),
            P(("cell", "gene")),
        ),
        out_specs=(P(), P(("cell", "gene"), "spot")),
        check_vma=False,
    )
```

time: 473 us -> 392 us (0.83)
  starting transfers between devices: 108 us -> 74.5 us
  waiting for transfers between devices: 169 us -> 139 us
  local copies, waits for them, and re-layouts: 29 us -> 4.46 us
  blocking collectives: 0 us -> 12.3 us
    ppermute x9 -> x0, waiting for transfers between devices: 35.8 us -> none  [the longest x3 35.8 us: start_swap(): st['y', c] = lax.ppermute(ya, 'spot', xor_pairs(2, 1))]
    ppermute x12, waiting for transfers between devices: 24.5 us -> 52.3 us  [over_spot(): return lax.ppermute(v, 'spot', xor_pairs(spot_size, step))]
    ppermute x9 -> x0, starting transfers between devices: 23 us -> none  [the longest x3 12.2 us: start_near(): lax.ppermute(st['n', c], ('spot', 'gene'), [(0, 4), (1, 5), (6, 2), (7, 3)])]
    unnamed x178 -> x2, local copies, waits for them, and re-layouts: 19 us -> 0.01 us
    ppermute x9 -> x6, waiting for transfers between devices: 23.8 us -> 10.7 us  [over_x(): return lax.ppermute(v, 'cell', xor_pairs(4, 2))]
    psum x0 -> x1, blocking collectives: none -> 12.3 us  [totals(): st['tot'] = lax.psum(v, 'cell')]
    ppermute x33, waiting for transfers between devices: 82.8 us -> 72.9 us  [over_gene(): return lax.ppermute(v, 'gene', xor_pairs(4, step))]
    ppermute x33, starting transfers between devices: 60.5 us -> 52.6 us  [over_gene(): return lax.ppermute(v, 'gene', xor_pairs(4, step))]
  transfers between devices with their start and end apart: 76 -> 60, of which waited for: 24 -> 30; matrix products, arithmetic and copies ran while one was open for 1% -> 0% of each run, Pallas kernels for 21% -> 29%
where the time goes in v2:
time: 392 us; the launch traced here: 390 us
  Pallas kernels  154 us (39%)
  waiting for transfers between devices  139 us (35%)
  starting transfers between devices  74.5 us (19%)
  blocking collectives  12.3 us (3%)
  local copies, waits for them, and re-layouts  4.46 us (1%)
  between operations  4.22 us (1%)
    pallas_call x51, Pallas kernels, run(): pl.pallas_call(kernel, out_shape=[s for s, _ in outs] + [sds(a.shape, a.d...  154 us
    ppermute x33, waiting for transfers between devices, over_gene(): return lax.ppermute(v, 'gene', xor_pairs(4, step))  72.9 us
    ppermute x33, starting transfers between devices, over_gene(): return lax.ppermute(v, 'gene', xor_pairs(4, step))  52.6 us
    ppermute x12, waiting for transfers between devices, over_spot(): return lax.ppermute(v, 'spot', xor_pairs(spot_size, step))  52.3 us
    ppermute x12, starting transfers between devices, over_spot(): return lax.ppermute(v, 'spot', xor_pairs(spot_size, step))  12.6 us
    psum x1, blocking collectives, totals(): st['tot'] = lax.psum(v, 'cell')  12.3 us
    ppermute x6, waiting for transfers between devices, over_x(): return lax.ppermute(v, 'cell', xor_pairs(4, 2))  10.7 us
    ppermute x6, starting transfers between devices, over_x(): return lax.ppermute(v, 'cell', xor_pairs(4, 2))  8.06 us
  transfers between devices with their start and end apart: 60, of which 30 were waited for; matrix products, arithmetic and copies ran while one was open for 0% of the time, Pallas kernels for 29%

profile of v2, /device:TPU:0, one launch (start us, length us, event | category | flops | bytes accessed | tf_op | source)
XLA Modules:
  0.0 390.1 jit_solution(3151154730524290756)
XLA Ops:
  1.9 2.9 swap0.1
  4.8 3.0 collective-permute-start.3
  9.1 3.9 totals.1
  13.0 3.0 swap1.1
  16.0 12.3 %psum.7.refs_1_ = f32[8,512]{1,0:T(8,128)S(1)} all-reduce(f32[8,512]{1,0:T(8,128)} %get-tuple-element.121), channel_id=1, replica_groups=mesh['cell'=4,'spot'=2,'gene'=4] {'cell'}, use_global_device_ids=true, to_apply=%region_0.1 | all-reduce | flops 4096 | bytes 32768 | tf_op jit(solution)/shard_map/psum | solution.py:223
  34.6 3.4 collective-permute-done.2.refs_2_.refs_4_
  38.7 3.0 swap2.1
  41.8 3.7 along0.1
  52.1 9.0 %prob.1 = (bf16[512,2816]{1,0:T(8,128)(2,1)}, f32[8,2816]{1,0:T(8,128)}, f32[8,512]{1,0:T(8,128)}, f32[8,512]{1,0:T(8,128)}, f32[8,128]{1,0:T(8,128)}) custom-call(s32[5]{0:T(128)} %stack.42.flags, bf16[2816,512]{1,0:T(8,128)(2,1)} %refs_0_.9, f32[8,512]{1,0:T(8,128)} %copy-done, ...), custom_call_target="tpu_custom_call", output_to_operand_aliasing={{4}: (6, {})} | custom-call | tf_op jit(solution)/shard_map/prob/pallas_call | solution.py:63
  63.4 8.1 %collective-permute-done.6.refs_0_.refs_1_.refs_6_.refs_7_ = bf16[2,2816,128]{2,1,0:T(8,128)(2,1)} collective-permute-done((bf16[2,2816,128]{2,1,0:T(8,128)(2,1)}, bf16[2,2816,128]{2,1,0:T(8,128)(2,1)}, u32[]{:S(2)}, u32[]{:S(2)}) %collective-permute-start.6) | collective-permute-done | bytes 1441824 | tf_op jit(solution)/shard_map/ppermute | solution.py:124
  71.4 3.7 along1.1
  75.1 3.0 swap3.1
  86.5 15.8 %collective-permute-done.5.refs_0_.refs_1_.refs_6_.refs_7_.refs_2_ = bf16[2,2816,128]{2,1,0:T(8,128)(2,1)} collective-permute-done((bf16[2,2816,128]{2,1,0:T(8,128)(2,1)}, bf16[2,2816,128]{2,1,0:T(8,128)(2,1)}, u32[]{:S(2)}, u32[]{:S(2)}) %collective-permute-start.5) | collective-permute-done | bytes 1441824 | tf_op jit(solution)/shard_map/ppermute | solution.py:124
  102.3 3.8 along2.1
  106.9 7.1 %collective-permute-done.11.refs_1_ = bf16[1408,128]{1,0:T(8,128)(2,1)} collective-permute-done((bf16[1408,128]{1,0:T(8,128)(2,1)}, bf16[1408,128]{1,0:T(8,128)(2,1)}, u32[]{:S(2)}, u32[]{:S(2)}) %collective-permute-start.11) | collective-permute-done | bytes 360480 | tf_op jit(solution)/shard_map/ppermute | solution.py:121
  121.0 2.7 back0.1
  123.8 9.4 %collective-permute-done.17.refs_0_.refs_1_.refs_6_.refs_7_ = bf16[2,2816,128]{2,1,0:T(8,128)(2,1)} collective-permute-done((bf16[2,2816,128]{2,1,0:T(8,128)(2,1)}, bf16[2,2816,128]{2,1,0:T(8,128)(2,1)}, u32[]{:S(2)}, u32[]{:S(2)}) %collective-permute-start.17) | collective-permute-done | bytes 1441824 | tf_op jit(solution)/shard_map/ppermute | solution.py:124
  133.2 3.8 along3.1
  138.6 6.2 %collective-permute-done.15.refs_1_ = bf16[1408,128]{1,0:T(8,128)(2,1)} collective-permute-done((bf16[1408,128]{1,0:T(8,128)(2,1)}, bf16[1408,128]{1,0:T(8,128)(2,1)}, u32[]{:S(2)}, u32[]{:S(2)}) %collective-permute-start.15) | collective-permute-done | bytes 360480 | tf_op jit(solution)/shard_map/ppermute | solution.py:121
  146.1 2.7 back1.1
  156.5 2.7 back2.1
  159.2 4.1 %collective-permute-done.22.refs_0_.refs_9_ = bf16[2,1408,128]{2,1,0:T(8,128)(2,1)} collective-permute-done((bf16[2,1408,128]{2,1,0:T(8,128)(2,1)}, bf16[2,1408,128]{2,1,0:T(8,128)(2,1)}, u32[]{:S(2)}, u32[]{:S(2)}) %collective-permute-start.22) | collective-permute-done | bytes 720928 | tf_op jit(solution)/shard_map/ppermute | solution.py:124
  164.0 9.7 %forward0.1 = (bf16[2816,512]{1,0:T(8,128)(2,1)}, bf16[2816,512]{1,0:T(8,128)(2,1)}, f32[2,128,1024]{2,1,0:T(8,128)}, f32[2,128,1024]{2,1,0:T(8,128)}, f32[8,128]{1,0:T(8,128)}) custom-call(s32[5]{0:T(128)} %stack.42.flags, bf16[512,2816]{1,0:T(8,128)(2,1)} %get-tuple-element.133.refs_0_, ...), custom_call_target="tpu_custom_call", output_to_operand_aliasing={{4}: (11, {})} | custom-call | tf_op jit(solution)/shard_map/forward0/pallas_call | solution.py:63
  174.0 6.5 %collective-permute-done.21.refs_1_ = bf16[1408,128]{1,0:T(8,128)(2,1)} collective-permute-done((bf16[1408,128]{1,0:T(8,128)(2,1)}, bf16[1408,128]{1,0:T(8,128)(2,1)}, u32[]{:S(2)}, u32[]{:S(2)}) %collective-permute-start.21) | collective-permute-done | bytes 360480 | tf_op jit(solution)/shard_map/ppermute | solution.py:121
  181.2 2.7 back3.1
  188.9 3.2 core0.1
  195.9 8.0 %collective-permute-done.18.refs_0_.refs_5_ = bf16[2,1408,128]{2,1,0:T(8,128)(2,1)} collective-permute-done((bf16[2,1408,128]{2,1,0:T(8,128)(2,1)}, bf16[2,1408,128]{2,1,0:T(8,128)(2,1)}, u32[]{:S(2)}, u32[]{:S(2)}) %collective-permute-start.18) | collective-permute-done | bytes 720928 | tf_op jit(solution)/shard_map/ppermute | solution.py:124
  206.3 4.8 %collective-permute-done.28.refs_3_ = bf16[128,512]{1,0:T(8,128)(2,1)} collective-permute-done((bf16[128,512]{1,0:T(8,128)(2,1)}, bf16[128,512]{1,0:T(8,128)(2,1)}, u32[]{:S(2)}, u32[]{:S(2)}) %collective-permute-start.28) | collective-permute-done | bytes 131104 | tf_op jit(solution)/shard_map/ppermute | solution.py:121
  211.1 2.6 target1.1
  213.7 2.7 x0.1
  219.6 9.8 %forward1.1 = (bf16[2816,512]{1,0:T(8,128)(2,1)}, bf16[2816,512]{1,0:T(8,128)(2,1)}, f32[2,128,1024]{2,1,0:T(8,128)}, f32[2,128,1024]{2,1,0:T(8,128)}, f32[8,128]{1,0:T(8,128)}) custom-call(s32[5]{0:T(128)} %stack.42.flags, bf16[512,2816]{1,0:T(8,128)(2,1)} %get-tuple-element.133.refs_0_, ...), custom_call_target="tpu_custom_call", output_to_operand_aliasing={{4}: (11, {})} | custom-call | tf_op jit(solution)/shard_map/forward1/pallas_call | solution.py:63
  233.1 3.2 core1.1
  242.2 2.9 collective-permute-done.32.refs_1_
  245.2 6.9 %collective-permute-done.33.refs_2_ = f32[128,256]{1,0:T(8,128)} collective-permute-done((f32[128,256]{1,0:T(8,128)}, f32[128,256]{1,0:T(8,128)}, u32[]{:S(2)}, u32[]{:S(2)}) %collective-permute-start.33) | collective-permute-done | bytes 131104 | tf_op jit(solution)/shard_map/ppermute | solution.py:121
  259.6 2.7 x1.1
  262.3 6.5 %collective-permute-done.39.refs_2_ = f32[128,256]{1,0:T(8,128)} collective-permute-done((f32[128,256]{1,0:T(8,128)}, f32[128,256]{1,0:T(8,128)}, u32[]{:S(2)}, u32[]{:S(2)}) %collective-permute-start.39) | collective-permute-done | bytes 131104 | tf_op jit(solution)/shard_map/ppermute | solution.py:121
  278.4 7.3 %collective-permute-done.36.refs_2_ = f32[128,256]{1,0:T(8,128)} collective-permute-done((f32[128,256]{1,0:T(8,128)}, f32[128,256]{1,0:T(8,128)}, u32[]{:S(2)}, u32[]{:S(2)}) %collective-permute-start.36) | collective-permute-done | bytes 131104 | tf_op jit(solution)/shard_map/ppermute | solution.py:121
  294.8 7.8 %collective-permute-done.42.refs_2_ = f32[128,256]{1,0:T(8,128)} collective-permute-done((f32[128,256]{1,0:T(8,128)}, f32[128,256]{1,0:T(8,128)}, u32[]{:S(2)}, u32[]{:S(2)}) %collective-permute-start.42) | collective-permute-done | bytes 131104 | tf_op jit(solution)/shard_map/ppermute | solution.py:121
  307.6 8.4 %collective-permute-done.45.refs_0_.refs_2_.refs_14_ = f32[128,1024]{1,0:T(8,128)} collective-permute-done((f32[128,1024]{1,0:T(8,128)}, f32[128,1024]{1,0:T(8,128)}, u32[]{:S(2)}, u32[]{:S(2)}) %collective-permute-start.45) | collective-permute-done | bytes 524320 | tf_op jit(solution)/shard_map/ppermute | solution.py:118
  316.4 6.0 %stats0.1 = (f32[16,1024]{1,0:T(8,128)}, f32[512,128]{1,0:T(8,128)}, f32[8,128]{1,0:T(8,128)}) custom-call(s32[5]{0:T(128)} %stack.42.flags, f32[128,1024]{1,0:T(8,128)} %get-tuple-element.209.refs_0_.refs_8_, f32[128,1024]{1,0:T(8,128)} %collective-permute-done.46.refs_1_.refs_9_, ...), custom_call_target="tpu_custom_call", output_to_operand_aliasing={{2}: (10, {})} | custom-call | tf_op jit(solution)/shard_map/stats0/pallas_call | solution.py:63
  324.8 3.3 shares.1
  328.1 6.3 %stats1.1 = (f32[16,1024]{1,0:T(8,128)}, f32[512,128]{1,0:T(8,128)}, f32[8,128]{1,0:T(8,128)}) custom-call(s32[5]{0:T(128)} %stack.42.flags, f32[128,1024]{1,0:T(8,128)} %get-tuple-element.211.refs_0_.refs_12_, f32[128,1024]{1,0:T(8,128)} %collective-permute-done.50.refs_1_.refs_13_, ...), custom_call_target="tpu_custom_call", output_to_operand_aliasing={{2}: (11, {})} | custom-call | tf_op jit(solution)/shard_map/stats1/pallas_call | solution.py:63
  334.7 4.3 %collective-permute-done.53.refs_7_ = f32[16,1024]{1,0:T(8,128)} collective-permute-done((f32[16,1024]{1,0:T(8,128)}, f32[16,1024]{1,0:T(8,128)}, u32[]{:S(2)}, u32[]{:S(2)}) %collective-permute-start.53) | collective-permute-done | bytes 65568 | tf_op jit(solution)/shard_map/ppermute | solution.py:124
  338.9 8.0 %grads.1 = (bf16[512,512]{1,0:T(8,128)(2,1)}, bf16[512,512]{1,0:T(8,128)(2,1)}, bf16[512,512]{1,0:T(8,128)(2,1)}, bf16[512,512]{1,0:T(8,128)(2,1)}, f32[8,512]{1,0:T(8,128)}, /*index=5*/f32[8,128]{1,0:T(8,128)}) custom-call(s32[5]{0:T(128)} %stack.42.flags, f32[512,128]{1,0:T(8,128)} %get-tuple-element.212.refs_8_.refs_0_, ...), custom_call_target="tpu_custom_call", output_to_operand_aliasing={{5}: (21, {})} | custom-call | tf_op jit(solution)/shard_map/grads/pallas_call | solution.py:63
  346.9 13.1 %backward.1 = (f32[2816,512]{1,0:T(8,128)}, f32[8,512]{1,0:T(8,128)}, f32[8,128]{1,0:T(8,128)}) custom-call(s32[5]{0:T(128)} %stack.42.flags, bf16[2816,512]{1,0:T(8,128)(2,1)} %refs_0_.9, f32[8,512]{1,0:T(8,128)} %get-tuple-element.131.refs_1_, f32[2816,128]{1,0:T(8,128)} %get-tuple-element.215.refs_2_, ...), custom_call_target="tpu_custom_call", output_to_operand_aliasing={{2}: (13, {})} | custom-call | tf_op jit(solution)/shard_map/backward/pallas_call | solution.py:63
  365.9 3.4 collective-permute-start.56
  374.1 2.7 collective-permute-done.58
  377.8 6.4 %final.1 = (f32[2816,512]{1,0:T(8,128)}, f32[8,128]{1,0:T(8,128)}) custom-call(s32[5]{0:T(128)} %stack.42.flags, bf16[2816,512]{1,0:T(8,128)(2,1)} %refs_0_.9, f32[8,512]{1,0:T(8,128)} %get-tuple-element.131.refs_1_, f32[2816,512]{1,0:T(8,128)} %get-tuple-element.235.refs_2_, f32[8,512]{1,0:T(8,128)} %add_add_fusion.refs_3_, ...), custom_call_target="tpu_custom_call", output_to_operand_aliasing={{1}: (5, {})} | custom-call | tf_op jit(solution)/shard_map/final/pallas_call | solution.py:63
  (135 shorter events, 119.7 us)
Async XLA Ops:
  4.8 36.9 %collective-permute-start.3 = (bf16[2,2816,128]{2,1,0:T(8,128)(2,1)}, bf16[2,2816,128]{2,1,0:T(8,128)(2,1)}, u32[]{:S(2)}, u32[]{:S(2)}) collective-permute-start(bf16[2,2816,128]{2,1,0:T(8,128)(2,1)} %get-tuple-element.122), channel_id=1, source_target_pairs={{0,4},{4,0},{1,5},{5,1},{2,6},{6,2},{3,7},{7,3},{8,12},{12,8},{9,1... | collective-permute-start | bytes 4325384 | tf_op jit(solution)/shard_map/ppermute | solution.py:124
  16.0 55.4 %collective-permute-start.6 = (bf16[2,2816,128]{2,1,0:T(8,128)(2,1)}, bf16[2,2816,128]{2,1,0:T(8,128)(2,1)}, u32[]{:S(2)}, u32[]{:S(2)}) collective-permute-start(bf16[2,2816,128]{2,1,0:T(8,128)(2,1)} %get-tuple-element.135), channel_id=1, source_target_pairs={{0,4},{4,0},{1,5},{5,1},{2,6},{6,2},{3,7},{7,3},{8,12},{12,8},{9,1... | collective-permute-start | bytes 4325384 | tf_op jit(solution)/shard_map/ppermute | solution.py:124
  46.1 33.1 %collective-permute-start.9 = (bf16[2,1408,128]{2,1,0:T(8,128)(2,1)}, bf16[2,1408,128]{2,1,0:T(8,128)(2,1)}, u32[]{:S(2)}, u32[]{:S(2)}) collective-permute-start(bf16[2,1408,128]{2,1,0:T(8,128)(2,1)} %get-tuple-element.143), channel_id=1, source_target_pairs={{0,1},{1,0},{2,3},{3,2},{4,5},{5,4},{6,7},{7,6},{8,9},{9,8},{10,11... | collective-permute-start | bytes 2162696 | tf_op jit(solution)/shard_map/ppermute | solution.py:121
  47.0 55.3 %collective-permute-start.5 = (bf16[2,2816,128]{2,1,0:T(8,128)(2,1)}, bf16[2,2816,128]{2,1,0:T(8,128)(2,1)}, u32[]{:S(2)}, u32[]{:S(2)}) collective-permute-start(bf16[2,2816,128]{2,1,0:T(8,128)(2,1)} %get-tuple-element.134), channel_id=1, source_target_pairs={{0,4},{4,0},{1,5},{5,1},{2,6},{6,2},{3,7},{7,3},{8,12},{12,8},{9,1... | collective-permute-start | bytes 4325384 | tf_op jit(solution)/shard_map/ppermute | solution.py:124
  48.6 29.5 %collective-permute-start.7 = (bf16[1408,128]{1,0:T(8,128)(2,1)}, bf16[1408,128]{1,0:T(8,128)(2,1)}, u32[]{:S(2)}, u32[]{:S(2)}) collective-permute-start(bf16[1408,128]{1,0:T(8,128)(2,1)} %get-tuple-element.141), channel_id=1, source_target_pairs={{0,2},{1,3},{2,0},{3,1},{4,6},{5,7},{6,4},{7,5},{8,10},{9,11},{10,... | collective-permute-start | bytes 1081352 | tf_op jit(solution)/shard_map/ppermute | solution.py:121
  51.2 28.1 %collective-permute-start.8 = (bf16[1408,128]{1,0:T(8,128)(2,1)}, bf16[1408,128]{1,0:T(8,128)(2,1)}, u32[]{:S(2)}, u32[]{:S(2)}) collective-permute-start(bf16[1408,128]{1,0:T(8,128)(2,1)} %get-tuple-element.142), channel_id=1, source_target_pairs={{0,3},{1,2},{2,1},{3,0},{4,7},{5,6},{6,5},{7,4},{8,11},{9,10},{10,... | collective-permute-start | bytes 1081352 | tf_op jit(solution)/shard_map/ppermute | solution.py:121
  80.6 33.4 %collective-permute-start.12 = (bf16[2,1408,128]{2,1,0:T(8,128)(2,1)}, bf16[2,1408,128]{2,1,0:T(8,128)(2,1)}, u32[]{:S(2)}, u32[]{:S(2)}) collective-permute-start(bf16[2,1408,128]{2,1,0:T(8,128)(2,1)} %get-tuple-element.152), channel_id=1, source_target_pairs={{0,1},{1,0},{2,3},{3,2},{4,5},{5,4},{6,7},{7,6},{8,9},{9,8},{10,11... | collective-permute-start | bytes 2162696 | tf_op jit(solution)/shard_map/ppermute | solution.py:121
  82.5 50.7 %collective-permute-start.17 = (bf16[2,2816,128]{2,1,0:T(8,128)(2,1)}, bf16[2,2816,128]{2,1,0:T(8,128)(2,1)}, u32[]{:S(2)}, u32[]{:S(2)}) collective-permute-start(bf16[2,2816,128]{2,1,0:T(8,128)(2,1)} %get-tuple-element.159), channel_id=1, source_target_pairs={{0,4},{4,0},{1,5},{5,1},{2,6},{6,2},{3,7},{7,3},{8,12},{12,8},{9,1... | collective-permute-start | bytes 4325384 | tf_op jit(solution)/shard_map/ppermute | solution.py:124
  83.1 23.8 %collective-permute-start.10 = (bf16[1408,128]{1,0:T(8,128)(2,1)}, bf16[1408,128]{1,0:T(8,128)(2,1)}, u32[]{:S(2)}, u32[]{:S(2)}) collective-permute-start(bf16[1408,128]{1,0:T(8,128)(2,1)} %get-tuple-element.150), channel_id=1, source_target_pairs={{0,2},{1,3},{2,0},{3,1},{4,6},{5,7},{6,4},{7,5},{8,10},{9,11},{10,... | collective-permute-start | bytes 1081352 | tf_op jit(solution)/shard_map/ppermute | solution.py:121
  85.7 28.3 %collective-permute-start.11 = (bf16[1408,128]{1,0:T(8,128)(2,1)}, bf16[1408,128]{1,0:T(8,128)(2,1)}, u32[]{:S(2)}, u32[]{:S(2)}) collective-permute-start(bf16[1408,128]{1,0:T(8,128)(2,1)} %get-tuple-element.151), channel_id=1, source_target_pairs={{0,3},{1,2},{2,1},{3,0},{4,7},{5,6},{6,5},{7,4},{8,11},{9,10},{10,... | collective-permute-start | bytes 1081352 | tf_op jit(solution)/shard_map/ppermute | solution.py:121
  115.4 29.4 %collective-permute-start.13 = (bf16[2,1408,128]{2,1,0:T(8,128)(2,1)}, bf16[2,1408,128]{2,1,0:T(8,128)(2,1)}, u32[]{:S(2)}, u32[]{:S(2)}) collective-permute-start(bf16[2,1408,128]{2,1,0:T(8,128)(2,1)} %get-tuple-element.154), channel_id=1, source_target_pairs={{0,1},{1,0},{2,3},{3,2},{4,5},{5,4},{6,7},{7,6},{8,9},{9,8},{10,11... | collective-permute-start | bytes 2162696 | tf_op jit(solution)/shard_map/ppermute | solution.py:121
  117.6 21.0 %collective-permute-start.14 = (bf16[1408,128]{1,0:T(8,128)(2,1)}, bf16[1408,128]{1,0:T(8,128)(2,1)}, u32[]{:S(2)}, u32[]{:S(2)}) collective-permute-start(bf16[1408,128]{1,0:T(8,128)(2,1)} %get-tuple-element.155), channel_id=1, source_target_pairs={{0,2},{1,3},{2,0},{3,1},{4,6},{5,7},{6,4},{7,5},{8,10},{9,11},{10,... | collective-permute-start | bytes 1081352 | tf_op jit(solution)/shard_map/ppermute | solution.py:121
  119.6 25.2 %collective-permute-start.15 = (bf16[1408,128]{1,0:T(8,128)(2,1)}, bf16[1408,128]{1,0:T(8,128)(2,1)}, u32[]{:S(2)}, u32[]{:S(2)}) collective-permute-start(bf16[1408,128]{1,0:T(8,128)(2,1)} %get-tuple-element.156), channel_id=1, source_target_pairs={{0,3},{1,2},{2,1},{3,0},{4,7},{5,6},{6,5},{7,4},{8,11},{9,10},{10,... | collective-permute-start | bytes 1081352 | tf_op jit(solution)/shard_map/ppermute | solution.py:121
  123.7 32.2 %collective-permute-start.16 = (bf16[2,1408,128]{2,1,0:T(8,128)(2,1)}, bf16[2,1408,128]{2,1,0:T(8,128)(2,1)}, u32[]{:S(2)}, u32[]{:S(2)}) collective-permute-start(bf16[2,1408,128]{2,1,0:T(8,128)(2,1)} %get-tuple-element.158.refs_4_), channel_id=1, source_target_pairs={{0,4},{4,0},{1,5},{5,1},{2,6},{6,2},{3,7},{7,3},{8,12},{12,8},{9,1... | collective-permute-start | bytes 2162696 | tf_op jit(solution)/shard_map/ppermute | solution.py:124
  148.9 14.4 %collective-permute-start.22 = (bf16[2,1408,128]{2,1,0:T(8,128)(2,1)}, bf16[2,1408,128]{2,1,0:T(8,128)(2,1)}, u32[]{:S(2)}, u32[]{:S(2)}) collective-permute-start(bf16[2,1408,128]{2,1,0:T(8,128)(2,1)} %get-tuple-element.171.refs_8_), channel_id=1, source_target_pairs={{0,4},{4,0},{1,5},{5,1},{2,6},{6,2},{3,7},{7,3},{8,12},{12,8},{9,1... | collective-permute-start | bytes 2162696 | tf_op jit(solution)/shard_map/ppermute | solution.py:124
  151.4 29.1 %collective-permute-start.19 = (bf16[2,1408,128]{2,1,0:T(8,128)(2,1)}, bf16[2,1408,128]{2,1,0:T(8,128)(2,1)}, u32[]{:S(2)}, u32[]{:S(2)}) collective-permute-start(bf16[2,1408,128]{2,1,0:T(8,128)(2,1)} %get-tuple-element.168), channel_id=1, source_target_pairs={{0,1},{1,0},{2,3},{3,2},{4,5},{5,4},{6,7},{7,6},{8,9},{9,8},{10,11... | collective-permute-start | bytes 2162696 | tf_op jit(solution)/shard_map/ppermute | solution.py:121
  153.0 21.0 %collective-permute-start.20 = (bf16[1408,128]{1,0:T(8,128)(2,1)}, bf16[1408,128]{1,0:T(8,128)(2,1)}, u32[]{:S(2)}, u32[]{:S(2)}) collective-permute-start(bf16[1408,128]{1,0:T(8,128)(2,1)} %get-tuple-element.169), channel_id=1, source_target_pairs={{0,2},{1,3},{2,0},{3,1},{4,6},{5,7},{6,4},{7,5},{8,10},{9,11},{10,... | collective-permute-start | bytes 1081352 | tf_op jit(solution)/shard_map/ppermute | solution.py:121
  154.2 26.3 %collective-permute-start.21 = (bf16[1408,128]{1,0:T(8,128)(2,1)}, bf16[1408,128]{1,0:T(8,128)(2,1)}, u32[]{:S(2)}, u32[]{:S(2)}) collective-permute-start(bf16[1408,128]{1,0:T(8,128)(2,1)} %get-tuple-element.170), channel_id=1, source_target_pairs={{0,3},{1,2},{2,1},{3,0},{4,7},{5,6},{6,5},{7,4},{8,11},{9,10},{10,... | collective-permute-start | bytes 1081352 | tf_op jit(solution)/shard_map/ppermute | solution.py:121
  184.6 19.3 %collective-permute-start.18 = (bf16[2,1408,128]{2,1,0:T(8,128)(2,1)}, bf16[2,1408,128]{2,1,0:T(8,128)(2,1)}, u32[]{:S(2)}, u32[]{:S(2)}) collective-permute-start(bf16[2,1408,128]{2,1,0:T(8,128)(2,1)} %get-tuple-element.167.refs_4_), channel_id=1, source_target_pairs={{0,4},{4,0},{1,5},{5,1},{2,6},{6,2},{3,7},{7,3},{8,12},{12,8},{9,1... | collective-permute-start | bytes 2162696 | tf_op jit(solution)/shard_map/ppermute | solution.py:124
  185.0 34.0 %collective-permute-start.23 = (bf16[2,1408,128]{2,1,0:T(8,128)(2,1)}, bf16[2,1408,128]{2,1,0:T(8,128)(2,1)}, u32[]{:S(2)}, u32[]{:S(2)}) collective-permute-start(bf16[2,1408,128]{2,1,0:T(8,128)(2,1)} %get-tuple-element.174.refs_8_), channel_id=1, source_target_pairs={{0,4},{4,0},{1,5},{5,1},{2,6},{6,2},{3,7},{7,3},{8,12},{12,8},{9,1... | collective-permute-start | bytes 2162696 | tf_op jit(solution)/shard_map/ppermute | solution.py:124
  192.2 21.5 %collective-permute-start.25 = (f32[128,1024]{1,0:T(8,128)}, f32[128,1024]{1,0:T(8,128)}, u32[]{:S(2)}, u32[]{:S(2)}) collective-permute-start(f32[128,1024]{1,0:T(8,128)} %get-tuple-element.182), channel_id=1, source_target_pairs={{0,16},{8,24},{16,0},{24,8},{1,17},{9,25},{17,1},{25,9},{2,18},{10... | collective-permute-start | bytes 1572872 | tf_op jit(solution)/shard_map/ppermute | solution.py:118
  193.6 12.6 %collective-permute-start.26 = (bf16[128,512]{1,0:T(8,128)(2,1)}, bf16[128,512]{1,0:T(8,128)(2,1)}, u32[]{:S(2)}, u32[]{:S(2)}) collective-permute-start(bf16[128,512]{1,0:T(8,128)(2,1)} %get-tuple-element.183.refs_0_), channel_id=1, source_target_pairs={{0,1},{1,0},{2,3},{3,2},{4,5},{5,4},{6,7},{7,6},{8,9},{9,8},{10,11... | collective-permute-start | bytes 393224 | tf_op jit(solution)/shard_map/ppermute | solution.py:121
  194.7 11.6 %collective-permute-start.27 = (bf16[128,512]{1,0:T(8,128)(2,1)}, bf16[128,512]{1,0:T(8,128)(2,1)}, u32[]{:S(2)}, u32[]{:S(2)}) collective-permute-start(bf16[128,512]{1,0:T(8,128)(2,1)} %get-tuple-element.183.refs_0_), channel_id=1, source_target_pairs={{0,2},{1,3},{2,0},{3,1},{4,6},{5,7},{6,4},{7,5},{8,10},{9,11},{10,... | collective-permute-start | bytes 393224 | tf_op jit(solution)/shard_map/ppermute | solution.py:121
  203.9 7.1 %collective-permute-start.28 = (bf16[128,512]{1,0:T(8,128)(2,1)}, bf16[128,512]{1,0:T(8,128)(2,1)}, u32[]{:S(2)}, u32[]{:S(2)}) collective-permute-start(bf16[128,512]{1,0:T(8,128)(2,1)} %get-tuple-element.183.refs_0_), channel_id=1, source_target_pairs={{0,3},{1,2},{2,1},{3,0},{4,7},{5,6},{6,5},{7,4},{8,11},{9,10},{10,... | collective-permute-start | bytes 393224 | tf_op jit(solution)/shard_map/ppermute | solution.py:121
  230.1 28.8 %collective-permute-start.31 = (bf16[4,128,512]{2,1,0:T(8,128)(2,1)}, bf16[4,128,512]{2,1,0:T(8,128)(2,1)}, u32[]{:S(2)}, u32[]{:S(2)}) collective-permute-start(bf16[4,128,512]{2,1,0:T(8,128)(2,1)} %get-tuple-element.194.refs_4_.refs_16_), channel_id=1, source_target_pairs={{0,16},{8,24},{16,0},{24,8},{1,17},{9,25},{17,1},{25,9},{2,18},{10... | collective-permute-start | bytes 1572872 | tf_op jit(solution)/shard_map/ppermute | solution.py:118
  236.4 23.3 %collective-permute-start.30 = (f32[128,1024]{1,0:T(8,128)}, f32[128,1024]{1,0:T(8,128)}, u32[]{:S(2)}, u32[]{:S(2)}) collective-permute-start(f32[128,1024]{1,0:T(8,128)} %get-tuple-element.193), channel_id=1, source_target_pairs={{0,16},{8,24},{16,0},{24,8},{1,17},{9,25},{17,1},{25,9},{2,18},{10... | collective-permute-start | bytes 1572872 | tf_op jit(solution)/shard_map/ppermute | solution.py:118
  237.9 7.3 %collective-permute-start.32 = (f32[128,256]{1,0:T(8,128)}, f32[128,256]{1,0:T(8,128)}, u32[]{:S(2)}, u32[]{:S(2)}) collective-permute-start(f32[128,256]{1,0:T(8,128)} %get-tuple-element.196), channel_id=1, source_target_pairs={{0,1},{1,0},{2,3},{3,2},{4,5},{5,4},{6,7},{7,6},{8,9},{9,8},{10,11... | collective-permute-start | bytes 393224 | tf_op jit(solution)/shard_map/ppermute | solution.py:121
  238.9 13.1 %collective-permute-start.33 = (f32[128,256]{1,0:T(8,128)}, f32[128,256]{1,0:T(8,128)}, u32[]{:S(2)}, u32[]{:S(2)}) collective-permute-start(f32[128,256]{1,0:T(8,128)} %get-tuple-element.197), channel_id=1, source_target_pairs={{0,2},{1,3},{2,0},{3,1},{4,6},{5,7},{6,4},{7,5},{8,10},{9,11},{10,... | collective-permute-start | bytes 393224 | tf_op jit(solution)/shard_map/ppermute | solution.py:121
  240.1 12.0 %collective-permute-start.34 = (f32[128,256]{1,0:T(8,128)}, f32[128,256]{1,0:T(8,128)}, u32[]{:S(2)}, u32[]{:S(2)}) collective-permute-start(f32[128,256]{1,0:T(8,128)} %get-tuple-element.198), channel_id=1, source_target_pairs={{0,3},{1,2},{2,1},{3,0},{4,7},{5,6},{6,5},{7,4},{8,11},{9,10},{10,... | collective-permute-start | bytes 393224 | tf_op jit(solution)/shard_map/ppermute | solution.py:121
  254.5 7.8 %collective-permute-start.38 = (f32[128,256]{1,0:T(8,128)}, f32[128,256]{1,0:T(8,128)}, u32[]{:S(2)}, u32[]{:S(2)}) collective-permute-start(f32[128,256]{1,0:T(8,128)} %get-tuple-element.205.refs_0_), channel_id=1, source_target_pairs={{0,1},{1,0},{2,3},{3,2},{4,5},{5,4},{6,7},{7,6},{8,9},{9,8},{10,11... | collective-permute-start | bytes 393224 | tf_op jit(solution)/shard_map/ppermute | solution.py:121
  256.6 12.2 %collective-permute-start.39 = (f32[128,256]{1,0:T(8,128)}, f32[128,256]{1,0:T(8,128)}, u32[]{:S(2)}, u32[]{:S(2)}) collective-permute-start(f32[128,256]{1,0:T(8,128)} %get-tuple-element.205.refs_0_), channel_id=1, source_target_pairs={{0,2},{1,3},{2,0},{3,1},{4,6},{5,7},{6,4},{7,5},{8,10},{9,11},{10,... | collective-permute-start | bytes 393224 | tf_op jit(solution)/shard_map/ppermute | solution.py:121
  257.2 11.6 %collective-permute-start.40 = (f32[128,256]{1,0:T(8,128)}, f32[128,256]{1,0:T(8,128)}, u32[]{:S(2)}, u32[]{:S(2)}) collective-permute-start(f32[128,256]{1,0:T(8,128)} %get-tuple-element.205.refs_0_), channel_id=1, source_target_pairs={{0,3},{1,2},{2,1},{3,0},{4,7},{5,6},{6,5},{7,4},{8,11},{9,10},{10,... | collective-permute-start | bytes 393224 | tf_op jit(solution)/shard_map/ppermute | solution.py:121
  271.4 21.1 %collective-permute-start.44 = (f32[128,1024]{1,0:T(8,128)}, f32[128,1024]{1,0:T(8,128)}, u32[]{:S(2)}, u32[]{:S(2)}) collective-permute-start(f32[128,1024]{1,0:T(8,128)} %get-tuple-element.209.refs_0_.refs_8_), channel_id=1, source_target_pairs={{0,16},{8,24},{16,0},{24,8},{1,17},{9,25},{17,1},{25,9},{2,18},{10... | collective-permute-start | bytes 1572872 | tf_op jit(solution)/shard_map/ppermute | solution.py:118
  273.9 11.7 %collective-permute-start.36 = (f32[128,256]{1,0:T(8,128)}, f32[128,256]{1,0:T(8,128)}, u32[]{:S(2)}, u32[]{:S(2)}) collective-permute-start(f32[128,256]{1,0:T(8,128)} %get-tuple-element.203), channel_id=1, source_target_pairs={{0,2},{1,3},{2,0},{3,1},{4,6},{5,7},{6,4},{7,5},{8,10},{9,11},{10,... | collective-permute-start | bytes 393224 | tf_op jit(solution)/shard_map/ppermute | solution.py:121
  274.6 11.0 %collective-permute-start.37 = (f32[128,256]{1,0:T(8,128)}, f32[128,256]{1,0:T(8,128)}, u32[]{:S(2)}, u32[]{:S(2)}) collective-permute-start(f32[128,256]{1,0:T(8,128)} %get-tuple-element.204), channel_id=1, source_target_pairs={{0,3},{1,2},{2,1},{3,0},{4,7},{5,6},{6,5},{7,4},{8,11},{9,10},{10,... | collective-permute-start | bytes 393224 | tf_op jit(solution)/shard_map/ppermute | solution.py:121
  290.0 12.5 %collective-permute-start.42 = (f32[128,256]{1,0:T(8,128)}, f32[128,256]{1,0:T(8,128)}, u32[]{:S(2)}, u32[]{:S(2)}) collective-permute-start(f32[128,256]{1,0:T(8,128)} %get-tuple-element.208.refs_0_), channel_id=1, source_target_pairs={{0,2},{1,3},{2,0},{3,1},{4,6},{5,7},{6,4},{7,5},{8,10},{9,11},{10,... | collective-permute-start | bytes 393224 | tf_op jit(solution)/shard_map/ppermute | solution.py:121
  290.9 11.6 %collective-permute-start.43 = (f32[128,256]{1,0:T(8,128)}, f32[128,256]{1,0:T(8,128)}, u32[]{:S(2)}, u32[]{:S(2)}) collective-permute-start(f32[128,256]{1,0:T(8,128)} %get-tuple-element.208.refs_0_), channel_id=1, source_target_pairs={{0,3},{1,2},{2,1},{3,0},{4,7},{5,6},{6,5},{7,4},{8,11},{9,10},{10,... | collective-permute-start | bytes 393224 | tf_op jit(solution)/shard_map/ppermute | solution.py:121
  292.5 14.7 %collective-permute-start.48 = (bf16[4,128,512]{2,1,0:T(8,128)(2,1)}, bf16[4,128,512]{2,1,0:T(8,128)(2,1)}, u32[]{:S(2)}, u32[]{:S(2)}) collective-permute-start(bf16[4,128,512]{2,1,0:T(8,128)(2,1)} %get-tuple-element.194.refs_4_.refs_16_), channel_id=1, source_target_pairs={{0,8},{8,0},{16,24},{24,16},{1,9},{9,1},{17,25},{25,17},{2,10},{10... | collective-permute-start | bytes 1572872 | tf_op jit(solution)/shard_map/ppermute | solution.py:115
  305.1 10.9 %collective-permute-start.45 = (f32[128,1024]{1,0:T(8,128)}, f32[128,1024]{1,0:T(8,128)}, u32[]{:S(2)}, u32[]{:S(2)}) collective-permute-start(f32[128,1024]{1,0:T(8,128)} %get-tuple-element.211.refs_0_.refs_12_), channel_id=1, source_target_pairs={{0,16},{8,24},{16,0},{24,8},{1,17},{9,25},{17,1},{25,9},{2,18},{10... | collective-permute-start | bytes 1572872 | tf_op jit(solution)/shard_map/ppermute | solution.py:118
  306.6 9.5 %collective-permute-start.49 = (bf16[4,128,512]{2,1,0:T(8,128)(2,1)}, bf16[4,128,512]{2,1,0:T(8,128)(2,1)}, u32[]{:S(2)}, u32[]{:S(2)}) collective-permute-start(bf16[4,128,512]{2,1,0:T(8,128)(2,1)} %collective-permute-done.31.refs_0_.refs_6_.refs_18_), channel_id=1, source_target_pairs={{0,8},{8,0},{16,24},{24,16},{1,9},{9,1},{17,25},{25,17},{2,10},{10... | collective-permute-start | bytes 1572872 | tf_op jit(solution)/shard_map/ppermute | solution.py:115
  306.6 9.8 %collective-permute-start.46 = (f32[128,1024]{1,0:T(8,128)}, f32[128,1024]{1,0:T(8,128)}, u32[]{:S(2)}, u32[]{:S(2)}) collective-permute-start(f32[128,1024]{1,0:T(8,128)} %get-tuple-element.209.refs_0_.refs_8_), channel_id=1, source_target_pairs={{0,8},{8,0},{16,24},{24,16},{1,9},{9,1},{17,25},{25,17},{2,10},{10... | collective-permute-start | bytes 1572872 | tf_op jit(solution)/shard_map/ppermute | solution.py:115
  307.1 9.3 %collective-permute-start.47 = (f32[128,1024]{1,0:T(8,128)}, f32[128,1024]{1,0:T(8,128)}, u32[]{:S(2)}, u32[]{:S(2)}) collective-permute-start(f32[128,1024]{1,0:T(8,128)} %collective-permute-done.44.refs_0_.refs_2_.refs_10_), channel_id=1, source_target_pairs={{0,8},{8,0},{16,24},{24,16},{1,9},{9,1},{17,25},{25,17},{2,10},{10... | collective-permute-start | bytes 1572872 | tf_op jit(solution)/shard_map/ppermute | solution.py:115
  307.1 20.9 %collective-permute-start.50 = (f32[128,1024]{1,0:T(8,128)}, f32[128,1024]{1,0:T(8,128)}, u32[]{:S(2)}, u32[]{:S(2)}) collective-permute-start(f32[128,1024]{1,0:T(8,128)} %get-tuple-element.211.refs_0_.refs_12_), channel_id=1, source_target_pairs={{0,8},{8,0},{16,24},{24,16},{1,9},{9,1},{17,25},{25,17},{2,10},{10... | collective-permute-start | bytes 1572872 | tf_op jit(solution)/shard_map/ppermute | solution.py:115
  316.1 12.0 %collective-permute-start.51 = (f32[128,1024]{1,0:T(8,128)}, f32[128,1024]{1,0:T(8,128)}, u32[]{:S(2)}, u32[]{:S(2)}) collective-permute-start(f32[128,1024]{1,0:T(8,128)} %collective-permute-done.45.refs_0_.refs_2_.refs_14_), channel_id=1, source_target_pairs={{0,8},{8,0},{16,24},{24,16},{1,9},{9,1},{17,25},{25,17},{2,10},{10... | collective-permute-start | bytes 1572872 | tf_op jit(solution)/shard_map/ppermute | solution.py:115
  316.1 8.7 %collective-permute-start.4 = (f32[8,2816]{1,0:T(8,128)}, f32[8,2816]{1,0:T(8,128)}, u32[]{:S(2)}, u32[]{:S(2)}) collective-permute-start(f32[8,2816]{1,0:T(8,128)} %get-tuple-element.132.refs_2_), channel_id=1, source_target_pairs={{0,4},{4,0},{1,5},{5,1},{2,6},{6,2},{3,7},{7,3},{8,12},{12,8},{9,1... | collective-permute-start | bytes 270344 | tf_op jit(solution)/shard_map/ppermute | solution.py:124
  322.4 12.3 %collective-permute-start.52 = (f32[16,1024]{1,0:T(8,128)}, f32[16,1024]{1,0:T(8,128)}, u32[]{:S(2)}, u32[]{:S(2)}) collective-permute-start(f32[16,1024]{1,0:T(8,128)} %get-tuple-element.221.refs_4_), channel_id=1, source_target_pairs={{0,4},{4,0},{1,5},{5,1},{2,6},{6,2},{3,7},{7,3},{8,12},{12,8},{9,1... | collective-permute-start | bytes 196616 | tf_op jit(solution)/shard_map/ppermute | solution.py:124
  365.9 6.8 %collective-permute-start.56 = (f32[8,512]{1,0:T(8,128)S(1)}, f32[8,512]{1,0:T(8,128)S(1)}, u32[]{:S(2)}, u32[]{:S(2)}) collective-permute-start(f32[8,512]{1,0:T(8,128)S(1)} %add.27), channel_id=1, source_target_pairs={{0,1},{1,0},{2,3},{3,2},{4,5},{5,4},{6,7},{7,6},{8,9},{9,8},{10,11... | collective-permute-start | bytes 49160 | tf_op jit(solution)/shard_map/ppermute | solution.py:121
  377.5 6.8 %collective-permute-start.59 = (f32[8,512]{1,0:T(8,128)}, f32[8,512]{1,0:T(8,128)}, u32[]{:S(2)}, u32[]{:S(2)}) collective-permute-start(f32[8,512]{1,0:T(8,128)} %add_add_fusion.refs_3_), channel_id=1, source_target_pairs={{0,4},{4,0},{1,5},{5,1},{2,6},{6,2},{3,7},{7,3},{8,12},{12,8},{9,1... | collective-permute-start | bytes 49160 | tf_op jit(solution)/shard_map/ppermute | solution.py:124
  (13 other events, 59.7 us)

commit v3 on v2

--- a/solution.py
+++ b/solution.py
@@ -11,7 +11,7 @@
 ANY = pl.BlockSpec(memory_space=pl.ANY)
 BF = jnp.bfloat16
 F32 = jnp.float32
-VMEM_BYTES = 64 * 1024 * 1024
+VMEM_BYTES = 30 * 1024 * 1024
 WIDTHS = (128, 128, 128, 128)
 GROUPS = ((0, 1), (2, 3))
 ORDER = (
@@ -21,12 +21,10 @@
     "a1 A2 w:f21+f31+n1 a2",
     "S0 A3 w:f22+f32+n2 a3",
     "S1 w:s0 S2 w:s1",
-    "F0 w:f23+f33+n3 S3 f0",
-    "t0 P0 w:s2 t1",
-    "Q0 w:s3 F1 f1",
-    "P1 R0 t2 Q1",
-    "W0 R1 H0 W1",
-    "T0 H1 m0 T1",
+    "F0 w:s2+f23+f33+n3 S3 f0",
+    "P0 w:s3 F1 w:rx0",
+    "f1 P1 Q0 m0",
+    "R0 Q1 R1",
 )
 
 
@@ -199,15 +197,12 @@
     def members_of(_):
         def body(fl, i, out):
             ids, valid = column(i[0][...].astype(F32)), column(i[1][...].astype(F32))
-            lane = lax.broadcasted_iota(jnp.int32, (spots, LANES), 1)
+            lane = lax.broadcasted_iota(jnp.int32, (quarter, LANES), 1)
             inside = (lane < SLIDES) & (lane.astype(F32) == ids) & (valid == 1.0)
-            value = jnp.where(inside, 1.0, jnp.where(lane == SLIDES, valid, 0.0))
-            for q in range(sizes["cell"]):
-                at = pl.multiple_of((fl[2] ^ q) * quarter, quarter)
-                out[0][pl.ds(at, quarter), :] = value[q * quarter : (q + 1) * quarter]
-
-        row, tall = whole((1, spots)), whole((spots, LANES))
-        (st["member"],) = run("member", body, [(ids_row, row), (mask_row, row)], [(sds((spots, LANES), F32), tall)])
+            out[0][...] = jnp.where(inside, 1.0, jnp.where(lane == SLIDES, valid, 0.0))
+
+        row, tall = pl.BlockSpec((1, quarter), lambda g, f: (0, f[2])), whole((quarter, LANES))
+        (st["member"],) = run("member", body, [(ids_row, row), (mask_row, row)], [(sds((quarter, LANES), F32), tall)])
 
     def totals(n):
         sp = whole((8, spots))
@@ -282,33 +277,6 @@
             + [(m, whole((8, rows))) for m in masses],
             [(sds((rows, LANES), F32), whole((rows, LANES))), (sds((8, LANES), F32), whole((8, LANES)))],
         )
-
-    def target(n):
-        blk = (quarter, genes)
-        if n == 0:
-
-            def body(fl, i, out):
-                out[0][...] = i[0][...]
-
-            (v,) = run(
-                "target", body, [(spatial, pl.BlockSpec(blk, lambda g, f: (f[2], 0)))], [(sds(blk, BF), whole(blk))]
-            )
-            st["t"] = v
-            for s in (1, 2, 3):
-                sent[f"tz{s}"] = over_gene(v, s)
-        elif n == 1:
-            shape = (slots, *blk)
-
-            def body(fl, i, out):
-                for s in range(slots):
-                    out[0][s] = i[s][...]
-
-            parts = [st["t"]] + [sent[f"tz{s}"] for s in (1, 2, 3)]
-            (v,) = run("target1", body, [(a, whole(blk)) for a in parts], [(sds(shape, BF), whole(shape))])
-            st["t"], sent["tc"], sent["tx"] = v, over_core(v), over_x(v)
-        else:
-            run("target2", None, after=[sent["tx"]])
-            sent["tc2"] = over_core(sent["tx"])
 
     def forward(g):
         members, wide_all = GROUPS[g], group_width[g] * slots
@@ -420,83 +388,10 @@
         parts = [st["r", g]] + [sent[f"rz{s}{g}"] for s in (1, 2, 3)]
         (v,) = run(f"gene{g}", body, [(a, whole(part)) for a in parts], [(sds(part, F32), whole(part))])
         st["r", g] = v
-        for s in (1, 2, 3):
-            sent[f"gz{s}{g}"] = over_gene(v, s)
-
-    def gather_x(g):
-        w = group_width[g]
-        one, part = (quarter, slots * w), (quarter, w)
-
-        def body(fl, i, out):
-            for s in range(slots):
-                out[0][:, s * w : (s + 1) * w] = i[s][...]
-
-        parts = [st["r", g]] + [sent[f"gz{s}{g}"] for s in (1, 2, 3)]
-        (v,) = run(f"gather{g}", body, [(a, whole(part)) for a in parts], [(sds(one, F32), whole(one))])
-        st["p", g], sent[f"gc{g}"], sent[f"gx{g}"] = v, over_core(v), over_x(v)
-
-    def gather_core(g):
-        v = sent[f"gx{g}"]
-        run(f"gathercore{g}", None, after=[v])
-        sent[f"gd{g}"] = over_core(v)
-
-    def blocks_of(g):
-        return [st["p", g], sent[f"gc{g}"], sent[f"gx{g}"], sent[f"gd{g}"]]
-
-    def blocks_of_target():
-        return [st["t"], sent["tc"], sent["tx"], sent["tc2"]]
-
-    def stats(c):
-        w = group_width[c]
-        wide, o = slots * w, offsets[GROUPS[c][0]] // w
-        n_blk = sizes["cell"]
-        first = c == 0
-
-        def body(fl, i, out):
-            preds, targets, memb = i[:n_blk], i[n_blk : 2 * n_blk], i[2 * n_blk]
-            lane = lax.broadcasted_iota(jnp.int32, (quarter, LANES), 1)
-            valid = jnp.sum(memb[:, SLIDES : SLIDES + 1])
-            out[0][9:16, :] = jnp.broadcast_to(valid, (7, wide))
-            for s in range(slots):
-                at = slice(s * w, (s + 1) * w)
-                rows_k = [jnp.zeros((1, w), F32) for _ in range(9)]
-                for b in range(n_blk):
-                    pr, ta = preds[b][:, at], targets[b][s].astype(F32)
-                    prods = (pr * ta, pr * pr, ta * ta)
-                    mb = slice(b * quarter, (b + 1) * quarter)
-                    spot_vals = [jnp.sum(v, axis=1, keepdims=True) for v in prods]
-                    new = jnp.where(lane == 0, spot_vals[0], 0.0)
-                    new = jnp.where(lane == 1, spot_vals[1], new)
-                    new = jnp.where(lane == 2, spot_vals[2], new)
-                    if s > 0:
-                        new = new + out[1][mb, :]
-                    elif not first:
-                        new = new + i[2 * n_blk + 1][mb, :]
-                    out[1][mb, :] = new
-                    for k in range(SLIDES):
-                        col = memb[mb, k : k + 1]
-                        for j, v in enumerate(prods):
-                            rows_k[3 * j + k] += jnp.sum(col * v, axis=0, keepdims=True)
-                for n, v in enumerate(rows_k):
-                    out[0][n : n + 1, at] = v
-
-        ins = [(a, whole((quarter, wide))) for a in blocks_of(c)]
-        ins += [(a, pl.BlockSpec((slots, quarter, w), lambda *_: (0, 0, o))) for a in blocks_of_target()]
-        ins += [(st["member"], whole((spots, LANES)))]
-        if not first:
-            ins += [(st["sp"], whole((spots, LANES)))]
-        gs, st["sp"] = run(
-            f"stats{c}", body, ins,
-            [(sds((16, wide), F32), whole((16, wide))), (sds((spots, LANES), F32), whole((spots, LANES)))],
-        )
-        if spot_size == 2:
-            sent[f"gs{c}"] = over_spot(gs)
-        st["gs", c] = [gs, sent[f"gs{c}"]] if spot_size == 2 else [sum_spot(gs)]
 
     steps = {
         "Y": start_swap, "A": start_along, "a": along_send, "S": start_back,
-        "e": totals, "m": shares, "t": target, "F": forward, "f": forward_send, "b": members_of, "P": reduce_core, "Q": reduce_x, "R": reduce_gene,
-        "W": gather_x, "H": gather_core, "T": stats,
+        "e": totals, "m": shares, "F": forward, "f": forward_send, "b": members_of, "P": reduce_core, "Q": reduce_x, "R": reduce_gene,
     }
     if spot_size != 2:
         full = lax.all_gather(expression, "spot", axis=0, tiled=True).reshape(slots, rows, genes)
@@ -509,88 +404,99 @@
         elif spot_size == 2 or word[0] not in "YAaS":
             steps[word[0]](int(word[1]))
 
-    n_blk = sizes["cell"]
     n_ch, n_gr = len(WIDTHS), len(GROUPS)
-    n_gs = len(st["gs", 0])
-
-    def grads_body(fl, i, out, coef_t, coef_p):
-        i = list(i)
-        memb, sp, kl, ent = i[:4]
+    starts = [offsets[g[0]] for g in GROUPS]
+    preds = [(st["r", g], whole((quarter, group_width[g]))) for g in range(n_gr)]
+    mine = (spatial, pl.BlockSpec((quarter, genes), lambda g, f: (f[2], 0)))
+    memb = (st["member"], whole((quarter, LANES)))
+    gene_spec, spot_spec = whole((16, genes)), whole((8, quarter))
+
+    def stats_body(fl, i, out):
+        memb = i[0]
+        cols = [jnp.broadcast_to(memb[:, k : k + 1], (quarter, LANES)) for k in range(SLIDES)]
+        valid = jnp.sum(memb[:, SLIDES : SLIDES + 1])
+        out[0][...] = jnp.broadcast_to(valid, (16, genes))
+        totals = [jnp.zeros((quarter, LANES), F32) for _ in range(3)]
+        for g in range(n_gr):
+            for o in range(0, group_width[g], LANES):
+                at = slice(starts[g] + o, starts[g] + o + LANES)
+                pr, ta = i[2 + g][:, o : o + LANES], i[1][:, at].astype(F32)
+                for j, v in enumerate((pr * ta, pr * pr, ta * ta)):
+                    totals[j] += v
+                    for k in range(SLIDES):
+                        n = 3 * j + k
+                        out[0][n : n + 1, at] = jnp.sum(cols[k] * v, axis=0, keepdims=True)
+        out[1][...] = jnp.zeros((8, quarter), F32)
+        for j in range(3):
+            out[1][j : j + 1, :] = jnp.sum(jnp.transpose(totals[j]), axis=0, keepdims=True)
+
+    gene_sums, spot_sums = run(
+        "stats", stats_body, [memb, mine, *preds],
+        [(sds((16, genes), F32), gene_spec), (sds((8, quarter), F32), spot_spec)],
+    )
+    spot_parts = [spot_sums] + [over_gene(spot_sums, s) for s in (1, 2, 3)]
+    gene_sums = gene_sums + over_core(gene_sums)
+    gene_sums = gene_sums + over_x(gene_sums)
+    gene_parts = [gene_sums, over_spot(gene_sums)] if spot_size == 2 else [sum_spot(gene_sums)]
+
+    def grads_body(fl, i, out):
+        memb, ta_ref, kl, ent = i[:4]
         i = i[4:]
-        gss, i = i[: n_gr * n_gs], i[n_gr * n_gs :]
-        preds, targets = i[: n_gr * n_blk], i[n_gr * n_blk :]
+        spot_in, gene_in, preds_in = i[:4], i[4 : 4 + len(gene_parts)], i[4 + len(gene_parts) :]
         scale = -1.0 / (SLIDES * genes_all)
-        sums, weights = [], []
+        sums = sum(ref[...] for ref in gene_in)
+        num, psq, tsq = sums[0:3], sums[3:6], sums[6:9]
+        p_floor, t_floor = jnp.maximum(psq, 1.0), jnp.maximum(tsq, 1.0)
+        root = jnp.sqrt(p_floor * t_floor)
+        cosine = num / root
+        w_t = scale / root
+        w_p = jnp.where(psq > 1.0, -scale * cosine / p_floor, 0.0)
+        valid_total = jnp.maximum(sums[9, 0], 1.0)
+        spot_all = (spot_in[0][...] + spot_in[1][...]) + (spot_in[2][...] + spot_in[3][...])
+        s_num, s_p, s_t = [column(spot_all[n : n + 1, :]) for n in range(3)]
+        s_p, s_t = s_p + 1e-06, s_t + 1e-06
+        root = jnp.sqrt(s_p * s_t)
+        cos_spot = s_num / root
+        valid = jnp.broadcast_to(memb[:, SLIDES : SLIDES + 1], (quarter, LANES))
+        coef = -valid / valid_total
+        coef_t, coef_p = coef / root, -coef * cos_spot / s_p
+        first = [(fl[n] == 0).astype(F32) for n in (2, 4, 3)]
+        terms = [
+            jnp.sum(cosine) * first[0] * first[1],
+            jnp.sum((valid * cos_spot)[:, 0:1]) * first[2],
+            kl[0, 0] * first[1],
+            jnp.sum(ent[0:1, :]),
+            valid_total * first[0] * first[1] * first[2],
+        ]
+        lane = lax.broadcasted_iota(jnp.int32, (8, spots), 1)
+        value = jnp.zeros((8, spots), F32)
+        for n, term in enumerate(terms):
+            value = jnp.where(lane == n, term, value)
+        out[1][...] = value
+        cols = [jnp.broadcast_to(memb[:, k : k + 1], (quarter, LANES)) for k in range(SLIDES)]
         for g in range(n_gr):
-            sums.append(sum(ref[...] for ref in gss[g * n_gs : (g + 1) * n_gs]))
-            num, psq, tsq = sums[g][0:3], sums[g][3:6], sums[g][6:9]
-            p_floor, t_floor = jnp.maximum(psq, 1.0), jnp.maximum(tsq, 1.0)
-            root = jnp.sqrt(p_floor * t_floor)
-            cosine = num / root
-            weights.append((scale / root, jnp.where(psq > 1.0, -scale * cosine / p_floor, 0.0), cosine))
-
-        @pl.when(pl.program_id(0) == 0)
-        def _():
-            valid_total = jnp.maximum(sums[0][9, 0], 1.0)
-            s_num = sp[:, 0:1]
-            s_p, s_t = sp[:, 1:2] + 1e-06, sp[:, 2:3] + 1e-06
-            root = jnp.sqrt(s_p * s_t)
-            cos_spot = s_num / root
-            valid = memb[:, SLIDES : SLIDES + 1]
-            coef = -valid / valid_total
-            coef_t[...] = jnp.broadcast_to(coef / root, (spots, LANES))
-            coef_p[...] = jnp.broadcast_to(-coef * cos_spot / s_p, (spots, LANES))
-            first = [(fl[n] == 0).astype(F32) for n in (2, 4, 3)]
-            terms = [
-                sum(jnp.sum(w[2]) for w in weights) * first[0] * first[1],
-                jnp.sum(valid * cos_spot) * first[0] * first[2],
-                kl[0, 0] * first[1],
-                jnp.sum(ent[0:1, :]),
-                valid_total * first[0] * first[1] * first[2],
-            ]
-            lane = lax.broadcasted_iota(jnp.int32, (8, spots), 1)
-            value = jnp.zeros((8, spots), F32)
-            for n, term in enumerate(terms):
-                value = jnp.where(lane == n, term, value)
-            out[n_ch][...] = value
-
-        for b in range(n_blk):
-            mb = slice(b * quarter, (b + 1) * quarter)
-            cols = [jnp.broadcast_to(memb[mb, k : k + 1], (quarter, LANES)) for k in range(SLIDES)]
-            to = pl.ds(pl.multiple_of((fl[2] ^ b) * quarter, quarter), quarter)
-            for g in range(n_gr):
-                w_t, w_p, _ = weights[g]
-                base = 0
-                for c in GROUPS[g]:
-                    for o in range(0, WIDTHS[c], LANES):
-                        at = slice(base + o, base + o + LANES)
-                        f_t, f_p = coef_t[mb, :], coef_p[mb, :]
-                        for k in range(SLIDES):
-                            f_t = f_t + cols[k] * w_t[k : k + 1, at]
-                            f_p = f_p + cols[k] * w_p[k : k + 1, at]
-                        start = offsets[c] + o
-                        ta = targets[b][0, :, start : start + LANES].astype(F32)
-                        pr = preds[g * n_blk + b][:, at]
-                        out[c][to, o : o + LANES] = (f_t * ta + f_p * pr).astype(BF)
-                    base += WIDTHS[c]
-
-    def by_slot(rows_in, g):
-        return pl.BlockSpec((rows_in, group_width[g]), lambda s, f: (0, s))
-
-    tall, row8, flat = whole((spots, LANES)), whole((8, spots)), whole((8, LANES))
-    ins = [(st["member"], tall), (st["sp"], tall), (st["kl"], flat), (st["ent"], row8)]
-    ins += [(a, by_slot(16, g)) for g in range(n_gr) for a in st["gs", g]]
-    ins += [(a, by_slot(quarter, g)) for g in range(n_gr) for a in blocks_of(g)]
-    ins += [(a, pl.BlockSpec((1, quarter, genes), lambda s, f: (s, 0, 0))) for a in blocks_of_target()]
-    outs = [(sds((spots, slots * w), BF), pl.BlockSpec((spots, w), lambda s, f: (0, s))) for w in WIDTHS]
-    outs += [(sds((8, spots), F32), row8)]
-    *grads, terms = run(
-        "grads", grads_body, ins, outs, grid=(slots,), scratch=[pltpu.VMEM((spots, LANES), F32)] * 2
+            for o in range(0, group_width[g], LANES):
+                at = slice(starts[g] + o, starts[g] + o + LANES)
+                f_t, f_p = coef_t, coef_p
+                for k in range(SLIDES):
+                    f_t = f_t + cols[k] * w_t[k : k + 1, at]
+                    f_p = f_p + cols[k] * w_p[k : k + 1, at]
+                out[0][:, at] = (f_t * ta_ref[:, at].astype(F32) + f_p * preds_in[g][:, o : o + LANES]).astype(BF)
+
+    row8, flat = whole((8, spots)), whole((8, LANES))
+    ins = [memb, mine, (st["kl"], flat), (st["ent"], row8)]
+    ins += [(a, spot_spec) for a in spot_parts] + [(a, gene_spec) for a in gene_parts] + preds
+    grad, terms = run(
+        "grads", grads_body, ins,
+        [(sds((quarter, genes), BF), whole((quarter, genes))), (sds((8, spots), F32), row8)],
     )
+    grad = jnp.stack([grad] + [over_gene(grad, s) for s in (1, 2, 3)])
+    grad_x = over_x(grad)
+    grads = [grad, over_core(grad), grad_x, over_core(grad_x)]
 
     row_blk = rows // 4
 
-    def backward_body(fl, i, out):
+    def backward_body(fl, i, out, held, sems):
         lg, tot, sm, terms = i[:4]
         efs, gs = i[4 : 4 + n_ch], i[4 + n_ch :]
 
@@ -598,10 +504,16 @@
         def _():
             row = lax.broadcasted_iota(jnp.int32, (8, spots), 0)
             out[1][...] = jnp.where(row == 0, 0.0, terms[...])
+            copies = []
+            for b, ref in enumerate(gs):
+                at = pl.multiple_of((fl[2] ^ b) * quarter, quarter)
+                copies.append((None, ref, held.at[:, pl.ds(at, quarter), :]))
+            copy_all(copies, sems)
 
         acc = -jnp.broadcast_to(sm[:, 0:1], (row_blk, spots))
-        for ef, grad in zip(efs, gs):
-            acc += lax.dot_general(ef[...], grad[...], (((1,), (1,)), ((), ())), preferred_element_type=F32)
+        for s in range(slots):
+            left = jnp.concatenate([ef[:, s * w : (s + 1) * w] for w, ef in zip(WIDTHS, efs)], axis=1)
+            acc += lax.dot_general(left, held[s], (((1,), (1,)), ((), ())), preferred_element_type=F32)
         out[0][...] = acc
         prob = jnp.exp(lg[...].astype(F32)) * (1.0 / tot[0:1, :])
         out[1][0:1, :] += jnp.sum(prob * acc, axis=0, keepdims=True)
@@ -611,11 +523,12 @@
 
     ins = [(logits, by_rows(spots)), (st["tot"], row8), (st["sm"], by_rows(LANES)), (terms, row8)]
     ins += [(st["e", c], by_rows(slots * WIDTHS[c])) for c in chunks]
-    ins += [(a, whole(a.shape)) for a in grads]
+    ins += [(a, ANY) for a in grads]
     grad_probs, v = run(
         "backward", backward_body, ins,
         [(sds((rows, spots), F32), by_rows(spots)), (sds((8, spots), F32), row8)],
         grid=(rows // row_blk,),
+        scratch=[pltpu.VMEM((slots, spots, genes), BF), pltpu.SemaphoreType.DMA((len(grads),))],
     )
 
     v = v + over_core(v)

time: 392 us -> 324 us (0.83)
  Pallas kernels: 154 us -> 54.4 us
  waiting for transfers between devices: 139 us -> 171 us
  local copies, waits for them, and re-layouts: 4.46 us -> 15.9 us
  starting transfers between devices: 74.5 us -> 66.1 us
    pallas_call x51 -> x43, Pallas kernels: 154 us -> 54.4 us  [run(): pl.pallas_call(kernel, out_shape=[s for s, _ in outs] + [sds(a.shape, a.d...]
    ppermute x12 -> x11, waiting for transfers between devices: 52.3 us -> 82.3 us  [over_spot(): return lax.ppermute(v, 'spot', xor_pairs(spot_size, step))]
    unnamed x2 -> x58, local copies, waits for them, and re-layouts: 0.01 us -> 13.8 us
    ppermute x33 -> x30, waiting for transfers between devices: 72.9 us -> 63.9 us  [over_gene(): return lax.ppermute(v, 'gene', xor_pairs(4, step))]
    ppermute x9 -> x6, waiting for transfers between devices: 2.83 us -> 8.87 us  [over_core(): return lax.ppermute(v, 'cell', xor_pairs(4, 1))]
    ppermute x6 -> x5, waiting for transfers between devices: 10.7 us -> 15.8 us  [over_x(): return lax.ppermute(v, 'cell', xor_pairs(4, 2))]
    ppermute x33 -> x30, starting transfers between devices: 52.6 us -> 47.7 us  [over_gene(): return lax.ppermute(v, 'gene', xor_pairs(4, step))]
    ppermute x6 -> x5, starting transfers between devices: 8.06 us -> 4.72 us  [over_x(): return lax.ppermute(v, 'cell', xor_pairs(4, 2))]
  transfers between devices with their start and end apart: 60 -> 52, of which waited for: 30 -> 32; matrix products, arithmetic and copies ran while one was open for 0% -> 0% of each run, Pallas kernels for 29% -> 12%
where the time goes in v3:
time: 324 us; the launch traced here: 323 us
  waiting for transfers between devices  171 us (53%)
  starting transfers between devices  66.1 us (20%)
  Pallas kernels  54.4 us (17%)
  local copies, waits for them, and re-layouts  15.9 us (5%)
  blocking collectives  11.3 us (3%)
  between operations  4.57 us (1%)
    ppermute x11, waiting for transfers between devices, over_spot(): return lax.ppermute(v, 'spot', xor_pairs(spot_size, step))  82.3 us
    ppermute x30, waiting for transfers between devices, over_gene(): return lax.ppermute(v, 'gene', xor_pairs(4, step))  63.9 us
    pallas_call x43, Pallas kernels, run(): pl.pallas_call(kernel, out_shape=[s for s, _ in outs] + [sds(a.shape, a.d...  54.4 us
    ppermute x30, starting transfers between devices, over_gene(): return lax.ppermute(v, 'gene', xor_pairs(4, step))  47.7 us
    ppermute x5, waiting for transfers between devices, over_x(): return lax.ppermute(v, 'cell', xor_pairs(4, 2))  15.8 us
    unnamed x58, local copies, waits for them, and re-layouts  13.8 us
    ppermute x11, starting transfers between devices, over_spot(): return lax.ppermute(v, 'spot', xor_pairs(spot_size, step))  13.3 us
    psum x1, blocking collectives, totals(): st['tot'] = lax.psum(v, 'cell')  11.3 us
  transfers between devices with their start and end apart: 52, of which 32 were waited for; matrix products, arithmetic and copies ran while one was open for 0% of the time, Pallas kernels for 12%

profile of v3, /device:TPU:0, one launch (start us, length us, event | category | flops | bytes accessed | tf_op | source)
XLA Modules:
  0.0 323.3 jit_solution(11428017227503151565)
XLA Ops:
  0.8 2.6 copy-done
  4.3 3.0 collective-permute-start.3
  10.6 2.0 swap1.1
  13.1 11.3 %psum.7.refs_1_ = f32[8,512]{1,0:T(8,128)S(1)} all-reduce(f32[8,512]{1,0:T(8,128)S(1)} %get-tuple-element.107), channel_id=1, replica_groups=mesh['cell'=4,'spot'=2,'gene'=4] {'cell'}, use_global_device_ids=true, to_apply=%region_0.1 | all-reduce | flops 4096 | bytes 32768 | tf_op jit(solution)/shard_map/psum | solution.py:218
  26.1 2.6 collective-permute-start.1
  30.8 3.4 %collective-permute-done.2.refs_2_.refs_4_ = f32[8,512]{1,0:T(8,128)S(1)} collective-permute-done((f32[8,512]{1,0:T(8,128)S(1)}, f32[8,512]{1,0:T(8,128)S(1)}, u32[]{:S(2)}, u32[]{:S(2)}) %collective-permute-start.2) | collective-permute-done | bytes 16416 | tf_op jit(solution)/shard_map/ppermute | solution.py:119
  34.7 2.6 copy-done.2
  41.3 2.2 collective-permute-start.5
  45.0 2.6 collective-permute-start.6
  47.8 4.0 %prob.1 = (bf16[512,2816]{1,0:T(8,128)(2,1)S(1)}, f32[8,2816]{1,0:T(8,128)S(1)}, f32[8,512]{1,0:T(8,128)S(1)}, f32[8,512]{1,0:T(8,128)S(1)}, f32[8,128]{1,0:T(8,128)S(1)}) custom-call(s32[5]{0:T(128)S(1)} %stack.57.flags, bf16[2816,512]{1,0:T(8,128)(2,1)S(1)} %copy-done.4, f32[8,512]{1,0:T(8,128)S(1)} %psum.7.refs_1_, ...), custom_call_target="tpu_custom_call", output_to_operand_aliasing={{4}: (6, {})} | custom-call | tf_op jit(solution)/shard_map/prob/pallas_call | solution.py:61
  54.1 16.7 %collective-permute-done.9.refs_0_.refs_1_.refs_6_.refs_7_ = bf16[2,2816,128]{2,1,0:T(8,128)(2,1)} collective-permute-done((bf16[2,2816,128]{2,1,0:T(8,128)(2,1)}, bf16[2,2816,128]{2,1,0:T(8,128)(2,1)}, u32[]{:S(2)}, u32[]{:S(2)}) %collective-permute-start.9) | collective-permute-done | bytes 1441824 | tf_op jit(solution)/shard_map/ppermute | solution.py:122
  70.8 2.0 along1.1
  76.4 2.0 collective-permute-start.12
  78.9 2.3 collective-permute-start.10
  82.4 19.2 %collective-permute-done.8.refs_0_.refs_1_.refs_6_.refs_7_.refs_2_ = bf16[2,2816,128]{2,1,0:T(8,128)(2,1)S(1)} collective-permute-done((bf16[2,2816,128]{2,1,0:T(8,128)(2,1)S(1)}, bf16[2,2816,128]{2,1,0:T(8,128)(2,1)S(1)}, u32[]{:S(2)}, u32[]{:S(2)}) %collective-permute-start.8) | collective-permute-done | bytes 1441824 | tf_op jit(solution)/shard_map/ppermute | solution.py:122
  102.5 7.6 %collective-permute-done.11.refs_1_ = bf16[1408,128]{1,0:T(8,128)(2,1)S(1)} collective-permute-done((bf16[1408,128]{1,0:T(8,128)(2,1)S(1)}, bf16[1408,128]{1,0:T(8,128)(2,1)S(1)}, u32[]{:S(2)}, u32[]{:S(2)}) %collective-permute-start.11) | collective-permute-done | bytes 360480 | tf_op jit(solution)/shard_map/ppermute | solution.py:119
  114.4 2.4 collective-permute-start.16
  116.7 15.8 %collective-permute-done.14.refs_0_.refs_1_.refs_6_.refs_7_ = bf16[2,2816,128]{2,1,0:T(8,128)(2,1)S(1)} collective-permute-done((bf16[2,2816,128]{2,1,0:T(8,128)(2,1)S(1)}, bf16[2,2816,128]{2,1,0:T(8,128)(2,1)S(1)}, u32[]{:S(2)}, u32[]{:S(2)}) %collective-permute-start.14) | collective-permute-done | bytes 1441824 | tf_op jit(solution)/shard_map/ppermute | solution.py:122
  133.4 6.6 %collective-permute-done.16.refs_1_ = bf16[1408,128]{1,0:T(8,128)(2,1)S(1)} collective-permute-done((bf16[1408,128]{1,0:T(8,128)(2,1)S(1)}, bf16[1408,128]{1,0:T(8,128)(2,1)S(1)}, u32[]{:S(2)}, u32[]{:S(2)}) %collective-permute-start.16) | collective-permute-done | bytes 360480 | tf_op jit(solution)/shard_map/ppermute | solution.py:119
  143.5 4.4 %collective-permute-done.13.refs_0_.refs_5_ = bf16[2,1408,128]{2,1,0:T(8,128)(2,1)S(1)} collective-permute-done((bf16[2,1408,128]{2,1,0:T(8,128)(2,1)S(1)}, bf16[2,1408,128]{2,1,0:T(8,128)(2,1)S(1)}, u32[]{:S(2)}, u32[]{:S(2)}) %collective-permute-start.13) | collective-permute-done | bytes 720928 | tf_op jit(solution)/shard_map/ppermute | solution.py:122
  149.1 2.1 collective-permute-start.21
  152.8 2.6 collective-permute-start.19
  155.6 7.8 %collective-permute-done.18.refs_0_.refs_9_ = bf16[2,1408,128]{2,1,0:T(8,128)(2,1)S(1)} collective-permute-done((bf16[2,1408,128]{2,1,0:T(8,128)(2,1)S(1)}, bf16[2,1408,128]{2,1,0:T(8,128)(2,1)S(1)}, u32[]{:S(2)}, u32[]{:S(2)}) %collective-permute-start.18) | collective-permute-done | bytes 720928 | tf_op jit(solution)/shard_map/ppermute | solution.py:122
  163.9 5.0 %forward0.1 = (bf16[2816,512]{1,0:T(8,128)(2,1)S(1)}, bf16[2816,512]{1,0:T(8,128)(2,1)S(1)}, f32[2,128,1024]{2,1,0:T(8,128)S(1)}, f32[2,128,1024]{2,1,0:T(8,128)S(1)}, f32[8,128]{1,0:T(8,128)S(1)}) custom-call(s32[5]{0:T(128)S(1)} %stack.57.flags, bf16[512,2816]{1,0:T(8,128)(2,1)S(1)} %copy-done.6, ...), custom_call_target="tpu_custom_call", output_to_operand_aliasing={{4}: (11, {})} | custom-call | tf_op jit(solution)/shard_map/forward0/pallas_call | solution.py:61
  168.9 8.2 %collective-permute-done.19.refs_1_.refs_0_ = bf16[1408,128]{1,0:T(8,128)(2,1)S(1)} collective-permute-done((bf16[1408,128]{1,0:T(8,128)(2,1)S(1)}, bf16[1408,128]{1,0:T(8,128)(2,1)S(1)}, u32[]{:S(2)}, u32[]{:S(2)}) %collective-permute-start.19) | collective-permute-done | bytes 360480 | tf_op jit(solution)/shard_map/ppermute | solution.py:119
  177.2 7.2 %collective-permute-done.20.refs_2_.refs_1_ = bf16[1408,128]{1,0:T(8,128)(2,1)S(1)} collective-permute-done((bf16[1408,128]{1,0:T(8,128)(2,1)S(1)}, bf16[1408,128]{1,0:T(8,128)(2,1)S(1)}, u32[]{:S(2)}, u32[]{:S(2)}) %collective-permute-start.20) | collective-permute-done | bytes 360480 | tf_op jit(solution)/shard_map/ppermute | solution.py:119
  187.6 2.1 collective-permute-done.23.refs_1_
  192.7 12.9 %collective-permute-done.25.refs_0_.refs_9_ = bf16[2,1408,128]{2,1,0:T(8,128)(2,1)S(1)} collective-permute-done((bf16[2,1408,128]{2,1,0:T(8,128)(2,1)S(1)}, bf16[2,1408,128]{2,1,0:T(8,128)(2,1)S(1)}, u32[]{:S(2)}, u32[]{:S(2)}) %collective-permute-start.25) | collective-permute-done | bytes 720928 | tf_op jit(solution)/shard_map/ppermute | solution.py:122
  206.2 5.1 %forward1.1 = (bf16[2816,512]{1,0:T(8,128)(2,1)S(1)}, bf16[2816,512]{1,0:T(8,128)(2,1)S(1)}, f32[2,128,1024]{2,1,0:T(8,128)S(1)}, f32[2,128,1024]{2,1,0:T(8,128)S(1)}, f32[8,128]{1,0:T(8,128)S(1)}) custom-call(s32[5]{0:T(128)S(1)} %stack.57.flags, bf16[512,2816]{1,0:T(8,128)(2,1)S(1)} %copy-done.6, ...), custom_call_target="tpu_custom_call", output_to_operand_aliasing={{4}: (11, {})} | custom-call | tf_op jit(solution)/shard_map/forward1/pallas_call | solution.py:61
  214.2 2.6 collective-permute-done.26.refs_1_
  221.7 2.4 collective-permute-start.29
  224.6 4.0 %collective-permute-done.4.refs_3_ = f32[8,2816]{1,0:T(8,128)S(1)} collective-permute-done((f32[8,2816]{1,0:T(8,128)S(1)}, f32[8,2816]{1,0:T(8,128)S(1)}, u32[]{:S(2)}, u32[]{:S(2)}) %collective-permute-start.4) | collective-permute-done | bytes 90144 | tf_op jit(solution)/shard_map/ppermute | solution.py:122
  229.7 3.6 %collective-permute-done.28.refs_2_ = f32[128,256]{1,0:T(8,128)S(1)} collective-permute-done((f32[128,256]{1,0:T(8,128)S(1)}, f32[128,256]{1,0:T(8,128)S(1)}, u32[]{:S(2)}, u32[]{:S(2)}) %collective-permute-start.28) | collective-permute-done | bytes 131104 | tf_op jit(solution)/shard_map/ppermute | solution.py:119
  234.5 2.0 collective-permute-start.31
  239.0 2.0 collective-permute-done.31.refs_1_
  241.0 7.6 %collective-permute-done.32.refs_2_ = f32[128,256]{1,0:T(8,128)S(1)} collective-permute-done((f32[128,256]{1,0:T(8,128)S(1)}, f32[128,256]{1,0:T(8,128)S(1)}, u32[]{:S(2)}, u32[]{:S(2)}) %collective-permute-start.32) | collective-permute-done | bytes 131104 | tf_op jit(solution)/shard_map/ppermute | solution.py:119
  251.8 3.4 %collective-permute-done.38 = f32[16,512]{1,0:T(8,128)S(1)} collective-permute-done((f32[16,512]{1,0:T(8,128)S(1)}, f32[16,512]{1,0:T(8,128)S(1)}, u32[]{:S(2)}, u32[]{:S(2)}) %collective-permute-start.38) | collective-permute-done | bytes 32800 | tf_op jit(solution)/shard_map/ppermute | solution.py:116
  255.7 2.0 collective-permute-start.34
  260.1 2.1 collective-permute-done.35.refs_6_
  265.2 2.4 collective-permute-start.42
  268.6 6.5 %collective-permute-done.41 = bf16[128,512]{1,0:T(8,128)(2,1)S(1)} collective-permute-done((bf16[128,512]{1,0:T(8,128)(2,1)S(1)}, bf16[128,512]{1,0:T(8,128)(2,1)S(1)}, u32[]{:S(2)}, u32[]{:S(2)}) %collective-permute-start.41) | collective-permute-done | bytes 131104 | tf_op jit(solution)/shard_map/ppermute | solution.py:119
  275.9 9.3 %collective-permute-done.44.refs_10_ = bf16[4,128,512]{2,1,0:T(8,128)(2,1)S(1)} collective-permute-done((bf16[4,128,512]{2,1,0:T(8,128)(2,1)S(1)}, bf16[4,128,512]{2,1,0:T(8,128)(2,1)S(1)}, u32[]{:S(2)}, u32[]{:S(2)}) %collective-permute-start.44) | collective-permute-done | bytes 524320 | tf_op jit(solution)/shard_map/ppermute | solution.py:116
  285.2 1.9 collective-permute-done.45.refs_11_
  288.9 8.0 %backward.1 = (f32[2816,512]{1,0:T(8,128)S(1)}, f32[8,512]{1,0:T(8,128)S(1)}, f32[8,128]{1,0:T(8,128)S(1)}) custom-call(s32[5]{0:T(128)S(1)} %stack.57.flags, bf16[2816,512]{1,0:T(8,128)(2,1)S(1)} %copy-done.4, f32[8,512]{1,0:T(8,128)S(1)} %get-tuple-element.117.refs_1_, ...), custom_call_target="tpu_custom_call", output_to_operand_aliasing={{2}: (13, {})} | custom-call | tf_op jit(solution)/shard_map/backward/pallas_call | solution.py:61
  298.7 3.2 collective-permute-done.47
  301.9 4.8 %collective-permute-start.48 = (f32[8,512]{1,0:T(8,128)S(1)}, f32[8,512]{1,0:T(8,128)S(1)}, u32[]{:S(2)}, u32[]{:S(2)}) collective-permute-start(f32[8,512]{1,0:T(8,128)S(1)} %add.35), channel_id=1, source_target_pairs={{0,1},{1,0},{2,3},{3,2},{4,5},{5,4},{6,7},{7,6},{8,9},{9,8},{10,11... | collective-permute-start | bytes 49160 | tf_op jit(solution)/shard_map/ppermute | solution.py:119
  309.1 2.2 collective-permute-done.49
  314.5 3.7 %final.1 = (f32[2816,512]{1,0:T(8,128)}, f32[8,128]{1,0:T(8,128)S(1)}) custom-call(s32[5]{0:T(128)S(1)} %stack.57.flags, bf16[2816,512]{1,0:T(8,128)(2,1)S(1)} %copy-done.4, f32[8,512]{1,0:T(8,128)S(1)} %get-tuple-element.117.refs_1_, f32[2816,512]{1,0:T(8,128)S(1)} %get-tuple-element.207.refs_2_, ...), custom_call_target="tpu_custom_call", output_to_operand_aliasing={{1}: (5, {})} | custom-call | tf_op jit(solution)/shard_map/final/pallas_call | solution.py:61
  (171 shorter events, 76.7 us)
Async XLA Ops:
  4.3 35.4 %collective-permute-start.3 = (bf16[2,2816,128]{2,1,0:T(8,128)(2,1)S(1)}, bf16[2,2816,128]{2,1,0:T(8,128)(2,1)S(1)}, u32[]{:S(2)}, u32[]{:S(2)}) collective-permute-start(bf16[2,2816,128]{2,1,0:T(8,128)(2,1)S(1)} %get-tuple-element.108), channel_id=1, source_target_pairs={{0,4},{4,0},{1,5},{5,1},{2,6},{6,2},{3,7},{7,3},{8,12},{12,8},{9,1... | collective-permute-start | bytes 4325384 | tf_op jit(solution)/shard_map/ppermute | solution.py:122
  12.6 58.2 %collective-permute-start.9 = (bf16[2,2816,128]{2,1,0:T(8,128)(2,1)}, bf16[2,2816,128]{2,1,0:T(8,128)(2,1)}, u32[]{:S(2)}, u32[]{:S(2)}) collective-permute-start(bf16[2,2816,128]{2,1,0:T(8,128)(2,1)} %get-tuple-element.124), channel_id=1, source_target_pairs={{0,4},{4,0},{1,5},{5,1},{2,6},{6,2},{3,7},{7,3},{8,12},{12,8},{9,1... | collective-permute-start | bytes 4325384 | tf_op jit(solution)/shard_map/ppermute | solution.py:122
  24.5 4.4 %collective-permute-start = (f32[8,512]{1,0:T(8,128)S(1)}, f32[8,512]{1,0:T(8,128)S(1)}, u32[]{:S(2)}, u32[]{:S(2)}) collective-permute-start(f32[8,512]{1,0:T(8,128)S(1)} %psum.7.refs_1_), channel_id=1, source_target_pairs={{0,1},{1,0},{2,3},{3,2},{4,5},{5,4},{6,7},{7,6},{8,9},{9,8},{10,11... | collective-permute-start | bytes 49160 | tf_op jit(solution)/shard_map/ppermute | solution.py:119
  26.1 4.7 %collective-permute-start.1 = (f32[8,512]{1,0:T(8,128)S(1)}, f32[8,512]{1,0:T(8,128)S(1)}, u32[]{:S(2)}, u32[]{:S(2)}) collective-permute-start(f32[8,512]{1,0:T(8,128)S(1)} %psum.7.refs_1_), channel_id=1, source_target_pairs={{0,2},{1,3},{2,0},{3,1},{4,6},{5,7},{6,4},{7,5},{8,10},{9,11},{10,... | collective-permute-start | bytes 49160 | tf_op jit(solution)/shard_map/ppermute | solution.py:119
  28.6 5.5 %collective-permute-start.2 = (f32[8,512]{1,0:T(8,128)S(1)}, f32[8,512]{1,0:T(8,128)S(1)}, u32[]{:S(2)}, u32[]{:S(2)}) collective-permute-start(f32[8,512]{1,0:T(8,128)S(1)} %psum.7.refs_1_), channel_id=1, source_target_pairs={{0,3},{1,2},{2,1},{3,0},{4,7},{5,6},{6,5},{7,4},{8,11},{9,10},{10,... | collective-permute-start | bytes 49160 | tf_op jit(solution)/shard_map/ppermute | solution.py:119
  41.3 34.0 %collective-permute-start.5 = (bf16[2,1408,128]{2,1,0:T(8,128)(2,1)S(1)}, bf16[2,1408,128]{2,1,0:T(8,128)(2,1)S(1)}, u32[]{:S(2)}, u32[]{:S(2)}) collective-permute-start(bf16[2,1408,128]{2,1,0:T(8,128)(2,1)S(1)} %get-tuple-element.120), channel_id=1, source_target_pairs={{0,1},{1,0},{2,3},{3,2},{4,5},{5,4},{6,7},{7,6},{8,9},{9,8},{10,11... | collective-permute-start | bytes 2162696 | tf_op jit(solution)/shard_map/ppermute | solution.py:119
  43.5 58.1 %collective-permute-start.8 = (bf16[2,2816,128]{2,1,0:T(8,128)(2,1)S(1)}, bf16[2,2816,128]{2,1,0:T(8,128)(2,1)S(1)}, u32[]{:S(2)}, u32[]{:S(2)}) collective-permute-start(bf16[2,2816,128]{2,1,0:T(8,128)(2,1)S(1)} %get-tuple-element.123), channel_id=1, source_target_pairs={{0,4},{4,0},{1,5},{5,1},{2,6},{6,2},{3,7},{7,3},{8,12},{12,8},{9,1... | collective-permute-start | bytes 4325384 | tf_op jit(solution)/shard_map/ppermute | solution.py:122
  45.0 28.8 %collective-permute-start.6 = (bf16[1408,128]{1,0:T(8,128)(2,1)S(1)}, bf16[1408,128]{1,0:T(8,128)(2,1)S(1)}, u32[]{:S(2)}, u32[]{:S(2)}) collective-permute-start(bf16[1408,128]{1,0:T(8,128)(2,1)S(1)} %get-tuple-element.121), channel_id=1, source_target_pairs={{0,2},{1,3},{2,0},{3,1},{4,6},{5,7},{6,4},{7,5},{8,10},{9,11},{10,... | collective-permute-start | bytes 1081352 | tf_op jit(solution)/shard_map/ppermute | solution.py:119
  47.6 27.8 %collective-permute-start.7 = (bf16[1408,128]{1,0:T(8,128)(2,1)S(1)}, bf16[1408,128]{1,0:T(8,128)(2,1)S(1)}, u32[]{:S(2)}, u32[]{:S(2)}) collective-permute-start(bf16[1408,128]{1,0:T(8,128)(2,1)S(1)} %get-tuple-element.122), channel_id=1, source_target_pairs={{0,3},{1,2},{2,1},{3,0},{4,7},{5,6},{6,5},{7,4},{8,11},{9,10},{10,... | collective-permute-start | bytes 1081352 | tf_op jit(solution)/shard_map/ppermute | solution.py:119
  76.4 33.7 %collective-permute-start.12 = (bf16[2,1408,128]{2,1,0:T(8,128)(2,1)S(1)}, bf16[2,1408,128]{2,1,0:T(8,128)(2,1)S(1)}, u32[]{:S(2)}, u32[]{:S(2)}) collective-permute-start(bf16[2,1408,128]{2,1,0:T(8,128)(2,1)S(1)} %get-tuple-element.138), channel_id=1, source_target_pairs={{0,1},{1,0},{2,3},{3,2},{4,5},{5,4},{6,7},{7,6},{8,9},{9,8},{10,11... | collective-permute-start | bytes 2162696 | tf_op jit(solution)/shard_map/ppermute | solution.py:119
  78.4 54.1 %collective-permute-start.14 = (bf16[2,2816,128]{2,1,0:T(8,128)(2,1)S(1)}, bf16[2,2816,128]{2,1,0:T(8,128)(2,1)S(1)}, u32[]{:S(2)}, u32[]{:S(2)}) collective-permute-start(bf16[2,2816,128]{2,1,0:T(8,128)(2,1)S(1)} %get-tuple-element.142), channel_id=1, source_target_pairs={{0,4},{4,0},{1,5},{5,1},{2,6},{6,2},{3,7},{7,3},{8,12},{12,8},{9,1... | collective-permute-start | bytes 4325384 | tf_op jit(solution)/shard_map/ppermute | solution.py:122
  78.9 23.6 %collective-permute-start.10 = (bf16[1408,128]{1,0:T(8,128)(2,1)S(1)}, bf16[1408,128]{1,0:T(8,128)(2,1)S(1)}, u32[]{:S(2)}, u32[]{:S(2)}) collective-permute-start(bf16[1408,128]{1,0:T(8,128)(2,1)S(1)} %get-tuple-element.136), channel_id=1, source_target_pairs={{0,2},{1,3},{2,0},{3,1},{4,6},{5,7},{6,4},{7,5},{8,10},{9,11},{10,... | collective-permute-start | bytes 1081352 | tf_op jit(solution)/shard_map/ppermute | solution.py:119
  81.2 28.9 %collective-permute-start.11 = (bf16[1408,128]{1,0:T(8,128)(2,1)S(1)}, bf16[1408,128]{1,0:T(8,128)(2,1)S(1)}, u32[]{:S(2)}, u32[]{:S(2)}) collective-permute-start(bf16[1408,128]{1,0:T(8,128)(2,1)S(1)} %get-tuple-element.137), channel_id=1, source_target_pairs={{0,3},{1,2},{2,1},{3,0},{4,7},{5,6},{6,5},{7,4},{8,11},{9,10},{10,... | collective-permute-start | bytes 1081352 | tf_op jit(solution)/shard_map/ppermute | solution.py:119
  111.2 28.8 %collective-permute-start.17 = (bf16[2,1408,128]{2,1,0:T(8,128)(2,1)S(1)}, bf16[2,1408,128]{2,1,0:T(8,128)(2,1)S(1)}, u32[]{:S(2)}, u32[]{:S(2)}) collective-permute-start(bf16[2,1408,128]{2,1,0:T(8,128)(2,1)S(1)} %get-tuple-element.149), channel_id=1, source_target_pairs={{0,1},{1,0},{2,3},{3,2},{4,5},{5,4},{6,7},{7,6},{8,9},{9,8},{10,11... | collective-permute-start | bytes 2162696 | tf_op jit(solution)/shard_map/ppermute | solution.py:119
  112.7 35.3 %collective-permute-start.13 = (bf16[2,1408,128]{2,1,0:T(8,128)(2,1)S(1)}, bf16[2,1408,128]{2,1,0:T(8,128)(2,1)S(1)}, u32[]{:S(2)}, u32[]{:S(2)}) collective-permute-start(bf16[2,1408,128]{2,1,0:T(8,128)(2,1)S(1)} %get-tuple-element.141.refs_4_), channel_id=1, source_target_pairs={{0,4},{4,0},{1,5},{5,1},{2,6},{6,2},{3,7},{7,3},{8,12},{12,8},{9,1... | collective-permute-start | bytes 2162696 | tf_op jit(solution)/shard_map/ppermute | solution.py:122
  113.3 20.1 %collective-permute-start.15 = (bf16[1408,128]{1,0:T(8,128)(2,1)S(1)}, bf16[1408,128]{1,0:T(8,128)(2,1)S(1)}, u32[]{:S(2)}, u32[]{:S(2)}) collective-permute-start(bf16[1408,128]{1,0:T(8,128)(2,1)S(1)} %get-tuple-element.147), channel_id=1, source_target_pairs={{0,2},{1,3},{2,0},{3,1},{4,6},{5,7},{6,4},{7,5},{8,10},{9,11},{10,... | collective-permute-start | bytes 1081352 | tf_op jit(solution)/shard_map/ppermute | solution.py:119
  114.4 25.6 %collective-permute-start.16 = (bf16[1408,128]{1,0:T(8,128)(2,1)S(1)}, bf16[1408,128]{1,0:T(8,128)(2,1)S(1)}, u32[]{:S(2)}, u32[]{:S(2)}) collective-permute-start(bf16[1408,128]{1,0:T(8,128)(2,1)S(1)} %get-tuple-element.148), channel_id=1, source_target_pairs={{0,3},{1,2},{2,1},{3,0},{4,7},{5,6},{6,5},{7,4},{8,11},{9,10},{10,... | collective-permute-start | bytes 1081352 | tf_op jit(solution)/shard_map/ppermute | solution.py:119
  141.7 21.7 %collective-permute-start.18 = (bf16[2,1408,128]{2,1,0:T(8,128)(2,1)S(1)}, bf16[2,1408,128]{2,1,0:T(8,128)(2,1)S(1)}, u32[]{:S(2)}, u32[]{:S(2)}) collective-permute-start(bf16[2,1408,128]{2,1,0:T(8,128)(2,1)S(1)} %get-tuple-element.152.refs_8_), channel_id=1, source_target_pairs={{0,4},{4,0},{1,5},{5,1},{2,6},{6,2},{3,7},{7,3},{8,12},{12,8},{9,1... | collective-permute-start | bytes 2162696 | tf_op jit(solution)/shard_map/ppermute | solution.py:122
  149.1 35.3 %collective-permute-start.21 = (bf16[2,1408,128]{2,1,0:T(8,128)(2,1)S(1)}, bf16[2,1408,128]{2,1,0:T(8,128)(2,1)S(1)}, u32[]{:S(2)}, u32[]{:S(2)}) collective-permute-start(bf16[2,1408,128]{2,1,0:T(8,128)(2,1)S(1)} %get-tuple-element.159.refs_4_), channel_id=1, source_target_pairs={{0,4},{4,0},{1,5},{5,1},{2,6},{6,2},{3,7},{7,3},{8,12},{12,8},{9,1... | collective-permute-start | bytes 2162696 | tf_op jit(solution)/shard_map/ppermute | solution.py:122
  151.2 33.2 %collective-permute-start.22 = (bf16[2,1408,128]{2,1,0:T(8,128)(2,1)S(1)}, bf16[2,1408,128]{2,1,0:T(8,128)(2,1)S(1)}, u32[]{:S(2)}, u32[]{:S(2)}) collective-permute-start(bf16[2,1408,128]{2,1,0:T(8,128)(2,1)S(1)} %get-tuple-element.160), channel_id=1, source_target_pairs={{0,1},{1,0},{2,3},{3,2},{4,5},{5,4},{6,7},{7,6},{8,9},{9,8},{10,11... | collective-permute-start | bytes 2162696 | tf_op jit(solution)/shard_map/ppermute | solution.py:119
  152.8 24.4 %collective-permute-start.19 = (bf16[1408,128]{1,0:T(8,128)(2,1)S(1)}, bf16[1408,128]{1,0:T(8,128)(2,1)S(1)}, u32[]{:S(2)}, u32[]{:S(2)}) collective-permute-start(bf16[1408,128]{1,0:T(8,128)(2,1)S(1)} %get-tuple-element.157), channel_id=1, source_target_pairs={{0,2},{1,3},{2,0},{3,1},{4,6},{5,7},{6,4},{7,5},{8,10},{9,11},{10,... | collective-permute-start | bytes 1081352 | tf_op jit(solution)/shard_map/ppermute | solution.py:119
  155.4 29.0 %collective-permute-start.20 = (bf16[1408,128]{1,0:T(8,128)(2,1)S(1)}, bf16[1408,128]{1,0:T(8,128)(2,1)S(1)}, u32[]{:S(2)}, u32[]{:S(2)}) collective-permute-start(bf16[1408,128]{1,0:T(8,128)(2,1)S(1)} %get-tuple-element.158), channel_id=1, source_target_pairs={{0,3},{1,2},{2,1},{3,0},{4,7},{5,6},{6,5},{7,4},{8,11},{9,10},{10,... | collective-permute-start | bytes 1081352 | tf_op jit(solution)/shard_map/ppermute | solution.py:119
  187.0 2.7 collective-permute-start.23
  187.1 18.6 %collective-permute-start.25 = (bf16[2,1408,128]{2,1,0:T(8,128)(2,1)S(1)}, bf16[2,1408,128]{2,1,0:T(8,128)(2,1)S(1)}, u32[]{:S(2)}, u32[]{:S(2)}) collective-permute-start(bf16[2,1408,128]{2,1,0:T(8,128)(2,1)S(1)} %get-tuple-element.167.refs_8_), channel_id=1, source_target_pairs={{0,4},{4,0},{1,5},{5,1},{2,6},{6,2},{3,7},{7,3},{8,12},{12,8},{9,1... | collective-permute-start | bytes 2162696 | tf_op jit(solution)/shard_map/ppermute | solution.py:122
  191.2 21.8 %collective-permute-start.24 = (f32[128,1024]{1,0:T(8,128)S(1)}, f32[128,1024]{1,0:T(8,128)S(1)}, u32[]{:S(2)}, u32[]{:S(2)}) collective-permute-start(f32[128,1024]{1,0:T(8,128)S(1)} %get-tuple-element.166), channel_id=1, source_target_pairs={{0,16},{8,24},{16,0},{24,8},{1,17},{9,25},{17,1},{25,9},{2,18},{10... | collective-permute-start | bytes 1572872 | tf_op jit(solution)/shard_map/ppermute | solution.py:116
  217.5 16.4 %collective-permute-start.30 = (f32[128,1024]{1,0:T(8,128)S(1)}, f32[128,1024]{1,0:T(8,128)S(1)}, u32[]{:S(2)}, u32[]{:S(2)}) collective-permute-start(f32[128,1024]{1,0:T(8,128)S(1)} %get-tuple-element.187), channel_id=1, source_target_pairs={{0,16},{8,24},{16,0},{24,8},{1,17},{9,25},{17,1},{25,9},{2,18},{10... | collective-permute-start | bytes 1572872 | tf_op jit(solution)/shard_map/ppermute | solution.py:116
  219.6 10.1 %collective-permute-start.27 = (f32[128,256]{1,0:T(8,128)S(1)}, f32[128,256]{1,0:T(8,128)S(1)}, u32[]{:S(2)}, u32[]{:S(2)}) collective-permute-start(f32[128,256]{1,0:T(8,128)S(1)} %get-tuple-element.181), channel_id=1, source_target_pairs={{0,1},{1,0},{2,3},{3,2},{4,5},{5,4},{6,7},{7,6},{8,9},{9,8},{10,11... | collective-permute-start | bytes 393224 | tf_op jit(solution)/shard_map/ppermute | solution.py:119
  220.4 12.9 %collective-permute-start.28 = (f32[128,256]{1,0:T(8,128)S(1)}, f32[128,256]{1,0:T(8,128)S(1)}, u32[]{:S(2)}, u32[]{:S(2)}) collective-permute-start(f32[128,256]{1,0:T(8,128)S(1)} %get-tuple-element.182), channel_id=1, source_target_pairs={{0,2},{1,3},{2,0},{3,1},{4,6},{5,7},{6,4},{7,5},{8,10},{9,11},{10,... | collective-permute-start | bytes 393224 | tf_op jit(solution)/shard_map/ppermute | solution.py:119
  221.7 11.6 %collective-permute-start.29 = (f32[128,256]{1,0:T(8,128)S(1)}, f32[128,256]{1,0:T(8,128)S(1)}, u32[]{:S(2)}, u32[]{:S(2)}) collective-permute-start(f32[128,256]{1,0:T(8,128)S(1)} %get-tuple-element.183), channel_id=1, source_target_pairs={{0,3},{1,2},{2,1},{3,0},{4,7},{5,6},{6,5},{7,4},{8,11},{9,10},{10,... | collective-permute-start | bytes 393224 | tf_op jit(solution)/shard_map/ppermute | solution.py:119
  224.1 4.5 %collective-permute-start.4 = (f32[8,2816]{1,0:T(8,128)S(1)}, f32[8,2816]{1,0:T(8,128)S(1)}, u32[]{:S(2)}, u32[]{:S(2)}) collective-permute-start(f32[8,2816]{1,0:T(8,128)S(1)} %get-tuple-element.118.refs_2_), channel_id=1, source_target_pairs={{0,4},{4,0},{1,5},{5,1},{2,6},{6,2},{3,7},{7,3},{8,12},{12,8},{9,1... | collective-permute-start | bytes 270344 | tf_op jit(solution)/shard_map/ppermute | solution.py:122
  234.5 6.4 %collective-permute-start.31 = (f32[128,256]{1,0:T(8,128)S(1)}, f32[128,256]{1,0:T(8,128)S(1)}, u32[]{:S(2)}, u32[]{:S(2)}) collective-permute-start(f32[128,256]{1,0:T(8,128)S(1)} %get-tuple-element.190), channel_id=1, source_target_pairs={{0,1},{1,0},{2,3},{3,2},{4,5},{5,4},{6,7},{7,6},{8,9},{9,8},{10,11... | collective-permute-start | bytes 393224 | tf_op jit(solution)/shard_map/ppermute | solution.py:119
  236.6 12.0 %collective-permute-start.32 = (f32[128,256]{1,0:T(8,128)S(1)}, f32[128,256]{1,0:T(8,128)S(1)}, u32[]{:S(2)}, u32[]{:S(2)}) collective-permute-start(f32[128,256]{1,0:T(8,128)S(1)} %get-tuple-element.191), channel_id=1, source_target_pairs={{0,2},{1,3},{2,0},{3,1},{4,6},{5,7},{6,4},{7,5},{8,10},{9,11},{10,... | collective-permute-start | bytes 393224 | tf_op jit(solution)/shard_map/ppermute | solution.py:119
  237.6 10.9 %collective-permute-start.33 = (f32[128,256]{1,0:T(8,128)S(1)}, f32[128,256]{1,0:T(8,128)S(1)}, u32[]{:S(2)}, u32[]{:S(2)}) collective-permute-start(f32[128,256]{1,0:T(8,128)S(1)} %get-tuple-element.192), channel_id=1, source_target_pairs={{0,3},{1,2},{2,1},{3,0},{4,7},{5,6},{6,5},{7,4},{8,11},{9,10},{10,... | collective-permute-start | bytes 393224 | tf_op jit(solution)/shard_map/ppermute | solution.py:119
  251.3 3.9 %collective-permute-start.38 = (f32[16,512]{1,0:T(8,128)S(1)}, f32[16,512]{1,0:T(8,128)S(1)}, u32[]{:S(2)}, u32[]{:S(2)}) collective-permute-start(f32[16,512]{1,0:T(8,128)S(1)} %add.32), channel_id=1, source_target_pairs={{0,16},{8,24},{16,0},{24,8},{1,17},{9,25},{17,1},{25,9},{2,18},{10... | collective-permute-start | bytes 98312 | tf_op jit(solution)/shard_map/ppermute | solution.py:116
  255.2 8.9 %collective-permute-start.39 = (f32[16,512]{1,0:T(8,128)S(1)}, f32[16,512]{1,0:T(8,128)S(1)}, u32[]{:S(2)}, u32[]{:S(2)}) collective-permute-start(f32[16,512]{1,0:T(8,128)S(1)} %add.33.refs_8_), channel_id=1, source_target_pairs={{0,4},{4,0},{1,5},{5,1},{2,6},{6,2},{3,7},{7,3},{8,12},{12,8},{9,1... | collective-permute-start | bytes 98312 | tf_op jit(solution)/shard_map/ppermute | solution.py:122
  255.7 4.4 %collective-permute-start.34 = (f32[8,128]{1,0:T(8,128)S(1)}, f32[8,128]{1,0:T(8,128)S(1)}, u32[]{:S(2)}, u32[]{:S(2)}) collective-permute-start(f32[8,128]{1,0:T(8,128)S(1)} %get-tuple-element.196.refs_4_), channel_id=1, source_target_pairs={{0,1},{1,0},{2,3},{3,2},{4,5},{5,4},{6,7},{7,6},{8,9},{9,8},{10,11... | collective-permute-start | bytes 12296 | tf_op jit(solution)/shard_map/ppermute | solution.py:119
  257.7 4.5 %collective-permute-start.35 = (f32[8,128]{1,0:T(8,128)S(1)}, f32[8,128]{1,0:T(8,128)S(1)}, u32[]{:S(2)}, u32[]{:S(2)}) collective-permute-start(f32[8,128]{1,0:T(8,128)S(1)} %get-tuple-element.196.refs_4_), channel_id=1, source_target_pairs={{0,2},{1,3},{2,0},{3,1},{4,6},{5,7},{6,4},{7,5},{8,10},{9,11},{10,... | collective-permute-start | bytes 12296 | tf_op jit(solution)/shard_map/ppermute | solution.py:119
  258.7 5.4 %collective-permute-start.36 = (f32[8,128]{1,0:T(8,128)S(1)}, f32[8,128]{1,0:T(8,128)S(1)}, u32[]{:S(2)}, u32[]{:S(2)}) collective-permute-start(f32[8,128]{1,0:T(8,128)S(1)} %get-tuple-element.196.refs_4_), channel_id=1, source_target_pairs={{0,3},{1,2},{2,1},{3,0},{4,7},{5,6},{6,5},{7,4},{8,11},{9,10},{10,... | collective-permute-start | bytes 12296 | tf_op jit(solution)/shard_map/ppermute | solution.py:119
  265.0 10.1 %collective-permute-start.41 = (bf16[128,512]{1,0:T(8,128)(2,1)S(1)}, bf16[128,512]{1,0:T(8,128)(2,1)S(1)}, u32[]{:S(2)}, u32[]{:S(2)}) collective-permute-start(bf16[128,512]{1,0:T(8,128)(2,1)S(1)} %get-tuple-element.204), channel_id=1, source_target_pairs={{0,2},{1,3},{2,0},{3,1},{4,6},{5,7},{6,4},{7,5},{8,10},{9,11},{10,... | collective-permute-start | bytes 393224 | tf_op jit(solution)/shard_map/ppermute | solution.py:119
  265.2 9.9 %collective-permute-start.42 = (bf16[128,512]{1,0:T(8,128)(2,1)S(1)}, bf16[128,512]{1,0:T(8,128)(2,1)S(1)}, u32[]{:S(2)}, u32[]{:S(2)}) collective-permute-start(bf16[128,512]{1,0:T(8,128)(2,1)S(1)} %get-tuple-element.204), channel_id=1, source_target_pairs={{0,3},{1,2},{2,1},{3,0},{4,7},{5,6},{6,5},{7,4},{8,11},{9,10},{10,... | collective-permute-start | bytes 393224 | tf_op jit(solution)/shard_map/ppermute | solution.py:119
  267.7 7.6 %collective-permute-start.40 = (bf16[128,512]{1,0:T(8,128)(2,1)S(1)}, bf16[128,512]{1,0:T(8,128)(2,1)S(1)}, u32[]{:S(2)}, u32[]{:S(2)}) collective-permute-start(bf16[128,512]{1,0:T(8,128)(2,1)S(1)} %get-tuple-element.204), channel_id=1, source_target_pairs={{0,1},{1,0},{2,3},{3,2},{4,5},{5,4},{6,7},{7,6},{8,9},{9,8},{10,11... | collective-permute-start | bytes 393224 | tf_op jit(solution)/shard_map/ppermute | solution.py:119
  275.3 9.9 %collective-permute-start.44 = (bf16[4,128,512]{2,1,0:T(8,128)(2,1)S(1)}, bf16[4,128,512]{2,1,0:T(8,128)(2,1)S(1)}, u32[]{:S(2)}, u32[]{:S(2)}) collective-permute-start(bf16[4,128,512]{2,1,0:T(8,128)(2,1)S(1)} %pad_maximum_fusion.refs_8_), channel_id=1, source_target_pairs={{0,16},{8,24},{16,0},{24,8},{1,17},{9,25},{17,1},{25,9},{2,18},{10... | collective-permute-start | bytes 1572872 | tf_op jit(solution)/shard_map/ppermute | solution.py:116
  275.9 9.3 %collective-permute-start.43 = (bf16[4,128,512]{2,1,0:T(8,128)(2,1)S(1)}, bf16[4,128,512]{2,1,0:T(8,128)(2,1)S(1)}, u32[]{:S(2)}, u32[]{:S(2)}) collective-permute-start(bf16[4,128,512]{2,1,0:T(8,128)(2,1)S(1)} %pad_maximum_fusion.refs_8_), channel_id=1, source_target_pairs={{0,8},{8,0},{16,24},{24,16},{1,9},{9,1},{17,25},{25,17},{2,10},{10... | collective-permute-start | bytes 1572872 | tf_op jit(solution)/shard_map/ppermute | solution.py:113
  298.1 3.7 %collective-permute-start.47 = (f32[8,512]{1,0:T(8,128)S(1)}, f32[8,512]{1,0:T(8,128)S(1)}, u32[]{:S(2)}, u32[]{:S(2)}) collective-permute-start(f32[8,512]{1,0:T(8,128)S(1)} %add.34), channel_id=1, source_target_pairs={{0,16},{8,24},{16,0},{24,8},{1,17},{9,25},{17,1},{25,9},{2,18},{10... | collective-permute-start | bytes 49160 | tf_op jit(solution)/shard_map/ppermute | solution.py:116
  301.9 7.3 %collective-permute-start.48 = (f32[8,512]{1,0:T(8,128)S(1)}, f32[8,512]{1,0:T(8,128)S(1)}, u32[]{:S(2)}, u32[]{:S(2)}) collective-permute-start(f32[8,512]{1,0:T(8,128)S(1)} %add.35), channel_id=1, source_target_pairs={{0,1},{1,0},{2,3},{3,2},{4,5},{5,4},{6,7},{7,6},{8,9},{9,8},{10,11... | collective-permute-start | bytes 49160 | tf_op jit(solution)/shard_map/ppermute | solution.py:119
  306.7 4.6 %collective-permute-start.49 = (f32[8,512]{1,0:T(8,128)S(1)}, f32[8,512]{1,0:T(8,128)S(1)}, u32[]{:S(2)}, u32[]{:S(2)}) collective-permute-start(f32[8,512]{1,0:T(8,128)S(1)} %add.35), channel_id=1, source_target_pairs={{0,2},{1,3},{2,0},{3,1},{4,6},{5,7},{6,4},{7,5},{8,10},{9,11},{10,... | collective-permute-start | bytes 49160 | tf_op jit(solution)/shard_map/ppermute | solution.py:119
  307.3 5.5 %collective-permute-start.50 = (f32[8,512]{1,0:T(8,128)S(1)}, f32[8,512]{1,0:T(8,128)S(1)}, u32[]{:S(2)}, u32[]{:S(2)}) collective-permute-start(f32[8,512]{1,0:T(8,128)S(1)} %add.35), channel_id=1, source_target_pairs={{0,3},{1,2},{2,1},{3,0},{4,7},{5,6},{6,5},{7,4},{8,11},{9,10},{10,... | collective-permute-start | bytes 49160 | tf_op jit(solution)/shard_map/ppermute | solution.py:119
  312.9 5.2 %collective-permute-start.51 = (f32[8,512]{1,0:T(8,128)S(1)}, f32[8,512]{1,0:T(8,128)S(1)}, u32[]{:S(2)}, u32[]{:S(2)}) collective-permute-start(f32[8,512]{1,0:T(8,128)S(1)} %add_add_fusion.refs_3_), channel_id=1, source_target_pairs={{0,4},{4,0},{1,5},{5,1},{2,6},{6,2},{3,7},{7,3},{8,12},{12,8},{9,1... | collective-permute-start | bytes 49160 | tf_op jit(solution)/shard_map/ppermute | solution.py:122
  (33 other events, 547.8 us)

commit v4 on v3

--- a/solution.py
+++ b/solution.py
@@ -11,7 +11,8 @@
 ANY = pl.BlockSpec(memory_space=pl.ANY)
 BF = jnp.bfloat16
 F32 = jnp.float32
-VMEM_BYTES = 30 * 1024 * 1024
+VMEM_BYTES = 20 * 1024 * 1024
+BACK_COST = 6 * 10**9
 WIDTHS = (128, 128, 128, 128)
 GROUPS = ((0, 1), (2, 3))
 ORDER = (
@@ -21,9 +22,9 @@
     "a1 A2 w:f21+f31+n1 a2",
     "S0 A3 w:f22+f32+n2 a3",
     "S1 w:s0 S2 w:s1",
-    "F0 w:s2+f23+f33+n3 S3 f0",
-    "P0 w:s3 F1 w:rx0",
-    "f1 P1 Q0 m0",
+    "F0 w:f23+f33+n3 S3 w:s2",
+    "f0 P0 F1 w:rx0",
+    "G1 P1 Q0 m0",
     "R0 Q1 R1",
 )
 
@@ -46,14 +47,14 @@
         self.flags = flags
         self.token = jnp.zeros((8, LANES), F32)
 
-    def run(self, name, body, ins=(), outs=(), after=(), through=(), grid=(1,), scratch=()):
+    def run(self, name, body, ins=(), outs=(), after=(), through=(), grid=(1,), scratch=(), cost=0, vmem=VMEM_BYTES):
         ins = [*ins, *((a, ANY) for a in after)]
         carried = (*through, self.token)
         n_in, n_out, n_thr = len(ins), len(outs), len(carried)
 
         def kernel(flags, *refs):
             in_refs = refs[:n_in]
-            out_refs = refs[n_in + n_thr : n_in + n_thr + n_out]
+            out_refs = refs[n_in + n_thr : n_in + 2 * n_thr + n_out - 1]
             scratch_refs = refs[n_in + 2 * n_thr + n_out :]
             if body is not None:
                 body(flags, in_refs, out_refs, *scratch_refs)
@@ -69,8 +70,8 @@
                 scratch_shapes=list(scratch),
             ),
             input_output_aliases={1 + n_in + j: n_out + j for j in range(n_thr)},
-            compiler_params=pltpu.CompilerParams(vmem_limit_bytes=VMEM_BYTES),
-            cost_estimate=pl.CostEstimate(flops=0, bytes_accessed=0, transcendentals=0),
+            compiler_params=pltpu.CompilerParams(vmem_limit_bytes=vmem),
+            cost_estimate=pl.CostEstimate(flops=cost, bytes_accessed=0, transcendentals=0),
             name=name,
         )(self.flags, *[a for a, _ in ins], *carried)
         self.token = results[-1]
@@ -135,14 +136,15 @@
     st, sent = {}, {}
 
     def start_swap(c):
-        w, o = WIDTHS[c], offsets[c] // WIDTHS[c]
-
-        def body(fl, i, out):
-            out[0][...] = i[0][...]
-
+        w = WIDTHS[c]
+
+        def body(fl, i, out, sems):
+            copy_all([(None, i[0].at[p, :, pl.ds(offsets[c], w)], out[0].at[p]) for p in range(2)], sems)
+
+        shape = (2, rows, w)
         (v,) = run(
-            f"swap{c}", body, [(expr, pl.BlockSpec((1, rows, w), lambda g, f: (g, 0, o)))],
-            [(sds((2, rows, w), BF), pl.BlockSpec((1, rows, w), lambda g, f: (g, 0, 0)))], grid=(2,),
+            f"swap{c}", body, [(expr, pl.BlockSpec(memory_space=pltpu.HBM))], [(sds(shape, BF), whole(shape))],
+            scratch=[pltpu.SemaphoreType.DMA((2,))],
         )
         sent[f"y{c}"] = over_spot(v)
 
@@ -187,7 +189,8 @@
 
         one = whole((half, w))
         (st["f", c],) = run(
-            f"back{c}", body, [(sent[f"f2{c}"], one), (sent[f"f3{c}"], one)], [(sds((2, half, w), BF), whole((2, half, w)))]
+            f"back{c}", body, [(sent[f"f2{c}"], one), (sent[f"f3{c}"], one)], [(sds((2, half, w), BF), whole((2, half, w)))],
+            cost=BACK_COST if c == len(WIDTHS) - 1 else 0,
         )
         sent[f"s{c}"] = over_spot(st["f", c])
 
@@ -284,11 +287,19 @@
         outs = [(sds((rows, slots * WIDTHS[c]), BF), whole((rows, slots * WIDTHS[c]))) for c in members]
         outs += [(sds(shape, F32), whole(shape))] * 2
 
-        def product(pt, efs, keep, send):
+        late = members[-1] if spot_size == 2 and g == len(GROUPS) - 1 else None
+
+        def product(pt, efs, keep, send, direct=None):
             done = 0
             for c, ef in zip(members, efs):
                 w = WIDTHS[c]
-                acc = jnp.dot(pt[...], ef[...], preferred_element_type=F32)
+                if c == late:
+                    near = jnp.dot(pt[...], ef[:, : 2 * w], preferred_element_type=F32)
+                    at = pl.ds(pl.multiple_of(direct, LANES), half)
+                    far = jnp.dot(pt[:, at], ef[at, 2 * w :], preferred_element_type=F32)
+                    acc = jnp.concatenate([near, far], axis=1)
+                else:
+                    acc = jnp.dot(pt[...], ef[...], preferred_element_type=F32)
                 for q, ref in enumerate((keep, send, keep, send)):
                     rows_q = acc[q * quarter : (q + 1) * quarter]
                     for s in range(slots):
@@ -305,7 +316,7 @@
                 copies = []
                 for m, c in enumerate(members):
                     w, ef = WIDTHS[c], out[m]
-                    y, n, f, s = i[2 + 4 * m : 6 + 4 * m]
+                    y, n, f = i[2 + 4 * m : 5 + 4 * m]
                     copies += [
                         (at_home, e.at[fl[1], :, pl.ds(offsets[c], w)], ef.at[:, pl.ds(0, w)]),
                         (away, y.at[fl[1]], ef.at[:, pl.ds(0, w)]),
@@ -314,20 +325,18 @@
                     ]
                     for part in (0, 1):
                         cols = pl.ds((2 + part) * w, w)
-                        copies += [
-                            (at_home, f.at[part], ef.at[low, cols]),
-                            (at_home, s.at[part], ef.at[top, cols]),
-                            (away, f.at[part], ef.at[top, cols]),
-                            (away, s.at[part], ef.at[low, cols]),
-                        ]
+                        copies += [(at_home, f.at[part], ef.at[low, cols]), (away, f.at[part], ef.at[top, cols])]
+                        if c != late:
+                            s = i[5 + 4 * m]
+                            copies += [(at_home, s.at[part], ef.at[top, cols]), (away, s.at[part], ef.at[low, cols])]
                 copy_all(copies, sems)
-                product(pt, out[: len(members)], *out[len(members) :])
+                product(pt, out[: len(members)], *out[len(members) :], direct=fl[0] * half)
 
             ins = [(st["pt"], whole((spots, rows))), (expr, ANY)]
             ins += [
                 (a, ANY)
                 for c in members
-                for a in (sent[f"y{c}"], sent[f"n{c}"], st["f", c], sent[f"s{c}"])
+                for a in (sent[f"y{c}"], sent[f"n{c}"], st["f", c], *([] if c == late else [sent[f"s{c}"]]))
             ]
             scratch = [pltpu.SemaphoreType.DMA((12 * len(members),))]
         else:
@@ -349,6 +358,32 @@
             st["e", c] = ef
         st["r", g], st["send", g] = keep, send
 
+    def forward_late(g):
+        c = GROUPS[g][-1]
+        w, wide = WIDTHS[c], slots * group_width[g]
+        shape = (2, quarter, wide)
+
+        def body(fl, i, out, sems):
+            pt, swapped, keep, send = i
+            at = pl.ds(pl.multiple_of((1 - fl[0]) * half, LANES), half)
+            copy_all([(None, swapped.at[n], out[2].at[at, pl.ds((2 + n) * w, w)]) for n in (0, 1)], sems)
+            both = jnp.concatenate([swapped[0], swapped[1]], axis=1)
+            acc = jnp.dot(pt[:, at], both, preferred_element_type=F32)
+            out[0][...] = keep[...]
+            out[1][...] = send[...]
+            for q, ref in enumerate((out[0], out[1], out[0], out[1])):
+                for n in (0, 1):
+                    base = (3 + n) * group_width[g] - w
+                    ref[q // 2, :, base : base + w] += acc[q * quarter : (q + 1) * quarter, n * w : (n + 1) * w]
+
+        ins = [(st["pt"], whole((spots, rows))), (sent[f"s{c}"], whole((2, half, w)))]
+        ins += [(st["r", g], whole(shape)), (st["send", g], whole(shape))]
+        st["r", g], send, st["e", c] = run(
+            f"forwardlate{g}", body, ins, [(sds(shape, F32), whole(shape))] * 2, through=[st["e", c]],
+            scratch=[pltpu.SemaphoreType.DMA((2,))],
+        )
+        sent[f"rc{g}"] = over_core(send)
+
     def forward_send(g):
         (send,) = run(f"send{g}", None, through=[st["send", g]])
         sent[f"rc{g}"] = over_core(send)
@@ -391,7 +426,7 @@
 
     steps = {
         "Y": start_swap, "A": start_along, "a": along_send, "S": start_back,
-        "e": totals, "m": shares, "F": forward, "f": forward_send, "b": members_of, "P": reduce_core, "Q": reduce_x, "R": reduce_gene,
+        "e": totals, "m": shares, "F": forward, "f": forward_send, "G": forward_late, "b": members_of, "P": reduce_core, "Q": reduce_x, "R": reduce_gene,
     }
     if spot_size != 2:
         full = lax.all_gather(expression, "spot", axis=0, tiled=True).reshape(slots, rows, genes)
@@ -401,6 +436,8 @@
         if word[:2] == "w:":
             if spot_size == 2 or word == "w:ez1+ez2+ez3":
                 wait_for(word[2:])
+        elif spot_size != 2 and word[0] == "G":
+            forward_send(int(word[1]))
         elif spot_size == 2 or word[0] not in "YAaS":
             steps[word[0]](int(word[1]))
 
@@ -490,6 +527,7 @@
         "grads", grads_body, ins,
         [(sds((quarter, genes), BF), whole((quarter, genes))), (sds((8, spots), F32), row8)],
     )
+    terms = [terms, over_spot(terms)] if spot_size == 2 else [sum_spot(terms)]
     grad = jnp.stack([grad] + [over_gene(grad, s) for s in (1, 2, 3)])
     grad_x = over_x(grad)
     grads = [grad, over_core(grad), grad_x, over_core(grad_x)]
@@ -497,13 +535,13 @@
     row_blk = rows // 4
 
     def backward_body(fl, i, out, held, sems):
-        lg, tot, sm, terms = i[:4]
-        efs, gs = i[4 : 4 + n_ch], i[4 + n_ch :]
+        lg, tot, sm = i[:3]
+        efs, gs, terms = i[3 : 3 + n_ch], i[3 + n_ch : 7 + n_ch], i[7 + n_ch :]
 
         @pl.when(pl.program_id(0) == 0)
         def _():
             row = lax.broadcasted_iota(jnp.int32, (8, spots), 0)
-            out[1][...] = jnp.where(row == 0, 0.0, terms[...])
+            out[1][...] = jnp.where(row == 0, 0.0, sum(ref[...] for ref in terms))
             copies = []
             for b, ref in enumerate(gs):
                 at = pl.multiple_of((fl[2] ^ b) * quarter, quarter)
@@ -521,9 +559,9 @@
     def by_rows(width, size=row_blk):
         return pl.BlockSpec((size, width), lambda g, f: (g, 0))
 
-    ins = [(logits, by_rows(spots)), (st["tot"], row8), (st["sm"], by_rows(LANES)), (terms, row8)]
+    ins = [(logits, by_rows(spots)), (st["tot"], row8), (st["sm"], by_rows(LANES))]
     ins += [(st["e", c], by_rows(slots * WIDTHS[c])) for c in chunks]
-    ins += [(a, ANY) for a in grads]
+    ins += [(a, ANY) for a in grads] + [(a, row8) for a in terms]
     grad_probs, v = run(
         "backward", backward_body, ins,
         [(sds((rows, spots), F32), by_rows(spots)), (sds((8, spots), F32), row8)],
@@ -534,23 +572,27 @@
     v = v + over_core(v)
     v = v + over_x(v)
     v = (v + over_gene(v, 1)) + (over_gene(v, 2) + over_gene(v, 3))
-    sums = sum_spot(v)[1, :5]
 
     def final_body(fl, i, out):
         prob = jnp.exp(i[0][...].astype(F32)) * (1.0 / i[1][0:1, :])
         out[0][...] = prob * (i[2][...] - i[3][0:1, :])
 
+        @pl.when(pl.program_id(0) == 0)
+        def _():
+            sums = [i[3][1, n] for n in range(5)]
+            gene_term, spot_term = sums[0] / (SLIDES * genes_all), sums[1] / sums[4]
+            divergence, entropy = sums[2], sums[3] / spots_all
+            values = (divergence - gene_term - spot_term, gene_term, spot_term, divergence, entropy)
+            for n, value in enumerate(values):
+                out[1][n] = value
+
     last_blk = rows // 2
     blk = by_rows(spots, last_blk)
-    (grad_logits,) = run(
+    grad_logits, loss_terms = run(
         "final", final_body, [(logits, blk), (st["tot"], row8), (grad_probs, blk), (v, row8)],
-        [(sds((rows, spots), F32), blk)], grid=(rows // last_blk,),
+        [(sds((rows, spots), F32), blk), (sds((5,), F32), pl.BlockSpec(memory_space=pltpu.SMEM))],
+        grid=(rows // last_blk,),
     )
-    gene_term = sums[0] / (SLIDES * genes_all)
-    spot_term = sums[1] / sums[4]
-    divergence = sums[2]
-    entropy = sums[3] / spots_all
-    loss_terms = jnp.stack([divergence - gene_term - spot_term, gene_term, spot_term, divergence, entropy])
     return (loss_terms, grad_logits)
 
 

time: 324 us -> 305 us (0.941)
  waiting for transfers between devices: 171 us -> 161 us
  local copies, waits for them, and re-layouts: 15.9 us -> 7.23 us
  between operations: 4.57 us -> 1.23 us
  starting transfers between devices: 66.1 us -> 69.4 us
    ppermute x30, waiting for transfers between devices: 63.9 us -> 48.8 us  [over_gene(): return lax.ppermute(v, 'gene', xor_pairs(4, step))]
    ppermute x5, waiting for transfers between devices: 15.8 us -> 23.4 us  [over_x(): return lax.ppermute(v, 'cell', xor_pairs(4, 2))]
    unnamed x58 -> x30, local copies, waits for them, and re-layouts: 13.8 us -> 7.13 us
  transfers between devices with their start and end apart: 52 -> 52, of which waited for: 32 -> 33; matrix products, arithmetic and copies ran while one was open for 0% -> 0% of each run, Pallas kernels for 12% -> 11%
where the time goes in v4:
time: 305 us
  waiting for transfers between devices  161 us (53%)
  starting transfers between devices  69.4 us (23%)
  Pallas kernels  54.4 us (18%)
  blocking collectives  11.2 us (4%)
  local copies, waits for them, and re-layouts  7.23 us (2%)
    ppermute x11, waiting for transfers between devices, over_spot(): return lax.ppermute(v, 'spot', xor_pairs(spot_size, step))  83.2 us
    pallas_call x43, Pallas kernels, run(): pl.pallas_call(kernel, out_shape=[s for s, _ in outs] + [sds(a.shape, a.d...  54.4 us
    ppermute x30, starting transfers between devices, over_gene(): return lax.ppermute(v, 'gene', xor_pairs(4, step))  49 us
    ppermute x30, waiting for transfers between devices, over_gene(): return lax.ppermute(v, 'gene', xor_pairs(4, step))  48.8 us
    ppermute x5, waiting for transfers between devices, over_x(): return lax.ppermute(v, 'cell', xor_pairs(4, 2))  23.4 us
    ppermute x11, starting transfers between devices, over_spot(): return lax.ppermute(v, 'spot', xor_pairs(spot_size, step))  14.9 us
    psum x1, blocking collectives, totals(): st['tot'] = lax.psum(v, 'cell')  11.2 us
    unnamed x30, local copies, waits for them, and re-layouts  7.13 us
  transfers between devices with their start and end apart: 52, of which 33 were waited for; matrix products, arithmetic and copies ran while one was open for 0% of the time, Pallas kernels for 11%

profile of v4, /device:TPU:0, one launch (start us, length us, event | category | flops | bytes accessed | tf_op | source)
XLA Modules:
  0.0 304.8 jit_solution(16868229541079217717)
XLA Ops:
  0.8 2.6 copy-done
  3.4 1.9 swap0.1
  5.3 3.0 collective-permute-start.3
  11.6 1.9 swap1.1
  13.8 11.2 %psum.7.refs_1_ = f32[8,512]{1,0:T(8,128)S(1)} all-reduce(f32[8,512]{1,0:T(8,128)S(1)} %get-tuple-element.110), channel_id=1, replica_groups=mesh['cell'=4,'spot'=2,'gene'=4] {'cell'}, use_global_device_ids=true, to_apply=%region_0.1 | all-reduce | flops 4096 | bytes 32768 | tf_op jit(solution)/shard_map/psum | solution.py:221
  26.6 2.6 collective-permute-start.1
  29.4 1.9 collective-permute-done.1.refs_1_.refs_3_
  31.3 3.4 %collective-permute-done.2.refs_2_.refs_4_ = f32[8,512]{1,0:T(8,128)S(1)} collective-permute-done((f32[8,512]{1,0:T(8,128)S(1)}, f32[8,512]{1,0:T(8,128)S(1)}, u32[]{:S(2)}, u32[]{:S(2)}) %collective-permute-start.2) | collective-permute-done | bytes 16416 | tf_op jit(solution)/shard_map/ppermute | solution.py:120
  35.3 2.6 copy-done.2
  38.7 2.2 collective-permute-done.3.refs_0_.refs_1_.refs_6_.refs_7_.refs_2_
  42.4 2.2 collective-permute-start.5
  46.1 2.6 collective-permute-start.6
  49.0 4.0 %prob.1 = (bf16[512,2816]{1,0:T(8,128)(2,1)S(1)}, f32[8,2816]{1,0:T(8,128)S(1)}, f32[8,512]{1,0:T(8,128)S(1)}, f32[8,512]{1,0:T(8,128)S(1)}, f32[8,128]{1,0:T(8,128)S(1)}) custom-call(s32[5]{0:T(128)S(1)} %stack.42.flags, bf16[2816,512]{1,0:T(8,128)(2,1)S(1)} %copy-done.4, f32[8,512]{1,0:T(8,128)S(1)} %psum.7.refs_1_, ...), custom_call_target="tpu_custom_call", output_to_operand_aliasing={{4}: (6, {})} | custom-call | tf_op jit(solution)/shard_map/prob/pallas_call | solution.py:62
  53.7 18.2 %collective-permute-done.9.refs_0_.refs_1_.refs_6_.refs_7_ = bf16[2,2816,128]{2,1,0:T(8,128)(2,1)S(1)} collective-permute-done((bf16[2,2816,128]{2,1,0:T(8,128)(2,1)}, bf16[2,2816,128]{2,1,0:T(8,128)(2,1)S(1)}, u32[]{:S(2)}, u32[]{:S(2)}) %collective-permute-start.9) | collective-permute-done | bytes 1441824 | tf_op jit(solution)/shard_map/ppermute | solution.py:123
  73.6 2.9 collective-permute-done.7.refs_1_
  77.6 2.0 collective-permute-start.12
  81.2 2.4 collective-permute-start.11
  83.6 19.2 %collective-permute-done.8.refs_0_.refs_1_.refs_6_.refs_7_.refs_2_ = bf16[2,2816,128]{2,1,0:T(8,128)(2,1)S(1)} collective-permute-done((bf16[2,2816,128]{2,1,0:T(8,128)(2,1)S(1)}, bf16[2,2816,128]{2,1,0:T(8,128)(2,1)S(1)}, u32[]{:S(2)}, u32[]{:S(2)}) %collective-permute-start.8) | collective-permute-done | bytes 1441824 | tf_op jit(solution)/shard_map/ppermute | solution.py:123
  103.7 5.8 %collective-permute-done.11.refs_1_ = bf16[1408,128]{1,0:T(8,128)(2,1)S(1)} collective-permute-done((bf16[1408,128]{1,0:T(8,128)(2,1)S(1)}, bf16[1408,128]{1,0:T(8,128)(2,1)S(1)}, u32[]{:S(2)}, u32[]{:S(2)}) %collective-permute-start.11) | collective-permute-done | bytes 360480 | tf_op jit(solution)/shard_map/ppermute | solution.py:120
  110.6 2.8 collective-permute-start.17
  117.3 16.4 %collective-permute-done.14.refs_0_.refs_1_.refs_6_.refs_7_ = bf16[2,2816,128]{2,1,0:T(8,128)(2,1)S(1)} collective-permute-done((bf16[2,2816,128]{2,1,0:T(8,128)(2,1)S(1)}, bf16[2,2816,128]{2,1,0:T(8,128)(2,1)S(1)}, u32[]{:S(2)}, u32[]{:S(2)}) %collective-permute-start.14) | collective-permute-done | bytes 1441824 | tf_op jit(solution)/shard_map/ppermute | solution.py:123
  134.6 5.2 %collective-permute-done.16.refs_1_ = bf16[1408,128]{1,0:T(8,128)(2,1)S(1)} collective-permute-done((bf16[1408,128]{1,0:T(8,128)(2,1)S(1)}, bf16[1408,128]{1,0:T(8,128)(2,1)S(1)}, u32[]{:S(2)}, u32[]{:S(2)}) %collective-permute-start.16) | collective-permute-done | bytes 360480 | tf_op jit(solution)/shard_map/ppermute | solution.py:120
  145.1 2.4 collective-permute-start.21
  150.2 2.1 collective-permute-start.19
  152.4 12.2 %collective-permute-done.18.refs_0_.refs_9_ = bf16[2,1408,128]{2,1,0:T(8,128)(2,1)S(1)} collective-permute-done((bf16[2,1408,128]{2,1,0:T(8,128)(2,1)S(1)}, bf16[2,1408,128]{2,1,0:T(8,128)(2,1)S(1)}, u32[]{:S(2)}, u32[]{:S(2)}) %collective-permute-start.18) | collective-permute-done | bytes 720928 | tf_op jit(solution)/shard_map/ppermute | solution.py:123
  165.1 5.0 %forward0.1 = (bf16[2816,512]{1,0:T(8,128)(2,1)S(1)}, bf16[2816,512]{1,0:T(8,128)(2,1)S(1)}, f32[2,128,1024]{2,1,0:T(8,128)S(1)}, f32[2,128,1024]{2,1,0:T(8,128)S(1)}, f32[8,128]{1,0:T(8,128)S(1)}) custom-call(s32[5]{0:T(128)S(1)} %stack.42.flags, bf16[512,2816]{1,0:T(8,128)(2,1)S(1)} %get-tuple-element.122.refs_0_, ...), custom_call_target="tpu_custom_call", output_to_operand_aliasing={{4}: (11, {})} | custom-call | tf_op jit(solution)/shard_map/forward0/pallas_call | solution.py:62
  172.7 6.5 %collective-permute-done.19.refs_0_.refs_5_ = bf16[2,1408,128]{2,1,0:T(8,128)(2,1)S(1)} collective-permute-done((bf16[2,1408,128]{2,1,0:T(8,128)(2,1)S(1)}, bf16[2,1408,128]{2,1,0:T(8,128)(2,1)S(1)}, u32[]{:S(2)}, u32[]{:S(2)}) %collective-permute-start.19) | collective-permute-done | bytes 720928 | tf_op jit(solution)/shard_map/ppermute | solution.py:123
  185.4 4.7 %forward1.1 = (bf16[2816,512]{1,0:T(8,128)(2,1)S(1)}, bf16[2816,512]{1,0:T(8,128)(2,1)S(1)}, f32[2,128,1024]{2,1,0:T(8,128)S(1)}, f32[2,128,1024]{2,1,0:T(8,128)S(1)}, f32[8,128]{1,0:T(8,128)S(1)}) custom-call(s32[5]{0:T(128)S(1)} %stack.42.flags, bf16[512,2816]{1,0:T(8,128)(2,1)S(1)} %get-tuple-element.122.refs_0_, ...), custom_call_target="tpu_custom_call", output_to_operand_aliasing={{4}: (10, {})} | custom-call | tf_op jit(solution)/shard_map/forward1/pallas_call | solution.py:62
  190.1 7.5 %collective-permute-done.24.refs_0_.refs_1_ = f32[128,1024]{1,0:T(8,128)S(1)} collective-permute-done((f32[128,1024]{1,0:T(8,128)S(1)}, f32[128,1024]{1,0:T(8,128)S(1)}, u32[]{:S(2)}, u32[]{:S(2)}) %collective-permute-start.24) | collective-permute-done | bytes 524320 | tf_op jit(solution)/shard_map/ppermute | solution.py:117
  200.4 2.6 collective-permute-done.26.refs_1_
  207.7 2.6 collective-permute-start.28
  212.0 3.0 collective-permute-done.4.refs_3_
  216.1 4.5 %collective-permute-done.28.refs_2_ = f32[128,256]{1,0:T(8,128)S(1)} collective-permute-done((f32[128,256]{1,0:T(8,128)S(1)}, f32[128,256]{1,0:T(8,128)S(1)}, u32[]{:S(2)}, u32[]{:S(2)}) %collective-permute-start.28) | collective-permute-done | bytes 131104 | tf_op jit(solution)/shard_map/ppermute | solution.py:120
  221.8 2.0 collective-permute-start.31
  226.3 1.9 collective-permute-done.31.refs_1_
  228.3 7.3 %collective-permute-done.32.refs_2_ = f32[128,256]{1,0:T(8,128)S(1)} collective-permute-done((f32[128,256]{1,0:T(8,128)S(1)}, f32[128,256]{1,0:T(8,128)S(1)}, u32[]{:S(2)}, u32[]{:S(2)}) %collective-permute-start.32) | collective-permute-done | bytes 131104 | tf_op jit(solution)/shard_map/ppermute | solution.py:120
  238.9 3.4 %collective-permute-done.38 = f32[16,512]{1,0:T(8,128)S(1)} collective-permute-done((f32[16,512]{1,0:T(8,128)S(1)}, f32[16,512]{1,0:T(8,128)S(1)}, u32[]{:S(2)}, u32[]{:S(2)}) %collective-permute-start.38) | collective-permute-done | bytes 32800 | tf_op jit(solution)/shard_map/ppermute | solution.py:117
  243.8 2.0 collective-permute-start.34
  248.2 2.1 collective-permute-done.35.refs_6_
  253.3 2.4 collective-permute-start.42
  256.7 6.5 %collective-permute-done.41 = bf16[128,512]{1,0:T(8,128)(2,1)S(1)} collective-permute-done((bf16[128,512]{1,0:T(8,128)(2,1)S(1)}, bf16[128,512]{1,0:T(8,128)(2,1)S(1)}, u32[]{:S(2)}, u32[]{:S(2)}) %collective-permute-start.41) | collective-permute-done | bytes 131104 | tf_op jit(solution)/shard_map/ppermute | solution.py:120
  264.0 9.3 %collective-permute-done.44.refs_9_ = bf16[4,128,512]{2,1,0:T(8,128)(2,1)S(1)} collective-permute-done((bf16[4,128,512]{2,1,0:T(8,128)(2,1)S(1)}, bf16[4,128,512]{2,1,0:T(8,128)(2,1)S(1)}, u32[]{:S(2)}, u32[]{:S(2)}) %collective-permute-start.44) | collective-permute-done | bytes 524320 | tf_op jit(solution)/shard_map/ppermute | solution.py:117
  273.8 3.2 %collective-permute-done.46.refs_12_ = f32[8,512]{1,0:T(8,128)S(1)} collective-permute-done((f32[8,512]{1,0:T(8,128)S(1)}, f32[8,512]{1,0:T(8,128)S(1)}, u32[]{:S(2)}, u32[]{:S(2)}) %collective-permute-start.46) | collective-permute-done | bytes 16416 | tf_op jit(solution)/shard_map/ppermute | solution.py:123
  277.0 8.0 %backward.1 = (f32[2816,512]{1,0:T(8,128)S(1)}, f32[8,512]{1,0:T(8,128)S(1)}, f32[8,128]{1,0:T(8,128)S(1)}) custom-call(s32[5]{0:T(128)S(1)} %stack.42.flags, bf16[2816,512]{1,0:T(8,128)(2,1)S(1)} %copy-done.4, f32[8,512]{1,0:T(8,128)S(1)} %get-tuple-element.120.refs_1_, ...), custom_call_target="tpu_custom_call", output_to_operand_aliasing={{2}: (14, {})} | custom-call | tf_op jit(solution)/shard_map/backward/pallas_call | solution.py:62
  286.8 3.2 %collective-permute-done.48 = f32[8,512]{1,0:T(8,128)S(1)} collective-permute-done((f32[8,512]{1,0:T(8,128)S(1)}, f32[8,512]{1,0:T(8,128)S(1)}, u32[]{:S(2)}, u32[]{:S(2)}) %collective-permute-start.48) | collective-permute-done | bytes 16416 | tf_op jit(solution)/shard_map/ppermute | solution.py:117
  290.0 4.8 %collective-permute-start.49 = (f32[8,512]{1,0:T(8,128)S(1)}, f32[8,512]{1,0:T(8,128)S(1)}, u32[]{:S(2)}, u32[]{:S(2)}) collective-permute-start(f32[8,512]{1,0:T(8,128)S(1)} %add.32), channel_id=1, source_target_pairs={{0,1},{1,0},{2,3},{3,2},{4,5},{5,4},{6,7},{7,6},{8,9},{9,8},{10,11... | collective-permute-start | bytes 49160 | tf_op jit(solution)/shard_map/ppermute | solution.py:120
  297.3 2.2 collective-permute-done.50
  301.0 3.8 %final.1 = (f32[2816,512]{1,0:T(8,128)}, f32[5]{0:T(128)}, f32[8,128]{1,0:T(8,128)S(1)}) custom-call(s32[5]{0:T(128)S(1)} %stack.42.flags, bf16[2816,512]{1,0:T(8,128)(2,1)S(1)} %copy-done.4, f32[8,512]{1,0:T(8,128)S(1)} %get-tuple-element.120.refs_1_, f32[2816,512]{1,0:T(8,128)S(1)} %get-tuple-element.211.refs_2_, ...), custom_call_target="tpu_custom_call", output_to_operand_aliasing={{2}: (5, {})} | custom-call | tf_op jit(solution)/shard_map/final/pallas_call | solution.py:62
  (140 shorter events, 71.2 us)
Async XLA Ops:
  5.3 35.7 %collective-permute-start.3 = (bf16[2,2816,128]{2,1,0:T(8,128)(2,1)}, bf16[2,2816,128]{2,1,0:T(8,128)(2,1)S(1)}, u32[]{:S(2)}, u32[]{:S(2)}) collective-permute-start(bf16[2,2816,128]{2,1,0:T(8,128)(2,1)} %get-tuple-element.111), channel_id=1, source_target_pairs={{0,4},{4,0},{1,5},{5,1},{2,6},{6,2},{3,7},{7,3},{8,12},{12,8},{9,1... | collective-permute-start | bytes 4325384 | tf_op jit(solution)/shard_map/ppermute | solution.py:123
  13.5 58.3 %collective-permute-start.9 = (bf16[2,2816,128]{2,1,0:T(8,128)(2,1)}, bf16[2,2816,128]{2,1,0:T(8,128)(2,1)S(1)}, u32[]{:S(2)}, u32[]{:S(2)}) collective-permute-start(bf16[2,2816,128]{2,1,0:T(8,128)(2,1)} %get-tuple-element.127), channel_id=1, source_target_pairs={{0,4},{4,0},{1,5},{5,1},{2,6},{6,2},{3,7},{7,3},{8,12},{12,8},{9,1... | collective-permute-start | bytes 4325384 | tf_op jit(solution)/shard_map/ppermute | solution.py:123
  25.0 4.4 %collective-permute-start = (f32[8,512]{1,0:T(8,128)S(1)}, f32[8,512]{1,0:T(8,128)S(1)}, u32[]{:S(2)}, u32[]{:S(2)}) collective-permute-start(f32[8,512]{1,0:T(8,128)S(1)} %psum.7.refs_1_), channel_id=1, source_target_pairs={{0,1},{1,0},{2,3},{3,2},{4,5},{5,4},{6,7},{7,6},{8,9},{9,8},{10,11... | collective-permute-start | bytes 49160 | tf_op jit(solution)/shard_map/ppermute | solution.py:120
  26.6 4.7 %collective-permute-start.1 = (f32[8,512]{1,0:T(8,128)S(1)}, f32[8,512]{1,0:T(8,128)S(1)}, u32[]{:S(2)}, u32[]{:S(2)}) collective-permute-start(f32[8,512]{1,0:T(8,128)S(1)} %psum.7.refs_1_), channel_id=1, source_target_pairs={{0,2},{1,3},{2,0},{3,1},{4,6},{5,7},{6,4},{7,5},{8,10},{9,11},{10,... | collective-permute-start | bytes 49160 | tf_op jit(solution)/shard_map/ppermute | solution.py:120
  29.2 5.5 %collective-permute-start.2 = (f32[8,512]{1,0:T(8,128)S(1)}, f32[8,512]{1,0:T(8,128)S(1)}, u32[]{:S(2)}, u32[]{:S(2)}) collective-permute-start(f32[8,512]{1,0:T(8,128)S(1)} %psum.7.refs_1_), channel_id=1, source_target_pairs={{0,3},{1,2},{2,1},{3,0},{4,7},{5,6},{6,5},{7,4},{8,11},{9,10},{10,... | collective-permute-start | bytes 49160 | tf_op jit(solution)/shard_map/ppermute | solution.py:120
  42.4 34.0 %collective-permute-start.5 = (bf16[2,1408,128]{2,1,0:T(8,128)(2,1)S(1)}, bf16[2,1408,128]{2,1,0:T(8,128)(2,1)S(1)}, u32[]{:S(2)}, u32[]{:S(2)}) collective-permute-start(bf16[2,1408,128]{2,1,0:T(8,128)(2,1)S(1)} %get-tuple-element.123), channel_id=1, source_target_pairs={{0,1},{1,0},{2,3},{3,2},{4,5},{5,4},{6,7},{7,6},{8,9},{9,8},{10,11... | collective-permute-start | bytes 2162696 | tf_op jit(solution)/shard_map/ppermute | solution.py:120
  44.6 58.1 %collective-permute-start.8 = (bf16[2,2816,128]{2,1,0:T(8,128)(2,1)S(1)}, bf16[2,2816,128]{2,1,0:T(8,128)(2,1)S(1)}, u32[]{:S(2)}, u32[]{:S(2)}) collective-permute-start(bf16[2,2816,128]{2,1,0:T(8,128)(2,1)S(1)} %get-tuple-element.126), channel_id=1, source_target_pairs={{0,4},{4,0},{1,5},{5,1},{2,6},{6,2},{3,7},{7,3},{8,12},{12,8},{9,1... | collective-permute-start | bytes 4325384 | tf_op jit(solution)/shard_map/ppermute | solution.py:123
  46.1 27.4 %collective-permute-start.6 = (bf16[1408,128]{1,0:T(8,128)(2,1)S(1)}, bf16[1408,128]{1,0:T(8,128)(2,1)S(1)}, u32[]{:S(2)}, u32[]{:S(2)}) collective-permute-start(bf16[1408,128]{1,0:T(8,128)(2,1)S(1)} %get-tuple-element.124), channel_id=1, source_target_pairs={{0,2},{1,3},{2,0},{3,1},{4,6},{5,7},{6,4},{7,5},{8,10},{9,11},{10,... | collective-permute-start | bytes 1081352 | tf_op jit(solution)/shard_map/ppermute | solution.py:120
  48.7 27.8 %collective-permute-start.7 = (bf16[1408,128]{1,0:T(8,128)(2,1)S(1)}, bf16[1408,128]{1,0:T(8,128)(2,1)S(1)}, u32[]{:S(2)}, u32[]{:S(2)}) collective-permute-start(bf16[1408,128]{1,0:T(8,128)(2,1)S(1)} %get-tuple-element.125), channel_id=1, source_target_pairs={{0,3},{1,2},{2,1},{3,0},{4,7},{5,6},{6,5},{7,4},{8,11},{9,10},{10,... | collective-permute-start | bytes 1081352 | tf_op jit(solution)/shard_map/ppermute | solution.py:120
  77.6 31.9 %collective-permute-start.12 = (bf16[2,1408,128]{2,1,0:T(8,128)(2,1)S(1)}, bf16[2,1408,128]{2,1,0:T(8,128)(2,1)S(1)}, u32[]{:S(2)}, u32[]{:S(2)}) collective-permute-start(bf16[2,1408,128]{2,1,0:T(8,128)(2,1)S(1)} %get-tuple-element.141), channel_id=1, source_target_pairs={{0,1},{1,0},{2,3},{3,2},{4,5},{5,4},{6,7},{7,6},{8,9},{9,8},{10,11... | collective-permute-start | bytes 2162696 | tf_op jit(solution)/shard_map/ppermute | solution.py:120
  79.6 54.1 %collective-permute-start.14 = (bf16[2,2816,128]{2,1,0:T(8,128)(2,1)S(1)}, bf16[2,2816,128]{2,1,0:T(8,128)(2,1)S(1)}, u32[]{:S(2)}, u32[]{:S(2)}) collective-permute-start(bf16[2,2816,128]{2,1,0:T(8,128)(2,1)S(1)} %get-tuple-element.145), channel_id=1, source_target_pairs={{0,4},{4,0},{1,5},{5,1},{2,6},{6,2},{3,7},{7,3},{8,12},{12,8},{9,1... | collective-permute-start | bytes 4325384 | tf_op jit(solution)/shard_map/ppermute | solution.py:123
  80.1 23.6 %collective-permute-start.10 = (bf16[1408,128]{1,0:T(8,128)(2,1)S(1)}, bf16[1408,128]{1,0:T(8,128)(2,1)S(1)}, u32[]{:S(2)}, u32[]{:S(2)}) collective-permute-start(bf16[1408,128]{1,0:T(8,128)(2,1)S(1)} %get-tuple-element.139), channel_id=1, source_target_pairs={{0,2},{1,3},{2,0},{3,1},{4,6},{5,7},{6,4},{7,5},{8,10},{9,11},{10,... | collective-permute-start | bytes 1081352 | tf_op jit(solution)/shard_map/ppermute | solution.py:120
  81.2 28.3 %collective-permute-start.11 = (bf16[1408,128]{1,0:T(8,128)(2,1)S(1)}, bf16[1408,128]{1,0:T(8,128)(2,1)S(1)}, u32[]{:S(2)}, u32[]{:S(2)}) collective-permute-start(bf16[1408,128]{1,0:T(8,128)(2,1)S(1)} %get-tuple-element.140), channel_id=1, source_target_pairs={{0,3},{1,2},{2,1},{3,0},{4,7},{5,6},{6,5},{7,4},{8,11},{9,10},{10,... | collective-permute-start | bytes 1081352 | tf_op jit(solution)/shard_map/ppermute | solution.py:120
  110.6 29.1 %collective-permute-start.17 = (bf16[2,1408,128]{2,1,0:T(8,128)(2,1)S(1)}, bf16[2,1408,128]{2,1,0:T(8,128)(2,1)S(1)}, u32[]{:S(2)}, u32[]{:S(2)}) collective-permute-start(bf16[2,1408,128]{2,1,0:T(8,128)(2,1)S(1)} %get-tuple-element.152), channel_id=1, source_target_pairs={{0,1},{1,0},{2,3},{3,2},{4,5},{5,4},{6,7},{7,6},{8,9},{9,8},{10,11... | collective-permute-start | bytes 2162696 | tf_op jit(solution)/shard_map/ppermute | solution.py:120
  113.4 21.2 %collective-permute-start.15 = (bf16[1408,128]{1,0:T(8,128)(2,1)S(1)}, bf16[1408,128]{1,0:T(8,128)(2,1)S(1)}, u32[]{:S(2)}, u32[]{:S(2)}) collective-permute-start(bf16[1408,128]{1,0:T(8,128)(2,1)S(1)} %get-tuple-element.150), channel_id=1, source_target_pairs={{0,2},{1,3},{2,0},{3,1},{4,6},{5,7},{6,4},{7,5},{8,10},{9,11},{10,... | collective-permute-start | bytes 1081352 | tf_op jit(solution)/shard_map/ppermute | solution.py:120
  114.8 24.9 %collective-permute-start.16 = (bf16[1408,128]{1,0:T(8,128)(2,1)S(1)}, bf16[1408,128]{1,0:T(8,128)(2,1)S(1)}, u32[]{:S(2)}, u32[]{:S(2)}) collective-permute-start(bf16[1408,128]{1,0:T(8,128)(2,1)S(1)} %get-tuple-element.151), channel_id=1, source_target_pairs={{0,3},{1,2},{2,1},{3,0},{4,7},{5,6},{6,5},{7,4},{8,11},{9,10},{10,... | collective-permute-start | bytes 1081352 | tf_op jit(solution)/shard_map/ppermute | solution.py:120
  116.8 32.3 %collective-permute-start.13 = (bf16[2,1408,128]{2,1,0:T(8,128)(2,1)S(1)}, bf16[2,1408,128]{2,1,0:T(8,128)(2,1)S(1)}, u32[]{:S(2)}, u32[]{:S(2)}) collective-permute-start(bf16[2,1408,128]{2,1,0:T(8,128)(2,1)S(1)} %get-tuple-element.144.refs_4_), channel_id=1, source_target_pairs={{0,4},{4,0},{1,5},{5,1},{2,6},{6,2},{3,7},{7,3},{8,12},{12,8},{9,1... | collective-permute-start | bytes 2162696 | tf_op jit(solution)/shard_map/ppermute | solution.py:123
  141.4 23.1 %collective-permute-start.18 = (bf16[2,1408,128]{2,1,0:T(8,128)(2,1)S(1)}, bf16[2,1408,128]{2,1,0:T(8,128)(2,1)S(1)}, u32[]{:S(2)}, u32[]{:S(2)}) collective-permute-start(bf16[2,1408,128]{2,1,0:T(8,128)(2,1)S(1)} %get-tuple-element.155.refs_8_), channel_id=1, source_target_pairs={{0,4},{4,0},{1,5},{5,1},{2,6},{6,2},{3,7},{7,3},{8,12},{12,8},{9,1... | collective-permute-start | bytes 2162696 | tf_op jit(solution)/shard_map/ppermute | solution.py:123
  143.1 28.4 %collective-permute-start.22 = (bf16[2,1408,128]{2,1,0:T(8,128)(2,1)S(1)}, bf16[2,1408,128]{2,1,0:T(8,128)(2,1)S(1)}, u32[]{:S(2)}, u32[]{:S(2)}) collective-permute-start(bf16[2,1408,128]{2,1,0:T(8,128)(2,1)S(1)} %get-tuple-element.163), channel_id=1, source_target_pairs={{0,1},{1,0},{2,3},{3,2},{4,5},{5,4},{6,7},{7,6},{8,9},{9,8},{10,11... | collective-permute-start | bytes 2162696 | tf_op jit(solution)/shard_map/ppermute | solution.py:120
  144.3 25.8 %collective-permute-start.20 = (bf16[1408,128]{1,0:T(8,128)(2,1)S(1)}, bf16[1408,128]{1,0:T(8,128)(2,1)S(1)}, u32[]{:S(2)}, u32[]{:S(2)}) collective-permute-start(bf16[1408,128]{1,0:T(8,128)(2,1)S(1)} %get-tuple-element.161), channel_id=1, source_target_pairs={{0,2},{1,3},{2,0},{3,1},{4,6},{5,7},{6,4},{7,5},{8,10},{9,11},{10,... | collective-permute-start | bytes 1081352 | tf_op jit(solution)/shard_map/ppermute | solution.py:120
  145.1 26.4 %collective-permute-start.21 = (bf16[1408,128]{1,0:T(8,128)(2,1)S(1)}, bf16[1408,128]{1,0:T(8,128)(2,1)S(1)}, u32[]{:S(2)}, u32[]{:S(2)}) collective-permute-start(bf16[1408,128]{1,0:T(8,128)(2,1)S(1)} %get-tuple-element.162), channel_id=1, source_target_pairs={{0,3},{1,2},{2,1},{3,0},{4,7},{5,6},{6,5},{7,4},{8,11},{9,10},{10,... | collective-permute-start | bytes 1081352 | tf_op jit(solution)/shard_map/ppermute | solution.py:120
  150.2 28.9 %collective-permute-start.19 = (bf16[2,1408,128]{2,1,0:T(8,128)(2,1)S(1)}, bf16[2,1408,128]{2,1,0:T(8,128)(2,1)S(1)}, u32[]{:S(2)}, u32[]{:S(2)}) collective-permute-start(bf16[2,1408,128]{2,1,0:T(8,128)(2,1)S(1)} %get-tuple-element.160.refs_4_), channel_id=1, source_target_pairs={{0,4},{4,0},{1,5},{5,1},{2,6},{6,2},{3,7},{7,3},{8,12},{12,8},{9,1... | collective-permute-start | bytes 2162696 | tf_op jit(solution)/shard_map/ppermute | solution.py:123
  180.3 18.6 %collective-permute-start.25 = (bf16[2,1408,128]{2,1,0:T(8,128)(2,1)S(1)}, bf16[2,1408,128]{2,1,0:T(8,128)(2,1)S(1)}, u32[]{:S(2)}, u32[]{:S(2)}) collective-permute-start(bf16[2,1408,128]{2,1,0:T(8,128)(2,1)S(1)} %get-tuple-element.170.refs_8_), channel_id=1, source_target_pairs={{0,4},{4,0},{1,5},{5,1},{2,6},{6,2},{3,7},{7,3},{8,12},{12,8},{9,1... | collective-permute-start | bytes 2162696 | tf_op jit(solution)/shard_map/ppermute | solution.py:123
  183.6 14.0 %collective-permute-start.24 = (f32[128,1024]{1,0:T(8,128)S(1)}, f32[128,1024]{1,0:T(8,128)S(1)}, u32[]{:S(2)}, u32[]{:S(2)}) collective-permute-start(f32[128,1024]{1,0:T(8,128)S(1)} %get-tuple-element.169), channel_id=1, source_target_pairs={{0,16},{8,24},{16,0},{24,8},{1,17},{9,25},{17,1},{25,9},{2,18},{10... | collective-permute-start | bytes 1572872 | tf_op jit(solution)/shard_map/ppermute | solution.py:117
  203.7 17.6 %collective-permute-start.30 = (f32[128,1024]{1,0:T(8,128)S(1)}, f32[128,1024]{1,0:T(8,128)S(1)}, u32[]{:S(2)}, u32[]{:S(2)}) collective-permute-start(f32[128,1024]{1,0:T(8,128)S(1)} %get-tuple-element.196), channel_id=1, source_target_pairs={{0,16},{8,24},{16,0},{24,8},{1,17},{9,25},{17,1},{25,9},{2,18},{10... | collective-permute-start | bytes 1572872 | tf_op jit(solution)/shard_map/ppermute | solution.py:117
  206.1 10.1 %collective-permute-start.27 = (f32[128,256]{1,0:T(8,128)S(1)}, f32[128,256]{1,0:T(8,128)S(1)}, u32[]{:S(2)}, u32[]{:S(2)}) collective-permute-start(f32[128,256]{1,0:T(8,128)S(1)} %get-tuple-element.190), channel_id=1, source_target_pairs={{0,1},{1,0},{2,3},{3,2},{4,5},{5,4},{6,7},{7,6},{8,9},{9,8},{10,11... | collective-permute-start | bytes 393224 | tf_op jit(solution)/shard_map/ppermute | solution.py:120
  207.7 12.9 %collective-permute-start.28 = (f32[128,256]{1,0:T(8,128)S(1)}, f32[128,256]{1,0:T(8,128)S(1)}, u32[]{:S(2)}, u32[]{:S(2)}) collective-permute-start(f32[128,256]{1,0:T(8,128)S(1)} %get-tuple-element.191), channel_id=1, source_target_pairs={{0,2},{1,3},{2,0},{3,1},{4,6},{5,7},{6,4},{7,5},{8,10},{9,11},{10,... | collective-permute-start | bytes 393224 | tf_op jit(solution)/shard_map/ppermute | solution.py:120
  210.3 10.4 %collective-permute-start.29 = (f32[128,256]{1,0:T(8,128)S(1)}, f32[128,256]{1,0:T(8,128)S(1)}, u32[]{:S(2)}, u32[]{:S(2)}) collective-permute-start(f32[128,256]{1,0:T(8,128)S(1)} %get-tuple-element.192), channel_id=1, source_target_pairs={{0,3},{1,2},{2,1},{3,0},{4,7},{5,6},{6,5},{7,4},{8,11},{9,10},{10,... | collective-permute-start | bytes 393224 | tf_op jit(solution)/shard_map/ppermute | solution.py:120
  210.5 4.5 %collective-permute-start.4 = (f32[8,2816]{1,0:T(8,128)S(1)}, f32[8,2816]{1,0:T(8,128)S(1)}, u32[]{:S(2)}, u32[]{:S(2)}) collective-permute-start(f32[8,2816]{1,0:T(8,128)S(1)} %get-tuple-element.121.refs_2_), channel_id=1, source_target_pairs={{0,4},{4,0},{1,5},{5,1},{2,6},{6,2},{3,7},{7,3},{8,12},{12,8},{9,1... | collective-permute-start | bytes 270344 | tf_op jit(solution)/shard_map/ppermute | solution.py:123
  221.8 6.4 %collective-permute-start.31 = (f32[128,256]{1,0:T(8,128)S(1)}, f32[128,256]{1,0:T(8,128)S(1)}, u32[]{:S(2)}, u32[]{:S(2)}) collective-permute-start(f32[128,256]{1,0:T(8,128)S(1)} %get-tuple-element.199), channel_id=1, source_target_pairs={{0,1},{1,0},{2,3},{3,2},{4,5},{5,4},{6,7},{7,6},{8,9},{9,8},{10,11... | collective-permute-start | bytes 393224 | tf_op jit(solution)/shard_map/ppermute | solution.py:120
  223.9 11.7 %collective-permute-start.32 = (f32[128,256]{1,0:T(8,128)S(1)}, f32[128,256]{1,0:T(8,128)S(1)}, u32[]{:S(2)}, u32[]{:S(2)}) collective-permute-start(f32[128,256]{1,0:T(8,128)S(1)} %get-tuple-element.200), channel_id=1, source_target_pairs={{0,2},{1,3},{2,0},{3,1},{4,6},{5,7},{6,4},{7,5},{8,10},{9,11},{10,... | collective-permute-start | bytes 393224 | tf_op jit(solution)/shard_map/ppermute | solution.py:120
  225.0 10.7 %collective-permute-start.33 = (f32[128,256]{1,0:T(8,128)S(1)}, f32[128,256]{1,0:T(8,128)S(1)}, u32[]{:S(2)}, u32[]{:S(2)}) collective-permute-start(f32[128,256]{1,0:T(8,128)S(1)} %get-tuple-element.201), channel_id=1, source_target_pairs={{0,3},{1,2},{2,1},{3,0},{4,7},{5,6},{6,5},{7,4},{8,11},{9,10},{10,... | collective-permute-start | bytes 393224 | tf_op jit(solution)/shard_map/ppermute | solution.py:120
  238.4 3.9 %collective-permute-start.38 = (f32[16,512]{1,0:T(8,128)S(1)}, f32[16,512]{1,0:T(8,128)S(1)}, u32[]{:S(2)}, u32[]{:S(2)}) collective-permute-start(f32[16,512]{1,0:T(8,128)S(1)} %add.29), channel_id=1, source_target_pairs={{0,16},{8,24},{16,0},{24,8},{1,17},{9,25},{17,1},{25,9},{2,18},{10... | collective-permute-start | bytes 98312 | tf_op jit(solution)/shard_map/ppermute | solution.py:117
  242.3 9.9 %collective-permute-start.39 = (f32[16,512]{1,0:T(8,128)S(1)}, f32[16,512]{1,0:T(8,128)S(1)}, u32[]{:S(2)}, u32[]{:S(2)}) collective-permute-start(f32[16,512]{1,0:T(8,128)S(1)} %add.30.refs_8_), channel_id=1, source_target_pairs={{0,4},{4,0},{1,5},{5,1},{2,6},{6,2},{3,7},{7,3},{8,12},{12,8},{9,1... | collective-permute-start | bytes 98312 | tf_op jit(solution)/shard_map/ppermute | solution.py:123
  243.8 4.4 %collective-permute-start.34 = (f32[8,128]{1,0:T(8,128)S(1)}, f32[8,128]{1,0:T(8,128)S(1)}, u32[]{:S(2)}, u32[]{:S(2)}) collective-permute-start(f32[8,128]{1,0:T(8,128)S(1)} %get-tuple-element.205.refs_4_), channel_id=1, source_target_pairs={{0,1},{1,0},{2,3},{3,2},{4,5},{5,4},{6,7},{7,6},{8,9},{9,8},{10,11... | collective-permute-start | bytes 12296 | tf_op jit(solution)/shard_map/ppermute | solution.py:120
  245.8 4.5 %collective-permute-start.35 = (f32[8,128]{1,0:T(8,128)S(1)}, f32[8,128]{1,0:T(8,128)S(1)}, u32[]{:S(2)}, u32[]{:S(2)}) collective-permute-start(f32[8,128]{1,0:T(8,128)S(1)} %get-tuple-element.205.refs_4_), channel_id=1, source_target_pairs={{0,2},{1,3},{2,0},{3,1},{4,6},{5,7},{6,4},{7,5},{8,10},{9,11},{10,... | collective-permute-start | bytes 12296 | tf_op jit(solution)/shard_map/ppermute | solution.py:120
  246.8 5.4 %collective-permute-start.36 = (f32[8,128]{1,0:T(8,128)S(1)}, f32[8,128]{1,0:T(8,128)S(1)}, u32[]{:S(2)}, u32[]{:S(2)}) collective-permute-start(f32[8,128]{1,0:T(8,128)S(1)} %get-tuple-element.205.refs_4_), channel_id=1, source_target_pairs={{0,3},{1,2},{2,1},{3,0},{4,7},{5,6},{6,5},{7,4},{8,11},{9,10},{10,... | collective-permute-start | bytes 12296 | tf_op jit(solution)/shard_map/ppermute | solution.py:120
  253.1 10.1 %collective-permute-start.41 = (bf16[128,512]{1,0:T(8,128)(2,1)S(1)}, bf16[128,512]{1,0:T(8,128)(2,1)S(1)}, u32[]{:S(2)}, u32[]{:S(2)}) collective-permute-start(bf16[128,512]{1,0:T(8,128)(2,1)S(1)} %get-tuple-element.208), channel_id=1, source_target_pairs={{0,2},{1,3},{2,0},{3,1},{4,6},{5,7},{6,4},{7,5},{8,10},{9,11},{10,... | collective-permute-start | bytes 393224 | tf_op jit(solution)/shard_map/ppermute | solution.py:120
  253.3 9.9 %collective-permute-start.42 = (bf16[128,512]{1,0:T(8,128)(2,1)S(1)}, bf16[128,512]{1,0:T(8,128)(2,1)S(1)}, u32[]{:S(2)}, u32[]{:S(2)}) collective-permute-start(bf16[128,512]{1,0:T(8,128)(2,1)S(1)} %get-tuple-element.208), channel_id=1, source_target_pairs={{0,3},{1,2},{2,1},{3,0},{4,7},{5,6},{6,5},{7,4},{8,11},{9,10},{10,... | collective-permute-start | bytes 393224 | tf_op jit(solution)/shard_map/ppermute | solution.py:120
  255.8 7.6 %collective-permute-start.40 = (bf16[128,512]{1,0:T(8,128)(2,1)S(1)}, bf16[128,512]{1,0:T(8,128)(2,1)S(1)}, u32[]{:S(2)}, u32[]{:S(2)}) collective-permute-start(bf16[128,512]{1,0:T(8,128)(2,1)S(1)} %get-tuple-element.208), channel_id=1, source_target_pairs={{0,1},{1,0},{2,3},{3,2},{4,5},{5,4},{6,7},{7,6},{8,9},{9,8},{10,11... | collective-permute-start | bytes 393224 | tf_op jit(solution)/shard_map/ppermute | solution.py:120
  263.4 9.9 %collective-permute-start.44 = (bf16[4,128,512]{2,1,0:T(8,128)(2,1)S(1)}, bf16[4,128,512]{2,1,0:T(8,128)(2,1)S(1)}, u32[]{:S(2)}, u32[]{:S(2)}) collective-permute-start(bf16[4,128,512]{2,1,0:T(8,128)(2,1)S(1)} %pad_maximum_fusion.refs_7_), channel_id=1, source_target_pairs={{0,16},{8,24},{16,0},{24,8},{1,17},{9,25},{17,1},{25,9},{2,18},{10... | collective-permute-start | bytes 1572872 | tf_op jit(solution)/shard_map/ppermute | solution.py:117
  264.0 13.0 %collective-permute-start.43 = (bf16[4,128,512]{2,1,0:T(8,128)(2,1)S(1)}, bf16[4,128,512]{2,1,0:T(8,128)(2,1)S(1)}, u32[]{:S(2)}, u32[]{:S(2)}) collective-permute-start(bf16[4,128,512]{2,1,0:T(8,128)(2,1)S(1)} %pad_maximum_fusion.refs_7_), channel_id=1, source_target_pairs={{0,8},{8,0},{16,24},{24,16},{1,9},{9,1},{17,25},{25,17},{2,10},{10... | collective-permute-start | bytes 1572872 | tf_op jit(solution)/shard_map/ppermute | solution.py:114
  273.3 3.7 %collective-permute-start.45 = (bf16[4,128,512]{2,1,0:T(8,128)(2,1)S(1)}, bf16[4,128,512]{2,1,0:T(8,128)(2,1)S(1)}, u32[]{:S(2)}, u32[]{:S(2)}) collective-permute-start(bf16[4,128,512]{2,1,0:T(8,128)(2,1)S(1)} %collective-permute-done.44.refs_9_), channel_id=1, source_target_pairs={{0,8},{8,0},{16,24},{24,16},{1,9},{9,1},{17,25},{25,17},{2,10},{10... | collective-permute-start | bytes 1572872 | tf_op jit(solution)/shard_map/ppermute | solution.py:114
  273.3 3.7 %collective-permute-start.46 = (f32[8,512]{1,0:T(8,128)S(1)}, f32[8,512]{1,0:T(8,128)S(1)}, u32[]{:S(2)}, u32[]{:S(2)}) collective-permute-start(f32[8,512]{1,0:T(8,128)S(1)} %get-tuple-element.209.refs_11_), channel_id=1, source_target_pairs={{0,4},{4,0},{1,5},{5,1},{2,6},{6,2},{3,7},{7,3},{8,12},{12,8},{9,1... | collective-permute-start | bytes 49160 | tf_op jit(solution)/shard_map/ppermute | solution.py:123
  286.3 3.7 %collective-permute-start.48 = (f32[8,512]{1,0:T(8,128)S(1)}, f32[8,512]{1,0:T(8,128)S(1)}, u32[]{:S(2)}, u32[]{:S(2)}) collective-permute-start(f32[8,512]{1,0:T(8,128)S(1)} %add.31), channel_id=1, source_target_pairs={{0,16},{8,24},{16,0},{24,8},{1,17},{9,25},{17,1},{25,9},{2,18},{10... | collective-permute-start | bytes 49160 | tf_op jit(solution)/shard_map/ppermute | solution.py:117
  290.0 7.3 %collective-permute-start.49 = (f32[8,512]{1,0:T(8,128)S(1)}, f32[8,512]{1,0:T(8,128)S(1)}, u32[]{:S(2)}, u32[]{:S(2)}) collective-permute-start(f32[8,512]{1,0:T(8,128)S(1)} %add.32), channel_id=1, source_target_pairs={{0,1},{1,0},{2,3},{3,2},{4,5},{5,4},{6,7},{7,6},{8,9},{9,8},{10,11... | collective-permute-start | bytes 49160 | tf_op jit(solution)/shard_map/ppermute | solution.py:120
  294.9 4.6 %collective-permute-start.50 = (f32[8,512]{1,0:T(8,128)S(1)}, f32[8,512]{1,0:T(8,128)S(1)}, u32[]{:S(2)}, u32[]{:S(2)}) collective-permute-start(f32[8,512]{1,0:T(8,128)S(1)} %add.32), channel_id=1, source_target_pairs={{0,2},{1,3},{2,0},{3,1},{4,6},{5,7},{6,4},{7,5},{8,10},{9,11},{10,... | collective-permute-start | bytes 49160 | tf_op jit(solution)/shard_map/ppermute | solution.py:120
  295.5 5.5 %collective-permute-start.51 = (f32[8,512]{1,0:T(8,128)S(1)}, f32[8,512]{1,0:T(8,128)S(1)}, u32[]{:S(2)}, u32[]{:S(2)}) collective-permute-start(f32[8,512]{1,0:T(8,128)S(1)} %add.32), channel_id=1, source_target_pairs={{0,3},{1,2},{2,1},{3,0},{4,7},{5,6},{6,5},{7,4},{8,11},{9,10},{10,... | collective-permute-start | bytes 49160 | tf_op jit(solution)/shard_map/ppermute | solution.py:120
  (19 other events, 306.7 us)

commit v5 on v4

--- a/solution.py
+++ b/solution.py
@@ -8,13 +8,15 @@
 
 SLIDES = 3
 LANES = 128
+PAD = 8
 ANY = pl.BlockSpec(memory_space=pl.ANY)
 BF = jnp.bfloat16
 F32 = jnp.float32
 VMEM_BYTES = 20 * 1024 * 1024
-BACK_COST = 6 * 10**9
+COSTS = {"spots": 1, "back3": 6, "addx1": 9, "half0": 3}
 WIDTHS = (128, 128, 128, 128)
-GROUPS = ((0, 1), (2, 3))
+GROUPS = ((0, 1), (2,), (3,))
+SUMS = ((0,), (1, 2))
 ORDER = (
     "Y0 e0 Y1 w:ez1+ez2+ez3",
     "Y2 A0 a0 e3",
@@ -23,9 +25,10 @@
     "S0 A3 w:f22+f32+n2 a3",
     "S1 w:s0 S2 w:s1",
     "F0 w:f23+f33+n3 S3 w:s2",
-    "f0 P0 F1 w:rx0",
-    "G1 P1 Q0 m0",
-    "R0 Q1 R1",
+    "f0 P0 F1 f1",
+    "P1 F2 Q0 G2",
+    "P2 X1 Q1 U0",
+    "m0 R1 R0",
 )
 
 
@@ -47,7 +50,7 @@
         self.flags = flags
         self.token = jnp.zeros((8, LANES), F32)
 
-    def run(self, name, body, ins=(), outs=(), after=(), through=(), grid=(1,), scratch=(), cost=0, vmem=VMEM_BYTES):
+    def run(self, name, body, ins=(), outs=(), after=(), through=(), grid=(1,), scratch=()):
         ins = [*ins, *((a, ANY) for a in after)]
         carried = (*through, self.token)
         n_in, n_out, n_thr = len(ins), len(outs), len(carried)
@@ -70,8 +73,8 @@
                 scratch_shapes=list(scratch),
             ),
             input_output_aliases={1 + n_in + j: n_out + j for j in range(n_thr)},
-            compiler_params=pltpu.CompilerParams(vmem_limit_bytes=vmem),
-            cost_estimate=pl.CostEstimate(flops=cost, bytes_accessed=0, transcendentals=0),
+            compiler_params=pltpu.CompilerParams(vmem_limit_bytes=VMEM_BYTES),
+            cost_estimate=pl.CostEstimate(flops=COSTS.get(name, 0) * 10**9, bytes_accessed=0, transcendentals=0),
             name=name,
         )(self.flags, *[a for a, _ in ins], *carried)
         self.token = results[-1]
@@ -137,6 +140,9 @@
 
     def start_swap(c):
         w = WIDTHS[c]
+        if c == 0:
+            sent["y0"] = over_spot(expr[:, :, :w])
+            return
 
         def body(fl, i, out, sems):
             copy_all([(None, i[0].at[p, :, pl.ds(offsets[c], w)], out[0].at[p]) for p in range(2)], sems)
@@ -190,7 +196,6 @@
         one = whole((half, w))
         (st["f", c],) = run(
             f"back{c}", body, [(sent[f"f2{c}"], one), (sent[f"f3{c}"], one)], [(sds((2, half, w), BF), whole((2, half, w)))],
-            cost=BACK_COST if c == len(WIDTHS) - 1 else 0,
         )
         sent[f"s{c}"] = over_spot(st["f", c])
 
@@ -281,16 +286,24 @@
             [(sds((rows, LANES), F32), whole((rows, LANES))), (sds((8, LANES), F32), whole((8, LANES)))],
         )
 
+    def halves_of(g):
+        shape = (quarter, slots * group_width[g])
+        if len(GROUPS[g]) == 1:
+            return [(sds(shape, F32), whole(shape))] * 2
+        return [(sds((2, *shape), F32), whole((2, *shape)))]
+
     def forward(g):
         members, wide_all = GROUPS[g], group_width[g] * slots
         shape = (2, quarter, wide_all)
         outs = [(sds((rows, slots * WIDTHS[c]), BF), whole((rows, slots * WIDTHS[c]))) for c in members]
-        outs += [(sds(shape, F32), whole(shape))] * 2
+        outs += [(sds(shape, F32), whole(shape))]
+        outs += halves_of(g)
 
         late = members[-1] if spot_size == 2 and g == len(GROUPS) - 1 else None
 
-        def product(pt, efs, keep, send, direct=None):
+        def product(pt, efs, keep, *send, direct=None):
             done = 0
+            low, high = send if len(send) == 2 else (send[0].at[0], send[0].at[1])
             for c, ef in zip(members, efs):
                 w = WIDTHS[c]
                 if c == late:
@@ -300,11 +313,11 @@
                     acc = jnp.concatenate([near, far], axis=1)
                 else:
                     acc = jnp.dot(pt[...], ef[...], preferred_element_type=F32)
-                for q, ref in enumerate((keep, send, keep, send)):
+                for q, ref in enumerate((keep.at[0], low, keep.at[1], high)):
                     rows_q = acc[q * quarter : (q + 1) * quarter]
                     for s in range(slots):
                         base = s * group_width[g] + done
-                        ref[q // 2, :, base : base + w] = rows_q[:, s * w : (s + 1) * w]
+                        ref[:, base : base + w] = rows_q[:, s * w : (s + 1) * w]
                 done += w
 
         if spot_size == 2:
@@ -353,10 +366,10 @@
 
             ins = [(st["pt"], whole((spots, rows)))] + [(a, at_chunk(c)) for c in members for a in st["pieces"]]
             scratch = []
-        *efs, keep, send = run(f"forward{g}", body, ins, outs, scratch=scratch)
-        for c, ef in zip(members, efs):
+        results = run(f"forward{g}", body, ins, outs, scratch=scratch)
+        for c, ef in zip(members, results):
             st["e", c] = ef
-        st["r", g], st["send", g] = keep, send
+        st["r", g], st["send", g] = results[len(members)], results[len(members) + 1 :]
 
     def forward_late(g):
         c = GROUPS[g][-1]
@@ -364,69 +377,126 @@
         shape = (2, quarter, wide)
 
         def body(fl, i, out, sems):
-            pt, swapped, keep, send = i
+            pt, swapped, keep, low, high = i
             at = pl.ds(pl.multiple_of((1 - fl[0]) * half, LANES), half)
-            copy_all([(None, swapped.at[n], out[2].at[at, pl.ds((2 + n) * w, w)]) for n in (0, 1)], sems)
+            copy_all([(None, swapped.at[n], out[3].at[at, pl.ds((2 + n) * w, w)]) for n in (0, 1)], sems)
             both = jnp.concatenate([swapped[0], swapped[1]], axis=1)
             acc = jnp.dot(pt[:, at], both, preferred_element_type=F32)
-            out[0][...] = keep[...]
-            out[1][...] = send[...]
-            for q, ref in enumerate((out[0], out[1], out[0], out[1])):
+            for new, old in zip(out, (keep, low, high)):
+                new[...] = old[...]
+            for q, ref in enumerate((out[0].at[0], out[1], out[0].at[1], out[2])):
                 for n in (0, 1):
                     base = (3 + n) * group_width[g] - w
-                    ref[q // 2, :, base : base + w] += acc[q * quarter : (q + 1) * quarter, n * w : (n + 1) * w]
-
+                    ref[:, base : base + w] += acc[q * quarter : (q + 1) * quarter, n * w : (n + 1) * w]
+
+        one = whole((quarter, wide))
         ins = [(st["pt"], whole((spots, rows))), (sent[f"s{c}"], whole((2, half, w)))]
-        ins += [(st["r", g], whole(shape)), (st["send", g], whole(shape))]
-        st["r", g], send, st["e", c] = run(
-            f"forwardlate{g}", body, ins, [(sds(shape, F32), whole(shape))] * 2, through=[st["e", c]],
+        ins += [(st["r", g], whole(shape))] + [(a, one) for a in st["send", g]]
+        st["r", g], *send, st["e", c] = run(
+            f"forwardlate{g}", body, ins, [(sds(shape, F32), whole(shape)), *halves_of(g)], through=[st["e", c]],
             scratch=[pltpu.SemaphoreType.DMA((2,))],
         )
-        sent[f"rc{g}"] = over_core(send)
+        send_core(g, send)
+
+    def send_core(g, send):
+        for n, part in enumerate(send):
+            sent[f"rc{n}{g}"] = over_core(part)
 
     def forward_send(g):
-        (send,) = run(f"send{g}", None, through=[st["send", g]])
-        sent[f"rc{g}"] = over_core(send)
+        send_core(g, run(f"send{g}", None, through=st["send", g]))
 
     def reduce_core(g):
         wide = slots * group_width[g]
         shape, one = (2, quarter, wide), (quarter, wide)
 
-        def body(fl, i, out):
-            out[0][...] = i[0][0] + i[1][0]
-            out[1][...] = i[0][1] + i[1][1]
-
-        ins = [(st["r", g], whole(shape)), (sent[f"rc{g}"], whole(shape))]
-        st["r", g], b = run(f"core{g}", body, ins, [(sds(one, F32), whole(one))] * 2)
+        single = len(GROUPS[g]) == 1
+
+        def body(fl, i, out):
+            for n in (0, 1):
+                out[n][0:quarter, :] = i[0][n] + (i[1 + n][...] if single else i[1][n])
+            if single:
+                out[1][quarter:, :] = jnp.zeros((PAD, wide), F32)
+
+        ins = [(st["r", g], whole(shape))]
+        ins += [(sent[f"rc{n}{g}"], whole(one)) for n in (0, 1)] if single else [(sent[f"rc0{g}"], whole(shape))]
+        more = (quarter + PAD, wide) if single else one
+        st["r", g], b = run(f"core{g}", body, ins, [(sds(one, F32), whole(one)), (sds(more, F32), whole(more))])
         sent[f"rx{g}"] = over_x(b)
 
-    def reduce_x(g):
-        w = group_width[g]
-        one, part = (quarter, slots * w), (quarter, w)
-
-        def body(fl, i, out):
-            for s in range(slots):
-                at = slice(s * w, (s + 1) * w)
-                out[s][...] = i[0][:, at] + i[1][:, at]
-
-        ins = [(st["r", g], whole(one)), (sent[f"rx{g}"], whole(one))]
-        st["r", g], *parts = run(f"x{g}", body, ins, [(sds(part, F32), whole(part))] * slots)
-        for s in (1, 2, 3):
-            sent[f"rz{s}{g}"] = over_gene(parts[s - 1], s)
-
-    def reduce_gene(g):
-        part = (quarter, group_width[g])
-
-        def body(fl, i, out):
-            out[0][...] = (i[0][...] + i[1][...]) + (i[2][...] + i[3][...])
-
-        parts = [st["r", g]] + [sent[f"rz{s}{g}"] for s in (1, 2, 3)]
-        (v,) = run(f"gene{g}", body, [(a, whole(part)) for a in parts], [(sds(part, F32), whole(part))])
-        st["r", g] = v
+    sum_groups = [[g for g in z] for z in SUMS]
+    sum_width = [sum(group_width[g] for g in z) for z in SUMS]
+
+    def add_x(g):
+        one = whole((quarter, slots * group_width[g]))
+
+        def body(fl, i, out):
+            out[0][...] = i[0][...] + i[1][0:quarter, :]
+
+        ins = [(st["r", g], one), (sent[f"rx{g}"], whole(sent[f"rx{g}"].shape))]
+        (st["added", g],) = run(f"addx{g}", body, ins, [(sds(one.block_shape, F32), one)])
+
+    def reduce_x(z):
+        members, w = sum_groups[z], sum_width[z]
+        part = (quarter, w)
+        in_halves = z < len(SUMS) - 1
+
+        def body(fl, i, out):
+            done, i = 0, list(i)
+            for g in members:
+                v = group_width[g]
+                refs = [i.pop(0) for _ in parts_of[g]]
+                for s in range(slots):
+                    at = slice(s * v, (s + 1) * v)
+                    value = sum(ref[0:quarter, at] for ref in refs)
+                    if in_halves and s >= 2:
+                        out[2][s - 2, 0:quarter, done : done + v] = value
+                    else:
+                        out[s][:, done : done + v] = value
+                done += v
+            if in_halves:
+                out[2][:, quarter:, :] = jnp.zeros((2, PAD, w), F32)
+
+        parts_of = {g: [st["added", g]] if ("added", g) in st else [st["r", g], sent[f"rx{g}"]] for g in members}
+        ins = [(a, whole(a.shape)) for g in members for a in parts_of[g]]
+        outs = [(sds(part, F32), whole(part))] * (2 if in_halves else slots)
+        if in_halves:
+            padded = (2, quarter + PAD, w)
+            outs += [(sds(padded, F32), whole(padded))]
+        parts = run(f"x{z}", body, ins, outs)
+        if in_halves:
+            st["z", z] = parts[:2]
+            sent[f"rz2{z}"] = over_gene(parts[2], 2)
+        else:
+            st["z", z] = parts[:1]
+            for s in (1, 2, 3):
+                sent[f"rz{s}{z}"] = over_gene(parts[s], s)
+
+    def reduce_half(z):
+        part = (quarter, sum_width[z])
+
+        def body(fl, i, out):
+            for n in (0, 1):
+                out[n][...] = i[n][...] + i[2][n, 0:quarter, :]
+
+        ins = [(a, whole(part)) for a in st["z", z]] + [(sent[f"rz2{z}"], whole((2, quarter + PAD, sum_width[z])))]
+        a, b = run(f"half{z}", body, ins, [(sds(part, F32), whole(part))] * 2)
+        st["z", z], sent[f"rz1{z}"] = [a], over_gene(b, 1)
+
+    def reduce_gene(z):
+        part = (quarter, sum_width[z])
+        others = [sent[f"rz{s}{z}"] for s in ((1,) if z < len(SUMS) - 1 else (1, 2, 3))]
+
+        def body(fl, i, out):
+            out[0][...] = sum(ref[...] for ref in i)
+
+        ins = [(a, whole(part)) for a in (*st["z", z], *others)]
+        (st["sum", z],) = run(f"gene{z}", body, ins, [(sds(part, F32), whole(part))])
 
     steps = {
         "Y": start_swap, "A": start_along, "a": along_send, "S": start_back,
-        "e": totals, "m": shares, "F": forward, "f": forward_send, "G": forward_late, "b": members_of, "P": reduce_core, "Q": reduce_x, "R": reduce_gene,
+        "e": totals, "m": shares, "F": forward, "f": forward_send, "G": forward_late, "b": members_of,
+        "P": reduce_core, "X": add_x, "Q": reduce_x,
+        "U": reduce_half, "R": reduce_gene,
     }
     if spot_size != 2:
         full = lax.all_gather(expression, "spot", axis=0, tiled=True).reshape(slots, rows, genes)
@@ -441,9 +511,9 @@
         elif spot_size == 2 or word[0] not in "YAaS":
             steps[word[0]](int(word[1]))
 
-    n_ch, n_gr = len(WIDTHS), len(GROUPS)
-    starts = [offsets[g[0]] for g in GROUPS]
-    preds = [(st["r", g], whole((quarter, group_width[g]))) for g in range(n_gr)]
+    n_ch, n_sum = len(WIDTHS), len(SUMS)
+    starts = [offsets[GROUPS[z[0]][0]] for z in SUMS]
+    preds = [(st["sum", z], whole((quarter, sum_width[z]))) for z in range(n_sum)]
     mine = (spatial, pl.BlockSpec((quarter, genes), lambda g, f: (f[2], 0)))
     memb = (st["member"], whole((quarter, LANES)))
     gene_spec, spot_spec = whole((16, genes)), whole((8, quarter))
@@ -454,8 +524,8 @@
         valid = jnp.sum(memb[:, SLIDES : SLIDES + 1])
         out[0][...] = jnp.broadcast_to(valid, (16, genes))
         totals = [jnp.zeros((quarter, LANES), F32) for _ in range(3)]
-        for g in range(n_gr):
-            for o in range(0, group_width[g], LANES):
+        for g in range(n_sum):
+            for o in range(0, sum_width[g], LANES):
                 at = slice(starts[g] + o, starts[g] + o + LANES)
                 pr, ta = i[2 + g][:, o : o + LANES], i[1][:, at].astype(F32)
                 for j, v in enumerate((pr * ta, pr * pr, ta * ta)):
@@ -475,6 +545,8 @@
     gene_sums = gene_sums + over_core(gene_sums)
     gene_sums = gene_sums + over_x(gene_sums)
     gene_parts = [gene_sums, over_spot(gene_sums)] if spot_size == 2 else [sum_spot(gene_sums)]
+
+    run("spots", None, after=spot_parts)
 
     def grads_body(fl, i, out):
         memb, ta_ref, kl, ent = i[:4]
@@ -511,8 +583,8 @@
             value = jnp.where(lane == n, term, value)
         out[1][...] = value
         cols = [jnp.broadcast_to(memb[:, k : k + 1], (quarter, LANES)) for k in range(SLIDES)]
-        for g in range(n_gr):
-            for o in range(0, group_width[g], LANES):
+        for g in range(n_sum):
+            for o in range(0, sum_width[g], LANES):
                 at = slice(starts[g] + o, starts[g] + o + LANES)
                 f_t, f_p = coef_t, coef_p
                 for k in range(SLIDES):
@@ -528,24 +600,35 @@
         [(sds((quarter, genes), BF), whole((quarter, genes))), (sds((8, spots), F32), row8)],
     )
     terms = [terms, over_spot(terms)] if spot_size == 2 else [sum_spot(terms)]
-    grad = jnp.stack([grad] + [over_gene(grad, s) for s in (1, 2, 3)])
     grad_x = over_x(grad)
-    grads = [grad, over_core(grad), grad_x, over_core(grad_x)]
+    others = [over_gene(grad, s) for s in (1, 2, 3)]
+    one, rest = (quarter, genes), (slots - 1, quarter, genes)
+
+    def gather_body(fl, i, out):
+        for n in range(slots - 1):
+            out[0][n] = i[n][...]
+
+    (rest_z,) = run(
+        "gather", gather_body, [(a, whole(one)) for a in others], [(sds(rest, BF), whole(rest))], after=[grad_x]
+    )
+    rest_x = over_x(rest_z)
+    grads = [grad, over_core(grad), grad_x, over_core(grad_x), rest_z, over_core(rest_z), rest_x, over_core(rest_x)]
 
     row_blk = rows // 4
 
     def backward_body(fl, i, out, held, sems):
         lg, tot, sm = i[:3]
-        efs, gs, terms = i[3 : 3 + n_ch], i[3 + n_ch : 7 + n_ch], i[7 + n_ch :]
+        efs, gs, terms = i[3 : 3 + n_ch], i[3 + n_ch : 11 + n_ch], i[11 + n_ch :]
 
         @pl.when(pl.program_id(0) == 0)
         def _():
             row = lax.broadcasted_iota(jnp.int32, (8, spots), 0)
             out[1][...] = jnp.where(row == 0, 0.0, sum(ref[...] for ref in terms))
             copies = []
-            for b, ref in enumerate(gs):
-                at = pl.multiple_of((fl[2] ^ b) * quarter, quarter)
-                copies.append((None, ref, held.at[:, pl.ds(at, quarter), :]))
+            for b in range(sizes["cell"]):
+                at = pl.ds(pl.multiple_of((fl[2] ^ b) * quarter, quarter), quarter)
+                copies.append((None, gs[b], held.at[0, at, :]))
+                copies.append((None, gs[4 + b], held.at[pl.ds(1, slots - 1), at, :]))
             copy_all(copies, sems)
 
         acc = -jnp.broadcast_to(sm[:, 0:1], (row_blk, spots))

time: 305 us -> 293 us (0.961)
  waiting for transfers between devices: 161 us -> 137 us
  Pallas kernels: 54.4 us -> 59.4 us
  starting transfers between devices: 69.4 us -> 73.6 us
    ppermute x11, waiting for transfers between devices: 83.2 us -> 73.9 us  [over_spot(): return lax.ppermute(v, 'spot', xor_pairs(spot_size, step))]
    ppermute x30 -> x29, waiting for transfers between devices: 48.8 us -> 41.2 us  [over_gene(): return lax.ppermute(v, 'gene', xor_pairs(4, step))]
    ppermute x5 -> x7, waiting for transfers between devices: 23.4 us -> 17.4 us  [over_x(): return lax.ppermute(v, 'cell', xor_pairs(4, 2))]
    pallas_call x43 -> x48, Pallas kernels: 54.4 us -> 59.4 us  [run(): pl.pallas_call(kernel, out_shape=[s for s, _ in outs] + [sds(a.shape, a.d...]
    ppermute x5 -> x7, starting transfers between devices: 5.22 us -> 8.9 us  [over_x(): return lax.ppermute(v, 'cell', xor_pairs(4, 2))]
    ppermute x30 -> x29, starting transfers between devices: 49 us -> 46.6 us  [over_gene(): return lax.ppermute(v, 'gene', xor_pairs(4, step))]
    unnamed x30 -> x22, local copies, waits for them, and re-layouts: 7.13 us -> 6.87 us
  transfers between devices with their start and end apart: 52 -> 58, of which waited for: 33 -> 30; matrix products, arithmetic and copies ran while one was open for 0% -> 0% of each run, Pallas kernels for 11% -> 15%
where the time goes in v5:
time: 293 us
  waiting for transfers between devices  137 us (47%)
  starting transfers between devices  73.6 us (25%)
  Pallas kernels  59.4 us (20%)
  blocking collectives  11.6 us (4%)
  local copies, waits for them, and re-layouts  9.67 us (3%)
    ppermute x11, waiting for transfers between devices, over_spot(): return lax.ppermute(v, 'spot', xor_pairs(spot_size, step))  73.9 us
    pallas_call x48, Pallas kernels, run(): pl.pallas_call(kernel, out_shape=[s for s, _ in outs] + [sds(a.shape, a.d...  59.4 us
    ppermute x29, starting transfers between devices, over_gene(): return lax.ppermute(v, 'gene', xor_pairs(4, step))  46.6 us
    ppermute x29, waiting for transfers between devices, over_gene(): return lax.ppermute(v, 'gene', xor_pairs(4, step))  41.2 us
    ppermute x7, waiting for transfers between devices, over_x(): return lax.ppermute(v, 'cell', xor_pairs(4, 2))  17.4 us
    ppermute x11, starting transfers between devices, over_spot(): return lax.ppermute(v, 'spot', xor_pairs(spot_size, step))  16.2 us
    psum x1, blocking collectives, totals(): st['tot'] = lax.psum(v, 'cell')  11.6 us
    ppermute x7, starting transfers between devices, over_x(): return lax.ppermute(v, 'cell', xor_pairs(4, 2))  8.9 us
  transfers between devices with their start and end apart: 58, of which 30 were waited for; matrix products, arithmetic and copies ran while one was open for 0% of the time, Pallas kernels for 15%

profile of v5, /device:TPU:0, one launch (start us, length us, event | category | flops | bytes accessed | tf_op | source)
XLA Modules:
  0.0 292.6 jit_solution(1480749003814409150)
XLA Ops:
  0.6 2.7 slice.4
  3.4 3.0 %collective-permute-start.3 = (bf16[2,2816,128]{2,1,0:T(8,128)(2,1)}, bf16[2,2816,128]{2,1,0:T(8,128)(2,1)}, u32[]{:S(2)}, u32[]{:S(2)}) collective-permute-start(bf16[2,2816,128]{2,1,0:T(8,128)(2,1)} %slice.4), channel_id=1, source_target_pairs={{0,4},{4,0},{1,5},{5,1},{2,6},{6,2},{3,7},{7,3},{8,12},{12,8},{9,1... | collective-permute-start | bytes 4325384 | tf_op jit(solution)/shard_map/ppermute | solution.py:126
  7.8 2.6 copy-done
  10.4 2.0 swap1.1
  12.5 11.6 %psum.7.refs_1_ = f32[8,512]{1,0:T(8,128)S(1)} all-reduce(f32[8,512]{1,0:T(8,128)S(1)} %get-tuple-element.125), channel_id=1, replica_groups=mesh['cell'=4,'spot'=2,'gene'=4] {'cell'}, use_global_device_ids=true, to_apply=%region_0.1 | all-reduce | flops 4096 | bytes 32768 | tf_op jit(solution)/shard_map/psum | solution.py:226
  25.7 2.6 collective-permute-start.1
  30.4 3.4 %collective-permute-done.2.refs_2_.refs_4_ = f32[8,512]{1,0:T(8,128)S(1)} collective-permute-done((f32[8,512]{1,0:T(8,128)S(1)}, f32[8,512]{1,0:T(8,128)S(1)}, u32[]{:S(2)}, u32[]{:S(2)}) %collective-permute-start.2) | collective-permute-done | bytes 16416 | tf_op jit(solution)/shard_map/ppermute | solution.py:123
  34.4 2.6 copy-done.1
  39.1 2.4 along0.1
  42.0 2.2 collective-permute-start.5
  45.7 2.6 collective-permute-start.6
  48.5 4.0 %prob.1 = (bf16[512,2816]{1,0:T(8,128)(2,1)S(1)}, f32[8,2816]{1,0:T(8,128)S(1)}, f32[8,512]{1,0:T(8,128)S(1)}, f32[8,512]{1,0:T(8,128)S(1)}, f32[8,128]{1,0:T(8,128)S(1)}) custom-call(s32[5]{0:T(128)S(1)} %stack.27.flags, bf16[2816,512]{1,0:T(8,128)(2,1)S(1)} %copy-done.2, f32[8,512]{1,0:T(8,128)S(1)} %psum.7.refs_1_, ...), custom_call_target="tpu_custom_call", output_to_operand_aliasing={{4}: (6, {})} | custom-call | tf_op jit(solution)/shard_map/prob/pallas_call | solution.py:65
  53.2 16.7 %collective-permute-done.9.refs_0_.refs_1_.refs_6_.refs_7_ = bf16[2,2816,128]{2,1,0:T(8,128)(2,1)} collective-permute-done((bf16[2,2816,128]{2,1,0:T(8,128)(2,1)}, bf16[2,2816,128]{2,1,0:T(8,128)(2,1)}, u32[]{:S(2)}, u32[]{:S(2)}) %collective-permute-start.9) | collective-permute-done | bytes 1441824 | tf_op jit(solution)/shard_map/ppermute | solution.py:126
  70.0 2.0 along1.1
  72.8 3.2 %collective-permute-done.7.refs_1_ = bf16[1408,128]{1,0:T(8,128)(2,1)S(1)} collective-permute-done((bf16[1408,128]{1,0:T(8,128)(2,1)S(1)}, bf16[1408,128]{1,0:T(8,128)(2,1)S(1)}, u32[]{:S(2)}, u32[]{:S(2)}) %collective-permute-start.7) | collective-permute-done | bytes 360480 | tf_op jit(solution)/shard_map/ppermute | solution.py:123
  77.1 2.0 collective-permute-start.12
  80.8 2.4 collective-permute-start.11
  83.1 17.6 %collective-permute-done.8.refs_0_.refs_1_.refs_6_.refs_7_.refs_2_ = bf16[2,2816,128]{2,1,0:T(8,128)(2,1)S(1)} collective-permute-done((bf16[2,2816,128]{2,1,0:T(8,128)(2,1)S(1)}, bf16[2,2816,128]{2,1,0:T(8,128)(2,1)S(1)}, u32[]{:S(2)}, u32[]{:S(2)}) %collective-permute-start.8) | collective-permute-done | bytes 1441824 | tf_op jit(solution)/shard_map/ppermute | solution.py:126
  101.7 8.3 %collective-permute-done.11.refs_1_ = bf16[1408,128]{1,0:T(8,128)(2,1)S(1)} collective-permute-done((bf16[1408,128]{1,0:T(8,128)(2,1)S(1)}, bf16[1408,128]{1,0:T(8,128)(2,1)S(1)}, u32[]{:S(2)}, u32[]{:S(2)}) %collective-permute-start.11) | collective-permute-done | bytes 360480 | tf_op jit(solution)/shard_map/ppermute | solution.py:123
  111.1 2.0 collective-permute-start.17
  116.8 14.8 %collective-permute-done.14.refs_0_.refs_1_.refs_6_.refs_7_.refs_2_ = bf16[2,2816,128]{2,1,0:T(8,128)(2,1)S(1)} collective-permute-done((bf16[2,2816,128]{2,1,0:T(8,128)(2,1)S(1)}, bf16[2,2816,128]{2,1,0:T(8,128)(2,1)S(1)}, u32[]{:S(2)}, u32[]{:S(2)}) %collective-permute-start.14) | collective-permute-done | bytes 1441824 | tf_op jit(solution)/shard_map/ppermute | solution.py:126
  132.6 6.5 %collective-permute-done.16.refs_1_ = bf16[1408,128]{1,0:T(8,128)(2,1)S(1)} collective-permute-done((bf16[1408,128]{1,0:T(8,128)(2,1)S(1)}, bf16[1408,128]{1,0:T(8,128)(2,1)S(1)}, u32[]{:S(2)}, u32[]{:S(2)}) %collective-permute-start.16) | collective-permute-done | bytes 360480 | tf_op jit(solution)/shard_map/ppermute | solution.py:123
  140.8 2.7 collective-permute-start.18
  145.4 2.5 collective-permute-start.21
  150.4 12.2 %collective-permute-done.18.refs_0_.refs_9_ = bf16[2,1408,128]{2,1,0:T(8,128)(2,1)S(1)} collective-permute-done((bf16[2,1408,128]{2,1,0:T(8,128)(2,1)S(1)}, bf16[2,1408,128]{2,1,0:T(8,128)(2,1)S(1)}, u32[]{:S(2)}, u32[]{:S(2)}) %collective-permute-start.18) | collective-permute-done | bytes 720928 | tf_op jit(solution)/shard_map/ppermute | solution.py:126
  163.1 5.0 %forward0.1 = (bf16[2816,512]{1,0:T(8,128)(2,1)S(1)}, bf16[2816,512]{1,0:T(8,128)(2,1)S(1)}, f32[2,128,1024]{2,1,0:T(8,128)S(1)}, f32[2,128,1024]{2,1,0:T(8,128)S(1)}, f32[8,128]{1,0:T(8,128)S(1)}) custom-call(s32[5]{0:T(128)S(1)} %stack.27.flags, bf16[512,2816]{1,0:T(8,128)(2,1)S(1)} %get-tuple-element.136.refs_0_, ...), custom_call_target="tpu_custom_call", output_to_operand_aliasing={{4}: (11, {})} | custom-call | tf_op jit(solution)/shard_map/forward0/pallas_call | solution.py:65
  171.1 6.0 %collective-permute-done.19.refs_0_.refs_5_ = bf16[2,1408,128]{2,1,0:T(8,128)(2,1)S(1)} collective-permute-done((bf16[2,1408,128]{2,1,0:T(8,128)(2,1)S(1)}, bf16[2,1408,128]{2,1,0:T(8,128)(2,1)S(1)}, u32[]{:S(2)}, u32[]{:S(2)}) %collective-permute-start.19) | collective-permute-done | bytes 720928 | tf_op jit(solution)/shard_map/ppermute | solution.py:126
  183.4 3.0 %forward1.1 = (bf16[2816,512]{1,0:T(8,128)(2,1)S(1)}, f32[2,128,512]{2,1,0:T(8,128)S(1)}, f32[128,512]{1,0:T(8,128)S(1)}, f32[128,512]{1,0:T(8,128)S(1)}, f32[8,128]{1,0:T(8,128)S(1)}) custom-call(s32[5]{0:T(128)S(1)} %stack.27.flags, bf16[512,2816]{1,0:T(8,128)(2,1)S(1)} %get-tuple-element.136.refs_0_, ...), custom_call_target="tpu_custom_call", output_to_operand_aliasing={{4}: (7, {})} | custom-call | tf_op jit(solution)/shard_map/forward1/pallas_call | solution.py:65
  191.5 2.4 forward2.1
  193.9 2.5 collective-permute-done.24.refs_1_
  199.0 2.8 collective-permute-start.27
  204.5 6.3 %collective-permute-done.32.refs_2_ = f32[136,512]{1,0:T(8,128)S(1)} collective-permute-done((f32[136,512]{1,0:T(8,128)S(1)}, f32[136,512]{1,0:T(8,128)S(1)}, u32[]{:S(2)}, u32[]{:S(2)}) %collective-permute-start.32) | collective-permute-done | bytes 278560 | tf_op jit(solution)/shard_map/ppermute | solution.py:120
  218.7 3.0 %collective-permute-done.4.refs_3_ = f32[8,2816]{1,0:T(8,128)S(1)} collective-permute-done((f32[8,2816]{1,0:T(8,128)S(1)}, f32[8,2816]{1,0:T(8,128)S(1)}, u32[]{:S(2)}, u32[]{:S(2)}) %collective-permute-start.4) | collective-permute-done | bytes 90144 | tf_op jit(solution)/shard_map/ppermute | solution.py:126
  222.8 2.2 collective-permute-done.35.refs_2_
  231.8 2.4 collective-permute-start.38
  236.5 3.2 %collective-permute-done.39.refs_3_.refs_7_ = f32[8,128]{1,0:T(8,128)S(1)} collective-permute-done((f32[8,128]{1,0:T(8,128)S(1)}, f32[8,128]{1,0:T(8,128)S(1)}, u32[]{:S(2)}, u32[]{:S(2)}) %collective-permute-start.39) | collective-permute-done | bytes 4128 | tf_op jit(solution)/shard_map/ppermute | solution.py:123
  241.7 2.4 collective-permute-start.47
  244.1 2.0 collective-permute-start.48
  246.2 2.4 collective-permute-done.46.refs_0_
  248.6 4.4 %collective-permute-done.47.refs_1_ = bf16[128,512]{1,0:T(8,128)(2,1)S(1)} collective-permute-done((bf16[128,512]{1,0:T(8,128)(2,1)S(1)}, bf16[128,512]{1,0:T(8,128)(2,1)S(1)}, u32[]{:S(2)}, u32[]{:S(2)}) %collective-permute-start.47) | collective-permute-done | bytes 131104 | tf_op jit(solution)/shard_map/ppermute | solution.py:123
  255.1 6.3 %collective-permute-done.50.refs_13_ = bf16[3,128,512]{2,1,0:T(8,128)(2,1)S(1)} collective-permute-done((bf16[3,128,512]{2,1,0:T(8,128)(2,1)S(1)}, bf16[3,128,512]{2,1,0:T(8,128)(2,1)S(1)}, u32[]{:S(2)}, u32[]{:S(2)}) %collective-permute-start.50) | collective-permute-done | bytes 393248 | tf_op jit(solution)/shard_map/ppermute | solution.py:120
  263.5 2.2 collective-permute-done.52.refs_16_
  265.7 8.9 %backward.1 = (f32[2816,512]{1,0:T(8,128)S(1)}, f32[8,512]{1,0:T(8,128)S(1)}, f32[8,128]{1,0:T(8,128)S(1)}) custom-call(s32[5]{0:T(128)S(1)} %stack.27.flags, bf16[2816,512]{1,0:T(8,128)(2,1)S(1)} %copy-done.2, f32[8,512]{1,0:T(8,128)S(1)} %get-tuple-element.134.refs_1_, ...), custom_call_target="tpu_custom_call", output_to_operand_aliasing={{2}: (18, {})} | custom-call | tf_op jit(solution)/shard_map/backward/pallas_call | solution.py:65
  277.3 2.2 collective-permute-done.54
  279.6 3.4 %collective-permute-start.55 = (f32[8,512]{1,0:T(8,128)S(1)}, f32[8,512]{1,0:T(8,128)S(1)}, u32[]{:S(2)}, u32[]{:S(2)}) collective-permute-start(f32[8,512]{1,0:T(8,128)S(1)} %add.32), channel_id=1, source_target_pairs={{0,1},{1,0},{2,3},{3,2},{4,5},{5,4},{6,7},{7,6},{8,9},{9,8},{10,11... | collective-permute-start | bytes 49160 | tf_op jit(solution)/shard_map/ppermute | solution.py:123
  283.3 2.2 collective-permute-start.57
  285.4 2.2 collective-permute-done.56
  288.8 3.8 %final.1 = (f32[2816,512]{1,0:T(8,128)}, f32[5]{0:T(128)}, f32[8,128]{1,0:T(8,128)S(1)}) custom-call(s32[5]{0:T(128)S(1)} %stack.27.flags, bf16[2816,512]{1,0:T(8,128)(2,1)S(1)} %copy-done.2, f32[8,512]{1,0:T(8,128)S(1)} %get-tuple-element.134.refs_1_, f32[2816,512]{1,0:T(8,128)S(1)} %get-tuple-element.243.refs_2_, ...), custom_call_target="tpu_custom_call", output_to_operand_aliasing={{2}: (5, {})} | custom-call | tf_op jit(solution)/shard_map/final/pallas_call | solution.py:65
  (149 shorter events, 75.3 us)
Async XLA Ops:
  3.4 35.7 %collective-permute-start.3 = (bf16[2,2816,128]{2,1,0:T(8,128)(2,1)}, bf16[2,2816,128]{2,1,0:T(8,128)(2,1)}, u32[]{:S(2)}, u32[]{:S(2)}) collective-permute-start(bf16[2,2816,128]{2,1,0:T(8,128)(2,1)} %slice.4), channel_id=1, source_target_pairs={{0,4},{4,0},{1,5},{5,1},{2,6},{6,2},{3,7},{7,3},{8,12},{12,8},{9,1... | collective-permute-start | bytes 4325384 | tf_op jit(solution)/shard_map/ppermute | solution.py:126
  12.4 57.5 %collective-permute-start.9 = (bf16[2,2816,128]{2,1,0:T(8,128)(2,1)}, bf16[2,2816,128]{2,1,0:T(8,128)(2,1)}, u32[]{:S(2)}, u32[]{:S(2)}) collective-permute-start(bf16[2,2816,128]{2,1,0:T(8,128)(2,1)} %get-tuple-element.141), channel_id=1, source_target_pairs={{0,4},{4,0},{1,5},{5,1},{2,6},{6,2},{3,7},{7,3},{8,12},{12,8},{9,1... | collective-permute-start | bytes 4325384 | tf_op jit(solution)/shard_map/ppermute | solution.py:126
  24.1 4.4 %collective-permute-start = (f32[8,512]{1,0:T(8,128)S(1)}, f32[8,512]{1,0:T(8,128)S(1)}, u32[]{:S(2)}, u32[]{:S(2)}) collective-permute-start(f32[8,512]{1,0:T(8,128)S(1)} %psum.7.refs_1_), channel_id=1, source_target_pairs={{0,1},{1,0},{2,3},{3,2},{4,5},{5,4},{6,7},{7,6},{8,9},{9,8},{10,11... | collective-permute-start | bytes 49160 | tf_op jit(solution)/shard_map/ppermute | solution.py:123
  25.7 4.7 %collective-permute-start.1 = (f32[8,512]{1,0:T(8,128)S(1)}, f32[8,512]{1,0:T(8,128)S(1)}, u32[]{:S(2)}, u32[]{:S(2)}) collective-permute-start(f32[8,512]{1,0:T(8,128)S(1)} %psum.7.refs_1_), channel_id=1, source_target_pairs={{0,2},{1,3},{2,0},{3,1},{4,6},{5,7},{6,4},{7,5},{8,10},{9,11},{10,... | collective-permute-start | bytes 49160 | tf_op jit(solution)/shard_map/ppermute | solution.py:123
  28.3 5.5 %collective-permute-start.2 = (f32[8,512]{1,0:T(8,128)S(1)}, f32[8,512]{1,0:T(8,128)S(1)}, u32[]{:S(2)}, u32[]{:S(2)}) collective-permute-start(f32[8,512]{1,0:T(8,128)S(1)} %psum.7.refs_1_), channel_id=1, source_target_pairs={{0,3},{1,2},{2,1},{3,0},{4,7},{5,6},{6,5},{7,4},{8,11},{9,10},{10,... | collective-permute-start | bytes 49160 | tf_op jit(solution)/shard_map/ppermute | solution.py:123
  42.0 34.0 %collective-permute-start.5 = (bf16[2,1408,128]{2,1,0:T(8,128)(2,1)S(1)}, bf16[2,1408,128]{2,1,0:T(8,128)(2,1)S(1)}, u32[]{:S(2)}, u32[]{:S(2)}) collective-permute-start(bf16[2,1408,128]{2,1,0:T(8,128)(2,1)S(1)} %get-tuple-element.137), channel_id=1, source_target_pairs={{0,1},{1,0},{2,3},{3,2},{4,5},{5,4},{6,7},{7,6},{8,9},{9,8},{10,11... | collective-permute-start | bytes 2162696 | tf_op jit(solution)/shard_map/ppermute | solution.py:123
  44.2 56.5 %collective-permute-start.8 = (bf16[2,2816,128]{2,1,0:T(8,128)(2,1)S(1)}, bf16[2,2816,128]{2,1,0:T(8,128)(2,1)S(1)}, u32[]{:S(2)}, u32[]{:S(2)}) collective-permute-start(bf16[2,2816,128]{2,1,0:T(8,128)(2,1)S(1)} %get-tuple-element.140), channel_id=1, source_target_pairs={{0,4},{4,0},{1,5},{5,1},{2,6},{6,2},{3,7},{7,3},{8,12},{12,8},{9,1... | collective-permute-start | bytes 4325384 | tf_op jit(solution)/shard_map/ppermute | solution.py:126
  45.7 27.1 %collective-permute-start.6 = (bf16[1408,128]{1,0:T(8,128)(2,1)S(1)}, bf16[1408,128]{1,0:T(8,128)(2,1)S(1)}, u32[]{:S(2)}, u32[]{:S(2)}) collective-permute-start(bf16[1408,128]{1,0:T(8,128)(2,1)S(1)} %get-tuple-element.138), channel_id=1, source_target_pairs={{0,2},{1,3},{2,0},{3,1},{4,6},{5,7},{6,4},{7,5},{8,10},{9,11},{10,... | collective-permute-start | bytes 1081352 | tf_op jit(solution)/shard_map/ppermute | solution.py:123
  48.3 27.7 %collective-permute-start.7 = (bf16[1408,128]{1,0:T(8,128)(2,1)S(1)}, bf16[1408,128]{1,0:T(8,128)(2,1)S(1)}, u32[]{:S(2)}, u32[]{:S(2)}) collective-permute-start(bf16[1408,128]{1,0:T(8,128)(2,1)S(1)} %get-tuple-element.139), channel_id=1, source_target_pairs={{0,3},{1,2},{2,1},{3,0},{4,7},{5,6},{6,5},{7,4},{8,11},{9,10},{10,... | collective-permute-start | bytes 1081352 | tf_op jit(solution)/shard_map/ppermute | solution.py:123
  77.1 32.8 %collective-permute-start.12 = (bf16[2,1408,128]{2,1,0:T(8,128)(2,1)S(1)}, bf16[2,1408,128]{2,1,0:T(8,128)(2,1)S(1)}, u32[]{:S(2)}, u32[]{:S(2)}) collective-permute-start(bf16[2,1408,128]{2,1,0:T(8,128)(2,1)S(1)} %get-tuple-element.155), channel_id=1, source_target_pairs={{0,1},{1,0},{2,3},{3,2},{4,5},{5,4},{6,7},{7,6},{8,9},{9,8},{10,11... | collective-permute-start | bytes 2162696 | tf_op jit(solution)/shard_map/ppermute | solution.py:123
  79.1 52.5 %collective-permute-start.14 = (bf16[2,2816,128]{2,1,0:T(8,128)(2,1)S(1)}, bf16[2,2816,128]{2,1,0:T(8,128)(2,1)S(1)}, u32[]{:S(2)}, u32[]{:S(2)}) collective-permute-start(bf16[2,2816,128]{2,1,0:T(8,128)(2,1)S(1)} %get-tuple-element.159), channel_id=1, source_target_pairs={{0,4},{4,0},{1,5},{5,1},{2,6},{6,2},{3,7},{7,3},{8,12},{12,8},{9,1... | collective-permute-start | bytes 4325384 | tf_op jit(solution)/shard_map/ppermute | solution.py:126
  79.6 22.0 %collective-permute-start.10 = (bf16[1408,128]{1,0:T(8,128)(2,1)S(1)}, bf16[1408,128]{1,0:T(8,128)(2,1)S(1)}, u32[]{:S(2)}, u32[]{:S(2)}) collective-permute-start(bf16[1408,128]{1,0:T(8,128)(2,1)S(1)} %get-tuple-element.153), channel_id=1, source_target_pairs={{0,2},{1,3},{2,0},{3,1},{4,6},{5,7},{6,4},{7,5},{8,10},{9,11},{10,... | collective-permute-start | bytes 1081352 | tf_op jit(solution)/shard_map/ppermute | solution.py:123
  80.8 29.2 %collective-permute-start.11 = (bf16[1408,128]{1,0:T(8,128)(2,1)S(1)}, bf16[1408,128]{1,0:T(8,128)(2,1)S(1)}, u32[]{:S(2)}, u32[]{:S(2)}) collective-permute-start(bf16[1408,128]{1,0:T(8,128)(2,1)S(1)} %get-tuple-element.154), channel_id=1, source_target_pairs={{0,3},{1,2},{2,1},{3,0},{4,7},{5,6},{6,5},{7,4},{8,11},{9,10},{10,... | collective-permute-start | bytes 1081352 | tf_op jit(solution)/shard_map/ppermute | solution.py:123
  111.1 28.0 %collective-permute-start.17 = (bf16[2,1408,128]{2,1,0:T(8,128)(2,1)S(1)}, bf16[2,1408,128]{2,1,0:T(8,128)(2,1)S(1)}, u32[]{:S(2)}, u32[]{:S(2)}) collective-permute-start(bf16[2,1408,128]{2,1,0:T(8,128)(2,1)S(1)} %get-tuple-element.166), channel_id=1, source_target_pairs={{0,1},{1,0},{2,3},{3,2},{4,5},{5,4},{6,7},{7,6},{8,9},{9,8},{10,11... | collective-permute-start | bytes 2162696 | tf_op jit(solution)/shard_map/ppermute | solution.py:123
  113.1 19.4 %collective-permute-start.15 = (bf16[1408,128]{1,0:T(8,128)(2,1)S(1)}, bf16[1408,128]{1,0:T(8,128)(2,1)S(1)}, u32[]{:S(2)}, u32[]{:S(2)}) collective-permute-start(bf16[1408,128]{1,0:T(8,128)(2,1)S(1)} %get-tuple-element.164), channel_id=1, source_target_pairs={{0,2},{1,3},{2,0},{3,1},{4,6},{5,7},{6,4},{7,5},{8,10},{9,11},{10,... | collective-permute-start | bytes 1081352 | tf_op jit(solution)/shard_map/ppermute | solution.py:123
  113.8 25.3 %collective-permute-start.16 = (bf16[1408,128]{1,0:T(8,128)(2,1)S(1)}, bf16[1408,128]{1,0:T(8,128)(2,1)S(1)}, u32[]{:S(2)}, u32[]{:S(2)}) collective-permute-start(bf16[1408,128]{1,0:T(8,128)(2,1)S(1)} %get-tuple-element.165), channel_id=1, source_target_pairs={{0,3},{1,2},{2,1},{3,0},{4,7},{5,6},{6,5},{7,4},{8,11},{9,10},{10,... | collective-permute-start | bytes 1081352 | tf_op jit(solution)/shard_map/ppermute | solution.py:123
  116.2 31.7 %collective-permute-start.13 = (bf16[2,1408,128]{2,1,0:T(8,128)(2,1)S(1)}, bf16[2,1408,128]{2,1,0:T(8,128)(2,1)S(1)}, u32[]{:S(2)}, u32[]{:S(2)}) collective-permute-start(bf16[2,1408,128]{2,1,0:T(8,128)(2,1)S(1)} %get-tuple-element.158.refs_4_), channel_id=1, source_target_pairs={{0,4},{4,0},{1,5},{5,1},{2,6},{6,2},{3,7},{7,3},{8,12},{12,8},{9,1... | collective-permute-start | bytes 2162696 | tf_op jit(solution)/shard_map/ppermute | solution.py:126
  140.8 21.8 %collective-permute-start.18 = (bf16[2,1408,128]{2,1,0:T(8,128)(2,1)S(1)}, bf16[2,1408,128]{2,1,0:T(8,128)(2,1)S(1)}, u32[]{:S(2)}, u32[]{:S(2)}) collective-permute-start(bf16[2,1408,128]{2,1,0:T(8,128)(2,1)S(1)} %get-tuple-element.169.refs_8_), channel_id=1, source_target_pairs={{0,4},{4,0},{1,5},{5,1},{2,6},{6,2},{3,7},{7,3},{8,12},{12,8},{9,1... | collective-permute-start | bytes 2162696 | tf_op jit(solution)/shard_map/ppermute | solution.py:126
  143.5 26.5 %collective-permute-start.22 = (bf16[2,1408,128]{2,1,0:T(8,128)(2,1)S(1)}, bf16[2,1408,128]{2,1,0:T(8,128)(2,1)S(1)}, u32[]{:S(2)}, u32[]{:S(2)}) collective-permute-start(bf16[2,1408,128]{2,1,0:T(8,128)(2,1)S(1)} %get-tuple-element.177), channel_id=1, source_target_pairs={{0,1},{1,0},{2,3},{3,2},{4,5},{5,4},{6,7},{7,6},{8,9},{9,8},{10,11... | collective-permute-start | bytes 2162696 | tf_op jit(solution)/shard_map/ppermute | solution.py:123
  144.1 23.9 %collective-permute-start.20 = (bf16[1408,128]{1,0:T(8,128)(2,1)S(1)}, bf16[1408,128]{1,0:T(8,128)(2,1)S(1)}, u32[]{:S(2)}, u32[]{:S(2)}) collective-permute-start(bf16[1408,128]{1,0:T(8,128)(2,1)S(1)} %get-tuple-element.175), channel_id=1, source_target_pairs={{0,2},{1,3},{2,0},{3,1},{4,6},{5,7},{6,4},{7,5},{8,10},{9,11},{10,... | collective-permute-start | bytes 1081352 | tf_op jit(solution)/shard_map/ppermute | solution.py:123
  145.4 24.6 %collective-permute-start.21 = (bf16[1408,128]{1,0:T(8,128)(2,1)S(1)}, bf16[1408,128]{1,0:T(8,128)(2,1)S(1)}, u32[]{:S(2)}, u32[]{:S(2)}) collective-permute-start(bf16[1408,128]{1,0:T(8,128)(2,1)S(1)} %get-tuple-element.176), channel_id=1, source_target_pairs={{0,3},{1,2},{2,1},{3,0},{4,7},{5,6},{6,5},{7,4},{8,11},{9,10},{10,... | collective-permute-start | bytes 1081352 | tf_op jit(solution)/shard_map/ppermute | solution.py:123
  149.0 28.1 %collective-permute-start.19 = (bf16[2,1408,128]{2,1,0:T(8,128)(2,1)S(1)}, bf16[2,1408,128]{2,1,0:T(8,128)(2,1)S(1)}, u32[]{:S(2)}, u32[]{:S(2)}) collective-permute-start(bf16[2,1408,128]{2,1,0:T(8,128)(2,1)S(1)} %get-tuple-element.174.refs_4_), channel_id=1, source_target_pairs={{0,4},{4,0},{1,5},{5,1},{2,6},{6,2},{3,7},{7,3},{8,12},{12,8},{9,1... | collective-permute-start | bytes 2162696 | tf_op jit(solution)/shard_map/ppermute | solution.py:126
  178.3 18.7 %collective-permute-start.29 = (bf16[2,1408,128]{2,1,0:T(8,128)(2,1)S(1)}, bf16[2,1408,128]{2,1,0:T(8,128)(2,1)S(1)}, u32[]{:S(2)}, u32[]{:S(2)}) collective-permute-start(bf16[2,1408,128]{2,1,0:T(8,128)(2,1)S(1)} %get-tuple-element.184.refs_4_), channel_id=1, source_target_pairs={{0,4},{4,0},{1,5},{5,1},{2,6},{6,2},{3,7},{7,3},{8,12},{12,8},{9,1... | collective-permute-start | bytes 2162696 | tf_op jit(solution)/shard_map/ppermute | solution.py:126
  181.6 14.8 %collective-permute-start.24 = (f32[128,1024]{1,0:T(8,128)S(1)}, f32[128,1024]{1,0:T(8,128)S(1)}, u32[]{:S(2)}, u32[]{:S(2)}) collective-permute-start(f32[128,1024]{1,0:T(8,128)S(1)} %get-tuple-element.183), channel_id=1, source_target_pairs={{0,16},{8,24},{16,0},{24,8},{1,17},{9,25},{17,1},{25,9},{2,18},{10... | collective-permute-start | bytes 1572872 | tf_op jit(solution)/shard_map/ppermute | solution.py:120
  191.1 12.8 %collective-permute-start.28 = (f32[136,512]{1,0:T(8,128)S(1)}, f32[136,512]{1,0:T(8,128)S(1)}, u32[]{:S(2)}, u32[]{:S(2)}) collective-permute-start(f32[136,512]{1,0:T(8,128)S(1)} %get-tuple-element.199), channel_id=1, source_target_pairs={{0,16},{8,24},{16,0},{24,8},{1,17},{9,25},{17,1},{25,9},{2,18},{10... | collective-permute-start | bytes 835592 | tf_op jit(solution)/shard_map/ppermute | solution.py:120
  199.0 16.9 %collective-permute-start.27 = (f32[2,136,256]{2,1,0:T(8,128)S(1)}, f32[2,136,256]{2,1,0:T(8,128)S(1)}, u32[]{:S(2)}, u32[]{:S(2)}) collective-permute-start(f32[2,136,256]{2,1,0:T(8,128)S(1)} %get-tuple-element.197), channel_id=1, source_target_pairs={{0,2},{1,3},{2,0},{3,1},{4,6},{5,7},{6,4},{7,5},{8,10},{9,11},{10,... | collective-permute-start | bytes 835592 | tf_op jit(solution)/shard_map/ppermute | solution.py:123
  202.4 8.4 %collective-permute-start.32 = (f32[136,512]{1,0:T(8,128)S(1)}, f32[136,512]{1,0:T(8,128)S(1)}, u32[]{:S(2)}, u32[]{:S(2)}) collective-permute-start(f32[136,512]{1,0:T(8,128)S(1)} %get-tuple-element.212), channel_id=1, source_target_pairs={{0,16},{8,24},{16,0},{24,8},{1,17},{9,25},{17,1},{25,9},{2,18},{10... | collective-permute-start | bytes 835592 | tf_op jit(solution)/shard_map/ppermute | solution.py:120
  211.4 11.4 %collective-permute-start.34 = (f32[128,256]{1,0:T(8,128)S(1)}, f32[128,256]{1,0:T(8,128)S(1)}, u32[]{:S(2)}, u32[]{:S(2)}) collective-permute-start(f32[128,256]{1,0:T(8,128)S(1)} %get-tuple-element.227), channel_id=1, source_target_pairs={{0,1},{1,0},{2,3},{3,2},{4,5},{5,4},{6,7},{7,6},{8,9},{9,8},{10,11... | collective-permute-start | bytes 393224 | tf_op jit(solution)/shard_map/ppermute | solution.py:123
  213.1 12.0 %collective-permute-start.35 = (f32[128,256]{1,0:T(8,128)S(1)}, f32[128,256]{1,0:T(8,128)S(1)}, u32[]{:S(2)}, u32[]{:S(2)}) collective-permute-start(f32[128,256]{1,0:T(8,128)S(1)} %get-tuple-element.228), channel_id=1, source_target_pairs={{0,2},{1,3},{2,0},{3,1},{4,6},{5,7},{6,4},{7,5},{8,10},{9,11},{10,... | collective-permute-start | bytes 393224 | tf_op jit(solution)/shard_map/ppermute | solution.py:123
  214.8 10.2 %collective-permute-start.36 = (f32[128,256]{1,0:T(8,128)S(1)}, f32[128,256]{1,0:T(8,128)S(1)}, u32[]{:S(2)}, u32[]{:S(2)}) collective-permute-start(f32[128,256]{1,0:T(8,128)S(1)} %get-tuple-element.229), channel_id=1, source_target_pairs={{0,3},{1,2},{2,1},{3,0},{4,7},{5,6},{6,5},{7,4},{8,11},{9,10},{10,... | collective-permute-start | bytes 393224 | tf_op jit(solution)/shard_map/ppermute | solution.py:123
  216.4 9.4 %collective-permute-start.33 = (f32[128,256]{1,0:T(8,128)S(1)}, f32[128,256]{1,0:T(8,128)S(1)}, u32[]{:S(2)}, u32[]{:S(2)}) collective-permute-start(f32[128,256]{1,0:T(8,128)S(1)} %get-tuple-element.225), channel_id=1, source_target_pairs={{0,1},{1,0},{2,3},{3,2},{4,5},{5,4},{6,7},{7,6},{8,9},{9,8},{10,11... | collective-permute-start | bytes 393224 | tf_op jit(solution)/shard_map/ppermute | solution.py:123
  217.2 4.5 %collective-permute-start.4 = (f32[8,2816]{1,0:T(8,128)S(1)}, f32[8,2816]{1,0:T(8,128)S(1)}, u32[]{:S(2)}, u32[]{:S(2)}) collective-permute-start(f32[8,2816]{1,0:T(8,128)S(1)} %get-tuple-element.135.refs_2_), channel_id=1, source_target_pairs={{0,4},{4,0},{1,5},{5,1},{2,6},{6,2},{3,7},{7,3},{8,12},{12,8},{9,1... | collective-permute-start | bytes 270344 | tf_op jit(solution)/shard_map/ppermute | solution.py:126
  228.6 6.2 %collective-permute-start.41 = (f32[16,512]{1,0:T(8,128)S(1)}, f32[16,512]{1,0:T(8,128)S(1)}, u32[]{:S(2)}, u32[]{:S(2)}) collective-permute-start(f32[16,512]{1,0:T(8,128)S(1)} %add.29), channel_id=1, source_target_pairs={{0,16},{8,24},{16,0},{24,8},{1,17},{9,25},{17,1},{25,9},{2,18},{10... | collective-permute-start | bytes 98312 | tf_op jit(solution)/shard_map/ppermute | solution.py:120
  230.2 6.3 %collective-permute-start.37 = (f32[8,128]{1,0:T(8,128)S(1)}, f32[8,128]{1,0:T(8,128)S(1)}, u32[]{:S(2)}, u32[]{:S(2)}) collective-permute-start(f32[8,128]{1,0:T(8,128)S(1)} %get-tuple-element.235.refs_0_.refs_4_), channel_id=1, source_target_pairs={{0,1},{1,0},{2,3},{3,2},{4,5},{5,4},{6,7},{7,6},{8,9},{9,8},{10,11... | collective-permute-start | bytes 12296 | tf_op jit(solution)/shard_map/ppermute | solution.py:123
  231.8 4.6 %collective-permute-start.38 = (f32[8,128]{1,0:T(8,128)S(1)}, f32[8,128]{1,0:T(8,128)S(1)}, u32[]{:S(2)}, u32[]{:S(2)}) collective-permute-start(f32[8,128]{1,0:T(8,128)S(1)} %get-tuple-element.235.refs_0_.refs_4_), channel_id=1, source_target_pairs={{0,2},{1,3},{2,0},{3,1},{4,6},{5,7},{6,4},{7,5},{8,10},{9,11},{10,... | collective-permute-start | bytes 12296 | tf_op jit(solution)/shard_map/ppermute | solution.py:123
  234.2 5.4 %collective-permute-start.39 = (f32[8,128]{1,0:T(8,128)S(1)}, f32[8,128]{1,0:T(8,128)S(1)}, u32[]{:S(2)}, u32[]{:S(2)}) collective-permute-start(f32[8,128]{1,0:T(8,128)S(1)} %get-tuple-element.235.refs_0_.refs_4_), channel_id=1, source_target_pairs={{0,3},{1,2},{2,1},{3,0},{4,7},{5,6},{6,5},{7,4},{8,11},{9,10},{10,... | collective-permute-start | bytes 12296 | tf_op jit(solution)/shard_map/ppermute | solution.py:123
  234.9 5.3 %collective-permute-start.42 = (f32[16,512]{1,0:T(8,128)S(1)}, f32[16,512]{1,0:T(8,128)S(1)}, u32[]{:S(2)}, u32[]{:S(2)}) collective-permute-start(f32[16,512]{1,0:T(8,128)S(1)} %add.30.refs_8_), channel_id=1, source_target_pairs={{0,4},{4,0},{1,5},{5,1},{2,6},{6,2},{3,7},{7,3},{8,12},{12,8},{9,1... | collective-permute-start | bytes 98312 | tf_op jit(solution)/shard_map/ppermute | solution.py:126
  241.1 5.0 %collective-permute-start.44 = (bf16[128,512]{1,0:T(8,128)(2,1)S(1)}, bf16[128,512]{1,0:T(8,128)(2,1)S(1)}, u32[]{:S(2)}, u32[]{:S(2)}) collective-permute-start(bf16[128,512]{1,0:T(8,128)(2,1)S(1)} %get-tuple-element.238.refs_7_), channel_id=1, source_target_pairs={{0,16},{8,24},{16,0},{24,8},{1,17},{9,25},{17,1},{25,9},{2,18},{10... | collective-permute-start | bytes 393224 | tf_op jit(solution)/shard_map/ppermute | solution.py:120
  241.7 6.9 %collective-permute-start.46 = (bf16[128,512]{1,0:T(8,128)(2,1)S(1)}, bf16[128,512]{1,0:T(8,128)(2,1)S(1)}, u32[]{:S(2)}, u32[]{:S(2)}) collective-permute-start(bf16[128,512]{1,0:T(8,128)(2,1)S(1)} %get-tuple-element.238.refs_7_), channel_id=1, source_target_pairs={{0,1},{1,0},{2,3},{3,2},{4,5},{5,4},{6,7},{7,6},{8,9},{9,8},{10,11... | collective-permute-start | bytes 393224 | tf_op jit(solution)/shard_map/ppermute | solution.py:123
  241.7 11.3 %collective-permute-start.47 = (bf16[128,512]{1,0:T(8,128)(2,1)S(1)}, bf16[128,512]{1,0:T(8,128)(2,1)S(1)}, u32[]{:S(2)}, u32[]{:S(2)}) collective-permute-start(bf16[128,512]{1,0:T(8,128)(2,1)S(1)} %get-tuple-element.238.refs_7_), channel_id=1, source_target_pairs={{0,2},{1,3},{2,0},{3,1},{4,6},{5,7},{6,4},{7,5},{8,10},{9,11},{10,... | collective-permute-start | bytes 393224 | tf_op jit(solution)/shard_map/ppermute | solution.py:123
  244.1 8.9 %collective-permute-start.48 = (bf16[128,512]{1,0:T(8,128)(2,1)S(1)}, bf16[128,512]{1,0:T(8,128)(2,1)S(1)}, u32[]{:S(2)}, u32[]{:S(2)}) collective-permute-start(bf16[128,512]{1,0:T(8,128)(2,1)S(1)} %get-tuple-element.238.refs_7_), channel_id=1, source_target_pairs={{0,3},{1,2},{2,1},{3,0},{4,7},{5,6},{6,5},{7,4},{8,11},{9,10},{10,... | collective-permute-start | bytes 393224 | tf_op jit(solution)/shard_map/ppermute | solution.py:123
  253.6 7.8 %collective-permute-start.50 = (bf16[3,128,512]{2,1,0:T(8,128)(2,1)S(1)}, bf16[3,128,512]{2,1,0:T(8,128)(2,1)S(1)}, u32[]{:S(2)}, u32[]{:S(2)}) collective-permute-start(bf16[3,128,512]{2,1,0:T(8,128)(2,1)S(1)} %get-tuple-element.240.refs_11_), channel_id=1, source_target_pairs={{0,16},{8,24},{16,0},{24,8},{1,17},{9,25},{17,1},{25,9},{2,18},{10... | collective-permute-start | bytes 1179656 | tf_op jit(solution)/shard_map/ppermute | solution.py:120
  255.1 10.5 %collective-permute-start.49 = (bf16[3,128,512]{2,1,0:T(8,128)(2,1)S(1)}, bf16[3,128,512]{2,1,0:T(8,128)(2,1)S(1)}, u32[]{:S(2)}, u32[]{:S(2)}) collective-permute-start(bf16[3,128,512]{2,1,0:T(8,128)(2,1)S(1)} %get-tuple-element.240.refs_11_), channel_id=1, source_target_pairs={{0,8},{8,0},{16,24},{24,16},{1,9},{9,1},{17,25},{25,17},{2,10},{10... | collective-permute-start | bytes 1179656 | tf_op jit(solution)/shard_map/ppermute | solution.py:117
  261.4 4.3 %collective-permute-start.51 = (bf16[3,128,512]{2,1,0:T(8,128)(2,1)S(1)}, bf16[3,128,512]{2,1,0:T(8,128)(2,1)S(1)}, u32[]{:S(2)}, u32[]{:S(2)}) collective-permute-start(bf16[3,128,512]{2,1,0:T(8,128)(2,1)S(1)} %collective-permute-done.50.refs_13_), channel_id=1, source_target_pairs={{0,8},{8,0},{16,24},{24,16},{1,9},{9,1},{17,25},{25,17},{2,10},{10... | collective-permute-start | bytes 1179656 | tf_op jit(solution)/shard_map/ppermute | solution.py:117
  261.4 4.3 %collective-permute-start.43 = (bf16[128,512]{1,0:T(8,128)(2,1)S(1)}, bf16[128,512]{1,0:T(8,128)(2,1)S(1)}, u32[]{:S(2)}, u32[]{:S(2)}) collective-permute-start(bf16[128,512]{1,0:T(8,128)(2,1)S(1)} %get-tuple-element.238.refs_7_), channel_id=1, source_target_pairs={{0,8},{8,0},{16,24},{24,16},{1,9},{9,1},{17,25},{25,17},{2,10},{10... | collective-permute-start | bytes 393224 | tf_op jit(solution)/shard_map/ppermute | solution.py:117
  279.6 5.8 %collective-permute-start.55 = (f32[8,512]{1,0:T(8,128)S(1)}, f32[8,512]{1,0:T(8,128)S(1)}, u32[]{:S(2)}, u32[]{:S(2)}) collective-permute-start(f32[8,512]{1,0:T(8,128)S(1)} %add.32), channel_id=1, source_target_pairs={{0,1},{1,0},{2,3},{3,2},{4,5},{5,4},{6,7},{7,6},{8,9},{9,8},{10,11... | collective-permute-start | bytes 49160 | tf_op jit(solution)/shard_map/ppermute | solution.py:123
  283.0 4.6 %collective-permute-start.56 = (f32[8,512]{1,0:T(8,128)S(1)}, f32[8,512]{1,0:T(8,128)S(1)}, u32[]{:S(2)}, u32[]{:S(2)}) collective-permute-start(f32[8,512]{1,0:T(8,128)S(1)} %add.32), channel_id=1, source_target_pairs={{0,2},{1,3},{2,0},{3,1},{4,6},{5,7},{6,4},{7,5},{8,10},{9,11},{10,... | collective-permute-start | bytes 49160 | tf_op jit(solution)/shard_map/ppermute | solution.py:123
  283.3 5.5 %collective-permute-start.57 = (f32[8,512]{1,0:T(8,128)S(1)}, f32[8,512]{1,0:T(8,128)S(1)}, u32[]{:S(2)}, u32[]{:S(2)}) collective-permute-start(f32[8,512]{1,0:T(8,128)S(1)} %add.32), channel_id=1, source_target_pairs={{0,3},{1,2},{2,1},{3,0},{4,7},{5,6},{6,5},{7,4},{8,11},{9,10},{10,... | collective-permute-start | bytes 49160 | tf_op jit(solution)/shard_map/ppermute | solution.py:123
  (21 other events, 178.0 us)

commit v6 on v5

--- a/solution.py
+++ b/solution.py
@@ -13,7 +13,7 @@
 BF = jnp.bfloat16
 F32 = jnp.float32
 VMEM_BYTES = 20 * 1024 * 1024
-COSTS = {"spots": 1, "back3": 6, "addx1": 9, "half0": 3}
+COSTS = {"spots": 1, "back3": 1, "waits2": 3, "addx1": 9, "half0": 3}
 WIDTHS = (128, 128, 128, 128)
 GROUPS = ((0, 1), (2,), (3,))
 SUMS = ((0,), (1, 2))
@@ -24,8 +24,8 @@
     "a1 A2 w:f21+f31+n1 a2",
     "S0 A3 w:f22+f32+n2 a3",
     "S1 w:s0 S2 w:s1",
-    "F0 w:f23+f33+n3 S3 w:s2",
-    "f0 P0 F1 f1",
+    "F0 w:f23+f33+n3 S3 f0",
+    "P0 w:s2 F1 f1",
     "P1 F2 Q0 G2",
     "P2 X1 Q1 U0",
     "m0 R1 R0",
@@ -200,7 +200,7 @@
         sent[f"s{c}"] = over_spot(st["f", c])
 
     def wait_for(name):
-        run("wait", None, after=[sent[n] for n in name.split("+")])
+        run("wait" + name.split("+")[0], None, after=[sent[n] for n in name.split("+")])
 
     def members_of(_):
         def body(fl, i, out):
@@ -288,9 +288,7 @@
 
     def halves_of(g):
         shape = (quarter, slots * group_width[g])
-        if len(GROUPS[g]) == 1:
-            return [(sds(shape, F32), whole(shape))] * 2
-        return [(sds((2, *shape), F32), whole((2, *shape)))]
+        return [(sds(shape, F32), whole(shape))] * 2
 
     def forward(g):
         members, wide_all = GROUPS[g], group_width[g] * slots
@@ -303,7 +301,7 @@
 
         def product(pt, efs, keep, *send, direct=None):
             done = 0
-            low, high = send if len(send) == 2 else (send[0].at[0], send[0].at[1])
+            low, high = send
             for c, ef in zip(members, efs):
                 w = WIDTHS[c]
                 if c == late:
@@ -413,12 +411,12 @@
 
         def body(fl, i, out):
             for n in (0, 1):
-                out[n][0:quarter, :] = i[0][n] + (i[1 + n][...] if single else i[1][n])
+                out[n][0:quarter, :] = i[0][n] + i[1 + n][...]
             if single:
                 out[1][quarter:, :] = jnp.zeros((PAD, wide), F32)
 
         ins = [(st["r", g], whole(shape))]
-        ins += [(sent[f"rc{n}{g}"], whole(one)) for n in (0, 1)] if single else [(sent[f"rc0{g}"], whole(shape))]
+        ins += [(sent[f"rc{n}{g}"], whole(one)) for n in (0, 1)]
         more = (quarter + PAD, wide) if single else one
         st["r", g], b = run(f"core{g}", body, ins, [(sds(one, F32), whole(one)), (sds(more, F32), whole(more))])
         sent[f"rx{g}"] = over_x(b)

time: 293 us -> 288 us (0.983)
  waiting for transfers between devices: 137 us -> 131 us
    ppermute x11, waiting for transfers between devices: 73.9 us -> 70.4 us  [over_spot(): return lax.ppermute(v, 'spot', xor_pairs(spot_size, step))]
  transfers between devices with their start and end apart: 58 -> 59, of which waited for: 30 -> 30; matrix products, arithmetic and copies ran while one was open for 0% -> 0% of each run, Pallas kernels for 15% -> 15%
where the time goes in v6:
time: 288 us
  waiting for transfers between devices  131 us (45%)
  starting transfers between devices  75.2 us (26%)
  Pallas kernels  59.4 us (21%)
  blocking collectives  11.6 us (4%)
  local copies, waits for them, and re-layouts  9.67 us (3%)
    ppermute x11, waiting for transfers between devices, over_spot(): return lax.ppermute(v, 'spot', xor_pairs(spot_size, step))  70.4 us
    pallas_call x48, Pallas kernels, run(): pl.pallas_call(kernel, out_shape=[s for s, _ in outs] + [sds(a.shape, a.d...  59.4 us
    ppermute x29, starting transfers between devices, over_gene(): return lax.ppermute(v, 'gene', xor_pairs(4, step))  46.6 us
    ppermute x29, waiting for transfers between devices, over_gene(): return lax.ppermute(v, 'gene', xor_pairs(4, step))  41.2 us
    ppermute x11, starting transfers between devices, over_spot(): return lax.ppermute(v, 'spot', xor_pairs(spot_size, step))  15.8 us
    ppermute x7, waiting for transfers between devices, over_x(): return lax.ppermute(v, 'cell', xor_pairs(4, 2))  14.9 us
    psum x1, blocking collectives, totals(): st['tot'] = lax.psum(v, 'cell')  11.6 us
    ppermute x7, starting transfers between devices, over_x(): return lax.ppermute(v, 'cell', xor_pairs(4, 2))  10.4 us
  transfers between devices with their start and end apart: 59, of which 30 were waited for; matrix products, arithmetic and copies ran while one was open for 0% of the time, Pallas kernels for 15%

profile of v6, /device:TPU:0, one launch (start us, length us, event | category | flops | bytes accessed | tf_op | source)
XLA Modules:
  0.0 288.1 jit_solution(7402828979071984696)
XLA Ops:
  0.6 2.7 slice.4
  3.4 3.0 %collective-permute-start.3 = (bf16[2,2816,128]{2,1,0:T(8,128)(2,1)}, bf16[2,2816,128]{2,1,0:T(8,128)(2,1)}, u32[]{:S(2)}, u32[]{:S(2)}) collective-permute-start(bf16[2,2816,128]{2,1,0:T(8,128)(2,1)} %slice.4), channel_id=1, source_target_pairs={{0,4},{4,0},{1,5},{5,1},{2,6},{6,2},{3,7},{7,3},{8,12},{12,8},{9,1... | collective-permute-start | bytes 4325384 | tf_op jit(solution)/shard_map/ppermute | solution.py:126
  7.8 2.6 copy-done
  10.4 2.0 swap1.1
  12.5 11.6 %psum.7.refs_1_ = f32[8,512]{1,0:T(8,128)S(1)} all-reduce(f32[8,512]{1,0:T(8,128)S(1)} %get-tuple-element.127), channel_id=1, replica_groups=mesh['cell'=4,'spot'=2,'gene'=4] {'cell'}, use_global_device_ids=true, to_apply=%region_0.1 | all-reduce | flops 4096 | bytes 32768 | tf_op jit(solution)/shard_map/psum | solution.py:226
  25.7 2.6 collective-permute-start.1
  30.4 3.4 %collective-permute-done.2.refs_2_.refs_4_ = f32[8,512]{1,0:T(8,128)S(1)} collective-permute-done((f32[8,512]{1,0:T(8,128)S(1)}, f32[8,512]{1,0:T(8,128)S(1)}, u32[]{:S(2)}, u32[]{:S(2)}) %collective-permute-start.2) | collective-permute-done | bytes 16416 | tf_op jit(solution)/shard_map/ppermute | solution.py:123
  34.4 2.6 copy-done.1
  39.1 2.4 along0.1
  42.0 2.2 collective-permute-start.5
  45.7 2.6 collective-permute-start.6
  48.5 4.0 %prob.1 = (bf16[512,2816]{1,0:T(8,128)(2,1)S(1)}, f32[8,2816]{1,0:T(8,128)S(1)}, f32[8,512]{1,0:T(8,128)S(1)}, f32[8,512]{1,0:T(8,128)S(1)}, f32[8,128]{1,0:T(8,128)S(1)}) custom-call(s32[5]{0:T(128)S(1)} %stack.27.flags, bf16[2816,512]{1,0:T(8,128)(2,1)S(1)} %copy-done.2, f32[8,512]{1,0:T(8,128)S(1)} %psum.7.refs_1_, ...), custom_call_target="tpu_custom_call", output_to_operand_aliasing={{4}: (6, {})} | custom-call | tf_op jit(solution)/shard_map/prob/pallas_call | solution.py:65
  53.2 16.7 %collective-permute-done.9.refs_0_.refs_1_.refs_6_.refs_7_ = bf16[2,2816,128]{2,1,0:T(8,128)(2,1)} collective-permute-done((bf16[2,2816,128]{2,1,0:T(8,128)(2,1)}, bf16[2,2816,128]{2,1,0:T(8,128)(2,1)}, u32[]{:S(2)}, u32[]{:S(2)}) %collective-permute-start.9) | collective-permute-done | bytes 1441824 | tf_op jit(solution)/shard_map/ppermute | solution.py:126
  70.0 2.0 along1.1
  72.8 3.2 %collective-permute-done.7.refs_1_ = bf16[1408,128]{1,0:T(8,128)(2,1)S(1)} collective-permute-done((bf16[1408,128]{1,0:T(8,128)(2,1)S(1)}, bf16[1408,128]{1,0:T(8,128)(2,1)S(1)}, u32[]{:S(2)}, u32[]{:S(2)}) %collective-permute-start.7) | collective-permute-done | bytes 360480 | tf_op jit(solution)/shard_map/ppermute | solution.py:123
  77.1 2.0 collective-permute-start.12
  80.8 2.4 collective-permute-start.11
  83.1 17.6 %collective-permute-done.8.refs_0_.refs_1_.refs_6_.refs_7_.refs_2_ = bf16[2,2816,128]{2,1,0:T(8,128)(2,1)S(1)} collective-permute-done((bf16[2,2816,128]{2,1,0:T(8,128)(2,1)S(1)}, bf16[2,2816,128]{2,1,0:T(8,128)(2,1)S(1)}, u32[]{:S(2)}, u32[]{:S(2)}) %collective-permute-start.8) | collective-permute-done | bytes 1441824 | tf_op jit(solution)/shard_map/ppermute | solution.py:126
  101.7 8.3 %collective-permute-done.11.refs_1_ = bf16[1408,128]{1,0:T(8,128)(2,1)S(1)} collective-permute-done((bf16[1408,128]{1,0:T(8,128)(2,1)S(1)}, bf16[1408,128]{1,0:T(8,128)(2,1)S(1)}, u32[]{:S(2)}, u32[]{:S(2)}) %collective-permute-start.11) | collective-permute-done | bytes 360480 | tf_op jit(solution)/shard_map/ppermute | solution.py:123
  111.1 2.0 collective-permute-start.17
  116.8 14.8 %collective-permute-done.14.refs_0_.refs_1_.refs_6_.refs_7_.refs_2_ = bf16[2,2816,128]{2,1,0:T(8,128)(2,1)S(1)} collective-permute-done((bf16[2,2816,128]{2,1,0:T(8,128)(2,1)S(1)}, bf16[2,2816,128]{2,1,0:T(8,128)(2,1)S(1)}, u32[]{:S(2)}, u32[]{:S(2)}) %collective-permute-start.14) | collective-permute-done | bytes 1441824 | tf_op jit(solution)/shard_map/ppermute | solution.py:126
  132.6 6.5 %collective-permute-done.16.refs_1_ = bf16[1408,128]{1,0:T(8,128)(2,1)S(1)} collective-permute-done((bf16[1408,128]{1,0:T(8,128)(2,1)S(1)}, bf16[1408,128]{1,0:T(8,128)(2,1)S(1)}, u32[]{:S(2)}, u32[]{:S(2)}) %collective-permute-start.16) | collective-permute-done | bytes 360480 | tf_op jit(solution)/shard_map/ppermute | solution.py:123
  140.8 2.7 collective-permute-start.18
  145.4 2.5 collective-permute-start.20
  150.4 12.2 %collective-permute-done.18.refs_0_.refs_9_ = bf16[2,1408,128]{2,1,0:T(8,128)(2,1)S(1)} collective-permute-done((bf16[2,1408,128]{2,1,0:T(8,128)(2,1)S(1)}, bf16[2,1408,128]{2,1,0:T(8,128)(2,1)S(1)}, u32[]{:S(2)}, u32[]{:S(2)}) %collective-permute-start.18) | collective-permute-done | bytes 720928 | tf_op jit(solution)/shard_map/ppermute | solution.py:126
  163.1 5.0 %forward0.1 = (bf16[2816,512]{1,0:T(8,128)(2,1)S(1)}, bf16[2816,512]{1,0:T(8,128)(2,1)S(1)}, f32[2,128,1024]{2,1,0:T(8,128)S(1)}, f32[128,1024]{1,0:T(8,128)S(1)...) custom-call(s32[5]{0:T(128)S(1)} %stack.27.flags, ...), custom_call_target="tpu_custom_call", output_to_operand_aliasing={{5}: (11, {})} | custom-call | tf_op jit(solution)/shard_map/forward0/pallas_call | solution.py:65
  168.1 1.9 collective-permute-done.20.refs_1_
  178.5 3.0 %forward1.1 = (bf16[2816,512]{1,0:T(8,128)(2,1)S(1)}, f32[2,128,512]{2,1,0:T(8,128)S(1)}, f32[128,512]{1,0:T(8,128)S(1)}, f32[128,512]{1,0:T(8,128)S(1)}, f32[8,128]{1,0:T(8,128)S(1)}) custom-call(s32[5]{0:T(128)S(1)} %stack.27.flags, bf16[512,2816]{1,0:T(8,128)(2,1)S(1)} %get-tuple-element.138.refs_0_, ...), custom_call_target="tpu_custom_call", output_to_operand_aliasing={{4}: (7, {})} | custom-call | tf_op jit(solution)/shard_map/forward1/pallas_call | solution.py:65
  186.3 2.1 collective-permute-start.29
  188.4 2.4 forward2.1
  194.5 2.8 collective-permute-start.28
  200.0 6.3 %collective-permute-done.33.refs_2_ = f32[136,512]{1,0:T(8,128)S(1)} collective-permute-done((f32[136,512]{1,0:T(8,128)S(1)}, f32[136,512]{1,0:T(8,128)S(1)}, u32[]{:S(2)}, u32[]{:S(2)}) %collective-permute-start.33) | collective-permute-done | bytes 278560 | tf_op jit(solution)/shard_map/ppermute | solution.py:120
  214.2 3.0 %collective-permute-done.4.refs_3_ = f32[8,2816]{1,0:T(8,128)S(1)} collective-permute-done((f32[8,2816]{1,0:T(8,128)S(1)}, f32[8,2816]{1,0:T(8,128)S(1)}, u32[]{:S(2)}, u32[]{:S(2)}) %collective-permute-start.4) | collective-permute-done | bytes 90144 | tf_op jit(solution)/shard_map/ppermute | solution.py:126
  218.3 2.2 collective-permute-done.36.refs_2_
  227.4 2.4 collective-permute-start.39
  232.0 3.2 %collective-permute-done.40.refs_3_.refs_7_ = f32[8,128]{1,0:T(8,128)S(1)} collective-permute-done((f32[8,128]{1,0:T(8,128)S(1)}, f32[8,128]{1,0:T(8,128)S(1)}, u32[]{:S(2)}, u32[]{:S(2)}) %collective-permute-start.40) | collective-permute-done | bytes 4128 | tf_op jit(solution)/shard_map/ppermute | solution.py:123
  237.3 2.4 collective-permute-start.48
  239.7 2.0 collective-permute-start.49
  241.7 2.4 collective-permute-done.47.refs_0_
  244.1 4.4 %collective-permute-done.48.refs_1_ = bf16[128,512]{1,0:T(8,128)(2,1)S(1)} collective-permute-done((bf16[128,512]{1,0:T(8,128)(2,1)S(1)}, bf16[128,512]{1,0:T(8,128)(2,1)S(1)}, u32[]{:S(2)}, u32[]{:S(2)}) %collective-permute-start.48) | collective-permute-done | bytes 131104 | tf_op jit(solution)/shard_map/ppermute | solution.py:123
  250.7 6.3 %collective-permute-done.51.refs_13_ = bf16[3,128,512]{2,1,0:T(8,128)(2,1)S(1)} collective-permute-done((bf16[3,128,512]{2,1,0:T(8,128)(2,1)S(1)}, bf16[3,128,512]{2,1,0:T(8,128)(2,1)S(1)}, u32[]{:S(2)}, u32[]{:S(2)}) %collective-permute-start.51) | collective-permute-done | bytes 393248 | tf_op jit(solution)/shard_map/ppermute | solution.py:120
  259.0 2.2 collective-permute-done.53.refs_16_
  261.2 8.9 %backward.1 = (f32[2816,512]{1,0:T(8,128)S(1)}, f32[8,512]{1,0:T(8,128)S(1)}, f32[8,128]{1,0:T(8,128)S(1)}) custom-call(s32[5]{0:T(128)S(1)} %stack.27.flags, bf16[2816,512]{1,0:T(8,128)(2,1)S(1)} %copy-done.2, f32[8,512]{1,0:T(8,128)S(1)} %get-tuple-element.136.refs_1_, ...), custom_call_target="tpu_custom_call", output_to_operand_aliasing={{2}: (18, {})} | custom-call | tf_op jit(solution)/shard_map/backward/pallas_call | solution.py:65
  272.9 2.2 collective-permute-done.55
  275.1 3.4 %collective-permute-start.56 = (f32[8,512]{1,0:T(8,128)S(1)}, f32[8,512]{1,0:T(8,128)S(1)}, u32[]{:S(2)}, u32[]{:S(2)}) collective-permute-start(f32[8,512]{1,0:T(8,128)S(1)} %add.32), channel_id=1, source_target_pairs={{0,1},{1,0},{2,3},{3,2},{4,5},{5,4},{6,7},{7,6},{8,9},{9,8},{10,11... | collective-permute-start | bytes 49160 | tf_op jit(solution)/shard_map/ppermute | solution.py:123
  278.8 2.2 collective-permute-start.58
  280.9 2.2 collective-permute-done.57
  284.3 3.8 %final.1 = (f32[2816,512]{1,0:T(8,128)}, f32[5]{0:T(128)}, f32[8,128]{1,0:T(8,128)S(1)}) custom-call(s32[5]{0:T(128)S(1)} %stack.27.flags, bf16[2816,512]{1,0:T(8,128)(2,1)S(1)} %copy-done.2, f32[8,512]{1,0:T(8,128)S(1)} %get-tuple-element.136.refs_1_, f32[2816,512]{1,0:T(8,128)S(1)} %get-tuple-element.247.refs_2_, ...), custom_call_target="tpu_custom_call", output_to_operand_aliasing={{2}: (5, {})} | custom-call | tf_op jit(solution)/shard_map/final/pallas_call | solution.py:65
  (151 shorter events, 75.5 us)
Async XLA Ops:
  3.4 35.7 %collective-permute-start.3 = (bf16[2,2816,128]{2,1,0:T(8,128)(2,1)}, bf16[2,2816,128]{2,1,0:T(8,128)(2,1)}, u32[]{:S(2)}, u32[]{:S(2)}) collective-permute-start(bf16[2,2816,128]{2,1,0:T(8,128)(2,1)} %slice.4), channel_id=1, source_target_pairs={{0,4},{4,0},{1,5},{5,1},{2,6},{6,2},{3,7},{7,3},{8,12},{12,8},{9,1... | collective-permute-start | bytes 4325384 | tf_op jit(solution)/shard_map/ppermute | solution.py:126
  12.4 57.5 %collective-permute-start.9 = (bf16[2,2816,128]{2,1,0:T(8,128)(2,1)}, bf16[2,2816,128]{2,1,0:T(8,128)(2,1)}, u32[]{:S(2)}, u32[]{:S(2)}) collective-permute-start(bf16[2,2816,128]{2,1,0:T(8,128)(2,1)} %get-tuple-element.143), channel_id=1, source_target_pairs={{0,4},{4,0},{1,5},{5,1},{2,6},{6,2},{3,7},{7,3},{8,12},{12,8},{9,1... | collective-permute-start | bytes 4325384 | tf_op jit(solution)/shard_map/ppermute | solution.py:126
  24.1 4.4 %collective-permute-start = (f32[8,512]{1,0:T(8,128)S(1)}, f32[8,512]{1,0:T(8,128)S(1)}, u32[]{:S(2)}, u32[]{:S(2)}) collective-permute-start(f32[8,512]{1,0:T(8,128)S(1)} %psum.7.refs_1_), channel_id=1, source_target_pairs={{0,1},{1,0},{2,3},{3,2},{4,5},{5,4},{6,7},{7,6},{8,9},{9,8},{10,11... | collective-permute-start | bytes 49160 | tf_op jit(solution)/shard_map/ppermute | solution.py:123
  25.7 4.7 %collective-permute-start.1 = (f32[8,512]{1,0:T(8,128)S(1)}, f32[8,512]{1,0:T(8,128)S(1)}, u32[]{:S(2)}, u32[]{:S(2)}) collective-permute-start(f32[8,512]{1,0:T(8,128)S(1)} %psum.7.refs_1_), channel_id=1, source_target_pairs={{0,2},{1,3},{2,0},{3,1},{4,6},{5,7},{6,4},{7,5},{8,10},{9,11},{10,... | collective-permute-start | bytes 49160 | tf_op jit(solution)/shard_map/ppermute | solution.py:123
  28.3 5.5 %collective-permute-start.2 = (f32[8,512]{1,0:T(8,128)S(1)}, f32[8,512]{1,0:T(8,128)S(1)}, u32[]{:S(2)}, u32[]{:S(2)}) collective-permute-start(f32[8,512]{1,0:T(8,128)S(1)} %psum.7.refs_1_), channel_id=1, source_target_pairs={{0,3},{1,2},{2,1},{3,0},{4,7},{5,6},{6,5},{7,4},{8,11},{9,10},{10,... | collective-permute-start | bytes 49160 | tf_op jit(solution)/shard_map/ppermute | solution.py:123
  42.0 34.0 %collective-permute-start.5 = (bf16[2,1408,128]{2,1,0:T(8,128)(2,1)S(1)}, bf16[2,1408,128]{2,1,0:T(8,128)(2,1)S(1)}, u32[]{:S(2)}, u32[]{:S(2)}) collective-permute-start(bf16[2,1408,128]{2,1,0:T(8,128)(2,1)S(1)} %get-tuple-element.139), channel_id=1, source_target_pairs={{0,1},{1,0},{2,3},{3,2},{4,5},{5,4},{6,7},{7,6},{8,9},{9,8},{10,11... | collective-permute-start | bytes 2162696 | tf_op jit(solution)/shard_map/ppermute | solution.py:123
  44.2 56.5 %collective-permute-start.8 = (bf16[2,2816,128]{2,1,0:T(8,128)(2,1)S(1)}, bf16[2,2816,128]{2,1,0:T(8,128)(2,1)S(1)}, u32[]{:S(2)}, u32[]{:S(2)}) collective-permute-start(bf16[2,2816,128]{2,1,0:T(8,128)(2,1)S(1)} %get-tuple-element.142), channel_id=1, source_target_pairs={{0,4},{4,0},{1,5},{5,1},{2,6},{6,2},{3,7},{7,3},{8,12},{12,8},{9,1... | collective-permute-start | bytes 4325384 | tf_op jit(solution)/shard_map/ppermute | solution.py:126
  45.7 27.1 %collective-permute-start.6 = (bf16[1408,128]{1,0:T(8,128)(2,1)S(1)}, bf16[1408,128]{1,0:T(8,128)(2,1)S(1)}, u32[]{:S(2)}, u32[]{:S(2)}) collective-permute-start(bf16[1408,128]{1,0:T(8,128)(2,1)S(1)} %get-tuple-element.140), channel_id=1, source_target_pairs={{0,2},{1,3},{2,0},{3,1},{4,6},{5,7},{6,4},{7,5},{8,10},{9,11},{10,... | collective-permute-start | bytes 1081352 | tf_op jit(solution)/shard_map/ppermute | solution.py:123
  48.3 27.7 %collective-permute-start.7 = (bf16[1408,128]{1,0:T(8,128)(2,1)S(1)}, bf16[1408,128]{1,0:T(8,128)(2,1)S(1)}, u32[]{:S(2)}, u32[]{:S(2)}) collective-permute-start(bf16[1408,128]{1,0:T(8,128)(2,1)S(1)} %get-tuple-element.141), channel_id=1, source_target_pairs={{0,3},{1,2},{2,1},{3,0},{4,7},{5,6},{6,5},{7,4},{8,11},{9,10},{10,... | collective-permute-start | bytes 1081352 | tf_op jit(solution)/shard_map/ppermute | solution.py:123
  77.1 32.8 %collective-permute-start.12 = (bf16[2,1408,128]{2,1,0:T(8,128)(2,1)S(1)}, bf16[2,1408,128]{2,1,0:T(8,128)(2,1)S(1)}, u32[]{:S(2)}, u32[]{:S(2)}) collective-permute-start(bf16[2,1408,128]{2,1,0:T(8,128)(2,1)S(1)} %get-tuple-element.157), channel_id=1, source_target_pairs={{0,1},{1,0},{2,3},{3,2},{4,5},{5,4},{6,7},{7,6},{8,9},{9,8},{10,11... | collective-permute-start | bytes 2162696 | tf_op jit(solution)/shard_map/ppermute | solution.py:123
  79.1 52.5 %collective-permute-start.14 = (bf16[2,2816,128]{2,1,0:T(8,128)(2,1)S(1)}, bf16[2,2816,128]{2,1,0:T(8,128)(2,1)S(1)}, u32[]{:S(2)}, u32[]{:S(2)}) collective-permute-start(bf16[2,2816,128]{2,1,0:T(8,128)(2,1)S(1)} %get-tuple-element.161), channel_id=1, source_target_pairs={{0,4},{4,0},{1,5},{5,1},{2,6},{6,2},{3,7},{7,3},{8,12},{12,8},{9,1... | collective-permute-start | bytes 4325384 | tf_op jit(solution)/shard_map/ppermute | solution.py:126
  79.6 22.0 %collective-permute-start.10 = (bf16[1408,128]{1,0:T(8,128)(2,1)S(1)}, bf16[1408,128]{1,0:T(8,128)(2,1)S(1)}, u32[]{:S(2)}, u32[]{:S(2)}) collective-permute-start(bf16[1408,128]{1,0:T(8,128)(2,1)S(1)} %get-tuple-element.155), channel_id=1, source_target_pairs={{0,2},{1,3},{2,0},{3,1},{4,6},{5,7},{6,4},{7,5},{8,10},{9,11},{10,... | collective-permute-start | bytes 1081352 | tf_op jit(solution)/shard_map/ppermute | solution.py:123
  80.8 29.2 %collective-permute-start.11 = (bf16[1408,128]{1,0:T(8,128)(2,1)S(1)}, bf16[1408,128]{1,0:T(8,128)(2,1)S(1)}, u32[]{:S(2)}, u32[]{:S(2)}) collective-permute-start(bf16[1408,128]{1,0:T(8,128)(2,1)S(1)} %get-tuple-element.156), channel_id=1, source_target_pairs={{0,3},{1,2},{2,1},{3,0},{4,7},{5,6},{6,5},{7,4},{8,11},{9,10},{10,... | collective-permute-start | bytes 1081352 | tf_op jit(solution)/shard_map/ppermute | solution.py:123
  111.1 28.0 %collective-permute-start.17 = (bf16[2,1408,128]{2,1,0:T(8,128)(2,1)S(1)}, bf16[2,1408,128]{2,1,0:T(8,128)(2,1)S(1)}, u32[]{:S(2)}, u32[]{:S(2)}) collective-permute-start(bf16[2,1408,128]{2,1,0:T(8,128)(2,1)S(1)} %get-tuple-element.168), channel_id=1, source_target_pairs={{0,1},{1,0},{2,3},{3,2},{4,5},{5,4},{6,7},{7,6},{8,9},{9,8},{10,11... | collective-permute-start | bytes 2162696 | tf_op jit(solution)/shard_map/ppermute | solution.py:123
  113.1 19.4 %collective-permute-start.15 = (bf16[1408,128]{1,0:T(8,128)(2,1)S(1)}, bf16[1408,128]{1,0:T(8,128)(2,1)S(1)}, u32[]{:S(2)}, u32[]{:S(2)}) collective-permute-start(bf16[1408,128]{1,0:T(8,128)(2,1)S(1)} %get-tuple-element.166), channel_id=1, source_target_pairs={{0,2},{1,3},{2,0},{3,1},{4,6},{5,7},{6,4},{7,5},{8,10},{9,11},{10,... | collective-permute-start | bytes 1081352 | tf_op jit(solution)/shard_map/ppermute | solution.py:123
  113.8 25.3 %collective-permute-start.16 = (bf16[1408,128]{1,0:T(8,128)(2,1)S(1)}, bf16[1408,128]{1,0:T(8,128)(2,1)S(1)}, u32[]{:S(2)}, u32[]{:S(2)}) collective-permute-start(bf16[1408,128]{1,0:T(8,128)(2,1)S(1)} %get-tuple-element.167), channel_id=1, source_target_pairs={{0,3},{1,2},{2,1},{3,0},{4,7},{5,6},{6,5},{7,4},{8,11},{9,10},{10,... | collective-permute-start | bytes 1081352 | tf_op jit(solution)/shard_map/ppermute | solution.py:123
  116.2 31.7 %collective-permute-start.13 = (bf16[2,1408,128]{2,1,0:T(8,128)(2,1)S(1)}, bf16[2,1408,128]{2,1,0:T(8,128)(2,1)S(1)}, u32[]{:S(2)}, u32[]{:S(2)}) collective-permute-start(bf16[2,1408,128]{2,1,0:T(8,128)(2,1)S(1)} %get-tuple-element.160.refs_4_), channel_id=1, source_target_pairs={{0,4},{4,0},{1,5},{5,1},{2,6},{6,2},{3,7},{7,3},{8,12},{12,8},{9,1... | collective-permute-start | bytes 2162696 | tf_op jit(solution)/shard_map/ppermute | solution.py:126
  140.8 21.8 %collective-permute-start.18 = (bf16[2,1408,128]{2,1,0:T(8,128)(2,1)S(1)}, bf16[2,1408,128]{2,1,0:T(8,128)(2,1)S(1)}, u32[]{:S(2)}, u32[]{:S(2)}) collective-permute-start(bf16[2,1408,128]{2,1,0:T(8,128)(2,1)S(1)} %get-tuple-element.171.refs_8_), channel_id=1, source_target_pairs={{0,4},{4,0},{1,5},{5,1},{2,6},{6,2},{3,7},{7,3},{8,12},{12,8},{9,1... | collective-permute-start | bytes 2162696 | tf_op jit(solution)/shard_map/ppermute | solution.py:126
  143.5 26.5 %collective-permute-start.21 = (bf16[2,1408,128]{2,1,0:T(8,128)(2,1)S(1)}, bf16[2,1408,128]{2,1,0:T(8,128)(2,1)S(1)}, u32[]{:S(2)}, u32[]{:S(2)}) collective-permute-start(bf16[2,1408,128]{2,1,0:T(8,128)(2,1)S(1)} %get-tuple-element.179), channel_id=1, source_target_pairs={{0,1},{1,0},{2,3},{3,2},{4,5},{5,4},{6,7},{7,6},{8,9},{9,8},{10,11... | collective-permute-start | bytes 2162696 | tf_op jit(solution)/shard_map/ppermute | solution.py:123
  144.1 23.9 %collective-permute-start.19 = (bf16[1408,128]{1,0:T(8,128)(2,1)S(1)}, bf16[1408,128]{1,0:T(8,128)(2,1)S(1)}, u32[]{:S(2)}, u32[]{:S(2)}) collective-permute-start(bf16[1408,128]{1,0:T(8,128)(2,1)S(1)} %get-tuple-element.177), channel_id=1, source_target_pairs={{0,2},{1,3},{2,0},{3,1},{4,6},{5,7},{6,4},{7,5},{8,10},{9,11},{10,... | collective-permute-start | bytes 1081352 | tf_op jit(solution)/shard_map/ppermute | solution.py:123
  145.4 24.6 %collective-permute-start.20 = (bf16[1408,128]{1,0:T(8,128)(2,1)S(1)}, bf16[1408,128]{1,0:T(8,128)(2,1)S(1)}, u32[]{:S(2)}, u32[]{:S(2)}) collective-permute-start(bf16[1408,128]{1,0:T(8,128)(2,1)S(1)} %get-tuple-element.178), channel_id=1, source_target_pairs={{0,3},{1,2},{2,1},{3,0},{4,7},{5,6},{6,5},{7,4},{8,11},{9,10},{10,... | collective-permute-start | bytes 1081352 | tf_op jit(solution)/shard_map/ppermute | solution.py:123
  149.0 29.0 %collective-permute-start.25 = (bf16[2,1408,128]{2,1,0:T(8,128)(2,1)S(1)}, bf16[2,1408,128]{2,1,0:T(8,128)(2,1)S(1)}, u32[]{:S(2)}, u32[]{:S(2)}) collective-permute-start(bf16[2,1408,128]{2,1,0:T(8,128)(2,1)S(1)} %get-tuple-element.188.refs_4_), channel_id=1, source_target_pairs={{0,4},{4,0},{1,5},{5,1},{2,6},{6,2},{3,7},{7,3},{8,12},{12,8},{9,1... | collective-permute-start | bytes 2162696 | tf_op jit(solution)/shard_map/ppermute | solution.py:126
  172.2 20.4 %collective-permute-start.30 = (bf16[2,1408,128]{2,1,0:T(8,128)(2,1)S(1)}, bf16[2,1408,128]{2,1,0:T(8,128)(2,1)S(1)}, u32[]{:S(2)}, u32[]{:S(2)}) collective-permute-start(bf16[2,1408,128]{2,1,0:T(8,128)(2,1)S(1)} %get-tuple-element.187.refs_4_), channel_id=1, source_target_pairs={{0,4},{4,0},{1,5},{5,1},{2,6},{6,2},{3,7},{7,3},{8,12},{12,8},{9,1... | collective-permute-start | bytes 2162696 | tf_op jit(solution)/shard_map/ppermute | solution.py:126
  175.0 15.7 %collective-permute-start.24 = (f32[128,1024]{1,0:T(8,128)S(1)}, f32[128,1024]{1,0:T(8,128)S(1)}, u32[]{:S(2)}, u32[]{:S(2)}) collective-permute-start(f32[128,1024]{1,0:T(8,128)S(1)} %get-tuple-element.186), channel_id=1, source_target_pairs={{0,16},{8,24},{16,0},{24,8},{1,17},{9,25},{17,1},{25,9},{2,18},{10... | collective-permute-start | bytes 1572872 | tf_op jit(solution)/shard_map/ppermute | solution.py:120
  186.3 13.2 %collective-permute-start.29 = (f32[136,512]{1,0:T(8,128)S(1)}, f32[136,512]{1,0:T(8,128)S(1)}, u32[]{:S(2)}, u32[]{:S(2)}) collective-permute-start(f32[136,512]{1,0:T(8,128)S(1)} %get-tuple-element.203), channel_id=1, source_target_pairs={{0,16},{8,24},{16,0},{24,8},{1,17},{9,25},{17,1},{25,9},{2,18},{10... | collective-permute-start | bytes 835592 | tf_op jit(solution)/shard_map/ppermute | solution.py:120
  194.5 16.9 %collective-permute-start.28 = (f32[2,136,256]{2,1,0:T(8,128)S(1)}, f32[2,136,256]{2,1,0:T(8,128)S(1)}, u32[]{:S(2)}, u32[]{:S(2)}) collective-permute-start(f32[2,136,256]{2,1,0:T(8,128)S(1)} %get-tuple-element.201), channel_id=1, source_target_pairs={{0,2},{1,3},{2,0},{3,1},{4,6},{5,7},{6,4},{7,5},{8,10},{9,11},{10,... | collective-permute-start | bytes 835592 | tf_op jit(solution)/shard_map/ppermute | solution.py:123
  197.9 8.4 %collective-permute-start.33 = (f32[136,512]{1,0:T(8,128)S(1)}, f32[136,512]{1,0:T(8,128)S(1)}, u32[]{:S(2)}, u32[]{:S(2)}) collective-permute-start(f32[136,512]{1,0:T(8,128)S(1)} %get-tuple-element.216), channel_id=1, source_target_pairs={{0,16},{8,24},{16,0},{24,8},{1,17},{9,25},{17,1},{25,9},{2,18},{10... | collective-permute-start | bytes 835592 | tf_op jit(solution)/shard_map/ppermute | solution.py:120
  206.9 11.4 %collective-permute-start.35 = (f32[128,256]{1,0:T(8,128)S(1)}, f32[128,256]{1,0:T(8,128)S(1)}, u32[]{:S(2)}, u32[]{:S(2)}) collective-permute-start(f32[128,256]{1,0:T(8,128)S(1)} %get-tuple-element.231), channel_id=1, source_target_pairs={{0,1},{1,0},{2,3},{3,2},{4,5},{5,4},{6,7},{7,6},{8,9},{9,8},{10,11... | collective-permute-start | bytes 393224 | tf_op jit(solution)/shard_map/ppermute | solution.py:123
  208.6 12.0 %collective-permute-start.36 = (f32[128,256]{1,0:T(8,128)S(1)}, f32[128,256]{1,0:T(8,128)S(1)}, u32[]{:S(2)}, u32[]{:S(2)}) collective-permute-start(f32[128,256]{1,0:T(8,128)S(1)} %get-tuple-element.232), channel_id=1, source_target_pairs={{0,2},{1,3},{2,0},{3,1},{4,6},{5,7},{6,4},{7,5},{8,10},{9,11},{10,... | collective-permute-start | bytes 393224 | tf_op jit(solution)/shard_map/ppermute | solution.py:123
  210.3 10.2 %collective-permute-start.37 = (f32[128,256]{1,0:T(8,128)S(1)}, f32[128,256]{1,0:T(8,128)S(1)}, u32[]{:S(2)}, u32[]{:S(2)}) collective-permute-start(f32[128,256]{1,0:T(8,128)S(1)} %get-tuple-element.233), channel_id=1, source_target_pairs={{0,3},{1,2},{2,1},{3,0},{4,7},{5,6},{6,5},{7,4},{8,11},{9,10},{10,... | collective-permute-start | bytes 393224 | tf_op jit(solution)/shard_map/ppermute | solution.py:123
  212.0 9.4 %collective-permute-start.34 = (f32[128,256]{1,0:T(8,128)S(1)}, f32[128,256]{1,0:T(8,128)S(1)}, u32[]{:S(2)}, u32[]{:S(2)}) collective-permute-start(f32[128,256]{1,0:T(8,128)S(1)} %get-tuple-element.229), channel_id=1, source_target_pairs={{0,1},{1,0},{2,3},{3,2},{4,5},{5,4},{6,7},{7,6},{8,9},{9,8},{10,11... | collective-permute-start | bytes 393224 | tf_op jit(solution)/shard_map/ppermute | solution.py:123
  212.7 4.5 %collective-permute-start.4 = (f32[8,2816]{1,0:T(8,128)S(1)}, f32[8,2816]{1,0:T(8,128)S(1)}, u32[]{:S(2)}, u32[]{:S(2)}) collective-permute-start(f32[8,2816]{1,0:T(8,128)S(1)} %get-tuple-element.137.refs_2_), channel_id=1, source_target_pairs={{0,4},{4,0},{1,5},{5,1},{2,6},{6,2},{3,7},{7,3},{8,12},{12,8},{9,1... | collective-permute-start | bytes 270344 | tf_op jit(solution)/shard_map/ppermute | solution.py:126
  224.2 6.2 %collective-permute-start.42 = (f32[16,512]{1,0:T(8,128)S(1)}, f32[16,512]{1,0:T(8,128)S(1)}, u32[]{:S(2)}, u32[]{:S(2)}) collective-permute-start(f32[16,512]{1,0:T(8,128)S(1)} %add.29), channel_id=1, source_target_pairs={{0,16},{8,24},{16,0},{24,8},{1,17},{9,25},{17,1},{25,9},{2,18},{10... | collective-permute-start | bytes 98312 | tf_op jit(solution)/shard_map/ppermute | solution.py:120
  225.7 6.3 %collective-permute-start.38 = (f32[8,128]{1,0:T(8,128)S(1)}, f32[8,128]{1,0:T(8,128)S(1)}, u32[]{:S(2)}, u32[]{:S(2)}) collective-permute-start(f32[8,128]{1,0:T(8,128)S(1)} %get-tuple-element.239.refs_0_.refs_4_), channel_id=1, source_target_pairs={{0,1},{1,0},{2,3},{3,2},{4,5},{5,4},{6,7},{7,6},{8,9},{9,8},{10,11... | collective-permute-start | bytes 12296 | tf_op jit(solution)/shard_map/ppermute | solution.py:123
  227.4 4.6 %collective-permute-start.39 = (f32[8,128]{1,0:T(8,128)S(1)}, f32[8,128]{1,0:T(8,128)S(1)}, u32[]{:S(2)}, u32[]{:S(2)}) collective-permute-start(f32[8,128]{1,0:T(8,128)S(1)} %get-tuple-element.239.refs_0_.refs_4_), channel_id=1, source_target_pairs={{0,2},{1,3},{2,0},{3,1},{4,6},{5,7},{6,4},{7,5},{8,10},{9,11},{10,... | collective-permute-start | bytes 12296 | tf_op jit(solution)/shard_map/ppermute | solution.py:123
  229.8 5.4 %collective-permute-start.40 = (f32[8,128]{1,0:T(8,128)S(1)}, f32[8,128]{1,0:T(8,128)S(1)}, u32[]{:S(2)}, u32[]{:S(2)}) collective-permute-start(f32[8,128]{1,0:T(8,128)S(1)} %get-tuple-element.239.refs_0_.refs_4_), channel_id=1, source_target_pairs={{0,3},{1,2},{2,1},{3,0},{4,7},{5,6},{6,5},{7,4},{8,11},{9,10},{10,... | collective-permute-start | bytes 12296 | tf_op jit(solution)/shard_map/ppermute | solution.py:123
  230.4 5.3 %collective-permute-start.43 = (f32[16,512]{1,0:T(8,128)S(1)}, f32[16,512]{1,0:T(8,128)S(1)}, u32[]{:S(2)}, u32[]{:S(2)}) collective-permute-start(f32[16,512]{1,0:T(8,128)S(1)} %add.30.refs_8_), channel_id=1, source_target_pairs={{0,4},{4,0},{1,5},{5,1},{2,6},{6,2},{3,7},{7,3},{8,12},{12,8},{9,1... | collective-permute-start | bytes 98312 | tf_op jit(solution)/shard_map/ppermute | solution.py:126
  236.7 5.0 %collective-permute-start.45 = (bf16[128,512]{1,0:T(8,128)(2,1)S(1)}, bf16[128,512]{1,0:T(8,128)(2,1)S(1)}, u32[]{:S(2)}, u32[]{:S(2)}) collective-permute-start(bf16[128,512]{1,0:T(8,128)(2,1)S(1)} %get-tuple-element.242.refs_7_), channel_id=1, source_target_pairs={{0,16},{8,24},{16,0},{24,8},{1,17},{9,25},{17,1},{25,9},{2,18},{10... | collective-permute-start | bytes 393224 | tf_op jit(solution)/shard_map/ppermute | solution.py:120
  237.3 6.9 %collective-permute-start.47 = (bf16[128,512]{1,0:T(8,128)(2,1)S(1)}, bf16[128,512]{1,0:T(8,128)(2,1)S(1)}, u32[]{:S(2)}, u32[]{:S(2)}) collective-permute-start(bf16[128,512]{1,0:T(8,128)(2,1)S(1)} %get-tuple-element.242.refs_7_), channel_id=1, source_target_pairs={{0,1},{1,0},{2,3},{3,2},{4,5},{5,4},{6,7},{7,6},{8,9},{9,8},{10,11... | collective-permute-start | bytes 393224 | tf_op jit(solution)/shard_map/ppermute | solution.py:123
  237.3 11.3 %collective-permute-start.48 = (bf16[128,512]{1,0:T(8,128)(2,1)S(1)}, bf16[128,512]{1,0:T(8,128)(2,1)S(1)}, u32[]{:S(2)}, u32[]{:S(2)}) collective-permute-start(bf16[128,512]{1,0:T(8,128)(2,1)S(1)} %get-tuple-element.242.refs_7_), channel_id=1, source_target_pairs={{0,2},{1,3},{2,0},{3,1},{4,6},{5,7},{6,4},{7,5},{8,10},{9,11},{10,... | collective-permute-start | bytes 393224 | tf_op jit(solution)/shard_map/ppermute | solution.py:123
  239.7 8.9 %collective-permute-start.49 = (bf16[128,512]{1,0:T(8,128)(2,1)S(1)}, bf16[128,512]{1,0:T(8,128)(2,1)S(1)}, u32[]{:S(2)}, u32[]{:S(2)}) collective-permute-start(bf16[128,512]{1,0:T(8,128)(2,1)S(1)} %get-tuple-element.242.refs_7_), channel_id=1, source_target_pairs={{0,3},{1,2},{2,1},{3,0},{4,7},{5,6},{6,5},{7,4},{8,11},{9,10},{10,... | collective-permute-start | bytes 393224 | tf_op jit(solution)/shard_map/ppermute | solution.py:123
  249.1 7.8 %collective-permute-start.51 = (bf16[3,128,512]{2,1,0:T(8,128)(2,1)S(1)}, bf16[3,128,512]{2,1,0:T(8,128)(2,1)S(1)}, u32[]{:S(2)}, u32[]{:S(2)}) collective-permute-start(bf16[3,128,512]{2,1,0:T(8,128)(2,1)S(1)} %get-tuple-element.244.refs_11_), channel_id=1, source_target_pairs={{0,16},{8,24},{16,0},{24,8},{1,17},{9,25},{17,1},{25,9},{2,18},{10... | collective-permute-start | bytes 1179656 | tf_op jit(solution)/shard_map/ppermute | solution.py:120
  250.7 10.5 %collective-permute-start.50 = (bf16[3,128,512]{2,1,0:T(8,128)(2,1)S(1)}, bf16[3,128,512]{2,1,0:T(8,128)(2,1)S(1)}, u32[]{:S(2)}, u32[]{:S(2)}) collective-permute-start(bf16[3,128,512]{2,1,0:T(8,128)(2,1)S(1)} %get-tuple-element.244.refs_11_), channel_id=1, source_target_pairs={{0,8},{8,0},{16,24},{24,16},{1,9},{9,1},{17,25},{25,17},{2,10},{10... | collective-permute-start | bytes 1179656 | tf_op jit(solution)/shard_map/ppermute | solution.py:117
  256.9 4.3 %collective-permute-start.52 = (bf16[3,128,512]{2,1,0:T(8,128)(2,1)S(1)}, bf16[3,128,512]{2,1,0:T(8,128)(2,1)S(1)}, u32[]{:S(2)}, u32[]{:S(2)}) collective-permute-start(bf16[3,128,512]{2,1,0:T(8,128)(2,1)S(1)} %collective-permute-done.51.refs_13_), channel_id=1, source_target_pairs={{0,8},{8,0},{16,24},{24,16},{1,9},{9,1},{17,25},{25,17},{2,10},{10... | collective-permute-start | bytes 1179656 | tf_op jit(solution)/shard_map/ppermute | solution.py:117
  256.9 4.3 %collective-permute-start.44 = (bf16[128,512]{1,0:T(8,128)(2,1)S(1)}, bf16[128,512]{1,0:T(8,128)(2,1)S(1)}, u32[]{:S(2)}, u32[]{:S(2)}) collective-permute-start(bf16[128,512]{1,0:T(8,128)(2,1)S(1)} %get-tuple-element.242.refs_7_), channel_id=1, source_target_pairs={{0,8},{8,0},{16,24},{24,16},{1,9},{9,1},{17,25},{25,17},{2,10},{10... | collective-permute-start | bytes 393224 | tf_op jit(solution)/shard_map/ppermute | solution.py:117
  275.1 5.8 %collective-permute-start.56 = (f32[8,512]{1,0:T(8,128)S(1)}, f32[8,512]{1,0:T(8,128)S(1)}, u32[]{:S(2)}, u32[]{:S(2)}) collective-permute-start(f32[8,512]{1,0:T(8,128)S(1)} %add.32), channel_id=1, source_target_pairs={{0,1},{1,0},{2,3},{3,2},{4,5},{5,4},{6,7},{7,6},{8,9},{9,8},{10,11... | collective-permute-start | bytes 49160 | tf_op jit(solution)/shard_map/ppermute | solution.py:123
  278.5 4.6 %collective-permute-start.57 = (f32[8,512]{1,0:T(8,128)S(1)}, f32[8,512]{1,0:T(8,128)S(1)}, u32[]{:S(2)}, u32[]{:S(2)}) collective-permute-start(f32[8,512]{1,0:T(8,128)S(1)} %add.32), channel_id=1, source_target_pairs={{0,2},{1,3},{2,0},{3,1},{4,6},{5,7},{6,4},{7,5},{8,10},{9,11},{10,... | collective-permute-start | bytes 49160 | tf_op jit(solution)/shard_map/ppermute | solution.py:123
  278.8 5.5 %collective-permute-start.58 = (f32[8,512]{1,0:T(8,128)S(1)}, f32[8,512]{1,0:T(8,128)S(1)}, u32[]{:S(2)}, u32[]{:S(2)}) collective-permute-start(f32[8,512]{1,0:T(8,128)S(1)} %add.32), channel_id=1, source_target_pairs={{0,3},{1,2},{2,1},{3,0},{4,7},{5,6},{6,5},{7,4},{8,11},{9,10},{10,... | collective-permute-start | bytes 49160 | tf_op jit(solution)/shard_map/ppermute | solution.py:123
  (22 other events, 179.9 us)

commit v7 on v6

--- a/solution.py
+++ b/solution.py
@@ -12,7 +12,7 @@
 ANY = pl.BlockSpec(memory_space=pl.ANY)
 BF = jnp.bfloat16
 F32 = jnp.float32
-VMEM_BYTES = 20 * 1024 * 1024
+VMEM_BYTES = 14 * 1024 * 1024
 COSTS = {"spots": 1, "back3": 1, "waits2": 3, "addx1": 9, "half0": 3}
 WIDTHS = (128, 128, 128, 128)
 GROUPS = ((0, 1), (2,), (3,))
@@ -466,7 +466,7 @@
             sent[f"rz2{z}"] = over_gene(parts[2], 2)
         else:
             st["z", z] = parts[:1]
-            for s in (1, 2, 3):
+            for s in (3, 2, 1):
                 sent[f"rz{s}{z}"] = over_gene(parts[s], s)
 
     def reduce_half(z):
@@ -539,7 +539,8 @@
         "stats", stats_body, [memb, mine, *preds],
         [(sds((16, genes), F32), gene_spec), (sds((8, quarter), F32), spot_spec)],
     )
-    spot_parts = [spot_sums] + [over_gene(spot_sums, s) for s in (1, 2, 3)]
+    far = {s: over_gene(spot_sums, s) for s in (3, 2, 1)}
+    spot_parts = [spot_sums] + [far[s] for s in (1, 2, 3)]
     gene_sums = gene_sums + over_core(gene_sums)
     gene_sums = gene_sums + over_x(gene_sums)
     gene_parts = [gene_sums, over_spot(gene_sums)] if spot_size == 2 else [sum_spot(gene_sums)]
@@ -598,56 +599,80 @@
         [(sds((quarter, genes), BF), whole((quarter, genes))), (sds((8, spots), F32), row8)],
     )
     terms = [terms, over_spot(terms)] if spot_size == 2 else [sum_spot(terms)]
+    far = {s: over_gene(grad, s) for s in (3, 2, 1)}
+    others = [far[s] for s in (1, 2, 3)]
     grad_x = over_x(grad)
-    others = [over_gene(grad, s) for s in (1, 2, 3)]
+    own = [grad, over_core(grad), grad_x, over_core(grad_x)]
     one, rest = (quarter, genes), (slots - 1, quarter, genes)
+    row_blk = rows // 4
+
+    def by_rows(width, size=row_blk):
+        return pl.BlockSpec((size, width), lambda g, f: (g, 0))
+
+    def place(fl, refs, target, sems):
+        copies = []
+        for b, ref in enumerate(refs):
+            at = pl.ds(pl.multiple_of((fl[2] ^ b) * quarter, quarter), quarter)
+            copies.append((None, ref, target(at)))
+        copy_all(copies, sems)
+
+    def slot_product(efs, slot, held):
+        left = jnp.concatenate([ef[:, slot * w : (slot + 1) * w] for w, ef in zip(WIDTHS, efs)], axis=1)
+        return lax.dot_general(left, held, (((1,), (1,)), ((), ())), preferred_element_type=F32)
 
     def gather_body(fl, i, out):
         for n in range(slots - 1):
             out[0][n] = i[n][...]
 
     (rest_z,) = run(
-        "gather", gather_body, [(a, whole(one)) for a in others], [(sds(rest, BF), whole(rest))], after=[grad_x]
+        "gather", gather_body, [(a, whole(one)) for a in others], [(sds(rest, BF), whole(rest))], after=[grad_x, *terms[1:]]
     )
     rest_x = over_x(rest_z)
-    grads = [grad, over_core(grad), grad_x, over_core(grad_x), rest_z, over_core(rest_z), rest_x, over_core(rest_x)]
-
-    row_blk = rows // 4
+
+    def own_body(fl, i, out, held, sems):
+        sm, efs, gs = i[0], i[1 : 1 + n_ch], i[1 + n_ch :]
+
+        @pl.when(pl.program_id(0) == 0)
+        def _():
+            place(fl, gs, lambda at: held.at[at, :], sems)
+
+        out[0][...] = slot_product(efs, 0, held[...]) - jnp.broadcast_to(sm[:, 0:1], (row_blk, spots))
+
+    ins = [(st["sm"], by_rows(LANES))] + [(st["e", c], by_rows(WIDTHS[c])) for c in chunks]
+    ins += [(a, ANY) for a in own]
+    (own_part,) = run(
+        "own", own_body, ins, [(sds((rows, spots), F32), by_rows(spots))], grid=(rows // row_blk,),
+        scratch=[pltpu.VMEM((spots, genes), BF), pltpu.SemaphoreType.DMA((len(own),))],
+    )
+
+    (rest_x,) = run("rest", None, through=[rest_x])
+    grads = [rest_z, over_core(rest_z), rest_x, over_core(rest_x)]
 
     def backward_body(fl, i, out, held, sems):
-        lg, tot, sm = i[:3]
-        efs, gs, terms = i[3 : 3 + n_ch], i[3 + n_ch : 11 + n_ch], i[11 + n_ch :]
+        lg, tot, before = i[:3]
+        efs, gs, terms = i[3 : 3 + n_ch], i[3 + n_ch : 7 + n_ch], i[7 + n_ch :]
 
         @pl.when(pl.program_id(0) == 0)
         def _():
             row = lax.broadcasted_iota(jnp.int32, (8, spots), 0)
             out[1][...] = jnp.where(row == 0, 0.0, sum(ref[...] for ref in terms))
-            copies = []
-            for b in range(sizes["cell"]):
-                at = pl.ds(pl.multiple_of((fl[2] ^ b) * quarter, quarter), quarter)
-                copies.append((None, gs[b], held.at[0, at, :]))
-                copies.append((None, gs[4 + b], held.at[pl.ds(1, slots - 1), at, :]))
-            copy_all(copies, sems)
-
-        acc = -jnp.broadcast_to(sm[:, 0:1], (row_blk, spots))
-        for s in range(slots):
-            left = jnp.concatenate([ef[:, s * w : (s + 1) * w] for w, ef in zip(WIDTHS, efs)], axis=1)
-            acc += lax.dot_general(left, held[s], (((1,), (1,)), ((), ())), preferred_element_type=F32)
+            place(fl, gs, lambda at: held.at[:, at, :], sems)
+
+        acc = before[...]
+        for s in range(1, slots):
+            acc += slot_product(efs, s, held[s - 1])
         out[0][...] = acc
         prob = jnp.exp(lg[...].astype(F32)) * (1.0 / tot[0:1, :])
         out[1][0:1, :] += jnp.sum(prob * acc, axis=0, keepdims=True)
 
-    def by_rows(width, size=row_blk):
-        return pl.BlockSpec((size, width), lambda g, f: (g, 0))
-
-    ins = [(logits, by_rows(spots)), (st["tot"], row8), (st["sm"], by_rows(LANES))]
+    ins = [(logits, by_rows(spots)), (st["tot"], row8), (own_part, by_rows(spots))]
     ins += [(st["e", c], by_rows(slots * WIDTHS[c])) for c in chunks]
     ins += [(a, ANY) for a in grads] + [(a, row8) for a in terms]
     grad_probs, v = run(
         "backward", backward_body, ins,
         [(sds((rows, spots), F32), by_rows(spots)), (sds((8, spots), F32), row8)],
         grid=(rows // row_blk,),
-        scratch=[pltpu.VMEM((slots, spots, genes), BF), pltpu.SemaphoreType.DMA((len(grads),))],
+        scratch=[pltpu.VMEM((slots - 1, spots, genes), BF), pltpu.SemaphoreType.DMA((len(grads),))],
     )
 
     v = v + over_core(v)

time: 288 us -> 284 us (0.986)
  waiting for transfers between devices: 131 us -> 126 us
    ppermute x7, waiting for transfers between devices: 14.9 us -> 9.77 us  [over_x(): return lax.ppermute(v, 'cell', xor_pairs(4, 2))]
    ppermute x29, waiting for transfers between devices: 41.2 us -> 37.5 us  [over_gene(): return lax.ppermute(v, 'gene', xor_pairs(4, step))]
    pallas_call x48 -> x50, Pallas kernels: 59.4 us -> 61.9 us  [run(): pl.pallas_call(kernel, out_shape=[s for s, _ in outs] + [sds(a.shape, a.d...]
    unnamed x22 -> x18, local copies, waits for them, and re-layouts: 6.87 us -> 5.29 us
  transfers between devices with their start and end apart: 59 -> 59, of which waited for: 30 -> 33; matrix products, arithmetic and copies ran while one was open for 0% -> 0% of each run, Pallas kernels for 15% -> 17%
where the time goes in v7:
time: 284 us
  waiting for transfers between devices  126 us (44%)
  starting transfers between devices  75.4 us (27%)
  Pallas kernels  61.9 us (22%)
  blocking collectives  11.6 us (4%)
  local copies, waits for them, and re-layouts  8.1 us (3%)
    ppermute x11, waiting for transfers between devices, over_spot(): return lax.ppermute(v, 'spot', xor_pairs(spot_size, step))  71.3 us
    pallas_call x50, Pallas kernels, run(): pl.pallas_call(kernel, out_shape=[s for s, _ in outs] + [sds(a.shape, a.d...  61.9 us
    ppermute x29, starting transfers between devices, over_gene(): return lax.ppermute(v, 'gene', xor_pairs(4, step))  46.6 us
    ppermute x29, waiting for transfers between devices, over_gene(): return lax.ppermute(v, 'gene', xor_pairs(4, step))  37.5 us
    ppermute x11, starting transfers between devices, over_spot(): return lax.ppermute(v, 'spot', xor_pairs(spot_size, step))  15.8 us
    psum x1, blocking collectives, totals(): st['tot'] = lax.psum(v, 'cell')  11.6 us
    ppermute x7, starting transfers between devices, over_x(): return lax.ppermute(v, 'cell', xor_pairs(4, 2))  10.4 us
    ppermute x7, waiting for transfers between devices, over_x(): return lax.ppermute(v, 'cell', xor_pairs(4, 2))  9.77 us
  transfers between devices with their start and end apart: 59, of which 33 were waited for; matrix products, arithmetic and copies ran while one was open for 0% of the time, Pallas kernels for 17%

profile of v7, /device:TPU:0, one launch (start us, length us, event | category | flops | bytes accessed | tf_op | source)
XLA Modules:
  0.0 283.9 jit_solution(10379894959331789540)
XLA Ops:
  0.6 2.7 slice.4
  3.4 3.0 %collective-permute-start.3 = (bf16[2,2816,128]{2,1,0:T(8,128)(2,1)}, bf16[2,2816,128]{2,1,0:T(8,128)(2,1)}, u32[]{:S(2)}, u32[]{:S(2)}) collective-permute-start(bf16[2,2816,128]{2,1,0:T(8,128)(2,1)} %slice.4), channel_id=1, source_target_pairs={{0,4},{4,0},{1,5},{5,1},{2,6},{6,2},{3,7},{7,3},{8,12},{12,8},{9,1... | collective-permute-start | bytes 4325384 | tf_op jit(solution)/shard_map/ppermute | solution.py:126
  7.8 2.6 copy-done
  10.4 2.0 swap1.1
  12.5 11.6 %psum.7.refs_1_ = f32[8,512]{1,0:T(8,128)S(1)} all-reduce(f32[8,512]{1,0:T(8,128)S(1)} %get-tuple-element.131), channel_id=1, replica_groups=mesh['cell'=4,'spot'=2,'gene'=4] {'cell'}, use_global_device_ids=true, to_apply=%region_0.1 | all-reduce | flops 4096 | bytes 32768 | tf_op jit(solution)/shard_map/psum | solution.py:226
  25.7 2.6 collective-permute-start.1
  30.4 3.4 %collective-permute-done.2.refs_2_.refs_4_ = f32[8,512]{1,0:T(8,128)S(1)} collective-permute-done((f32[8,512]{1,0:T(8,128)S(1)}, f32[8,512]{1,0:T(8,128)S(1)}, u32[]{:S(2)}, u32[]{:S(2)}) %collective-permute-start.2) | collective-permute-done | bytes 16416 | tf_op jit(solution)/shard_map/ppermute | solution.py:123
  34.4 2.6 copy-done.1
  39.1 2.4 along0.1
  42.0 2.2 collective-permute-start.5
  45.7 2.6 collective-permute-start.6
  48.5 4.0 %prob.1 = (bf16[512,2816]{1,0:T(8,128)(2,1)S(1)}, f32[8,2816]{1,0:T(8,128)S(1)}, f32[8,512]{1,0:T(8,128)S(1)}, f32[8,512]{1,0:T(8,128)S(1)}, f32[8,128]{1,0:T(8,128)S(1)}) custom-call(s32[5]{0:T(128)S(1)} %stack.27.flags, bf16[2816,512]{1,0:T(8,128)(2,1)S(1)} %copy-done.2, f32[8,512]{1,0:T(8,128)S(1)} %psum.7.refs_1_, ...), custom_call_target="tpu_custom_call", output_to_operand_aliasing={{4}: (6, {})} | custom-call | tf_op jit(solution)/shard_map/prob/pallas_call | solution.py:65
  53.2 16.7 %collective-permute-done.9.refs_0_.refs_1_.refs_6_.refs_7_ = bf16[2,2816,128]{2,1,0:T(8,128)(2,1)} collective-permute-done((bf16[2,2816,128]{2,1,0:T(8,128)(2,1)}, bf16[2,2816,128]{2,1,0:T(8,128)(2,1)}, u32[]{:S(2)}, u32[]{:S(2)}) %collective-permute-start.9) | collective-permute-done | bytes 1441824 | tf_op jit(solution)/shard_map/ppermute | solution.py:126
  70.0 2.0 along1.1
  72.8 3.2 %collective-permute-done.7.refs_1_ = bf16[1408,128]{1,0:T(8,128)(2,1)S(1)} collective-permute-done((bf16[1408,128]{1,0:T(8,128)(2,1)S(1)}, bf16[1408,128]{1,0:T(8,128)(2,1)S(1)}, u32[]{:S(2)}, u32[]{:S(2)}) %collective-permute-start.7) | collective-permute-done | bytes 360480 | tf_op jit(solution)/shard_map/ppermute | solution.py:123
  77.1 2.0 collective-permute-start.12
  80.8 2.4 collective-permute-start.11
  83.1 17.6 %collective-permute-done.8.refs_0_.refs_1_.refs_6_.refs_7_.refs_2_ = bf16[2,2816,128]{2,1,0:T(8,128)(2,1)S(1)} collective-permute-done((bf16[2,2816,128]{2,1,0:T(8,128)(2,1)S(1)}, bf16[2,2816,128]{2,1,0:T(8,128)(2,1)S(1)}, u32[]{:S(2)}, u32[]{:S(2)}) %collective-permute-start.8) | collective-permute-done | bytes 1441824 | tf_op jit(solution)/shard_map/ppermute | solution.py:126
  101.7 8.3 %collective-permute-done.11.refs_1_ = bf16[1408,128]{1,0:T(8,128)(2,1)S(1)} collective-permute-done((bf16[1408,128]{1,0:T(8,128)(2,1)S(1)}, bf16[1408,128]{1,0:T(8,128)(2,1)S(1)}, u32[]{:S(2)}, u32[]{:S(2)}) %collective-permute-start.11) | collective-permute-done | bytes 360480 | tf_op jit(solution)/shard_map/ppermute | solution.py:123
  111.1 2.0 collective-permute-start.17
  116.8 14.8 %collective-permute-done.14.refs_0_.refs_1_.refs_6_.refs_7_.refs_2_ = bf16[2,2816,128]{2,1,0:T(8,128)(2,1)S(1)} collective-permute-done((bf16[2,2816,128]{2,1,0:T(8,128)(2,1)S(1)}, bf16[2,2816,128]{2,1,0:T(8,128)(2,1)S(1)}, u32[]{:S(2)}, u32[]{:S(2)}) %collective-permute-start.14) | collective-permute-done | bytes 1441824 | tf_op jit(solution)/shard_map/ppermute | solution.py:126
  132.6 6.5 %collective-permute-done.16.refs_1_ = bf16[1408,128]{1,0:T(8,128)(2,1)S(1)} collective-permute-done((bf16[1408,128]{1,0:T(8,128)(2,1)S(1)}, bf16[1408,128]{1,0:T(8,128)(2,1)S(1)}, u32[]{:S(2)}, u32[]{:S(2)}) %collective-permute-start.16) | collective-permute-done | bytes 360480 | tf_op jit(solution)/shard_map/ppermute | solution.py:123
  140.8 2.7 collective-permute-start.18
  145.4 2.5 collective-permute-start.20
  150.4 12.2 %collective-permute-done.18.refs_0_.refs_9_ = bf16[2,1408,128]{2,1,0:T(8,128)(2,1)S(1)} collective-permute-done((bf16[2,1408,128]{2,1,0:T(8,128)(2,1)S(1)}, bf16[2,1408,128]{2,1,0:T(8,128)(2,1)S(1)}, u32[]{:S(2)}, u32[]{:S(2)}) %collective-permute-start.18) | collective-permute-done | bytes 720928 | tf_op jit(solution)/shard_map/ppermute | solution.py:126
  163.1 5.0 %forward0.1 = (bf16[2816,512]{1,0:T(8,128)(2,1)S(1)}, bf16[2816,512]{1,0:T(8,128)(2,1)S(1)}, f32[2,128,1024]{2,1,0:T(8,128)S(1)}, f32[128,1024]{1,0:T(8,128)S(1)...) custom-call(s32[5]{0:T(128)S(1)} %stack.27.flags, ...), custom_call_target="tpu_custom_call", output_to_operand_aliasing={{5}: (11, {})} | custom-call | tf_op jit(solution)/shard_map/forward0/pallas_call | solution.py:65
  168.1 1.9 collective-permute-done.20.refs_1_
  178.5 3.0 %forward1.1 = (bf16[2816,512]{1,0:T(8,128)(2,1)S(1)}, f32[2,128,512]{2,1,0:T(8,128)S(1)}, f32[128,512]{1,0:T(8,128)S(1)}, f32[128,512]{1,0:T(8,128)S(1)}, f32[8,128]{1,0:T(8,128)S(1)}) custom-call(s32[5]{0:T(128)S(1)} %stack.27.flags, bf16[512,2816]{1,0:T(8,128)(2,1)S(1)} %get-tuple-element.142.refs_0_, ...), custom_call_target="tpu_custom_call", output_to_operand_aliasing={{4}: (7, {})} | custom-call | tf_op jit(solution)/shard_map/forward1/pallas_call | solution.py:65
  184.7 2.1 collective-permute-start.29
  186.8 2.4 forward2.1
  190.5 2.1 collective-permute-done.30.refs_1_
  194.5 2.8 collective-permute-start.28
  200.0 6.3 %collective-permute-done.33.refs_2_ = f32[136,512]{1,0:T(8,128)S(1)} collective-permute-done((f32[136,512]{1,0:T(8,128)S(1)}, f32[136,512]{1,0:T(8,128)S(1)}, u32[]{:S(2)}, u32[]{:S(2)}) %collective-permute-start.33) | collective-permute-done | bytes 278560 | tf_op jit(solution)/shard_map/ppermute | solution.py:120
  214.2 3.0 %collective-permute-done.4.refs_3_ = f32[8,2816]{1,0:T(8,128)S(1)} collective-permute-done((f32[8,2816]{1,0:T(8,128)S(1)}, f32[8,2816]{1,0:T(8,128)S(1)}, u32[]{:S(2)}, u32[]{:S(2)}) %collective-permute-start.4) | collective-permute-done | bytes 90144 | tf_op jit(solution)/shard_map/ppermute | solution.py:126
  218.3 2.2 collective-permute-done.36.refs_2_
  227.3 2.4 collective-permute-start.39
  232.0 3.2 %collective-permute-done.40.refs_3_.refs_7_ = f32[8,128]{1,0:T(8,128)S(1)} collective-permute-done((f32[8,128]{1,0:T(8,128)S(1)}, f32[8,128]{1,0:T(8,128)S(1)}, u32[]{:S(2)}, u32[]{:S(2)}) %collective-permute-start.40) | collective-permute-done | bytes 4128 | tf_op jit(solution)/shard_map/ppermute | solution.py:123
  237.2 2.4 collective-permute-start.48
  239.7 2.0 collective-permute-start.49
  243.1 2.2 collective-permute-done.50.refs_4_.refs_12_
  245.4 3.1 %collective-permute-done.48.refs_1_ = bf16[128,512]{1,0:T(8,128)(2,1)S(1)} collective-permute-done((bf16[128,512]{1,0:T(8,128)(2,1)S(1)}, bf16[128,512]{1,0:T(8,128)(2,1)S(1)}, u32[]{:S(2)}, u32[]{:S(2)}) %collective-permute-start.48) | collective-permute-done | bytes 131104 | tf_op jit(solution)/shard_map/ppermute | solution.py:123
  252.2 4.2 %own.1 = (f32[2816,512]{1,0:T(8,128)S(1)}, f32[8,128]{1,0:T(8,128)S(1)}) custom-call(s32[5]{0:T(128)S(1)} %stack.27.flags, f32[2816,128]{1,0:T(8,128)S(1)} %get-tuple-element.224.refs_0_, bf16[2816,512]{1,0:T(8,128)(2,1)S(1)} %get-tuple-element.225.refs_1_.refs_3_, ...), custom_call_target="tpu_custom_call", output_to_operand_aliasing={{1}: (10, {})} | custom-call | tf_op jit(solution)/shard_map/own/pallas_call | solution.py:65
  259.3 6.6 %backward.1 = (f32[2816,512]{1,0:T(8,128)S(1)}, f32[8,512]{1,0:T(8,128)S(1)}, f32[8,128]{1,0:T(8,128)S(1)}) custom-call(s32[5]{0:T(128)S(1)} %stack.27.flags, bf16[2816,512]{1,0:T(8,128)(2,1)S(1)} %copy-done.2, f32[8,512]{1,0:T(8,128)S(1)} %get-tuple-element.140.refs_1_, ...), custom_call_target="tpu_custom_call", output_to_operand_aliasing={{2}: (14, {})} | custom-call | tf_op jit(solution)/shard_map/backward/pallas_call | solution.py:65
  268.6 2.2 collective-permute-done.55
  270.9 3.4 %collective-permute-start.56 = (f32[8,512]{1,0:T(8,128)S(1)}, f32[8,512]{1,0:T(8,128)S(1)}, u32[]{:S(2)}, u32[]{:S(2)}) collective-permute-start(f32[8,512]{1,0:T(8,128)S(1)} %add.32), channel_id=1, source_target_pairs={{0,1},{1,0},{2,3},{3,2},{4,5},{5,4},{6,7},{7,6},{8,9},{9,8},{10,11... | collective-permute-start | bytes 49160 | tf_op jit(solution)/shard_map/ppermute | solution.py:123
  274.5 2.2 collective-permute-start.58
  276.7 2.2 collective-permute-done.57
  280.1 3.8 %final.1 = (f32[2816,512]{1,0:T(8,128)}, f32[5]{0:T(128)}, f32[8,128]{1,0:T(8,128)S(1)}) custom-call(s32[5]{0:T(128)S(1)} %stack.27.flags, bf16[2816,512]{1,0:T(8,128)(2,1)S(1)} %copy-done.2, f32[8,512]{1,0:T(8,128)S(1)} %get-tuple-element.140.refs_1_, f32[2816,512]{1,0:T(8,128)S(1)} %get-tuple-element.255.refs_2_, ...), custom_call_target="tpu_custom_call", output_to_operand_aliasing={{2}: (5, {})} | custom-call | tf_op jit(solution)/shard_map/final/pallas_call | solution.py:65
  (149 shorter events, 77.2 us)
Async XLA Ops:
  3.4 35.7 %collective-permute-start.3 = (bf16[2,2816,128]{2,1,0:T(8,128)(2,1)}, bf16[2,2816,128]{2,1,0:T(8,128)(2,1)}, u32[]{:S(2)}, u32[]{:S(2)}) collective-permute-start(bf16[2,2816,128]{2,1,0:T(8,128)(2,1)} %slice.4), channel_id=1, source_target_pairs={{0,4},{4,0},{1,5},{5,1},{2,6},{6,2},{3,7},{7,3},{8,12},{12,8},{9,1... | collective-permute-start | bytes 4325384 | tf_op jit(solution)/shard_map/ppermute | solution.py:126
  12.4 57.5 %collective-permute-start.9 = (bf16[2,2816,128]{2,1,0:T(8,128)(2,1)}, bf16[2,2816,128]{2,1,0:T(8,128)(2,1)}, u32[]{:S(2)}, u32[]{:S(2)}) collective-permute-start(bf16[2,2816,128]{2,1,0:T(8,128)(2,1)} %get-tuple-element.147), channel_id=1, source_target_pairs={{0,4},{4,0},{1,5},{5,1},{2,6},{6,2},{3,7},{7,3},{8,12},{12,8},{9,1... | collective-permute-start | bytes 4325384 | tf_op jit(solution)/shard_map/ppermute | solution.py:126
  24.1 4.4 %collective-permute-start = (f32[8,512]{1,0:T(8,128)S(1)}, f32[8,512]{1,0:T(8,128)S(1)}, u32[]{:S(2)}, u32[]{:S(2)}) collective-permute-start(f32[8,512]{1,0:T(8,128)S(1)} %psum.7.refs_1_), channel_id=1, source_target_pairs={{0,1},{1,0},{2,3},{3,2},{4,5},{5,4},{6,7},{7,6},{8,9},{9,8},{10,11... | collective-permute-start | bytes 49160 | tf_op jit(solution)/shard_map/ppermute | solution.py:123
  25.7 4.7 %collective-permute-start.1 = (f32[8,512]{1,0:T(8,128)S(1)}, f32[8,512]{1,0:T(8,128)S(1)}, u32[]{:S(2)}, u32[]{:S(2)}) collective-permute-start(f32[8,512]{1,0:T(8,128)S(1)} %psum.7.refs_1_), channel_id=1, source_target_pairs={{0,2},{1,3},{2,0},{3,1},{4,6},{5,7},{6,4},{7,5},{8,10},{9,11},{10,... | collective-permute-start | bytes 49160 | tf_op jit(solution)/shard_map/ppermute | solution.py:123
  28.3 5.5 %collective-permute-start.2 = (f32[8,512]{1,0:T(8,128)S(1)}, f32[8,512]{1,0:T(8,128)S(1)}, u32[]{:S(2)}, u32[]{:S(2)}) collective-permute-start(f32[8,512]{1,0:T(8,128)S(1)} %psum.7.refs_1_), channel_id=1, source_target_pairs={{0,3},{1,2},{2,1},{3,0},{4,7},{5,6},{6,5},{7,4},{8,11},{9,10},{10,... | collective-permute-start | bytes 49160 | tf_op jit(solution)/shard_map/ppermute | solution.py:123
  42.0 34.0 %collective-permute-start.5 = (bf16[2,1408,128]{2,1,0:T(8,128)(2,1)S(1)}, bf16[2,1408,128]{2,1,0:T(8,128)(2,1)S(1)}, u32[]{:S(2)}, u32[]{:S(2)}) collective-permute-start(bf16[2,1408,128]{2,1,0:T(8,128)(2,1)S(1)} %get-tuple-element.143), channel_id=1, source_target_pairs={{0,1},{1,0},{2,3},{3,2},{4,5},{5,4},{6,7},{7,6},{8,9},{9,8},{10,11... | collective-permute-start | bytes 2162696 | tf_op jit(solution)/shard_map/ppermute | solution.py:123
  44.2 56.5 %collective-permute-start.8 = (bf16[2,2816,128]{2,1,0:T(8,128)(2,1)S(1)}, bf16[2,2816,128]{2,1,0:T(8,128)(2,1)S(1)}, u32[]{:S(2)}, u32[]{:S(2)}) collective-permute-start(bf16[2,2816,128]{2,1,0:T(8,128)(2,1)S(1)} %get-tuple-element.146), channel_id=1, source_target_pairs={{0,4},{4,0},{1,5},{5,1},{2,6},{6,2},{3,7},{7,3},{8,12},{12,8},{9,1... | collective-permute-start | bytes 4325384 | tf_op jit(solution)/shard_map/ppermute | solution.py:126
  45.7 27.1 %collective-permute-start.6 = (bf16[1408,128]{1,0:T(8,128)(2,1)S(1)}, bf16[1408,128]{1,0:T(8,128)(2,1)S(1)}, u32[]{:S(2)}, u32[]{:S(2)}) collective-permute-start(bf16[1408,128]{1,0:T(8,128)(2,1)S(1)} %get-tuple-element.144), channel_id=1, source_target_pairs={{0,2},{1,3},{2,0},{3,1},{4,6},{5,7},{6,4},{7,5},{8,10},{9,11},{10,... | collective-permute-start | bytes 1081352 | tf_op jit(solution)/shard_map/ppermute | solution.py:123
  48.3 27.7 %collective-permute-start.7 = (bf16[1408,128]{1,0:T(8,128)(2,1)S(1)}, bf16[1408,128]{1,0:T(8,128)(2,1)S(1)}, u32[]{:S(2)}, u32[]{:S(2)}) collective-permute-start(bf16[1408,128]{1,0:T(8,128)(2,1)S(1)} %get-tuple-element.145), channel_id=1, source_target_pairs={{0,3},{1,2},{2,1},{3,0},{4,7},{5,6},{6,5},{7,4},{8,11},{9,10},{10,... | collective-permute-start | bytes 1081352 | tf_op jit(solution)/shard_map/ppermute | solution.py:123
  77.1 32.8 %collective-permute-start.12 = (bf16[2,1408,128]{2,1,0:T(8,128)(2,1)S(1)}, bf16[2,1408,128]{2,1,0:T(8,128)(2,1)S(1)}, u32[]{:S(2)}, u32[]{:S(2)}) collective-permute-start(bf16[2,1408,128]{2,1,0:T(8,128)(2,1)S(1)} %get-tuple-element.161), channel_id=1, source_target_pairs={{0,1},{1,0},{2,3},{3,2},{4,5},{5,4},{6,7},{7,6},{8,9},{9,8},{10,11... | collective-permute-start | bytes 2162696 | tf_op jit(solution)/shard_map/ppermute | solution.py:123
  79.1 52.5 %collective-permute-start.14 = (bf16[2,2816,128]{2,1,0:T(8,128)(2,1)S(1)}, bf16[2,2816,128]{2,1,0:T(8,128)(2,1)S(1)}, u32[]{:S(2)}, u32[]{:S(2)}) collective-permute-start(bf16[2,2816,128]{2,1,0:T(8,128)(2,1)S(1)} %get-tuple-element.165), channel_id=1, source_target_pairs={{0,4},{4,0},{1,5},{5,1},{2,6},{6,2},{3,7},{7,3},{8,12},{12,8},{9,1... | collective-permute-start | bytes 4325384 | tf_op jit(solution)/shard_map/ppermute | solution.py:126
  79.6 22.0 %collective-permute-start.10 = (bf16[1408,128]{1,0:T(8,128)(2,1)S(1)}, bf16[1408,128]{1,0:T(8,128)(2,1)S(1)}, u32[]{:S(2)}, u32[]{:S(2)}) collective-permute-start(bf16[1408,128]{1,0:T(8,128)(2,1)S(1)} %get-tuple-element.159), channel_id=1, source_target_pairs={{0,2},{1,3},{2,0},{3,1},{4,6},{5,7},{6,4},{7,5},{8,10},{9,11},{10,... | collective-permute-start | bytes 1081352 | tf_op jit(solution)/shard_map/ppermute | solution.py:123
  80.8 29.2 %collective-permute-start.11 = (bf16[1408,128]{1,0:T(8,128)(2,1)S(1)}, bf16[1408,128]{1,0:T(8,128)(2,1)S(1)}, u32[]{:S(2)}, u32[]{:S(2)}) collective-permute-start(bf16[1408,128]{1,0:T(8,128)(2,1)S(1)} %get-tuple-element.160), channel_id=1, source_target_pairs={{0,3},{1,2},{2,1},{3,0},{4,7},{5,6},{6,5},{7,4},{8,11},{9,10},{10,... | collective-permute-start | bytes 1081352 | tf_op jit(solution)/shard_map/ppermute | solution.py:123
  111.1 28.0 %collective-permute-start.17 = (bf16[2,1408,128]{2,1,0:T(8,128)(2,1)S(1)}, bf16[2,1408,128]{2,1,0:T(8,128)(2,1)S(1)}, u32[]{:S(2)}, u32[]{:S(2)}) collective-permute-start(bf16[2,1408,128]{2,1,0:T(8,128)(2,1)S(1)} %get-tuple-element.172), channel_id=1, source_target_pairs={{0,1},{1,0},{2,3},{3,2},{4,5},{5,4},{6,7},{7,6},{8,9},{9,8},{10,11... | collective-permute-start | bytes 2162696 | tf_op jit(solution)/shard_map/ppermute | solution.py:123
  113.1 19.4 %collective-permute-start.15 = (bf16[1408,128]{1,0:T(8,128)(2,1)S(1)}, bf16[1408,128]{1,0:T(8,128)(2,1)S(1)}, u32[]{:S(2)}, u32[]{:S(2)}) collective-permute-start(bf16[1408,128]{1,0:T(8,128)(2,1)S(1)} %get-tuple-element.170), channel_id=1, source_target_pairs={{0,2},{1,3},{2,0},{3,1},{4,6},{5,7},{6,4},{7,5},{8,10},{9,11},{10,... | collective-permute-start | bytes 1081352 | tf_op jit(solution)/shard_map/ppermute | solution.py:123
  113.8 25.3 %collective-permute-start.16 = (bf16[1408,128]{1,0:T(8,128)(2,1)S(1)}, bf16[1408,128]{1,0:T(8,128)(2,1)S(1)}, u32[]{:S(2)}, u32[]{:S(2)}) collective-permute-start(bf16[1408,128]{1,0:T(8,128)(2,1)S(1)} %get-tuple-element.171), channel_id=1, source_target_pairs={{0,3},{1,2},{2,1},{3,0},{4,7},{5,6},{6,5},{7,4},{8,11},{9,10},{10,... | collective-permute-start | bytes 1081352 | tf_op jit(solution)/shard_map/ppermute | solution.py:123
  116.2 31.7 %collective-permute-start.13 = (bf16[2,1408,128]{2,1,0:T(8,128)(2,1)S(1)}, bf16[2,1408,128]{2,1,0:T(8,128)(2,1)S(1)}, u32[]{:S(2)}, u32[]{:S(2)}) collective-permute-start(bf16[2,1408,128]{2,1,0:T(8,128)(2,1)S(1)} %get-tuple-element.164.refs_4_), channel_id=1, source_target_pairs={{0,4},{4,0},{1,5},{5,1},{2,6},{6,2},{3,7},{7,3},{8,12},{12,8},{9,1... | collective-permute-start | bytes 2162696 | tf_op jit(solution)/shard_map/ppermute | solution.py:126
  140.8 21.8 %collective-permute-start.18 = (bf16[2,1408,128]{2,1,0:T(8,128)(2,1)S(1)}, bf16[2,1408,128]{2,1,0:T(8,128)(2,1)S(1)}, u32[]{:S(2)}, u32[]{:S(2)}) collective-permute-start(bf16[2,1408,128]{2,1,0:T(8,128)(2,1)S(1)} %get-tuple-element.175.refs_8_), channel_id=1, source_target_pairs={{0,4},{4,0},{1,5},{5,1},{2,6},{6,2},{3,7},{7,3},{8,12},{12,8},{9,1... | collective-permute-start | bytes 2162696 | tf_op jit(solution)/shard_map/ppermute | solution.py:126
  143.5 26.5 %collective-permute-start.21 = (bf16[2,1408,128]{2,1,0:T(8,128)(2,1)S(1)}, bf16[2,1408,128]{2,1,0:T(8,128)(2,1)S(1)}, u32[]{:S(2)}, u32[]{:S(2)}) collective-permute-start(bf16[2,1408,128]{2,1,0:T(8,128)(2,1)S(1)} %get-tuple-element.183), channel_id=1, source_target_pairs={{0,1},{1,0},{2,3},{3,2},{4,5},{5,4},{6,7},{7,6},{8,9},{9,8},{10,11... | collective-permute-start | bytes 2162696 | tf_op jit(solution)/shard_map/ppermute | solution.py:123
  144.1 23.9 %collective-permute-start.19 = (bf16[1408,128]{1,0:T(8,128)(2,1)S(1)}, bf16[1408,128]{1,0:T(8,128)(2,1)S(1)}, u32[]{:S(2)}, u32[]{:S(2)}) collective-permute-start(bf16[1408,128]{1,0:T(8,128)(2,1)S(1)} %get-tuple-element.181), channel_id=1, source_target_pairs={{0,2},{1,3},{2,0},{3,1},{4,6},{5,7},{6,4},{7,5},{8,10},{9,11},{10,... | collective-permute-start | bytes 1081352 | tf_op jit(solution)/shard_map/ppermute | solution.py:123
  145.4 24.6 %collective-permute-start.20 = (bf16[1408,128]{1,0:T(8,128)(2,1)S(1)}, bf16[1408,128]{1,0:T(8,128)(2,1)S(1)}, u32[]{:S(2)}, u32[]{:S(2)}) collective-permute-start(bf16[1408,128]{1,0:T(8,128)(2,1)S(1)} %get-tuple-element.182), channel_id=1, source_target_pairs={{0,3},{1,2},{2,1},{3,0},{4,7},{5,6},{6,5},{7,4},{8,11},{9,10},{10,... | collective-permute-start | bytes 1081352 | tf_op jit(solution)/shard_map/ppermute | solution.py:123
  149.0 29.0 %collective-permute-start.25 = (bf16[2,1408,128]{2,1,0:T(8,128)(2,1)S(1)}, bf16[2,1408,128]{2,1,0:T(8,128)(2,1)S(1)}, u32[]{:S(2)}, u32[]{:S(2)}) collective-permute-start(bf16[2,1408,128]{2,1,0:T(8,128)(2,1)S(1)} %get-tuple-element.192.refs_4_), channel_id=1, source_target_pairs={{0,4},{4,0},{1,5},{5,1},{2,6},{6,2},{3,7},{7,3},{8,12},{12,8},{9,1... | collective-permute-start | bytes 2162696 | tf_op jit(solution)/shard_map/ppermute | solution.py:126
  172.2 20.4 %collective-permute-start.30 = (bf16[2,1408,128]{2,1,0:T(8,128)(2,1)S(1)}, bf16[2,1408,128]{2,1,0:T(8,128)(2,1)S(1)}, u32[]{:S(2)}, u32[]{:S(2)}) collective-permute-start(bf16[2,1408,128]{2,1,0:T(8,128)(2,1)S(1)} %get-tuple-element.191.refs_4_), channel_id=1, source_target_pairs={{0,4},{4,0},{1,5},{5,1},{2,6},{6,2},{3,7},{7,3},{8,12},{12,8},{9,1... | collective-permute-start | bytes 2162696 | tf_op jit(solution)/shard_map/ppermute | solution.py:126
  175.1 14.8 %collective-permute-start.24 = (f32[128,1024]{1,0:T(8,128)S(1)}, f32[128,1024]{1,0:T(8,128)S(1)}, u32[]{:S(2)}, u32[]{:S(2)}) collective-permute-start(f32[128,1024]{1,0:T(8,128)S(1)} %get-tuple-element.190), channel_id=1, source_target_pairs={{0,16},{8,24},{16,0},{24,8},{1,17},{9,25},{17,1},{25,9},{2,18},{10... | collective-permute-start | bytes 1572872 | tf_op jit(solution)/shard_map/ppermute | solution.py:120
  184.7 14.8 %collective-permute-start.29 = (f32[136,512]{1,0:T(8,128)S(1)}, f32[136,512]{1,0:T(8,128)S(1)}, u32[]{:S(2)}, u32[]{:S(2)}) collective-permute-start(f32[136,512]{1,0:T(8,128)S(1)} %get-tuple-element.207), channel_id=1, source_target_pairs={{0,16},{8,24},{16,0},{24,8},{1,17},{9,25},{17,1},{25,9},{2,18},{10... | collective-permute-start | bytes 835592 | tf_op jit(solution)/shard_map/ppermute | solution.py:120
  194.5 16.9 %collective-permute-start.28 = (f32[2,136,256]{2,1,0:T(8,128)S(1)}, f32[2,136,256]{2,1,0:T(8,128)S(1)}, u32[]{:S(2)}, u32[]{:S(2)}) collective-permute-start(f32[2,136,256]{2,1,0:T(8,128)S(1)} %get-tuple-element.205), channel_id=1, source_target_pairs={{0,2},{1,3},{2,0},{3,1},{4,6},{5,7},{6,4},{7,5},{8,10},{9,11},{10,... | collective-permute-start | bytes 835592 | tf_op jit(solution)/shard_map/ppermute | solution.py:123
  197.9 8.4 %collective-permute-start.33 = (f32[136,512]{1,0:T(8,128)S(1)}, f32[136,512]{1,0:T(8,128)S(1)}, u32[]{:S(2)}, u32[]{:S(2)}) collective-permute-start(f32[136,512]{1,0:T(8,128)S(1)} %get-tuple-element.220), channel_id=1, source_target_pairs={{0,16},{8,24},{16,0},{24,8},{1,17},{9,25},{17,1},{25,9},{2,18},{10... | collective-permute-start | bytes 835592 | tf_op jit(solution)/shard_map/ppermute | solution.py:120
  206.9 11.4 %collective-permute-start.35 = (f32[128,256]{1,0:T(8,128)S(1)}, f32[128,256]{1,0:T(8,128)S(1)}, u32[]{:S(2)}, u32[]{:S(2)}) collective-permute-start(f32[128,256]{1,0:T(8,128)S(1)} %get-tuple-element.235), channel_id=1, source_target_pairs={{0,1},{1,0},{2,3},{3,2},{4,5},{5,4},{6,7},{7,6},{8,9},{9,8},{10,11... | collective-permute-start | bytes 393224 | tf_op jit(solution)/shard_map/ppermute | solution.py:123
  208.6 12.0 %collective-permute-start.36 = (f32[128,256]{1,0:T(8,128)S(1)}, f32[128,256]{1,0:T(8,128)S(1)}, u32[]{:S(2)}, u32[]{:S(2)}) collective-permute-start(f32[128,256]{1,0:T(8,128)S(1)} %get-tuple-element.236), channel_id=1, source_target_pairs={{0,2},{1,3},{2,0},{3,1},{4,6},{5,7},{6,4},{7,5},{8,10},{9,11},{10,... | collective-permute-start | bytes 393224 | tf_op jit(solution)/shard_map/ppermute | solution.py:123
  210.3 10.2 %collective-permute-start.37 = (f32[128,256]{1,0:T(8,128)S(1)}, f32[128,256]{1,0:T(8,128)S(1)}, u32[]{:S(2)}, u32[]{:S(2)}) collective-permute-start(f32[128,256]{1,0:T(8,128)S(1)} %get-tuple-element.237), channel_id=1, source_target_pairs={{0,3},{1,2},{2,1},{3,0},{4,7},{5,6},{6,5},{7,4},{8,11},{9,10},{10,... | collective-permute-start | bytes 393224 | tf_op jit(solution)/shard_map/ppermute | solution.py:123
  212.0 9.4 %collective-permute-start.34 = (f32[128,256]{1,0:T(8,128)S(1)}, f32[128,256]{1,0:T(8,128)S(1)}, u32[]{:S(2)}, u32[]{:S(2)}) collective-permute-start(f32[128,256]{1,0:T(8,128)S(1)} %get-tuple-element.233), channel_id=1, source_target_pairs={{0,1},{1,0},{2,3},{3,2},{4,5},{5,4},{6,7},{7,6},{8,9},{9,8},{10,11... | collective-permute-start | bytes 393224 | tf_op jit(solution)/shard_map/ppermute | solution.py:123
  212.7 4.5 %collective-permute-start.4 = (f32[8,2816]{1,0:T(8,128)S(1)}, f32[8,2816]{1,0:T(8,128)S(1)}, u32[]{:S(2)}, u32[]{:S(2)}) collective-permute-start(f32[8,2816]{1,0:T(8,128)S(1)} %get-tuple-element.141.refs_2_), channel_id=1, source_target_pairs={{0,4},{4,0},{1,5},{5,1},{2,6},{6,2},{3,7},{7,3},{8,12},{12,8},{9,1... | collective-permute-start | bytes 270344 | tf_op jit(solution)/shard_map/ppermute | solution.py:126
  224.2 6.2 %collective-permute-start.42 = (f32[16,512]{1,0:T(8,128)S(1)}, f32[16,512]{1,0:T(8,128)S(1)}, u32[]{:S(2)}, u32[]{:S(2)}) collective-permute-start(f32[16,512]{1,0:T(8,128)S(1)} %add.29), channel_id=1, source_target_pairs={{0,16},{8,24},{16,0},{24,8},{1,17},{9,25},{17,1},{25,9},{2,18},{10... | collective-permute-start | bytes 98312 | tf_op jit(solution)/shard_map/ppermute | solution.py:120
  225.7 6.3 %collective-permute-start.38 = (f32[8,128]{1,0:T(8,128)S(1)}, f32[8,128]{1,0:T(8,128)S(1)}, u32[]{:S(2)}, u32[]{:S(2)}) collective-permute-start(f32[8,128]{1,0:T(8,128)S(1)} %get-tuple-element.243.refs_0_.refs_4_), channel_id=1, source_target_pairs={{0,1},{1,0},{2,3},{3,2},{4,5},{5,4},{6,7},{7,6},{8,9},{9,8},{10,11... | collective-permute-start | bytes 12296 | tf_op jit(solution)/shard_map/ppermute | solution.py:123
  227.3 4.6 %collective-permute-start.39 = (f32[8,128]{1,0:T(8,128)S(1)}, f32[8,128]{1,0:T(8,128)S(1)}, u32[]{:S(2)}, u32[]{:S(2)}) collective-permute-start(f32[8,128]{1,0:T(8,128)S(1)} %get-tuple-element.243.refs_0_.refs_4_), channel_id=1, source_target_pairs={{0,2},{1,3},{2,0},{3,1},{4,6},{5,7},{6,4},{7,5},{8,10},{9,11},{10,... | collective-permute-start | bytes 12296 | tf_op jit(solution)/shard_map/ppermute | solution.py:123
  229.8 5.4 %collective-permute-start.40 = (f32[8,128]{1,0:T(8,128)S(1)}, f32[8,128]{1,0:T(8,128)S(1)}, u32[]{:S(2)}, u32[]{:S(2)}) collective-permute-start(f32[8,128]{1,0:T(8,128)S(1)} %get-tuple-element.243.refs_0_.refs_4_), channel_id=1, source_target_pairs={{0,3},{1,2},{2,1},{3,0},{4,7},{5,6},{6,5},{7,4},{8,11},{9,10},{10,... | collective-permute-start | bytes 12296 | tf_op jit(solution)/shard_map/ppermute | solution.py:123
  230.4 5.3 %collective-permute-start.43 = (f32[16,512]{1,0:T(8,128)S(1)}, f32[16,512]{1,0:T(8,128)S(1)}, u32[]{:S(2)}, u32[]{:S(2)}) collective-permute-start(f32[16,512]{1,0:T(8,128)S(1)} %add.30.refs_8_), channel_id=1, source_target_pairs={{0,4},{4,0},{1,5},{5,1},{2,6},{6,2},{3,7},{7,3},{8,12},{12,8},{9,1... | collective-permute-start | bytes 98312 | tf_op jit(solution)/shard_map/ppermute | solution.py:126
  236.6 8.7 %collective-permute-start.45 = (bf16[128,512]{1,0:T(8,128)(2,1)S(1)}, bf16[128,512]{1,0:T(8,128)(2,1)S(1)}, u32[]{:S(2)}, u32[]{:S(2)}) collective-permute-start(bf16[128,512]{1,0:T(8,128)(2,1)S(1)} %get-tuple-element.246.refs_5_), channel_id=1, source_target_pairs={{0,16},{8,24},{16,0},{24,8},{1,17},{9,25},{17,1},{25,9},{2,18},{10... | collective-permute-start | bytes 393224 | tf_op jit(solution)/shard_map/ppermute | solution.py:120
  237.2 8.1 %collective-permute-start.47 = (bf16[128,512]{1,0:T(8,128)(2,1)S(1)}, bf16[128,512]{1,0:T(8,128)(2,1)S(1)}, u32[]{:S(2)}, u32[]{:S(2)}) collective-permute-start(bf16[128,512]{1,0:T(8,128)(2,1)S(1)} %get-tuple-element.246.refs_5_), channel_id=1, source_target_pairs={{0,1},{1,0},{2,3},{3,2},{4,5},{5,4},{6,7},{7,6},{8,9},{9,8},{10,11... | collective-permute-start | bytes 393224 | tf_op jit(solution)/shard_map/ppermute | solution.py:123
  237.2 11.3 %collective-permute-start.48 = (bf16[128,512]{1,0:T(8,128)(2,1)S(1)}, bf16[128,512]{1,0:T(8,128)(2,1)S(1)}, u32[]{:S(2)}, u32[]{:S(2)}) collective-permute-start(bf16[128,512]{1,0:T(8,128)(2,1)S(1)} %get-tuple-element.246.refs_5_), channel_id=1, source_target_pairs={{0,2},{1,3},{2,0},{3,1},{4,6},{5,7},{6,4},{7,5},{8,10},{9,11},{10,... | collective-permute-start | bytes 393224 | tf_op jit(solution)/shard_map/ppermute | solution.py:123
  239.7 8.9 %collective-permute-start.49 = (bf16[128,512]{1,0:T(8,128)(2,1)S(1)}, bf16[128,512]{1,0:T(8,128)(2,1)S(1)}, u32[]{:S(2)}, u32[]{:S(2)}) collective-permute-start(bf16[128,512]{1,0:T(8,128)(2,1)S(1)} %get-tuple-element.246.refs_5_), channel_id=1, source_target_pairs={{0,3},{1,2},{2,1},{3,0},{4,7},{5,6},{6,5},{7,4},{8,11},{9,10},{10,... | collective-permute-start | bytes 393224 | tf_op jit(solution)/shard_map/ppermute | solution.py:123
  241.6 3.7 %collective-permute-start.50 = (f32[8,512]{1,0:T(8,128)S(1)}, f32[8,512]{1,0:T(8,128)S(1)}, u32[]{:S(2)}, u32[]{:S(2)}) collective-permute-start(f32[8,512]{1,0:T(8,128)S(1)} %get-tuple-element.247.refs_11_), channel_id=1, source_target_pairs={{0,4},{4,0},{1,5},{5,1},{2,6},{6,2},{3,7},{7,3},{8,12},{12,8},{9,1... | collective-permute-start | bytes 49160 | tf_op jit(solution)/shard_map/ppermute | solution.py:126
  249.1 7.8 %collective-permute-start.52 = (bf16[3,128,512]{2,1,0:T(8,128)(2,1)S(1)}, bf16[3,128,512]{2,1,0:T(8,128)(2,1)S(1)}, u32[]{:S(2)}, u32[]{:S(2)}) collective-permute-start(bf16[3,128,512]{2,1,0:T(8,128)(2,1)S(1)} %get-tuple-element.251.refs_7_), channel_id=1, source_target_pairs={{0,16},{8,24},{16,0},{24,8},{1,17},{9,25},{17,1},{25,9},{2,18},{10... | collective-permute-start | bytes 1179656 | tf_op jit(solution)/shard_map/ppermute | solution.py:120
  251.2 6.4 %collective-permute-start.51 = (bf16[3,128,512]{2,1,0:T(8,128)(2,1)S(1)}, bf16[3,128,512]{2,1,0:T(8,128)(2,1)S(1)}, u32[]{:S(2)}, u32[]{:S(2)}) collective-permute-start(bf16[3,128,512]{2,1,0:T(8,128)(2,1)S(1)} %get-tuple-element.251.refs_7_), channel_id=1, source_target_pairs={{0,8},{8,0},{16,24},{24,16},{1,9},{9,1},{17,25},{25,17},{2,10},{10... | collective-permute-start | bytes 1179656 | tf_op jit(solution)/shard_map/ppermute | solution.py:117
  267.1 3.7 %collective-permute-start.55 = (f32[8,512]{1,0:T(8,128)S(1)}, f32[8,512]{1,0:T(8,128)S(1)}, u32[]{:S(2)}, u32[]{:S(2)}) collective-permute-start(f32[8,512]{1,0:T(8,128)S(1)} %add.31), channel_id=1, source_target_pairs={{0,16},{8,24},{16,0},{24,8},{1,17},{9,25},{17,1},{25,9},{2,18},{10... | collective-permute-start | bytes 49160 | tf_op jit(solution)/shard_map/ppermute | solution.py:120
  270.9 5.8 %collective-permute-start.56 = (f32[8,512]{1,0:T(8,128)S(1)}, f32[8,512]{1,0:T(8,128)S(1)}, u32[]{:S(2)}, u32[]{:S(2)}) collective-permute-start(f32[8,512]{1,0:T(8,128)S(1)} %add.32), channel_id=1, source_target_pairs={{0,1},{1,0},{2,3},{3,2},{4,5},{5,4},{6,7},{7,6},{8,9},{9,8},{10,11... | collective-permute-start | bytes 49160 | tf_op jit(solution)/shard_map/ppermute | solution.py:123
  274.3 4.6 %collective-permute-start.57 = (f32[8,512]{1,0:T(8,128)S(1)}, f32[8,512]{1,0:T(8,128)S(1)}, u32[]{:S(2)}, u32[]{:S(2)}) collective-permute-start(f32[8,512]{1,0:T(8,128)S(1)} %add.32), channel_id=1, source_target_pairs={{0,2},{1,3},{2,0},{3,1},{4,6},{5,7},{6,4},{7,5},{8,10},{9,11},{10,... | collective-permute-start | bytes 49160 | tf_op jit(solution)/shard_map/ppermute | solution.py:123
  274.5 5.5 %collective-permute-start.58 = (f32[8,512]{1,0:T(8,128)S(1)}, f32[8,512]{1,0:T(8,128)S(1)}, u32[]{:S(2)}, u32[]{:S(2)}) collective-permute-start(f32[8,512]{1,0:T(8,128)S(1)} %add.32), channel_id=1, source_target_pairs={{0,3},{1,2},{2,1},{3,0},{4,7},{5,6},{6,5},{7,4},{8,11},{9,10},{10,... | collective-permute-start | bytes 49160 | tf_op jit(solution)/shard_map/ppermute | solution.py:123
  (20 other events, 133.5 us)

commit v8 on v7

--- a/solution.py
+++ b/solution.py
@@ -12,6 +12,7 @@
 ANY = pl.BlockSpec(memory_space=pl.ANY)
 BF = jnp.bfloat16
 F32 = jnp.float32
+SHARED = (0, 0, 0, 256)
 VMEM_BYTES = 14 * 1024 * 1024
 COSTS = {"spots": 1, "back3": 1, "waits2": 3, "addx1": 9, "half0": 3}
 WIDTHS = (128, 128, 128, 128)
@@ -103,7 +104,6 @@
     genes_all = genes * sizes["gene"]
     slots = sizes["gene"]
     quarter = spots // sizes["cell"]
-    half = rows // 2
     cell, spot, gene = (lax.axis_index(a) for a in ("cell", "spot", "gene"))
     home = (gene // 2 == spot).astype(jnp.int32)
     side = (gene % 2).astype(jnp.int32)
@@ -135,7 +135,7 @@
     ids_row, mask_row = slide_ids.reshape(1, spots), spot_mask.reshape(1, spots)
     dens_row = densities.reshape(1, rows)
 
-    expr = expression.reshape(2, half * 2, genes) if spot_size == 2 else None
+    expr = expression.reshape(2, rows, genes) if spot_size == 2 else None
     st, sent = {}, {}
 
     def start_swap(c):
@@ -154,50 +154,58 @@
         )
         sent[f"y{c}"] = over_spot(v)
 
+    def parted(c):
+        lone = (rows - SHARED[c]) // 2
+        return lone, lone + SHARED[c]
+
     def start_along(c):
-        w, o = WIDTHS[c], offsets[c] // WIDTHS[c]
-        blk, one = (1, half, w), (half, w)
+        w = WIDTHS[c]
+        cols, (_, far) = pl.ds(offsets[c], w), parted(c)
+
+        def body(fl, i, out, sems):
+            y, e = i
+            at_home, away = fl[0] == 1, fl[0] == 0
+            same, other = fl[1], 1 - fl[1]
+            first, last = pl.ds(0, far), pl.ds(rows - far, far)
+            copies = [
+                (at_home, y.at[same, first, :], out[0]),
+                (at_home, y.at[other, first, :], out[1]),
+                (at_home, e.at[other, :, cols], out[2]),
+                (away, e.at[same, last, cols], out[0]),
+                (away, e.at[other, last, cols], out[1]),
+                (away, y.at[other], out[2]),
+            ]
+            copy_all(copies, sems)
+
+        shapes = ((far, w), (far, w), (rows, w))
+        st["along", c] = run(
+            f"along{c}", body, [(sent[f"y{c}"], ANY), (expr, ANY)], [(sds(v, BF), whole(v)) for v in shapes],
+            scratch=[pltpu.SemaphoreType.DMA((6,))],
+        )
+
+    def along_send(c):
+        a, b, n = run(f"alongsend{c}", None, through=st["along", c])
+        sent[f"f2{c}"], sent[f"f3{c}"], sent[f"n{c}"] = over_gene(a, 2), over_gene(b, 3), over_gene(n, 1)
+
+    def start_back(c):
+        w = WIDTHS[c]
+        lone, far = parted(c)
 
         def body(fl, i, out):
             @pl.when(fl[0] == 1)
             def _():
-                out[0][...] = i[0][0]
-                out[1][...] = i[1][0]
-                out[2][0] = i[2][0]
-                out[2][1] = i[3][0]
+                for n in (0, 1):
+                    out[0][n] = i[n][far - lone :, :]
 
             @pl.when(fl[0] == 0)
             def _():
-                out[0][...] = i[4][0]
-                out[1][...] = i[5][0]
-                out[2][0] = i[6][0]
-                out[2][1] = i[7][0]
-
-        def at(same, part, col):
-            return pl.BlockSpec(blk, lambda g, f: (f[1] if same else 1 - f[1], part, col))
-
-        y = sent[f"y{c}"]
-        ins = [(y, at(True, 0, 0)), (y, at(False, 0, 0)), (expr, at(False, 0, o)), (expr, at(False, 1, o))]
-        ins += [(expr, at(True, 1, o)), (expr, at(False, 1, o)), (y, at(False, 0, 0)), (y, at(False, 1, 0))]
-        outs = [(sds(one, BF), whole(one))] * 2 + [(sds((2, half, w), BF), whole((2, half, w)))]
-        st["along", c] = run(f"along{c}", body, ins, outs)
-
-    def along_send(c):
-        a, b, n = run(f"alongsend{c}", None, through=st["along", c])
-        sent[f"f2{c}"], sent[f"f3{c}"], sent[f"n{c}"] = over_gene(a, 2), over_gene(b, 3), over_gene(n, 1)
-
-    def start_back(c):
-        w = WIDTHS[c]
-
-        def body(fl, i, out):
-            out[0][0] = i[0][...]
-            out[0][1] = i[1][...]
-
-        one = whole((half, w))
-        (st["f", c],) = run(
-            f"back{c}", body, [(sent[f"f2{c}"], one), (sent[f"f3{c}"], one)], [(sds((2, half, w), BF), whole((2, half, w)))],
-        )
-        sent[f"s{c}"] = over_spot(st["f", c])
+                for n in (0, 1):
+                    out[0][n] = i[n][:lone, :]
+
+        shape = (2, lone, w)
+        ins = [(sent[f"f{n}{c}"], whole((far, w))) for n in (2, 3)]
+        (v,) = run(f"back{c}", body, ins, [(sds(shape, BF), whole(shape))])
+        sent[f"s{c}"] = over_spot(v)
 
     def wait_for(name):
         run("wait" + name.split("+")[0], None, after=[sent[n] for n in name.split("+")])
@@ -306,7 +314,8 @@
                 w = WIDTHS[c]
                 if c == late:
                     near = jnp.dot(pt[...], ef[:, : 2 * w], preferred_element_type=F32)
-                    at = pl.ds(pl.multiple_of(direct, LANES), half)
+                    lone, size = parted(c)
+                    at = pl.ds(pl.multiple_of(direct * lone, LANES), size)
                     far = jnp.dot(pt[:, at], ef[at, 2 * w :], preferred_element_type=F32)
                     acc = jnp.concatenate([near, far], axis=1)
                 else:
@@ -323,31 +332,32 @@
             def body(fl, i, out, sems):
                 pt, e = i[:2]
                 at_home, away = fl[0] == 1, fl[0] == 0
-                top, low = pl.ds(0, half), pl.ds(half, half)
                 copies = []
                 for m, c in enumerate(members):
                     w, ef = WIDTHS[c], out[m]
-                    y, n, f = i[2 + 4 * m : 5 + 4 * m]
+                    y, n, f2, f3 = i[2 + 5 * m : 6 + 5 * m]
+                    lone, far = parted(c)
+                    top, low = pl.ds(0, lone), pl.ds(rows - lone, lone)
+                    first, last = pl.ds(0, far), pl.ds(rows - far, far)
                     copies += [
                         (at_home, e.at[fl[1], :, pl.ds(offsets[c], w)], ef.at[:, pl.ds(0, w)]),
                         (away, y.at[fl[1]], ef.at[:, pl.ds(0, w)]),
-                        (None, n.at[0], ef.at[top, pl.ds(w, w)]),
-                        (None, n.at[1], ef.at[low, pl.ds(w, w)]),
+                        (None, n, ef.at[:, pl.ds(w, w)]),
                     ]
-                    for part in (0, 1):
+                    for part, f in enumerate((f2, f3)):
                         cols = pl.ds((2 + part) * w, w)
-                        copies += [(at_home, f.at[part], ef.at[low, cols]), (away, f.at[part], ef.at[top, cols])]
+                        copies += [(at_home, f, ef.at[last, cols]), (away, f, ef.at[first, cols])]
                         if c != late:
-                            s = i[5 + 4 * m]
+                            s = i[6 + 5 * m]
                             copies += [(at_home, s.at[part], ef.at[top, cols]), (away, s.at[part], ef.at[low, cols])]
                 copy_all(copies, sems)
-                product(pt, out[: len(members)], *out[len(members) :], direct=fl[0] * half)
+                product(pt, out[: len(members)], *out[len(members) :], direct=fl[0])
 
             ins = [(st["pt"], whole((spots, rows))), (expr, ANY)]
             ins += [
                 (a, ANY)
                 for c in members
-                for a in (sent[f"y{c}"], sent[f"n{c}"], st["f", c], *([] if c == late else [sent[f"s{c}"]]))
+                for a in (*(sent[f"{k}{c}"] for k in ("y", "n", "f2", "f3")), *([] if c == late else [sent[f"s{c}"]]))
             ]
             scratch = [pltpu.SemaphoreType.DMA((12 * len(members),))]
         else:
@@ -372,11 +382,11 @@
     def forward_late(g):
         c = GROUPS[g][-1]
         w, wide = WIDTHS[c], slots * group_width[g]
-        shape = (2, quarter, wide)
+        shape, lone = (2, quarter, wide), parted(c)[0]
 
         def body(fl, i, out, sems):
             pt, swapped, keep, low, high = i
-            at = pl.ds(pl.multiple_of((1 - fl[0]) * half, LANES), half)
+            at = pl.ds(pl.multiple_of((1 - fl[0]) * (rows - lone), LANES), lone)
             copy_all([(None, swapped.at[n], out[3].at[at, pl.ds((2 + n) * w, w)]) for n in (0, 1)], sems)
             both = jnp.concatenate([swapped[0], swapped[1]], axis=1)
             acc = jnp.dot(pt[:, at], both, preferred_element_type=F32)
@@ -388,7 +398,7 @@
                     ref[:, base : base + w] += acc[q * quarter : (q + 1) * quarter, n * w : (n + 1) * w]
 
         one = whole((quarter, wide))
-        ins = [(st["pt"], whole((spots, rows))), (sent[f"s{c}"], whole((2, half, w)))]
+        ins = [(st["pt"], whole((spots, rows))), (sent[f"s{c}"], whole((2, lone, w)))]
         ins += [(st["r", g], whole(shape))] + [(a, one) for a in st["send", g]]
         st["r", g], *send, st["e", c] = run(
             f"forwardlate{g}", body, ins, [(sds(shape, F32), whole(shape)), *halves_of(g)], through=[st["e", c]],
@@ -407,7 +417,7 @@
         wide = slots * group_width[g]
         shape, one = (2, quarter, wide), (quarter, wide)
 
-        single = len(GROUPS[g]) == 1
+        single = 0 < g < len(GROUPS) - 1
 
         def body(fl, i, out):
             for n in (0, 1):
@@ -447,19 +457,16 @@
                     at = slice(s * v, (s + 1) * v)
                     value = sum(ref[0:quarter, at] for ref in refs)
                     if in_halves and s >= 2:
-                        out[2][s - 2, 0:quarter, done : done + v] = value
+                        out[2][s - 2, :, done : done + v] = value
                     else:
                         out[s][:, done : done + v] = value
                 done += v
-            if in_halves:
-                out[2][:, quarter:, :] = jnp.zeros((2, PAD, w), F32)
 
         parts_of = {g: [st["added", g]] if ("added", g) in st else [st["r", g], sent[f"rx{g}"]] for g in members}
         ins = [(a, whole(a.shape)) for g in members for a in parts_of[g]]
         outs = [(sds(part, F32), whole(part))] * (2 if in_halves else slots)
         if in_halves:
-            padded = (2, quarter + PAD, w)
-            outs += [(sds(padded, F32), whole(padded))]
+            outs += [(sds((2, *part), F32), whole((2, *part)))]
         parts = run(f"x{z}", body, ins, outs)
         if in_halves:
             st["z", z] = parts[:2]
@@ -474,9 +481,9 @@
 
         def body(fl, i, out):
             for n in (0, 1):
-                out[n][...] = i[n][...] + i[2][n, 0:quarter, :]
-
-        ins = [(a, whole(part)) for a in st["z", z]] + [(sent[f"rz2{z}"], whole((2, quarter + PAD, sum_width[z])))]
+                out[n][...] = i[n][...] + i[2][n]
+
+        ins = [(a, whole(part)) for a in st["z", z]] + [(sent[f"rz2{z}"], whole((2, *part)))]
         a, b = run(f"half{z}", body, ins, [(sds(part, F32), whole(part))] * 2)
         st["z", z], sent[f"rz1{z}"] = [a], over_gene(b, 1)
 

time: 284 us -> 283 us (level)
  transfers between devices with their start and end apart: 59 -> 59, of which waited for: 33 -> 35; matrix products, arithmetic and copies ran while one was open for 0% -> 0% of each run, Pallas kernels for 17% -> 17%
where the time goes in v8:
time: 283 us; the launch traced here: 282 us
  waiting for transfers between devices  126 us (45%)
  starting transfers between devices  74.3 us (26%)
  Pallas kernels  61.4 us (22%)
  blocking collectives  11.6 us (4%)
  local copies, waits for them, and re-layouts  8.1 us (3%)
    ppermute x11, waiting for transfers between devices, over_spot(): return lax.ppermute(v, 'spot', xor_pairs(spot_size, step))  69.7 us
    pallas_call x50, Pallas kernels, run(): pl.pallas_call(kernel, out_shape=[s for s, _ in outs] + [sds(a.shape, a.d...  61.4 us
    ppermute x29, starting transfers between devices, over_gene(): return lax.ppermute(v, 'gene', xor_pairs(4, step))  46.9 us
    ppermute x29, waiting for transfers between devices, over_gene(): return lax.ppermute(v, 'gene', xor_pairs(4, step))  38.1 us
    ppermute x11, starting transfers between devices, over_spot(): return lax.ppermute(v, 'spot', xor_pairs(spot_size, step))  14.5 us
    psum x1, blocking collectives, totals(): st['tot'] = lax.psum(v, 'cell')  11.6 us
    ppermute x7, waiting for transfers between devices, over_x(): return lax.ppermute(v, 'cell', xor_pairs(4, 2))  10.7 us
    ppermute x7, starting transfers between devices, over_x(): return lax.ppermute(v, 'cell', xor_pairs(4, 2))  10.4 us
  transfers between devices with their start and end apart: 59, of which 35 were waited for; matrix products, arithmetic and copies ran while one was open for 0% of the time, Pallas kernels for 17%

profile of v8, /device:TPU:0, one launch (start us, length us, event | category | flops | bytes accessed | tf_op | source)
XLA Modules:
  0.0 282.5 jit_solution(7291017072776416583)
XLA Ops:
  0.6 2.7 slice.4
  3.4 3.0 %collective-permute-start.3 = (bf16[2,2816,128]{2,1,0:T(8,128)(2,1)}, bf16[2,2816,128]{2,1,0:T(8,128)(2,1)}, u32[]{:S(2)}, u32[]{:S(2)}) collective-permute-start(bf16[2,2816,128]{2,1,0:T(8,128)(2,1)} %slice.4), channel_id=1, source_target_pairs={{0,4},{4,0},{1,5},{5,1},{2,6},{6,2},{3,7},{7,3},{8,12},{12,8},{9,1... | collective-permute-start | bytes 4325384 | tf_op jit(solution)/shard_map/ppermute | solution.py:126
  7.8 2.6 copy-done
  10.4 2.0 swap1.1
  12.5 11.6 %psum.7.refs_1_ = f32[8,512]{1,0:T(8,128)S(1)} all-reduce(f32[8,512]{1,0:T(8,128)S(1)} %get-tuple-element.131), channel_id=1, replica_groups=mesh['cell'=4,'spot'=2,'gene'=4] {'cell'}, use_global_device_ids=true, to_apply=%region_0.1 | all-reduce | flops 4096 | bytes 32768 | tf_op jit(solution)/shard_map/psum | solution.py:234
  25.7 2.6 collective-permute-start.1
  28.5 1.9 collective-permute-done.1.refs_1_.refs_3_
  30.4 3.4 %collective-permute-done.2.refs_2_.refs_4_ = f32[8,512]{1,0:T(8,128)S(1)} collective-permute-done((f32[8,512]{1,0:T(8,128)S(1)}, f32[8,512]{1,0:T(8,128)S(1)}, u32[]{:S(2)}, u32[]{:S(2)}) %collective-permute-start.2) | collective-permute-done | bytes 16416 | tf_op jit(solution)/shard_map/ppermute | solution.py:123
  34.4 2.6 copy-done.1
  39.1 2.0 along0.1
  41.6 2.2 collective-permute-start.5
  45.5 2.4 collective-permute-start.6
  48.3 4.0 %prob.1 = (bf16[512,2816]{1,0:T(8,128)(2,1)S(1)}, f32[8,2816]{1,0:T(8,128)S(1)}, f32[8,512]{1,0:T(8,128)S(1)}, f32[8,512]{1,0:T(8,128)S(1)}, f32[8,128]{1,0:T(8,128)S(1)}) custom-call(s32[5]{0:T(128)S(1)} %stack.27.flags, bf16[2816,512]{1,0:T(8,128)(2,1)S(1)} %copy-done.2, f32[8,512]{1,0:T(8,128)S(1)} %psum.7.refs_1_, ...), custom_call_target="tpu_custom_call", output_to_operand_aliasing={{4}: (6, {})} | custom-call | tf_op jit(solution)/shard_map/prob/pallas_call | solution.py:66
  53.0 16.9 %collective-permute-done.9.refs_0_.refs_7_ = bf16[2,2816,128]{2,1,0:T(8,128)(2,1)} collective-permute-done((bf16[2,2816,128]{2,1,0:T(8,128)(2,1)}, bf16[2,2816,128]{2,1,0:T(8,128)(2,1)}, u32[]{:S(2)}, u32[]{:S(2)}) %collective-permute-start.9) | collective-permute-done | bytes 1441824 | tf_op jit(solution)/shard_map/ppermute | solution.py:126
  72.5 3.4 %collective-permute-done.7.refs_1_.refs_5_ = bf16[1408,128]{1,0:T(8,128)(2,1)S(1)} collective-permute-done((bf16[1408,128]{1,0:T(8,128)(2,1)S(1)}, bf16[1408,128]{1,0:T(8,128)(2,1)S(1)}, u32[]{:S(2)}, u32[]{:S(2)}) %collective-permute-start.7) | collective-permute-done | bytes 360480 | tf_op jit(solution)/shard_map/ppermute | solution.py:123
  77.0 2.0 collective-permute-start.12
  80.5 2.2 collective-permute-start.11
  82.7 18.0 %collective-permute-done.8.refs_0_.refs_2_ = bf16[2,2816,128]{2,1,0:T(8,128)(2,1)S(1)} collective-permute-done((bf16[2,2816,128]{2,1,0:T(8,128)(2,1)S(1)}, bf16[2,2816,128]{2,1,0:T(8,128)(2,1)S(1)}, u32[]{:S(2)}, u32[]{:S(2)}) %collective-permute-start.8) | collective-permute-done | bytes 1441824 | tf_op jit(solution)/shard_map/ppermute | solution.py:126
  101.8 7.7 %collective-permute-done.11.refs_1_.refs_10_ = bf16[1408,128]{1,0:T(8,128)(2,1)S(1)} collective-permute-done((bf16[1408,128]{1,0:T(8,128)(2,1)S(1)}, bf16[1408,128]{1,0:T(8,128)(2,1)S(1)}, u32[]{:S(2)}, u32[]{:S(2)}) %collective-permute-start.11) | collective-permute-done | bytes 360480 | tf_op jit(solution)/shard_map/ppermute | solution.py:123
  110.6 2.0 collective-permute-start.17
  116.7 15.0 %collective-permute-done.14.refs_0_.refs_2_ = bf16[2,2816,128]{2,1,0:T(8,128)(2,1)S(1)} collective-permute-done((bf16[2,2816,128]{2,1,0:T(8,128)(2,1)S(1)}, bf16[2,2816,128]{2,1,0:T(8,128)(2,1)S(1)}, u32[]{:S(2)}, u32[]{:S(2)}) %collective-permute-start.14) | collective-permute-done | bytes 1441824 | tf_op jit(solution)/shard_map/ppermute | solution.py:126
  132.8 6.0 %collective-permute-done.16.refs_1_.refs_5_ = bf16[1408,128]{1,0:T(8,128)(2,1)S(1)} collective-permute-done((bf16[1408,128]{1,0:T(8,128)(2,1)S(1)}, bf16[1408,128]{1,0:T(8,128)(2,1)S(1)}, u32[]{:S(2)}, u32[]{:S(2)}) %collective-permute-start.16) | collective-permute-done | bytes 360480 | tf_op jit(solution)/shard_map/ppermute | solution.py:123
  140.5 2.0 collective-permute-start.18
  145.0 1.9 collective-permute-start.20
  148.2 2.1 collective-permute-start.25
  150.4 12.2 %collective-permute-done.18.refs_0_.refs_11_ = bf16[2,1408,128]{2,1,0:T(8,128)(2,1)S(1)} collective-permute-done((bf16[2,1408,128]{2,1,0:T(8,128)(2,1)S(1)}, bf16[2,1408,128]{2,1,0:T(8,128)(2,1)S(1)}, u32[]{:S(2)}, u32[]{:S(2)}) %collective-permute-start.18) | collective-permute-done | bytes 720928 | tf_op jit(solution)/shard_map/ppermute | solution.py:126
  163.1 5.0 %forward0.1 = (bf16[2816,512]{1,0:T(8,128)(2,1)S(1)}, bf16[2816,512]{1,0:T(8,128)(2,1)S(1)}, f32[2,128,1024]{2,1,0:T(8,128)S(1)}, f32[128,1024]{1,0:T(8,128)S(1)...) custom-call(s32[5]{0:T(128)S(1)} %stack.27.flags, ...), custom_call_target="tpu_custom_call", output_to_operand_aliasing={{5}: (13, {})} | custom-call | tf_op jit(solution)/shard_map/forward0/pallas_call | solution.py:66
  168.1 3.2 %collective-permute-done.20.refs_1_.refs_5_ = bf16[1536,128]{1,0:T(8,128)(2,1)S(1)} collective-permute-done((bf16[1536,128]{1,0:T(8,128)(2,1)S(1)}, bf16[1536,128]{1,0:T(8,128)(2,1)S(1)}, u32[]{:S(2)}, u32[]{:S(2)}) %collective-permute-start.20) | collective-permute-done | bytes 393248 | tf_op jit(solution)/shard_map/ppermute | solution.py:123
  178.5 2.8 %forward1.1 = (bf16[2816,512]{1,0:T(8,128)(2,1)S(1)}, f32[2,128,512]{2,1,0:T(8,128)S(1)}, f32[128,512]{1,0:T(8,128)S(1)}, f32[128,512]{1,0:T(8,128)S(1)}, f32[8,128]{1,0:T(8,128)S(1)}) custom-call(s32[5]{0:T(128)S(1)} %stack.27.flags, bf16[512,2816]{1,0:T(8,128)(2,1)S(1)} %get-tuple-element.142.refs_0_, ...), custom_call_target="tpu_custom_call", output_to_operand_aliasing={{4}: (8, {})} | custom-call | tf_op jit(solution)/shard_map/forward1/pallas_call | solution.py:66
  184.5 2.1 collective-permute-start.29
  186.6 2.6 forward2.1
  189.2 2.0 collective-permute-done.24.refs_1_
  193.6 4.0 %collective-permute-start.28 = (f32[2,128,256]{2,1,0:T(8,128)S(1)}, f32[2,128,256]{2,1,0:T(8,128)S(1)}, u32[]{:S(2)}, u32[]{:S(2)}) collective-permute-start(f32[2,128,256]{2,1,0:T(8,128)S(1)} %get-tuple-element.204), channel_id=1, source_target_pairs={{0,2},{1,3},{2,0},{3,1},{4,6},{5,7},{6,4},{7,5},{8,10},{9,11},{10,... | collective-permute-start | bytes 786440 | tf_op jit(solution)/shard_map/ppermute | solution.py:123
  200.3 5.9 %collective-permute-done.33.refs_2_ = f32[128,512]{1,0:T(8,128)S(1)} collective-permute-done((f32[128,512]{1,0:T(8,128)S(1)}, f32[128,512]{1,0:T(8,128)S(1)}, u32[]{:S(2)}, u32[]{:S(2)}) %collective-permute-start.33) | collective-permute-done | bytes 262176 | tf_op jit(solution)/shard_map/ppermute | solution.py:120
  209.2 2.1 collective-permute-start.37
  212.9 3.8 %collective-permute-done.4.refs_3_ = f32[8,2816]{1,0:T(8,128)S(1)} collective-permute-done((f32[8,2816]{1,0:T(8,128)S(1)}, f32[8,2816]{1,0:T(8,128)S(1)}, u32[]{:S(2)}, u32[]{:S(2)}) %collective-permute-start.4) | collective-permute-done | bytes 90144 | tf_op jit(solution)/shard_map/ppermute | solution.py:126
  217.8 2.5 collective-permute-done.36.refs_2_
  225.2 2.0 collective-permute-start.38
  237.7 2.0 collective-permute-start.49
  241.1 2.3 collective-permute-done.50.refs_4_.refs_12_
  243.4 3.5 %collective-permute-done.48.refs_1_ = bf16[128,512]{1,0:T(8,128)(2,1)S(1)} collective-permute-done((bf16[128,512]{1,0:T(8,128)(2,1)S(1)}, bf16[128,512]{1,0:T(8,128)(2,1)S(1)}, u32[]{:S(2)}, u32[]{:S(2)}) %collective-permute-start.48) | collective-permute-done | bytes 131104 | tf_op jit(solution)/shard_map/ppermute | solution.py:123
  250.6 4.2 %own.1 = (f32[2816,512]{1,0:T(8,128)S(1)}, f32[8,128]{1,0:T(8,128)S(1)}) custom-call(s32[5]{0:T(128)S(1)} %stack.27.flags, f32[2816,128]{1,0:T(8,128)S(1)} %get-tuple-element.224.refs_0_, bf16[2816,512]{1,0:T(8,128)(2,1)S(1)} %get-tuple-element.225.refs_1_.refs_3_, ...), custom_call_target="tpu_custom_call", output_to_operand_aliasing={{1}: (10, {})} | custom-call | tf_op jit(solution)/shard_map/own/pallas_call | solution.py:66
  257.6 6.6 %backward.1 = (f32[2816,512]{1,0:T(8,128)S(1)}, f32[8,512]{1,0:T(8,128)S(1)}, f32[8,128]{1,0:T(8,128)S(1)}) custom-call(s32[5]{0:T(128)S(1)} %stack.27.flags, bf16[2816,512]{1,0:T(8,128)(2,1)S(1)} %copy-done.2, f32[8,512]{1,0:T(8,128)S(1)} %get-tuple-element.140.refs_1_, ...), custom_call_target="tpu_custom_call", output_to_operand_aliasing={{2}: (14, {})} | custom-call | tf_op jit(solution)/shard_map/backward/pallas_call | solution.py:66
  267.0 2.2 collective-permute-done.55
  269.2 3.4 %collective-permute-start.56 = (f32[8,512]{1,0:T(8,128)S(1)}, f32[8,512]{1,0:T(8,128)S(1)}, u32[]{:S(2)}, u32[]{:S(2)}) collective-permute-start(f32[8,512]{1,0:T(8,128)S(1)} %add.32), channel_id=1, source_target_pairs={{0,1},{1,0},{2,3},{3,2},{4,5},{5,4},{6,7},{7,6},{8,9},{9,8},{10,11... | collective-permute-start | bytes 49160 | tf_op jit(solution)/shard_map/ppermute | solution.py:123
  273.1 1.9 collective-permute-start.58
  275.1 2.2 collective-permute-done.57
  278.7 3.8 %final.1 = (f32[2816,512]{1,0:T(8,128)}, f32[5]{0:T(128)}, f32[8,128]{1,0:T(8,128)S(1)}) custom-call(s32[5]{0:T(128)S(1)} %stack.27.flags, bf16[2816,512]{1,0:T(8,128)(2,1)S(1)} %copy-done.2, f32[8,512]{1,0:T(8,128)S(1)} %get-tuple-element.140.refs_1_, f32[2816,512]{1,0:T(8,128)S(1)} %get-tuple-element.255.refs_2_, ...), custom_call_target="tpu_custom_call", output_to_operand_aliasing={{2}: (5, {})} | custom-call | tf_op jit(solution)/shard_map/final/pallas_call | solution.py:66
  (149 shorter events, 77.0 us)
Async XLA Ops:
  3.4 35.7 %collective-permute-start.3 = (bf16[2,2816,128]{2,1,0:T(8,128)(2,1)}, bf16[2,2816,128]{2,1,0:T(8,128)(2,1)}, u32[]{:S(2)}, u32[]{:S(2)}) collective-permute-start(bf16[2,2816,128]{2,1,0:T(8,128)(2,1)} %slice.4), channel_id=1, source_target_pairs={{0,4},{4,0},{1,5},{5,1},{2,6},{6,2},{3,7},{7,3},{8,12},{12,8},{9,1... | collective-permute-start | bytes 4325384 | tf_op jit(solution)/shard_map/ppermute | solution.py:126
  12.4 57.5 %collective-permute-start.9 = (bf16[2,2816,128]{2,1,0:T(8,128)(2,1)}, bf16[2,2816,128]{2,1,0:T(8,128)(2,1)}, u32[]{:S(2)}, u32[]{:S(2)}) collective-permute-start(bf16[2,2816,128]{2,1,0:T(8,128)(2,1)} %get-tuple-element.147), channel_id=1, source_target_pairs={{0,4},{4,0},{1,5},{5,1},{2,6},{6,2},{3,7},{7,3},{8,12},{12,8},{9,1... | collective-permute-start | bytes 4325384 | tf_op jit(solution)/shard_map/ppermute | solution.py:126
  24.1 4.4 %collective-permute-start = (f32[8,512]{1,0:T(8,128)S(1)}, f32[8,512]{1,0:T(8,128)S(1)}, u32[]{:S(2)}, u32[]{:S(2)}) collective-permute-start(f32[8,512]{1,0:T(8,128)S(1)} %psum.7.refs_1_), channel_id=1, source_target_pairs={{0,1},{1,0},{2,3},{3,2},{4,5},{5,4},{6,7},{7,6},{8,9},{9,8},{10,11... | collective-permute-start | bytes 49160 | tf_op jit(solution)/shard_map/ppermute | solution.py:123
  25.7 4.7 %collective-permute-start.1 = (f32[8,512]{1,0:T(8,128)S(1)}, f32[8,512]{1,0:T(8,128)S(1)}, u32[]{:S(2)}, u32[]{:S(2)}) collective-permute-start(f32[8,512]{1,0:T(8,128)S(1)} %psum.7.refs_1_), channel_id=1, source_target_pairs={{0,2},{1,3},{2,0},{3,1},{4,6},{5,7},{6,4},{7,5},{8,10},{9,11},{10,... | collective-permute-start | bytes 49160 | tf_op jit(solution)/shard_map/ppermute | solution.py:123
  28.3 5.5 %collective-permute-start.2 = (f32[8,512]{1,0:T(8,128)S(1)}, f32[8,512]{1,0:T(8,128)S(1)}, u32[]{:S(2)}, u32[]{:S(2)}) collective-permute-start(f32[8,512]{1,0:T(8,128)S(1)} %psum.7.refs_1_), channel_id=1, source_target_pairs={{0,3},{1,2},{2,1},{3,0},{4,7},{5,6},{6,5},{7,4},{8,11},{9,10},{10,... | collective-permute-start | bytes 49160 | tf_op jit(solution)/shard_map/ppermute | solution.py:123
  41.6 34.3 %collective-permute-start.5 = (bf16[2816,128]{1,0:T(8,128)(2,1)S(1)}, bf16[2816,128]{1,0:T(8,128)(2,1)S(1)}, u32[]{:S(2)}, u32[]{:S(2)}) collective-permute-start(bf16[2816,128]{1,0:T(8,128)(2,1)S(1)} %get-tuple-element.143), channel_id=1, source_target_pairs={{0,1},{1,0},{2,3},{3,2},{4,5},{5,4},{6,7},{7,6},{8,9},{9,8},{10,11... | collective-permute-start | bytes 2162696 | tf_op jit(solution)/shard_map/ppermute | solution.py:123
  43.8 57.0 %collective-permute-start.8 = (bf16[2,2816,128]{2,1,0:T(8,128)(2,1)S(1)}, bf16[2,2816,128]{2,1,0:T(8,128)(2,1)S(1)}, u32[]{:S(2)}, u32[]{:S(2)}) collective-permute-start(bf16[2,2816,128]{2,1,0:T(8,128)(2,1)S(1)} %get-tuple-element.146), channel_id=1, source_target_pairs={{0,4},{4,0},{1,5},{5,1},{2,6},{6,2},{3,7},{7,3},{8,12},{12,8},{9,1... | collective-permute-start | bytes 4325384 | tf_op jit(solution)/shard_map/ppermute | solution.py:126
  45.5 27.0 %collective-permute-start.6 = (bf16[1408,128]{1,0:T(8,128)(2,1)S(1)}, bf16[1408,128]{1,0:T(8,128)(2,1)S(1)}, u32[]{:S(2)}, u32[]{:S(2)}) collective-permute-start(bf16[1408,128]{1,0:T(8,128)(2,1)S(1)} %get-tuple-element.144), channel_id=1, source_target_pairs={{0,2},{1,3},{2,0},{3,1},{4,6},{5,7},{6,4},{7,5},{8,10},{9,11},{10,... | collective-permute-start | bytes 1081352 | tf_op jit(solution)/shard_map/ppermute | solution.py:123
  47.9 28.0 %collective-permute-start.7 = (bf16[1408,128]{1,0:T(8,128)(2,1)S(1)}, bf16[1408,128]{1,0:T(8,128)(2,1)S(1)}, u32[]{:S(2)}, u32[]{:S(2)}) collective-permute-start(bf16[1408,128]{1,0:T(8,128)(2,1)S(1)} %get-tuple-element.145), channel_id=1, source_target_pairs={{0,3},{1,2},{2,1},{3,0},{4,7},{5,6},{6,5},{7,4},{8,11},{9,10},{10,... | collective-permute-start | bytes 1081352 | tf_op jit(solution)/shard_map/ppermute | solution.py:123
  77.0 32.5 %collective-permute-start.12 = (bf16[2816,128]{1,0:T(8,128)(2,1)S(1)}, bf16[2816,128]{1,0:T(8,128)(2,1)S(1)}, u32[]{:S(2)}, u32[]{:S(2)}) collective-permute-start(bf16[2816,128]{1,0:T(8,128)(2,1)S(1)} %get-tuple-element.161), channel_id=1, source_target_pairs={{0,1},{1,0},{2,3},{3,2},{4,5},{5,4},{6,7},{7,6},{8,9},{9,8},{10,11... | collective-permute-start | bytes 2162696 | tf_op jit(solution)/shard_map/ppermute | solution.py:123
  78.9 52.7 %collective-permute-start.14 = (bf16[2,2816,128]{2,1,0:T(8,128)(2,1)S(1)}, bf16[2,2816,128]{2,1,0:T(8,128)(2,1)S(1)}, u32[]{:S(2)}, u32[]{:S(2)}) collective-permute-start(bf16[2,2816,128]{2,1,0:T(8,128)(2,1)S(1)} %get-tuple-element.165), channel_id=1, source_target_pairs={{0,4},{4,0},{1,5},{5,1},{2,6},{6,2},{3,7},{7,3},{8,12},{12,8},{9,1... | collective-permute-start | bytes 4325384 | tf_op jit(solution)/shard_map/ppermute | solution.py:126
  79.4 22.4 %collective-permute-start.10 = (bf16[1408,128]{1,0:T(8,128)(2,1)S(1)}, bf16[1408,128]{1,0:T(8,128)(2,1)S(1)}, u32[]{:S(2)}, u32[]{:S(2)}) collective-permute-start(bf16[1408,128]{1,0:T(8,128)(2,1)S(1)} %get-tuple-element.159), channel_id=1, source_target_pairs={{0,2},{1,3},{2,0},{3,1},{4,6},{5,7},{6,4},{7,5},{8,10},{9,11},{10,... | collective-permute-start | bytes 1081352 | tf_op jit(solution)/shard_map/ppermute | solution.py:123
  80.5 28.9 %collective-permute-start.11 = (bf16[1408,128]{1,0:T(8,128)(2,1)S(1)}, bf16[1408,128]{1,0:T(8,128)(2,1)S(1)}, u32[]{:S(2)}, u32[]{:S(2)}) collective-permute-start(bf16[1408,128]{1,0:T(8,128)(2,1)S(1)} %get-tuple-element.160), channel_id=1, source_target_pairs={{0,3},{1,2},{2,1},{3,0},{4,7},{5,6},{6,5},{7,4},{8,11},{9,10},{10,... | collective-permute-start | bytes 1081352 | tf_op jit(solution)/shard_map/ppermute | solution.py:123
  110.6 28.2 %collective-permute-start.17 = (bf16[2816,128]{1,0:T(8,128)(2,1)S(1)}, bf16[2816,128]{1,0:T(8,128)(2,1)S(1)}, u32[]{:S(2)}, u32[]{:S(2)}) collective-permute-start(bf16[2816,128]{1,0:T(8,128)(2,1)S(1)} %get-tuple-element.172), channel_id=1, source_target_pairs={{0,1},{1,0},{2,3},{3,2},{4,5},{5,4},{6,7},{7,6},{8,9},{9,8},{10,11... | collective-permute-start | bytes 2162696 | tf_op jit(solution)/shard_map/ppermute | solution.py:123
  112.6 20.2 %collective-permute-start.15 = (bf16[1408,128]{1,0:T(8,128)(2,1)S(1)}, bf16[1408,128]{1,0:T(8,128)(2,1)S(1)}, u32[]{:S(2)}, u32[]{:S(2)}) collective-permute-start(bf16[1408,128]{1,0:T(8,128)(2,1)S(1)} %get-tuple-element.170), channel_id=1, source_target_pairs={{0,2},{1,3},{2,0},{3,1},{4,6},{5,7},{6,4},{7,5},{8,10},{9,11},{10,... | collective-permute-start | bytes 1081352 | tf_op jit(solution)/shard_map/ppermute | solution.py:123
  113.2 25.6 %collective-permute-start.16 = (bf16[1408,128]{1,0:T(8,128)(2,1)S(1)}, bf16[1408,128]{1,0:T(8,128)(2,1)S(1)}, u32[]{:S(2)}, u32[]{:S(2)}) collective-permute-start(bf16[1408,128]{1,0:T(8,128)(2,1)S(1)} %get-tuple-element.171), channel_id=1, source_target_pairs={{0,3},{1,2},{2,1},{3,0},{4,7},{5,6},{6,5},{7,4},{8,11},{9,10},{10,... | collective-permute-start | bytes 1081352 | tf_op jit(solution)/shard_map/ppermute | solution.py:123
  115.6 31.5 %collective-permute-start.13 = (bf16[2,1408,128]{2,1,0:T(8,128)(2,1)S(1)}, bf16[2,1408,128]{2,1,0:T(8,128)(2,1)S(1)}, u32[]{:S(2)}, u32[]{:S(2)}) collective-permute-start(bf16[2,1408,128]{2,1,0:T(8,128)(2,1)S(1)} %get-tuple-element.164), channel_id=1, source_target_pairs={{0,4},{4,0},{1,5},{5,1},{2,6},{6,2},{3,7},{7,3},{8,12},{12,8},{9,1... | collective-permute-start | bytes 2162696 | tf_op jit(solution)/shard_map/ppermute | solution.py:126
  140.5 22.0 %collective-permute-start.18 = (bf16[2,1408,128]{2,1,0:T(8,128)(2,1)S(1)}, bf16[2,1408,128]{2,1,0:T(8,128)(2,1)S(1)}, u32[]{:S(2)}, u32[]{:S(2)}) collective-permute-start(bf16[2,1408,128]{2,1,0:T(8,128)(2,1)S(1)} %get-tuple-element.175), channel_id=1, source_target_pairs={{0,4},{4,0},{1,5},{5,1},{2,6},{6,2},{3,7},{7,3},{8,12},{12,8},{9,1... | collective-permute-start | bytes 2162696 | tf_op jit(solution)/shard_map/ppermute | solution.py:126
  142.5 28.7 %collective-permute-start.21 = (bf16[2816,128]{1,0:T(8,128)(2,1)S(1)}, bf16[2816,128]{1,0:T(8,128)(2,1)S(1)}, u32[]{:S(2)}, u32[]{:S(2)}) collective-permute-start(bf16[2816,128]{1,0:T(8,128)(2,1)S(1)} %get-tuple-element.183), channel_id=1, source_target_pairs={{0,1},{1,0},{2,3},{3,2},{4,5},{5,4},{6,7},{7,6},{8,9},{9,8},{10,11... | collective-permute-start | bytes 2162696 | tf_op jit(solution)/shard_map/ppermute | solution.py:123
  144.2 23.9 %collective-permute-start.19 = (bf16[1536,128]{1,0:T(8,128)(2,1)S(1)}, bf16[1536,128]{1,0:T(8,128)(2,1)S(1)}, u32[]{:S(2)}, u32[]{:S(2)}) collective-permute-start(bf16[1536,128]{1,0:T(8,128)(2,1)S(1)} %get-tuple-element.181), channel_id=1, source_target_pairs={{0,2},{1,3},{2,0},{3,1},{4,6},{5,7},{6,4},{7,5},{8,10},{9,11},{10,... | collective-permute-start | bytes 1179656 | tf_op jit(solution)/shard_map/ppermute | solution.py:123
  145.0 26.2 %collective-permute-start.20 = (bf16[1536,128]{1,0:T(8,128)(2,1)S(1)}, bf16[1536,128]{1,0:T(8,128)(2,1)S(1)}, u32[]{:S(2)}, u32[]{:S(2)}) collective-permute-start(bf16[1536,128]{1,0:T(8,128)(2,1)S(1)} %get-tuple-element.182), channel_id=1, source_target_pairs={{0,3},{1,2},{2,1},{3,0},{4,7},{5,6},{6,5},{7,4},{8,11},{9,10},{10,... | collective-permute-start | bytes 1179656 | tf_op jit(solution)/shard_map/ppermute | solution.py:123
  148.2 29.7 %collective-permute-start.25 = (bf16[2,1408,128]{2,1,0:T(8,128)(2,1)S(1)}, bf16[2,1408,128]{2,1,0:T(8,128)(2,1)S(1)}, u32[]{:S(2)}, u32[]{:S(2)}) collective-permute-start(bf16[2,1408,128]{2,1,0:T(8,128)(2,1)S(1)} %get-tuple-element.191), channel_id=1, source_target_pairs={{0,4},{4,0},{1,5},{5,1},{2,6},{6,2},{3,7},{7,3},{8,12},{12,8},{9,1... | collective-permute-start | bytes 2162696 | tf_op jit(solution)/shard_map/ppermute | solution.py:126
  173.5 18.2 %collective-permute-start.30 = (bf16[2,1280,128]{2,1,0:T(8,128)(2,1)S(1)}, bf16[2,1280,128]{2,1,0:T(8,128)(2,1)S(1)}, u32[]{:S(2)}, u32[]{:S(2)}) collective-permute-start(bf16[2,1280,128]{2,1,0:T(8,128)(2,1)S(1)} %get-tuple-element.207), channel_id=1, source_target_pairs={{0,4},{4,0},{1,5},{5,1},{2,6},{6,2},{3,7},{7,3},{8,12},{12,8},{9,1... | collective-permute-start | bytes 1966088 | tf_op jit(solution)/shard_map/ppermute | solution.py:126
  176.3 14.8 %collective-permute-start.24 = (f32[128,1024]{1,0:T(8,128)S(1)}, f32[128,1024]{1,0:T(8,128)S(1)}, u32[]{:S(2)}, u32[]{:S(2)}) collective-permute-start(f32[128,1024]{1,0:T(8,128)S(1)} %get-tuple-element.190), channel_id=1, source_target_pairs={{0,16},{8,24},{16,0},{24,8},{1,17},{9,25},{17,1},{25,9},{2,18},{10... | collective-permute-start | bytes 1572872 | tf_op jit(solution)/shard_map/ppermute | solution.py:120
  184.5 15.2 %collective-permute-start.29 = (f32[136,512]{1,0:T(8,128)S(1)}, f32[136,512]{1,0:T(8,128)S(1)}, u32[]{:S(2)}, u32[]{:S(2)}) collective-permute-start(f32[136,512]{1,0:T(8,128)S(1)} %get-tuple-element.206), channel_id=1, source_target_pairs={{0,16},{8,24},{16,0},{24,8},{1,17},{9,25},{17,1},{25,9},{2,18},{10... | collective-permute-start | bytes 835592 | tf_op jit(solution)/shard_map/ppermute | solution.py:120
  193.0 4.6 %collective-permute-start.31 = (f32[128,512]{1,0:T(8,128)S(1)}, f32[128,512]{1,0:T(8,128)S(1)}, u32[]{:S(2)}, u32[]{:S(2)}) collective-permute-start(f32[128,512]{1,0:T(8,128)S(1)} %get-tuple-element.214), channel_id=1, source_target_pairs={{0,8},{8,0},{16,24},{24,16},{1,9},{9,1},{17,25},{25,17},{2,10},{10... | collective-permute-start | bytes 786440 | tf_op jit(solution)/shard_map/ppermute | solution.py:117
  193.1 4.5 %collective-permute-start.32 = (f32[128,512]{1,0:T(8,128)S(1)}, f32[128,512]{1,0:T(8,128)S(1)}, u32[]{:S(2)}, u32[]{:S(2)}) collective-permute-start(f32[128,512]{1,0:T(8,128)S(1)} %get-tuple-element.215), channel_id=1, source_target_pairs={{0,8},{8,0},{16,24},{24,16},{1,9},{9,1},{17,25},{25,17},{2,10},{10... | collective-permute-start | bytes 786440 | tf_op jit(solution)/shard_map/ppermute | solution.py:117
  193.6 17.7 %collective-permute-start.28 = (f32[2,128,256]{2,1,0:T(8,128)S(1)}, f32[2,128,256]{2,1,0:T(8,128)S(1)}, u32[]{:S(2)}, u32[]{:S(2)}) collective-permute-start(f32[2,128,256]{2,1,0:T(8,128)S(1)} %get-tuple-element.204), channel_id=1, source_target_pairs={{0,2},{1,3},{2,0},{3,1},{4,6},{5,7},{6,4},{7,5},{8,10},{9,11},{10,... | collective-permute-start | bytes 786440 | tf_op jit(solution)/shard_map/ppermute | solution.py:123
  198.2 8.1 %collective-permute-start.33 = (f32[128,512]{1,0:T(8,128)S(1)}, f32[128,512]{1,0:T(8,128)S(1)}, u32[]{:S(2)}, u32[]{:S(2)}) collective-permute-start(f32[128,512]{1,0:T(8,128)S(1)} %get-tuple-element.220), channel_id=1, source_target_pairs={{0,16},{8,24},{16,0},{24,8},{1,17},{9,25},{17,1},{25,9},{2,18},{10... | collective-permute-start | bytes 786440 | tf_op jit(solution)/shard_map/ppermute | solution.py:120
  206.9 10.9 %collective-permute-start.35 = (f32[128,256]{1,0:T(8,128)S(1)}, f32[128,256]{1,0:T(8,128)S(1)}, u32[]{:S(2)}, u32[]{:S(2)}) collective-permute-start(f32[128,256]{1,0:T(8,128)S(1)} %get-tuple-element.235), channel_id=1, source_target_pairs={{0,1},{1,0},{2,3},{3,2},{4,5},{5,4},{6,7},{7,6},{8,9},{9,8},{10,11... | collective-permute-start | bytes 393224 | tf_op jit(solution)/shard_map/ppermute | solution.py:123
  208.0 12.2 %collective-permute-start.36 = (f32[128,256]{1,0:T(8,128)S(1)}, f32[128,256]{1,0:T(8,128)S(1)}, u32[]{:S(2)}, u32[]{:S(2)}) collective-permute-start(f32[128,256]{1,0:T(8,128)S(1)} %get-tuple-element.236), channel_id=1, source_target_pairs={{0,2},{1,3},{2,0},{3,1},{4,6},{5,7},{6,4},{7,5},{8,10},{9,11},{10,... | collective-permute-start | bytes 393224 | tf_op jit(solution)/shard_map/ppermute | solution.py:123
  209.2 11.1 %collective-permute-start.37 = (f32[128,256]{1,0:T(8,128)S(1)}, f32[128,256]{1,0:T(8,128)S(1)}, u32[]{:S(2)}, u32[]{:S(2)}) collective-permute-start(f32[128,256]{1,0:T(8,128)S(1)} %get-tuple-element.237), channel_id=1, source_target_pairs={{0,3},{1,2},{2,1},{3,0},{4,7},{5,6},{6,5},{7,4},{8,11},{9,10},{10,... | collective-permute-start | bytes 393224 | tf_op jit(solution)/shard_map/ppermute | solution.py:123
  211.9 9.1 %collective-permute-start.34 = (f32[128,256]{1,0:T(8,128)S(1)}, f32[128,256]{1,0:T(8,128)S(1)}, u32[]{:S(2)}, u32[]{:S(2)}) collective-permute-start(f32[128,256]{1,0:T(8,128)S(1)} %get-tuple-element.233), channel_id=1, source_target_pairs={{0,1},{1,0},{2,3},{3,2},{4,5},{5,4},{6,7},{7,6},{8,9},{9,8},{10,11... | collective-permute-start | bytes 393224 | tf_op jit(solution)/shard_map/ppermute | solution.py:123
  212.2 4.5 %collective-permute-start.4 = (f32[8,2816]{1,0:T(8,128)S(1)}, f32[8,2816]{1,0:T(8,128)S(1)}, u32[]{:S(2)}, u32[]{:S(2)}) collective-permute-start(f32[8,2816]{1,0:T(8,128)S(1)} %get-tuple-element.141.refs_2_), channel_id=1, source_target_pairs={{0,4},{4,0},{1,5},{5,1},{2,6},{6,2},{3,7},{7,3},{8,12},{12,8},{9,1... | collective-permute-start | bytes 270344 | tf_op jit(solution)/shard_map/ppermute | solution.py:126
  223.7 5.9 %collective-permute-start.42 = (f32[16,512]{1,0:T(8,128)S(1)}, f32[16,512]{1,0:T(8,128)S(1)}, u32[]{:S(2)}, u32[]{:S(2)}) collective-permute-start(f32[16,512]{1,0:T(8,128)S(1)} %add.29), channel_id=1, source_target_pairs={{0,16},{8,24},{16,0},{24,8},{1,17},{9,25},{17,1},{25,9},{2,18},{10... | collective-permute-start | bytes 98312 | tf_op jit(solution)/shard_map/ppermute | solution.py:120
  225.2 5.1 %collective-permute-start.38 = (f32[8,128]{1,0:T(8,128)S(1)}, f32[8,128]{1,0:T(8,128)S(1)}, u32[]{:S(2)}, u32[]{:S(2)}) collective-permute-start(f32[8,128]{1,0:T(8,128)S(1)} %get-tuple-element.243.refs_0_.refs_4_), channel_id=1, source_target_pairs={{0,1},{1,0},{2,3},{3,2},{4,5},{5,4},{6,7},{7,6},{8,9},{9,8},{10,11... | collective-permute-start | bytes 12296 | tf_op jit(solution)/shard_map/ppermute | solution.py:123
  227.2 4.5 %collective-permute-start.39 = (f32[8,128]{1,0:T(8,128)S(1)}, f32[8,128]{1,0:T(8,128)S(1)}, u32[]{:S(2)}, u32[]{:S(2)}) collective-permute-start(f32[8,128]{1,0:T(8,128)S(1)} %get-tuple-element.243.refs_0_.refs_4_), channel_id=1, source_target_pairs={{0,2},{1,3},{2,0},{3,1},{4,6},{5,7},{6,4},{7,5},{8,10},{9,11},{10,... | collective-permute-start | bytes 12296 | tf_op jit(solution)/shard_map/ppermute | solution.py:123
  227.8 5.4 %collective-permute-start.40 = (f32[8,128]{1,0:T(8,128)S(1)}, f32[8,128]{1,0:T(8,128)S(1)}, u32[]{:S(2)}, u32[]{:S(2)}) collective-permute-start(f32[8,128]{1,0:T(8,128)S(1)} %get-tuple-element.243.refs_0_.refs_4_), channel_id=1, source_target_pairs={{0,3},{1,2},{2,1},{3,0},{4,7},{5,6},{6,5},{7,4},{8,11},{9,10},{10,... | collective-permute-start | bytes 12296 | tf_op jit(solution)/shard_map/ppermute | solution.py:123
  229.6 4.1 %collective-permute-start.43 = (f32[16,512]{1,0:T(8,128)S(1)}, f32[16,512]{1,0:T(8,128)S(1)}, u32[]{:S(2)}, u32[]{:S(2)}) collective-permute-start(f32[16,512]{1,0:T(8,128)S(1)} %add.30.refs_8_), channel_id=1, source_target_pairs={{0,4},{4,0},{1,5},{5,1},{2,6},{6,2},{3,7},{7,3},{8,12},{12,8},{9,1... | collective-permute-start | bytes 98312 | tf_op jit(solution)/shard_map/ppermute | solution.py:126
  234.7 8.7 %collective-permute-start.45 = (bf16[128,512]{1,0:T(8,128)(2,1)S(1)}, bf16[128,512]{1,0:T(8,128)(2,1)S(1)}, u32[]{:S(2)}, u32[]{:S(2)}) collective-permute-start(bf16[128,512]{1,0:T(8,128)(2,1)S(1)} %get-tuple-element.246.refs_5_), channel_id=1, source_target_pairs={{0,16},{8,24},{16,0},{24,8},{1,17},{9,25},{17,1},{25,9},{2,18},{10... | collective-permute-start | bytes 393224 | tf_op jit(solution)/shard_map/ppermute | solution.py:120
  235.3 8.1 %collective-permute-start.47 = (bf16[128,512]{1,0:T(8,128)(2,1)S(1)}, bf16[128,512]{1,0:T(8,128)(2,1)S(1)}, u32[]{:S(2)}, u32[]{:S(2)}) collective-permute-start(bf16[128,512]{1,0:T(8,128)(2,1)S(1)} %get-tuple-element.246.refs_5_), channel_id=1, source_target_pairs={{0,1},{1,0},{2,3},{3,2},{4,5},{5,4},{6,7},{7,6},{8,9},{9,8},{10,11... | collective-permute-start | bytes 393224 | tf_op jit(solution)/shard_map/ppermute | solution.py:123
  236.2 10.7 %collective-permute-start.48 = (bf16[128,512]{1,0:T(8,128)(2,1)S(1)}, bf16[128,512]{1,0:T(8,128)(2,1)S(1)}, u32[]{:S(2)}, u32[]{:S(2)}) collective-permute-start(bf16[128,512]{1,0:T(8,128)(2,1)S(1)} %get-tuple-element.246.refs_5_), channel_id=1, source_target_pairs={{0,2},{1,3},{2,0},{3,1},{4,6},{5,7},{6,4},{7,5},{8,10},{9,11},{10,... | collective-permute-start | bytes 393224 | tf_op jit(solution)/shard_map/ppermute | solution.py:123
  237.7 9.2 %collective-permute-start.49 = (bf16[128,512]{1,0:T(8,128)(2,1)S(1)}, bf16[128,512]{1,0:T(8,128)(2,1)S(1)}, u32[]{:S(2)}, u32[]{:S(2)}) collective-permute-start(bf16[128,512]{1,0:T(8,128)(2,1)S(1)} %get-tuple-element.246.refs_5_), channel_id=1, source_target_pairs={{0,3},{1,2},{2,1},{3,0},{4,7},{5,6},{6,5},{7,4},{8,11},{9,10},{10,... | collective-permute-start | bytes 393224 | tf_op jit(solution)/shard_map/ppermute | solution.py:123
  247.5 7.8 %collective-permute-start.52 = (bf16[3,128,512]{2,1,0:T(8,128)(2,1)S(1)}, bf16[3,128,512]{2,1,0:T(8,128)(2,1)S(1)}, u32[]{:S(2)}, u32[]{:S(2)}) collective-permute-start(bf16[3,128,512]{2,1,0:T(8,128)(2,1)S(1)} %get-tuple-element.251.refs_7_), channel_id=1, source_target_pairs={{0,16},{8,24},{16,0},{24,8},{1,17},{9,25},{17,1},{25,9},{2,18},{10... | collective-permute-start | bytes 1179656 | tf_op jit(solution)/shard_map/ppermute | solution.py:120
  249.5 6.4 %collective-permute-start.51 = (bf16[3,128,512]{2,1,0:T(8,128)(2,1)S(1)}, bf16[3,128,512]{2,1,0:T(8,128)(2,1)S(1)}, u32[]{:S(2)}, u32[]{:S(2)}) collective-permute-start(bf16[3,128,512]{2,1,0:T(8,128)(2,1)S(1)} %get-tuple-element.251.refs_7_), channel_id=1, source_target_pairs={{0,8},{8,0},{16,24},{24,16},{1,9},{9,1},{17,25},{25,17},{2,10},{10... | collective-permute-start | bytes 1179656 | tf_op jit(solution)/shard_map/ppermute | solution.py:117
  269.2 5.8 %collective-permute-start.56 = (f32[8,512]{1,0:T(8,128)S(1)}, f32[8,512]{1,0:T(8,128)S(1)}, u32[]{:S(2)}, u32[]{:S(2)}) collective-permute-start(f32[8,512]{1,0:T(8,128)S(1)} %add.32), channel_id=1, source_target_pairs={{0,1},{1,0},{2,3},{3,2},{4,5},{5,4},{6,7},{7,6},{8,9},{9,8},{10,11... | collective-permute-start | bytes 49160 | tf_op jit(solution)/shard_map/ppermute | solution.py:123
  272.6 4.6 %collective-permute-start.57 = (f32[8,512]{1,0:T(8,128)S(1)}, f32[8,512]{1,0:T(8,128)S(1)}, u32[]{:S(2)}, u32[]{:S(2)}) collective-permute-start(f32[8,512]{1,0:T(8,128)S(1)} %add.32), channel_id=1, source_target_pairs={{0,2},{1,3},{2,0},{3,1},{4,6},{5,7},{6,4},{7,5},{8,10},{9,11},{10,... | collective-permute-start | bytes 49160 | tf_op jit(solution)/shard_map/ppermute | solution.py:123
  273.1 5.5 %collective-permute-start.58 = (f32[8,512]{1,0:T(8,128)S(1)}, f32[8,512]{1,0:T(8,128)S(1)}, u32[]{:S(2)}, u32[]{:S(2)}) collective-permute-start(f32[8,512]{1,0:T(8,128)S(1)} %add.32), channel_id=1, source_target_pairs={{0,3},{1,2},{2,1},{3,0},{4,7},{5,6},{6,5},{7,4},{8,11},{9,10},{10,... | collective-permute-start | bytes 49160 | tf_op jit(solution)/shard_map/ppermute | solution.py:123
  (20 other events, 134.2 us)

commit v9 on v8

--- a/solution.py
+++ b/solution.py
@@ -13,8 +13,8 @@
 BF = jnp.bfloat16
 F32 = jnp.float32
 SHARED = (0, 0, 0, 256)
-VMEM_BYTES = 14 * 1024 * 1024
-COSTS = {"spots": 1, "back3": 1, "waits2": 3, "addx1": 9, "half0": 3}
+VMEM_BYTES = 12 * 1024 * 1024
+COSTS = {"spots": 1, "back3": 3, "waits2": 3, "addx1": 9, "half0": 3}
 WIDTHS = (128, 128, 128, 128)
 GROUPS = ((0, 1), (2,), (3,))
 SUMS = ((0,), (1, 2))
@@ -682,9 +682,9 @@
         scratch=[pltpu.VMEM((slots - 1, spots, genes), BF), pltpu.SemaphoreType.DMA((len(grads),))],
     )
 
+    v = (v + over_gene(v, 1)) + (over_gene(v, 2) + over_gene(v, 3))
+    v = v + over_x(v)
     v = v + over_core(v)
-    v = v + over_x(v)
-    v = (v + over_gene(v, 1)) + (over_gene(v, 2) + over_gene(v, 3))
 
     def final_body(fl, i, out):
         prob = jnp.exp(i[0][...].astype(F32)) * (1.0 / i[1][0:1, :])

time: 283 us -> 283 us (level)
  no operation moved by 1% of the time
where the time goes in v9:
time: 283 us
  waiting for transfers between devices  126 us (45%)
  starting transfers between devices  74.2 us (26%)
  Pallas kernels  61.5 us (22%)
  blocking collectives  11.6 us (4%)
  local copies, waits for them, and re-layouts  8.1 us (3%)
    ppermute x11, waiting for transfers between devices, over_spot(): return lax.ppermute(v, 'spot', xor_pairs(spot_size, step))  69.7 us
    pallas_call x50, Pallas kernels, run(): pl.pallas_call(kernel, out_shape=[s for s, _ in outs] + [sds(a.shape, a.d...  61.5 us
    ppermute x29, starting transfers between devices, over_gene(): return lax.ppermute(v, 'gene', xor_pairs(4, step))  46.9 us
    ppermute x29, waiting for transfers between devices, over_gene(): return lax.ppermute(v, 'gene', xor_pairs(4, step))  38.1 us
    ppermute x11, starting transfers between devices, over_spot(): return lax.ppermute(v, 'spot', xor_pairs(spot_size, step))  14.5 us
    psum x1, blocking collectives, totals(): st['tot'] = lax.psum(v, 'cell')  11.6 us
    ppermute x7, waiting for transfers between devices, over_x(): return lax.ppermute(v, 'cell', xor_pairs(4, 2))  10.7 us
    ppermute x7, starting transfers between devices, over_x(): return lax.ppermute(v, 'cell', xor_pairs(4, 2))  10.4 us
  transfers between devices with their start and end apart: 59, of which 35 were waited for; matrix products, arithmetic and copies ran while one was open for 0% of the time, Pallas kernels for 17%

profile of v9, /device:TPU:0, one launch (start us, length us, event | category | flops | bytes accessed | tf_op | source)
XLA Modules:
  0.0 282.6 jit_solution(16371531841933769920)
XLA Ops:
  0.6 2.7 slice.4
  3.4 3.0 %collective-permute-start.3 = (bf16[2,2816,128]{2,1,0:T(8,128)(2,1)}, bf16[2,2816,128]{2,1,0:T(8,128)(2,1)}, u32[]{:S(2)}, u32[]{:S(2)}) collective-permute-start(bf16[2,2816,128]{2,1,0:T(8,128)(2,1)} %slice.4), channel_id=1, source_target_pairs={{0,4},{4,0},{1,5},{5,1},{2,6},{6,2},{3,7},{7,3},{8,12},{12,8},{9,1... | collective-permute-start | bytes 4325384 | tf_op jit(solution)/shard_map/ppermute | solution.py:126
  7.8 2.6 copy-done
  10.4 2.0 swap1.1
  12.5 11.6 %psum.7.refs_1_ = f32[8,512]{1,0:T(8,128)S(1)} all-reduce(f32[8,512]{1,0:T(8,128)S(1)} %get-tuple-element.131), channel_id=1, replica_groups=mesh['cell'=4,'spot'=2,'gene'=4] {'cell'}, use_global_device_ids=true, to_apply=%region_0.1 | all-reduce | flops 4096 | bytes 32768 | tf_op jit(solution)/shard_map/psum | solution.py:234
  25.7 2.6 collective-permute-start.1
  28.5 1.9 collective-permute-done.1.refs_1_.refs_3_
  30.4 3.4 %collective-permute-done.2.refs_2_.refs_4_ = f32[8,512]{1,0:T(8,128)S(1)} collective-permute-done((f32[8,512]{1,0:T(8,128)S(1)}, f32[8,512]{1,0:T(8,128)S(1)}, u32[]{:S(2)}, u32[]{:S(2)}) %collective-permute-start.2) | collective-permute-done | bytes 16416 | tf_op jit(solution)/shard_map/ppermute | solution.py:123
  34.4 2.6 copy-done.1
  39.1 2.0 along0.1
  41.6 2.2 collective-permute-start.5
  45.5 2.4 collective-permute-start.6
  48.3 4.0 %prob.1 = (bf16[512,2816]{1,0:T(8,128)(2,1)S(1)}, f32[8,2816]{1,0:T(8,128)S(1)}, f32[8,512]{1,0:T(8,128)S(1)}, f32[8,512]{1,0:T(8,128)S(1)}, f32[8,128]{1,0:T(8,128)S(1)}) custom-call(s32[5]{0:T(128)S(1)} %stack.27.flags, bf16[2816,512]{1,0:T(8,128)(2,1)S(1)} %copy-done.2, f32[8,512]{1,0:T(8,128)S(1)} %psum.7.refs_1_, ...), custom_call_target="tpu_custom_call", output_to_operand_aliasing={{4}: (6, {})} | custom-call | tf_op jit(solution)/shard_map/prob/pallas_call | solution.py:66
  53.0 16.9 %collective-permute-done.9.refs_0_.refs_7_ = bf16[2,2816,128]{2,1,0:T(8,128)(2,1)} collective-permute-done((bf16[2,2816,128]{2,1,0:T(8,128)(2,1)}, bf16[2,2816,128]{2,1,0:T(8,128)(2,1)}, u32[]{:S(2)}, u32[]{:S(2)}) %collective-permute-start.9) | collective-permute-done | bytes 1441824 | tf_op jit(solution)/shard_map/ppermute | solution.py:126
  72.5 3.4 %collective-permute-done.7.refs_1_.refs_5_ = bf16[1408,128]{1,0:T(8,128)(2,1)S(1)} collective-permute-done((bf16[1408,128]{1,0:T(8,128)(2,1)S(1)}, bf16[1408,128]{1,0:T(8,128)(2,1)S(1)}, u32[]{:S(2)}, u32[]{:S(2)}) %collective-permute-start.7) | collective-permute-done | bytes 360480 | tf_op jit(solution)/shard_map/ppermute | solution.py:123
  77.0 2.0 collective-permute-start.12
  80.5 2.2 collective-permute-start.11
  82.7 18.0 %collective-permute-done.8.refs_0_.refs_2_ = bf16[2,2816,128]{2,1,0:T(8,128)(2,1)S(1)} collective-permute-done((bf16[2,2816,128]{2,1,0:T(8,128)(2,1)S(1)}, bf16[2,2816,128]{2,1,0:T(8,128)(2,1)S(1)}, u32[]{:S(2)}, u32[]{:S(2)}) %collective-permute-start.8) | collective-permute-done | bytes 1441824 | tf_op jit(solution)/shard_map/ppermute | solution.py:126
  101.8 7.7 %collective-permute-done.11.refs_1_.refs_10_ = bf16[1408,128]{1,0:T(8,128)(2,1)S(1)} collective-permute-done((bf16[1408,128]{1,0:T(8,128)(2,1)S(1)}, bf16[1408,128]{1,0:T(8,128)(2,1)S(1)}, u32[]{:S(2)}, u32[]{:S(2)}) %collective-permute-start.11) | collective-permute-done | bytes 360480 | tf_op jit(solution)/shard_map/ppermute | solution.py:123
  110.6 2.0 collective-permute-start.17
  116.7 15.0 %collective-permute-done.14.refs_0_.refs_2_ = bf16[2,2816,128]{2,1,0:T(8,128)(2,1)S(1)} collective-permute-done((bf16[2,2816,128]{2,1,0:T(8,128)(2,1)S(1)}, bf16[2,2816,128]{2,1,0:T(8,128)(2,1)S(1)}, u32[]{:S(2)}, u32[]{:S(2)}) %collective-permute-start.14) | collective-permute-done | bytes 1441824 | tf_op jit(solution)/shard_map/ppermute | solution.py:126
  132.8 6.0 %collective-permute-done.16.refs_1_.refs_5_ = bf16[1408,128]{1,0:T(8,128)(2,1)S(1)} collective-permute-done((bf16[1408,128]{1,0:T(8,128)(2,1)S(1)}, bf16[1408,128]{1,0:T(8,128)(2,1)S(1)}, u32[]{:S(2)}, u32[]{:S(2)}) %collective-permute-start.16) | collective-permute-done | bytes 360480 | tf_op jit(solution)/shard_map/ppermute | solution.py:123
  140.5 2.0 collective-permute-start.18
  145.0 1.9 collective-permute-start.20
  148.2 2.1 collective-permute-start.25
  150.4 12.2 %collective-permute-done.18.refs_0_.refs_11_ = bf16[2,1408,128]{2,1,0:T(8,128)(2,1)S(1)} collective-permute-done((bf16[2,1408,128]{2,1,0:T(8,128)(2,1)S(1)}, bf16[2,1408,128]{2,1,0:T(8,128)(2,1)S(1)}, u32[]{:S(2)}, u32[]{:S(2)}) %collective-permute-start.18) | collective-permute-done | bytes 720928 | tf_op jit(solution)/shard_map/ppermute | solution.py:126
  163.1 5.0 %forward0.1 = (bf16[2816,512]{1,0:T(8,128)(2,1)S(1)}, bf16[2816,512]{1,0:T(8,128)(2,1)S(1)}, f32[2,128,1024]{2,1,0:T(8,128)S(1)}, f32[128,1024]{1,0:T(8,128)S(1)...) custom-call(s32[5]{0:T(128)S(1)} %stack.27.flags, ...), custom_call_target="tpu_custom_call", output_to_operand_aliasing={{5}: (13, {})} | custom-call | tf_op jit(solution)/shard_map/forward0/pallas_call | solution.py:66
  168.1 3.2 %collective-permute-done.20.refs_1_.refs_5_ = bf16[1536,128]{1,0:T(8,128)(2,1)S(1)} collective-permute-done((bf16[1536,128]{1,0:T(8,128)(2,1)S(1)}, bf16[1536,128]{1,0:T(8,128)(2,1)S(1)}, u32[]{:S(2)}, u32[]{:S(2)}) %collective-permute-start.20) | collective-permute-done | bytes 393248 | tf_op jit(solution)/shard_map/ppermute | solution.py:123
  178.5 2.8 %forward1.1 = (bf16[2816,512]{1,0:T(8,128)(2,1)S(1)}, f32[2,128,512]{2,1,0:T(8,128)S(1)}, f32[128,512]{1,0:T(8,128)S(1)}, f32[128,512]{1,0:T(8,128)S(1)}, f32[8,128]{1,0:T(8,128)S(1)}) custom-call(s32[5]{0:T(128)S(1)} %stack.27.flags, bf16[512,2816]{1,0:T(8,128)(2,1)S(1)} %get-tuple-element.142.refs_0_, ...), custom_call_target="tpu_custom_call", output_to_operand_aliasing={{4}: (8, {})} | custom-call | tf_op jit(solution)/shard_map/forward1/pallas_call | solution.py:66
  184.5 2.1 collective-permute-start.29
  186.6 2.6 forward2.1
  189.2 2.0 collective-permute-done.24.refs_1_
  193.6 4.0 %collective-permute-start.28 = (f32[2,128,256]{2,1,0:T(8,128)S(1)}, f32[2,128,256]{2,1,0:T(8,128)S(1)}, u32[]{:S(2)}, u32[]{:S(2)}) collective-permute-start(f32[2,128,256]{2,1,0:T(8,128)S(1)} %get-tuple-element.204), channel_id=1, source_target_pairs={{0,2},{1,3},{2,0},{3,1},{4,6},{5,7},{6,4},{7,5},{8,10},{9,11},{10,... | collective-permute-start | bytes 786440 | tf_op jit(solution)/shard_map/ppermute | solution.py:123
  200.3 5.9 %collective-permute-done.33.refs_2_ = f32[128,512]{1,0:T(8,128)S(1)} collective-permute-done((f32[128,512]{1,0:T(8,128)S(1)}, f32[128,512]{1,0:T(8,128)S(1)}, u32[]{:S(2)}, u32[]{:S(2)}) %collective-permute-start.33) | collective-permute-done | bytes 262176 | tf_op jit(solution)/shard_map/ppermute | solution.py:120
  209.2 2.1 collective-permute-start.37
  212.9 3.8 %collective-permute-done.4.refs_3_ = f32[8,2816]{1,0:T(8,128)S(1)} collective-permute-done((f32[8,2816]{1,0:T(8,128)S(1)}, f32[8,2816]{1,0:T(8,128)S(1)}, u32[]{:S(2)}, u32[]{:S(2)}) %collective-permute-start.4) | collective-permute-done | bytes 90144 | tf_op jit(solution)/shard_map/ppermute | solution.py:126
  217.8 2.5 collective-permute-done.36.refs_2_
  225.2 2.0 collective-permute-start.38
  237.7 2.0 collective-permute-start.49
  241.1 2.4 collective-permute-done.50.refs_4_.refs_12_
  243.5 3.5 %collective-permute-done.48.refs_1_ = bf16[128,512]{1,0:T(8,128)(2,1)S(1)} collective-permute-done((bf16[128,512]{1,0:T(8,128)(2,1)S(1)}, bf16[128,512]{1,0:T(8,128)(2,1)S(1)}, u32[]{:S(2)}, u32[]{:S(2)}) %collective-permute-start.48) | collective-permute-done | bytes 131104 | tf_op jit(solution)/shard_map/ppermute | solution.py:123
  250.6 4.2 %own.1 = (f32[2816,512]{1,0:T(8,128)S(1)}, f32[8,128]{1,0:T(8,128)S(1)}) custom-call(s32[5]{0:T(128)S(1)} %stack.27.flags, f32[2816,128]{1,0:T(8,128)S(1)} %get-tuple-element.224.refs_0_, bf16[2816,512]{1,0:T(8,128)(2,1)S(1)} %get-tuple-element.225.refs_1_.refs_3_, ...), custom_call_target="tpu_custom_call", output_to_operand_aliasing={{1}: (10, {})} | custom-call | tf_op jit(solution)/shard_map/own/pallas_call | solution.py:66
  257.7 6.6 %backward.1 = (f32[2816,512]{1,0:T(8,128)S(1)}, f32[8,512]{1,0:T(8,128)S(1)}, f32[8,128]{1,0:T(8,128)S(1)}) custom-call(s32[5]{0:T(128)S(1)} %stack.27.flags, bf16[2816,512]{1,0:T(8,128)(2,1)S(1)} %copy-done.2, f32[8,512]{1,0:T(8,128)S(1)} %get-tuple-element.140.refs_1_, ...), custom_call_target="tpu_custom_call", output_to_operand_aliasing={{2}: (14, {})} | custom-call | tf_op jit(solution)/shard_map/backward/pallas_call | solution.py:66
  264.3 3.5 %collective-permute-start.54 = (f32[8,512]{1,0:T(8,128)S(1)}, f32[8,512]{1,0:T(8,128)S(1)}, u32[]{:S(2)}, u32[]{:S(2)}) collective-permute-start(f32[8,512]{1,0:T(8,128)S(1)} %get-tuple-element.256), channel_id=1, source_target_pairs={{0,1},{1,0},{2,3},{3,2},{4,5},{5,4},{6,7},{7,6},{8,9},{9,8},{10,11... | collective-permute-start | bytes 49160 | tf_op jit(solution)/shard_map/ppermute | solution.py:123
  268.2 1.9 collective-permute-start.56
  270.2 2.2 collective-permute-done.55
  275.3 2.2 collective-permute-done.57
  278.8 3.8 %final.1 = (f32[2816,512]{1,0:T(8,128)}, f32[5]{0:T(128)}, f32[8,128]{1,0:T(8,128)S(1)}) custom-call(s32[5]{0:T(128)S(1)} %stack.27.flags, bf16[2816,512]{1,0:T(8,128)(2,1)S(1)} %copy-done.2, f32[8,512]{1,0:T(8,128)S(1)} %get-tuple-element.140.refs_1_, f32[2816,512]{1,0:T(8,128)S(1)} %get-tuple-element.255.refs_2_, ...), custom_call_target="tpu_custom_call", output_to_operand_aliasing={{2}: (5, {})} | custom-call | tf_op jit(solution)/shard_map/final/pallas_call | solution.py:66
  (149 shorter events, 76.9 us)
Async XLA Ops:
  3.4 35.7 %collective-permute-start.3 = (bf16[2,2816,128]{2,1,0:T(8,128)(2,1)}, bf16[2,2816,128]{2,1,0:T(8,128)(2,1)}, u32[]{:S(2)}, u32[]{:S(2)}) collective-permute-start(bf16[2,2816,128]{2,1,0:T(8,128)(2,1)} %slice.4), channel_id=1, source_target_pairs={{0,4},{4,0},{1,5},{5,1},{2,6},{6,2},{3,7},{7,3},{8,12},{12,8},{9,1... | collective-permute-start | bytes 4325384 | tf_op jit(solution)/shard_map/ppermute | solution.py:126
  12.4 57.5 %collective-permute-start.9 = (bf16[2,2816,128]{2,1,0:T(8,128)(2,1)}, bf16[2,2816,128]{2,1,0:T(8,128)(2,1)}, u32[]{:S(2)}, u32[]{:S(2)}) collective-permute-start(bf16[2,2816,128]{2,1,0:T(8,128)(2,1)} %get-tuple-element.147), channel_id=1, source_target_pairs={{0,4},{4,0},{1,5},{5,1},{2,6},{6,2},{3,7},{7,3},{8,12},{12,8},{9,1... | collective-permute-start | bytes 4325384 | tf_op jit(solution)/shard_map/ppermute | solution.py:126
  24.1 4.4 %collective-permute-start = (f32[8,512]{1,0:T(8,128)S(1)}, f32[8,512]{1,0:T(8,128)S(1)}, u32[]{:S(2)}, u32[]{:S(2)}) collective-permute-start(f32[8,512]{1,0:T(8,128)S(1)} %psum.7.refs_1_), channel_id=1, source_target_pairs={{0,1},{1,0},{2,3},{3,2},{4,5},{5,4},{6,7},{7,6},{8,9},{9,8},{10,11... | collective-permute-start | bytes 49160 | tf_op jit(solution)/shard_map/ppermute | solution.py:123
  25.7 4.7 %collective-permute-start.1 = (f32[8,512]{1,0:T(8,128)S(1)}, f32[8,512]{1,0:T(8,128)S(1)}, u32[]{:S(2)}, u32[]{:S(2)}) collective-permute-start(f32[8,512]{1,0:T(8,128)S(1)} %psum.7.refs_1_), channel_id=1, source_target_pairs={{0,2},{1,3},{2,0},{3,1},{4,6},{5,7},{6,4},{7,5},{8,10},{9,11},{10,... | collective-permute-start | bytes 49160 | tf_op jit(solution)/shard_map/ppermute | solution.py:123
  28.3 5.5 %collective-permute-start.2 = (f32[8,512]{1,0:T(8,128)S(1)}, f32[8,512]{1,0:T(8,128)S(1)}, u32[]{:S(2)}, u32[]{:S(2)}) collective-permute-start(f32[8,512]{1,0:T(8,128)S(1)} %psum.7.refs_1_), channel_id=1, source_target_pairs={{0,3},{1,2},{2,1},{3,0},{4,7},{5,6},{6,5},{7,4},{8,11},{9,10},{10,... | collective-permute-start | bytes 49160 | tf_op jit(solution)/shard_map/ppermute | solution.py:123
  41.6 34.3 %collective-permute-start.5 = (bf16[2816,128]{1,0:T(8,128)(2,1)S(1)}, bf16[2816,128]{1,0:T(8,128)(2,1)S(1)}, u32[]{:S(2)}, u32[]{:S(2)}) collective-permute-start(bf16[2816,128]{1,0:T(8,128)(2,1)S(1)} %get-tuple-element.143), channel_id=1, source_target_pairs={{0,1},{1,0},{2,3},{3,2},{4,5},{5,4},{6,7},{7,6},{8,9},{9,8},{10,11... | collective-permute-start | bytes 2162696 | tf_op jit(solution)/shard_map/ppermute | solution.py:123
  43.8 57.0 %collective-permute-start.8 = (bf16[2,2816,128]{2,1,0:T(8,128)(2,1)S(1)}, bf16[2,2816,128]{2,1,0:T(8,128)(2,1)S(1)}, u32[]{:S(2)}, u32[]{:S(2)}) collective-permute-start(bf16[2,2816,128]{2,1,0:T(8,128)(2,1)S(1)} %get-tuple-element.146), channel_id=1, source_target_pairs={{0,4},{4,0},{1,5},{5,1},{2,6},{6,2},{3,7},{7,3},{8,12},{12,8},{9,1... | collective-permute-start | bytes 4325384 | tf_op jit(solution)/shard_map/ppermute | solution.py:126
  45.5 27.0 %collective-permute-start.6 = (bf16[1408,128]{1,0:T(8,128)(2,1)S(1)}, bf16[1408,128]{1,0:T(8,128)(2,1)S(1)}, u32[]{:S(2)}, u32[]{:S(2)}) collective-permute-start(bf16[1408,128]{1,0:T(8,128)(2,1)S(1)} %get-tuple-element.144), channel_id=1, source_target_pairs={{0,2},{1,3},{2,0},{3,1},{4,6},{5,7},{6,4},{7,5},{8,10},{9,11},{10,... | collective-permute-start | bytes 1081352 | tf_op jit(solution)/shard_map/ppermute | solution.py:123
  47.9 28.0 %collective-permute-start.7 = (bf16[1408,128]{1,0:T(8,128)(2,1)S(1)}, bf16[1408,128]{1,0:T(8,128)(2,1)S(1)}, u32[]{:S(2)}, u32[]{:S(2)}) collective-permute-start(bf16[1408,128]{1,0:T(8,128)(2,1)S(1)} %get-tuple-element.145), channel_id=1, source_target_pairs={{0,3},{1,2},{2,1},{3,0},{4,7},{5,6},{6,5},{7,4},{8,11},{9,10},{10,... | collective-permute-start | bytes 1081352 | tf_op jit(solution)/shard_map/ppermute | solution.py:123
  77.0 32.5 %collective-permute-start.12 = (bf16[2816,128]{1,0:T(8,128)(2,1)S(1)}, bf16[2816,128]{1,0:T(8,128)(2,1)S(1)}, u32[]{:S(2)}, u32[]{:S(2)}) collective-permute-start(bf16[2816,128]{1,0:T(8,128)(2,1)S(1)} %get-tuple-element.161), channel_id=1, source_target_pairs={{0,1},{1,0},{2,3},{3,2},{4,5},{5,4},{6,7},{7,6},{8,9},{9,8},{10,11... | collective-permute-start | bytes 2162696 | tf_op jit(solution)/shard_map/ppermute | solution.py:123
  78.9 52.7 %collective-permute-start.14 = (bf16[2,2816,128]{2,1,0:T(8,128)(2,1)S(1)}, bf16[2,2816,128]{2,1,0:T(8,128)(2,1)S(1)}, u32[]{:S(2)}, u32[]{:S(2)}) collective-permute-start(bf16[2,2816,128]{2,1,0:T(8,128)(2,1)S(1)} %get-tuple-element.165), channel_id=1, source_target_pairs={{0,4},{4,0},{1,5},{5,1},{2,6},{6,2},{3,7},{7,3},{8,12},{12,8},{9,1... | collective-permute-start | bytes 4325384 | tf_op jit(solution)/shard_map/ppermute | solution.py:126
  79.4 22.4 %collective-permute-start.10 = (bf16[1408,128]{1,0:T(8,128)(2,1)S(1)}, bf16[1408,128]{1,0:T(8,128)(2,1)S(1)}, u32[]{:S(2)}, u32[]{:S(2)}) collective-permute-start(bf16[1408,128]{1,0:T(8,128)(2,1)S(1)} %get-tuple-element.159), channel_id=1, source_target_pairs={{0,2},{1,3},{2,0},{3,1},{4,6},{5,7},{6,4},{7,5},{8,10},{9,11},{10,... | collective-permute-start | bytes 1081352 | tf_op jit(solution)/shard_map/ppermute | solution.py:123
  80.5 28.9 %collective-permute-start.11 = (bf16[1408,128]{1,0:T(8,128)(2,1)S(1)}, bf16[1408,128]{1,0:T(8,128)(2,1)S(1)}, u32[]{:S(2)}, u32[]{:S(2)}) collective-permute-start(bf16[1408,128]{1,0:T(8,128)(2,1)S(1)} %get-tuple-element.160), channel_id=1, source_target_pairs={{0,3},{1,2},{2,1},{3,0},{4,7},{5,6},{6,5},{7,4},{8,11},{9,10},{10,... | collective-permute-start | bytes 1081352 | tf_op jit(solution)/shard_map/ppermute | solution.py:123
  110.6 28.2 %collective-permute-start.17 = (bf16[2816,128]{1,0:T(8,128)(2,1)S(1)}, bf16[2816,128]{1,0:T(8,128)(2,1)S(1)}, u32[]{:S(2)}, u32[]{:S(2)}) collective-permute-start(bf16[2816,128]{1,0:T(8,128)(2,1)S(1)} %get-tuple-element.172), channel_id=1, source_target_pairs={{0,1},{1,0},{2,3},{3,2},{4,5},{5,4},{6,7},{7,6},{8,9},{9,8},{10,11... | collective-permute-start | bytes 2162696 | tf_op jit(solution)/shard_map/ppermute | solution.py:123
  112.6 20.2 %collective-permute-start.15 = (bf16[1408,128]{1,0:T(8,128)(2,1)S(1)}, bf16[1408,128]{1,0:T(8,128)(2,1)S(1)}, u32[]{:S(2)}, u32[]{:S(2)}) collective-permute-start(bf16[1408,128]{1,0:T(8,128)(2,1)S(1)} %get-tuple-element.170), channel_id=1, source_target_pairs={{0,2},{1,3},{2,0},{3,1},{4,6},{5,7},{6,4},{7,5},{8,10},{9,11},{10,... | collective-permute-start | bytes 1081352 | tf_op jit(solution)/shard_map/ppermute | solution.py:123
  113.2 25.6 %collective-permute-start.16 = (bf16[1408,128]{1,0:T(8,128)(2,1)S(1)}, bf16[1408,128]{1,0:T(8,128)(2,1)S(1)}, u32[]{:S(2)}, u32[]{:S(2)}) collective-permute-start(bf16[1408,128]{1,0:T(8,128)(2,1)S(1)} %get-tuple-element.171), channel_id=1, source_target_pairs={{0,3},{1,2},{2,1},{3,0},{4,7},{5,6},{6,5},{7,4},{8,11},{9,10},{10,... | collective-permute-start | bytes 1081352 | tf_op jit(solution)/shard_map/ppermute | solution.py:123
  115.6 31.5 %collective-permute-start.13 = (bf16[2,1408,128]{2,1,0:T(8,128)(2,1)S(1)}, bf16[2,1408,128]{2,1,0:T(8,128)(2,1)S(1)}, u32[]{:S(2)}, u32[]{:S(2)}) collective-permute-start(bf16[2,1408,128]{2,1,0:T(8,128)(2,1)S(1)} %get-tuple-element.164), channel_id=1, source_target_pairs={{0,4},{4,0},{1,5},{5,1},{2,6},{6,2},{3,7},{7,3},{8,12},{12,8},{9,1... | collective-permute-start | bytes 2162696 | tf_op jit(solution)/shard_map/ppermute | solution.py:126
  140.5 22.0 %collective-permute-start.18 = (bf16[2,1408,128]{2,1,0:T(8,128)(2,1)S(1)}, bf16[2,1408,128]{2,1,0:T(8,128)(2,1)S(1)}, u32[]{:S(2)}, u32[]{:S(2)}) collective-permute-start(bf16[2,1408,128]{2,1,0:T(8,128)(2,1)S(1)} %get-tuple-element.175), channel_id=1, source_target_pairs={{0,4},{4,0},{1,5},{5,1},{2,6},{6,2},{3,7},{7,3},{8,12},{12,8},{9,1... | collective-permute-start | bytes 2162696 | tf_op jit(solution)/shard_map/ppermute | solution.py:126
  142.5 28.7 %collective-permute-start.21 = (bf16[2816,128]{1,0:T(8,128)(2,1)S(1)}, bf16[2816,128]{1,0:T(8,128)(2,1)S(1)}, u32[]{:S(2)}, u32[]{:S(2)}) collective-permute-start(bf16[2816,128]{1,0:T(8,128)(2,1)S(1)} %get-tuple-element.183), channel_id=1, source_target_pairs={{0,1},{1,0},{2,3},{3,2},{4,5},{5,4},{6,7},{7,6},{8,9},{9,8},{10,11... | collective-permute-start | bytes 2162696 | tf_op jit(solution)/shard_map/ppermute | solution.py:123
  144.2 23.9 %collective-permute-start.19 = (bf16[1536,128]{1,0:T(8,128)(2,1)S(1)}, bf16[1536,128]{1,0:T(8,128)(2,1)S(1)}, u32[]{:S(2)}, u32[]{:S(2)}) collective-permute-start(bf16[1536,128]{1,0:T(8,128)(2,1)S(1)} %get-tuple-element.181), channel_id=1, source_target_pairs={{0,2},{1,3},{2,0},{3,1},{4,6},{5,7},{6,4},{7,5},{8,10},{9,11},{10,... | collective-permute-start | bytes 1179656 | tf_op jit(solution)/shard_map/ppermute | solution.py:123
  145.0 26.2 %collective-permute-start.20 = (bf16[1536,128]{1,0:T(8,128)(2,1)S(1)}, bf16[1536,128]{1,0:T(8,128)(2,1)S(1)}, u32[]{:S(2)}, u32[]{:S(2)}) collective-permute-start(bf16[1536,128]{1,0:T(8,128)(2,1)S(1)} %get-tuple-element.182), channel_id=1, source_target_pairs={{0,3},{1,2},{2,1},{3,0},{4,7},{5,6},{6,5},{7,4},{8,11},{9,10},{10,... | collective-permute-start | bytes 1179656 | tf_op jit(solution)/shard_map/ppermute | solution.py:123
  148.2 29.7 %collective-permute-start.25 = (bf16[2,1408,128]{2,1,0:T(8,128)(2,1)S(1)}, bf16[2,1408,128]{2,1,0:T(8,128)(2,1)S(1)}, u32[]{:S(2)}, u32[]{:S(2)}) collective-permute-start(bf16[2,1408,128]{2,1,0:T(8,128)(2,1)S(1)} %get-tuple-element.191), channel_id=1, source_target_pairs={{0,4},{4,0},{1,5},{5,1},{2,6},{6,2},{3,7},{7,3},{8,12},{12,8},{9,1... | collective-permute-start | bytes 2162696 | tf_op jit(solution)/shard_map/ppermute | solution.py:126
  173.5 18.3 %collective-permute-start.30 = (bf16[2,1280,128]{2,1,0:T(8,128)(2,1)S(1)}, bf16[2,1280,128]{2,1,0:T(8,128)(2,1)S(1)}, u32[]{:S(2)}, u32[]{:S(2)}) collective-permute-start(bf16[2,1280,128]{2,1,0:T(8,128)(2,1)S(1)} %get-tuple-element.207), channel_id=1, source_target_pairs={{0,4},{4,0},{1,5},{5,1},{2,6},{6,2},{3,7},{7,3},{8,12},{12,8},{9,1... | collective-permute-start | bytes 1966088 | tf_op jit(solution)/shard_map/ppermute | solution.py:126
  176.3 14.8 %collective-permute-start.24 = (f32[128,1024]{1,0:T(8,128)S(1)}, f32[128,1024]{1,0:T(8,128)S(1)}, u32[]{:S(2)}, u32[]{:S(2)}) collective-permute-start(f32[128,1024]{1,0:T(8,128)S(1)} %get-tuple-element.190), channel_id=1, source_target_pairs={{0,16},{8,24},{16,0},{24,8},{1,17},{9,25},{17,1},{25,9},{2,18},{10... | collective-permute-start | bytes 1572872 | tf_op jit(solution)/shard_map/ppermute | solution.py:120
  184.5 15.3 %collective-permute-start.29 = (f32[136,512]{1,0:T(8,128)S(1)}, f32[136,512]{1,0:T(8,128)S(1)}, u32[]{:S(2)}, u32[]{:S(2)}) collective-permute-start(f32[136,512]{1,0:T(8,128)S(1)} %get-tuple-element.206), channel_id=1, source_target_pairs={{0,16},{8,24},{16,0},{24,8},{1,17},{9,25},{17,1},{25,9},{2,18},{10... | collective-permute-start | bytes 835592 | tf_op jit(solution)/shard_map/ppermute | solution.py:120
  193.0 4.6 %collective-permute-start.31 = (f32[128,512]{1,0:T(8,128)S(1)}, f32[128,512]{1,0:T(8,128)S(1)}, u32[]{:S(2)}, u32[]{:S(2)}) collective-permute-start(f32[128,512]{1,0:T(8,128)S(1)} %get-tuple-element.214), channel_id=1, source_target_pairs={{0,8},{8,0},{16,24},{24,16},{1,9},{9,1},{17,25},{25,17},{2,10},{10... | collective-permute-start | bytes 786440 | tf_op jit(solution)/shard_map/ppermute | solution.py:117
  193.1 4.5 %collective-permute-start.32 = (f32[128,512]{1,0:T(8,128)S(1)}, f32[128,512]{1,0:T(8,128)S(1)}, u32[]{:S(2)}, u32[]{:S(2)}) collective-permute-start(f32[128,512]{1,0:T(8,128)S(1)} %get-tuple-element.215), channel_id=1, source_target_pairs={{0,8},{8,0},{16,24},{24,16},{1,9},{9,1},{17,25},{25,17},{2,10},{10... | collective-permute-start | bytes 786440 | tf_op jit(solution)/shard_map/ppermute | solution.py:117
  193.6 17.7 %collective-permute-start.28 = (f32[2,128,256]{2,1,0:T(8,128)S(1)}, f32[2,128,256]{2,1,0:T(8,128)S(1)}, u32[]{:S(2)}, u32[]{:S(2)}) collective-permute-start(f32[2,128,256]{2,1,0:T(8,128)S(1)} %get-tuple-element.204), channel_id=1, source_target_pairs={{0,2},{1,3},{2,0},{3,1},{4,6},{5,7},{6,4},{7,5},{8,10},{9,11},{10,... | collective-permute-start | bytes 786440 | tf_op jit(solution)/shard_map/ppermute | solution.py:123
  198.2 8.1 %collective-permute-start.33 = (f32[128,512]{1,0:T(8,128)S(1)}, f32[128,512]{1,0:T(8,128)S(1)}, u32[]{:S(2)}, u32[]{:S(2)}) collective-permute-start(f32[128,512]{1,0:T(8,128)S(1)} %get-tuple-element.220), channel_id=1, source_target_pairs={{0,16},{8,24},{16,0},{24,8},{1,17},{9,25},{17,1},{25,9},{2,18},{10... | collective-permute-start | bytes 786440 | tf_op jit(solution)/shard_map/ppermute | solution.py:120
  206.9 10.9 %collective-permute-start.35 = (f32[128,256]{1,0:T(8,128)S(1)}, f32[128,256]{1,0:T(8,128)S(1)}, u32[]{:S(2)}, u32[]{:S(2)}) collective-permute-start(f32[128,256]{1,0:T(8,128)S(1)} %get-tuple-element.235), channel_id=1, source_target_pairs={{0,1},{1,0},{2,3},{3,2},{4,5},{5,4},{6,7},{7,6},{8,9},{9,8},{10,11... | collective-permute-start | bytes 393224 | tf_op jit(solution)/shard_map/ppermute | solution.py:123
  208.1 12.2 %collective-permute-start.36 = (f32[128,256]{1,0:T(8,128)S(1)}, f32[128,256]{1,0:T(8,128)S(1)}, u32[]{:S(2)}, u32[]{:S(2)}) collective-permute-start(f32[128,256]{1,0:T(8,128)S(1)} %get-tuple-element.236), channel_id=1, source_target_pairs={{0,2},{1,3},{2,0},{3,1},{4,6},{5,7},{6,4},{7,5},{8,10},{9,11},{10,... | collective-permute-start | bytes 393224 | tf_op jit(solution)/shard_map/ppermute | solution.py:123
  209.2 11.1 %collective-permute-start.37 = (f32[128,256]{1,0:T(8,128)S(1)}, f32[128,256]{1,0:T(8,128)S(1)}, u32[]{:S(2)}, u32[]{:S(2)}) collective-permute-start(f32[128,256]{1,0:T(8,128)S(1)} %get-tuple-element.237), channel_id=1, source_target_pairs={{0,3},{1,2},{2,1},{3,0},{4,7},{5,6},{6,5},{7,4},{8,11},{9,10},{10,... | collective-permute-start | bytes 393224 | tf_op jit(solution)/shard_map/ppermute | solution.py:123
  211.9 9.1 %collective-permute-start.34 = (f32[128,256]{1,0:T(8,128)S(1)}, f32[128,256]{1,0:T(8,128)S(1)}, u32[]{:S(2)}, u32[]{:S(2)}) collective-permute-start(f32[128,256]{1,0:T(8,128)S(1)} %get-tuple-element.233), channel_id=1, source_target_pairs={{0,1},{1,0},{2,3},{3,2},{4,5},{5,4},{6,7},{7,6},{8,9},{9,8},{10,11... | collective-permute-start | bytes 393224 | tf_op jit(solution)/shard_map/ppermute | solution.py:123
  212.2 4.5 %collective-permute-start.4 = (f32[8,2816]{1,0:T(8,128)S(1)}, f32[8,2816]{1,0:T(8,128)S(1)}, u32[]{:S(2)}, u32[]{:S(2)}) collective-permute-start(f32[8,2816]{1,0:T(8,128)S(1)} %get-tuple-element.141.refs_2_), channel_id=1, source_target_pairs={{0,4},{4,0},{1,5},{5,1},{2,6},{6,2},{3,7},{7,3},{8,12},{12,8},{9,1... | collective-permute-start | bytes 270344 | tf_op jit(solution)/shard_map/ppermute | solution.py:126
  223.7 5.9 %collective-permute-start.42 = (f32[16,512]{1,0:T(8,128)S(1)}, f32[16,512]{1,0:T(8,128)S(1)}, u32[]{:S(2)}, u32[]{:S(2)}) collective-permute-start(f32[16,512]{1,0:T(8,128)S(1)} %add.29), channel_id=1, source_target_pairs={{0,16},{8,24},{16,0},{24,8},{1,17},{9,25},{17,1},{25,9},{2,18},{10... | collective-permute-start | bytes 98312 | tf_op jit(solution)/shard_map/ppermute | solution.py:120
  225.2 5.1 %collective-permute-start.38 = (f32[8,128]{1,0:T(8,128)S(1)}, f32[8,128]{1,0:T(8,128)S(1)}, u32[]{:S(2)}, u32[]{:S(2)}) collective-permute-start(f32[8,128]{1,0:T(8,128)S(1)} %get-tuple-element.243.refs_0_.refs_4_), channel_id=1, source_target_pairs={{0,1},{1,0},{2,3},{3,2},{4,5},{5,4},{6,7},{7,6},{8,9},{9,8},{10,11... | collective-permute-start | bytes 12296 | tf_op jit(solution)/shard_map/ppermute | solution.py:123
  227.2 4.5 %collective-permute-start.39 = (f32[8,128]{1,0:T(8,128)S(1)}, f32[8,128]{1,0:T(8,128)S(1)}, u32[]{:S(2)}, u32[]{:S(2)}) collective-permute-start(f32[8,128]{1,0:T(8,128)S(1)} %get-tuple-element.243.refs_0_.refs_4_), channel_id=1, source_target_pairs={{0,2},{1,3},{2,0},{3,1},{4,6},{5,7},{6,4},{7,5},{8,10},{9,11},{10,... | collective-permute-start | bytes 12296 | tf_op jit(solution)/shard_map/ppermute | solution.py:123
  227.8 5.4 %collective-permute-start.40 = (f32[8,128]{1,0:T(8,128)S(1)}, f32[8,128]{1,0:T(8,128)S(1)}, u32[]{:S(2)}, u32[]{:S(2)}) collective-permute-start(f32[8,128]{1,0:T(8,128)S(1)} %get-tuple-element.243.refs_0_.refs_4_), channel_id=1, source_target_pairs={{0,3},{1,2},{2,1},{3,0},{4,7},{5,6},{6,5},{7,4},{8,11},{9,10},{10,... | collective-permute-start | bytes 12296 | tf_op jit(solution)/shard_map/ppermute | solution.py:123
  229.6 4.1 %collective-permute-start.43 = (f32[16,512]{1,0:T(8,128)S(1)}, f32[16,512]{1,0:T(8,128)S(1)}, u32[]{:S(2)}, u32[]{:S(2)}) collective-permute-start(f32[16,512]{1,0:T(8,128)S(1)} %add.30.refs_8_), channel_id=1, source_target_pairs={{0,4},{4,0},{1,5},{5,1},{2,6},{6,2},{3,7},{7,3},{8,12},{12,8},{9,1... | collective-permute-start | bytes 98312 | tf_op jit(solution)/shard_map/ppermute | solution.py:126
  234.7 8.7 %collective-permute-start.45 = (bf16[128,512]{1,0:T(8,128)(2,1)S(1)}, bf16[128,512]{1,0:T(8,128)(2,1)S(1)}, u32[]{:S(2)}, u32[]{:S(2)}) collective-permute-start(bf16[128,512]{1,0:T(8,128)(2,1)S(1)} %get-tuple-element.246.refs_5_), channel_id=1, source_target_pairs={{0,16},{8,24},{16,0},{24,8},{1,17},{9,25},{17,1},{25,9},{2,18},{10... | collective-permute-start | bytes 393224 | tf_op jit(solution)/shard_map/ppermute | solution.py:120
  235.3 8.1 %collective-permute-start.47 = (bf16[128,512]{1,0:T(8,128)(2,1)S(1)}, bf16[128,512]{1,0:T(8,128)(2,1)S(1)}, u32[]{:S(2)}, u32[]{:S(2)}) collective-permute-start(bf16[128,512]{1,0:T(8,128)(2,1)S(1)} %get-tuple-element.246.refs_5_), channel_id=1, source_target_pairs={{0,1},{1,0},{2,3},{3,2},{4,5},{5,4},{6,7},{7,6},{8,9},{9,8},{10,11... | collective-permute-start | bytes 393224 | tf_op jit(solution)/shard_map/ppermute | solution.py:123
  236.2 10.7 %collective-permute-start.48 = (bf16[128,512]{1,0:T(8,128)(2,1)S(1)}, bf16[128,512]{1,0:T(8,128)(2,1)S(1)}, u32[]{:S(2)}, u32[]{:S(2)}) collective-permute-start(bf16[128,512]{1,0:T(8,128)(2,1)S(1)} %get-tuple-element.246.refs_5_), channel_id=1, source_target_pairs={{0,2},{1,3},{2,0},{3,1},{4,6},{5,7},{6,4},{7,5},{8,10},{9,11},{10,... | collective-permute-start | bytes 393224 | tf_op jit(solution)/shard_map/ppermute | solution.py:123
  237.7 9.2 %collective-permute-start.49 = (bf16[128,512]{1,0:T(8,128)(2,1)S(1)}, bf16[128,512]{1,0:T(8,128)(2,1)S(1)}, u32[]{:S(2)}, u32[]{:S(2)}) collective-permute-start(bf16[128,512]{1,0:T(8,128)(2,1)S(1)} %get-tuple-element.246.refs_5_), channel_id=1, source_target_pairs={{0,3},{1,2},{2,1},{3,0},{4,7},{5,6},{6,5},{7,4},{8,11},{9,10},{10,... | collective-permute-start | bytes 393224 | tf_op jit(solution)/shard_map/ppermute | solution.py:123
  247.5 7.8 %collective-permute-start.52 = (bf16[3,128,512]{2,1,0:T(8,128)(2,1)S(1)}, bf16[3,128,512]{2,1,0:T(8,128)(2,1)S(1)}, u32[]{:S(2)}, u32[]{:S(2)}) collective-permute-start(bf16[3,128,512]{2,1,0:T(8,128)(2,1)S(1)} %get-tuple-element.251.refs_7_), channel_id=1, source_target_pairs={{0,16},{8,24},{16,0},{24,8},{1,17},{9,25},{17,1},{25,9},{2,18},{10... | collective-permute-start | bytes 1179656 | tf_op jit(solution)/shard_map/ppermute | solution.py:120
  249.6 6.4 %collective-permute-start.51 = (bf16[3,128,512]{2,1,0:T(8,128)(2,1)S(1)}, bf16[3,128,512]{2,1,0:T(8,128)(2,1)S(1)}, u32[]{:S(2)}, u32[]{:S(2)}) collective-permute-start(bf16[3,128,512]{2,1,0:T(8,128)(2,1)S(1)} %get-tuple-element.251.refs_7_), channel_id=1, source_target_pairs={{0,8},{8,0},{16,24},{24,16},{1,9},{9,1},{17,25},{25,17},{2,10},{10... | collective-permute-start | bytes 1179656 | tf_op jit(solution)/shard_map/ppermute | solution.py:117
  264.3 5.9 %collective-permute-start.54 = (f32[8,512]{1,0:T(8,128)S(1)}, f32[8,512]{1,0:T(8,128)S(1)}, u32[]{:S(2)}, u32[]{:S(2)}) collective-permute-start(f32[8,512]{1,0:T(8,128)S(1)} %get-tuple-element.256), channel_id=1, source_target_pairs={{0,1},{1,0},{2,3},{3,2},{4,5},{5,4},{6,7},{7,6},{8,9},{9,8},{10,11... | collective-permute-start | bytes 49160 | tf_op jit(solution)/shard_map/ppermute | solution.py:123
  267.7 4.6 %collective-permute-start.55 = (f32[8,512]{1,0:T(8,128)S(1)}, f32[8,512]{1,0:T(8,128)S(1)}, u32[]{:S(2)}, u32[]{:S(2)}) collective-permute-start(f32[8,512]{1,0:T(8,128)S(1)} %get-tuple-element.256), channel_id=1, source_target_pairs={{0,2},{1,3},{2,0},{3,1},{4,6},{5,7},{6,4},{7,5},{8,10},{9,11},{10,... | collective-permute-start | bytes 49160 | tf_op jit(solution)/shard_map/ppermute | solution.py:123
  268.2 5.5 %collective-permute-start.56 = (f32[8,512]{1,0:T(8,128)S(1)}, f32[8,512]{1,0:T(8,128)S(1)}, u32[]{:S(2)}, u32[]{:S(2)}) collective-permute-start(f32[8,512]{1,0:T(8,128)S(1)} %get-tuple-element.256), channel_id=1, source_target_pairs={{0,3},{1,2},{2,1},{3,0},{4,7},{5,6},{6,5},{7,4},{8,11},{9,10},{10,... | collective-permute-start | bytes 49160 | tf_op jit(solution)/shard_map/ppermute | solution.py:123
  (20 other events, 134.2 us)

commit v10 on v8

--- a/solution.py
+++ b/solution.py
@@ -687,8 +687,9 @@
     v = (v + over_gene(v, 1)) + (over_gene(v, 2) + over_gene(v, 3))
 
     def final_body(fl, i, out):
-        prob = jnp.exp(i[0][...].astype(F32)) * (1.0 / i[1][0:1, :])
-        out[0][...] = prob * (i[2][...] - i[3][0:1, :])
+        at = pl.ds(pl.multiple_of(pl.program_id(0) * last_blk, last_blk), last_blk)
+        prob = jnp.exp(i[0][at, :].astype(F32)) * (1.0 / i[1][0:1, :])
+        out[0][...] = prob * (i[2][at, :] - i[3][0:1, :])
 
         @pl.when(pl.program_id(0) == 0)
         def _():
@@ -699,10 +700,11 @@
             for n, value in enumerate(values):
                 out[1][n] = value
 
-    last_blk = rows // 2
+    last_blk = rows // 4
+    held = pl.BlockSpec(memory_space=pltpu.VMEM)
     blk = by_rows(spots, last_blk)
     grad_logits, loss_terms = run(
-        "final", final_body, [(logits, blk), (st["tot"], row8), (grad_probs, blk), (v, row8)],
+        "final", final_body, [(logits, held), (st["tot"], row8), (grad_probs, held), (v, row8)],
         [(sds((rows, spots), F32), blk), (sds((5,), F32), pl.BlockSpec(memory_space=pltpu.SMEM))],
         grid=(rows // last_blk,),
     )

time: 283 us -> 283 us (level)
  no operation moved by 1% of the time
where the time goes in v10:
time: 283 us
  waiting for transfers between devices  126 us (45%)
  starting transfers between devices  74.3 us (26%)
  Pallas kernels  61.6 us (22%)
  blocking collectives  11.6 us (4%)
  local copies, waits for them, and re-layouts  8.1 us (3%)
    ppermute x11, waiting for transfers between devices, over_spot(): return lax.ppermute(v, 'spot', xor_pairs(spot_size, step))  69.7 us
    pallas_call x50, Pallas kernels, run(): pl.pallas_call(kernel, out_shape=[s for s, _ in outs] + [sds(a.shape, a.d...  61.6 us
    ppermute x29, starting transfers between devices, over_gene(): return lax.ppermute(v, 'gene', xor_pairs(4, step))  46.9 us
    ppermute x29, waiting for transfers between devices, over_gene(): return lax.ppermute(v, 'gene', xor_pairs(4, step))  38.1 us
    ppermute x11, starting transfers between devices, over_spot(): return lax.ppermute(v, 'spot', xor_pairs(spot_size, step))  14.5 us
    psum x1, blocking collectives, totals(): st['tot'] = lax.psum(v, 'cell')  11.6 us
    ppermute x7, waiting for transfers between devices, over_x(): return lax.ppermute(v, 'cell', xor_pairs(4, 2))  10.7 us
    ppermute x7, starting transfers between devices, over_x(): return lax.ppermute(v, 'cell', xor_pairs(4, 2))  10.4 us
  transfers between devices with their start and end apart: 59, of which 35 were waited for; matrix products, arithmetic and copies ran while one was open for 0% of the time, Pallas kernels for 17%

profile of v10, /device:TPU:0, one launch (start us, length us, event | category | flops | bytes accessed | tf_op | source)
XLA Modules:
  0.0 282.6 jit_solution(7961557458572219730)
XLA Ops:
  0.6 2.7 slice.4
  3.4 3.0 %collective-permute-start.3 = (bf16[2,2816,128]{2,1,0:T(8,128)(2,1)}, bf16[2,2816,128]{2,1,0:T(8,128)(2,1)}, u32[]{:S(2)}, u32[]{:S(2)}) collective-permute-start(bf16[2,2816,128]{2,1,0:T(8,128)(2,1)} %slice.4), channel_id=1, source_target_pairs={{0,4},{4,0},{1,5},{5,1},{2,6},{6,2},{3,7},{7,3},{8,12},{12,8},{9,1... | collective-permute-start | bytes 4325384 | tf_op jit(solution)/shard_map/ppermute | solution.py:126
  7.8 2.6 copy-done
  10.4 2.0 swap1.1
  12.5 11.6 %psum.7.refs_1_ = f32[8,512]{1,0:T(8,128)S(1)} all-reduce(f32[8,512]{1,0:T(8,128)S(1)} %get-tuple-element.131), channel_id=1, replica_groups=mesh['cell'=4,'spot'=2,'gene'=4] {'cell'}, use_global_device_ids=true, to_apply=%region_0.1 | all-reduce | flops 4096 | bytes 32768 | tf_op jit(solution)/shard_map/psum | solution.py:234
  25.7 2.6 collective-permute-start.1
  28.5 1.9 collective-permute-done.1.refs_1_.refs_3_
  30.4 3.4 %collective-permute-done.2.refs_2_.refs_4_ = f32[8,512]{1,0:T(8,128)S(1)} collective-permute-done((f32[8,512]{1,0:T(8,128)S(1)}, f32[8,512]{1,0:T(8,128)S(1)}, u32[]{:S(2)}, u32[]{:S(2)}) %collective-permute-start.2) | collective-permute-done | bytes 16416 | tf_op jit(solution)/shard_map/ppermute | solution.py:123
  34.4 2.6 copy-done.1
  39.1 2.0 along0.1
  41.6 2.2 collective-permute-start.5
  45.5 2.4 collective-permute-start.6
  48.3 4.0 %prob.1 = (bf16[512,2816]{1,0:T(8,128)(2,1)S(1)}, f32[8,2816]{1,0:T(8,128)S(1)}, f32[8,512]{1,0:T(8,128)S(1)}, f32[8,512]{1,0:T(8,128)S(1)}, f32[8,128]{1,0:T(8,128)S(1)}) custom-call(s32[5]{0:T(128)S(1)} %stack.27.flags, bf16[2816,512]{1,0:T(8,128)(2,1)S(1)} %copy-done.2, f32[8,512]{1,0:T(8,128)S(1)} %psum.7.refs_1_, ...), custom_call_target="tpu_custom_call", output_to_operand_aliasing={{4}: (6, {})} | custom-call | tf_op jit(solution)/shard_map/prob/pallas_call | solution.py:66
  53.0 16.9 %collective-permute-done.9.refs_0_.refs_7_ = bf16[2,2816,128]{2,1,0:T(8,128)(2,1)} collective-permute-done((bf16[2,2816,128]{2,1,0:T(8,128)(2,1)}, bf16[2,2816,128]{2,1,0:T(8,128)(2,1)}, u32[]{:S(2)}, u32[]{:S(2)}) %collective-permute-start.9) | collective-permute-done | bytes 1441824 | tf_op jit(solution)/shard_map/ppermute | solution.py:126
  72.5 3.4 %collective-permute-done.7.refs_1_.refs_5_ = bf16[1408,128]{1,0:T(8,128)(2,1)S(1)} collective-permute-done((bf16[1408,128]{1,0:T(8,128)(2,1)S(1)}, bf16[1408,128]{1,0:T(8,128)(2,1)S(1)}, u32[]{:S(2)}, u32[]{:S(2)}) %collective-permute-start.7) | collective-permute-done | bytes 360480 | tf_op jit(solution)/shard_map/ppermute | solution.py:123
  77.0 2.0 collective-permute-start.12
  80.5 2.2 collective-permute-start.11
  82.7 18.0 %collective-permute-done.8.refs_0_.refs_2_ = bf16[2,2816,128]{2,1,0:T(8,128)(2,1)S(1)} collective-permute-done((bf16[2,2816,128]{2,1,0:T(8,128)(2,1)S(1)}, bf16[2,2816,128]{2,1,0:T(8,128)(2,1)S(1)}, u32[]{:S(2)}, u32[]{:S(2)}) %collective-permute-start.8) | collective-permute-done | bytes 1441824 | tf_op jit(solution)/shard_map/ppermute | solution.py:126
  101.8 7.7 %collective-permute-done.11.refs_1_.refs_10_ = bf16[1408,128]{1,0:T(8,128)(2,1)S(1)} collective-permute-done((bf16[1408,128]{1,0:T(8,128)(2,1)S(1)}, bf16[1408,128]{1,0:T(8,128)(2,1)S(1)}, u32[]{:S(2)}, u32[]{:S(2)}) %collective-permute-start.11) | collective-permute-done | bytes 360480 | tf_op jit(solution)/shard_map/ppermute | solution.py:123
  110.6 2.0 collective-permute-start.17
  116.7 15.0 %collective-permute-done.14.refs_0_.refs_2_ = bf16[2,2816,128]{2,1,0:T(8,128)(2,1)S(1)} collective-permute-done((bf16[2,2816,128]{2,1,0:T(8,128)(2,1)S(1)}, bf16[2,2816,128]{2,1,0:T(8,128)(2,1)S(1)}, u32[]{:S(2)}, u32[]{:S(2)}) %collective-permute-start.14) | collective-permute-done | bytes 1441824 | tf_op jit(solution)/shard_map/ppermute | solution.py:126
  132.8 6.0 %collective-permute-done.16.refs_1_.refs_5_ = bf16[1408,128]{1,0:T(8,128)(2,1)S(1)} collective-permute-done((bf16[1408,128]{1,0:T(8,128)(2,1)S(1)}, bf16[1408,128]{1,0:T(8,128)(2,1)S(1)}, u32[]{:S(2)}, u32[]{:S(2)}) %collective-permute-start.16) | collective-permute-done | bytes 360480 | tf_op jit(solution)/shard_map/ppermute | solution.py:123
  140.5 2.0 collective-permute-start.18
  145.0 1.9 collective-permute-start.20
  148.2 2.1 collective-permute-start.25
  150.4 12.2 %collective-permute-done.18.refs_0_.refs_11_ = bf16[2,1408,128]{2,1,0:T(8,128)(2,1)S(1)} collective-permute-done((bf16[2,1408,128]{2,1,0:T(8,128)(2,1)S(1)}, bf16[2,1408,128]{2,1,0:T(8,128)(2,1)S(1)}, u32[]{:S(2)}, u32[]{:S(2)}) %collective-permute-start.18) | collective-permute-done | bytes 720928 | tf_op jit(solution)/shard_map/ppermute | solution.py:126
  163.1 5.0 %forward0.1 = (bf16[2816,512]{1,0:T(8,128)(2,1)S(1)}, bf16[2816,512]{1,0:T(8,128)(2,1)S(1)}, f32[2,128,1024]{2,1,0:T(8,128)S(1)}, f32[128,1024]{1,0:T(8,128)S(1)...) custom-call(s32[5]{0:T(128)S(1)} %stack.27.flags, ...), custom_call_target="tpu_custom_call", output_to_operand_aliasing={{5}: (13, {})} | custom-call | tf_op jit(solution)/shard_map/forward0/pallas_call | solution.py:66
  168.1 3.2 %collective-permute-done.20.refs_1_.refs_5_ = bf16[1536,128]{1,0:T(8,128)(2,1)S(1)} collective-permute-done((bf16[1536,128]{1,0:T(8,128)(2,1)S(1)}, bf16[1536,128]{1,0:T(8,128)(2,1)S(1)}, u32[]{:S(2)}, u32[]{:S(2)}) %collective-permute-start.20) | collective-permute-done | bytes 393248 | tf_op jit(solution)/shard_map/ppermute | solution.py:123
  178.5 2.8 %forward1.1 = (bf16[2816,512]{1,0:T(8,128)(2,1)S(1)}, f32[2,128,512]{2,1,0:T(8,128)S(1)}, f32[128,512]{1,0:T(8,128)S(1)}, f32[128,512]{1,0:T(8,128)S(1)}, f32[8,128]{1,0:T(8,128)S(1)}) custom-call(s32[5]{0:T(128)S(1)} %stack.27.flags, bf16[512,2816]{1,0:T(8,128)(2,1)S(1)} %get-tuple-element.142.refs_0_, ...), custom_call_target="tpu_custom_call", output_to_operand_aliasing={{4}: (8, {})} | custom-call | tf_op jit(solution)/shard_map/forward1/pallas_call | solution.py:66
  184.5 2.1 collective-permute-start.29
  186.6 2.6 forward2.1
  189.2 2.0 collective-permute-done.24.refs_1_
  193.6 4.0 %collective-permute-start.28 = (f32[2,128,256]{2,1,0:T(8,128)S(1)}, f32[2,128,256]{2,1,0:T(8,128)S(1)}, u32[]{:S(2)}, u32[]{:S(2)}) collective-permute-start(f32[2,128,256]{2,1,0:T(8,128)S(1)} %get-tuple-element.204), channel_id=1, source_target_pairs={{0,2},{1,3},{2,0},{3,1},{4,6},{5,7},{6,4},{7,5},{8,10},{9,11},{10,... | collective-permute-start | bytes 786440 | tf_op jit(solution)/shard_map/ppermute | solution.py:123
  200.3 5.9 %collective-permute-done.33.refs_2_ = f32[128,512]{1,0:T(8,128)S(1)} collective-permute-done((f32[128,512]{1,0:T(8,128)S(1)}, f32[128,512]{1,0:T(8,128)S(1)}, u32[]{:S(2)}, u32[]{:S(2)}) %collective-permute-start.33) | collective-permute-done | bytes 262176 | tf_op jit(solution)/shard_map/ppermute | solution.py:120
  209.2 2.1 collective-permute-start.37
  212.9 3.8 %collective-permute-done.4.refs_3_ = f32[8,2816]{1,0:T(8,128)S(1)} collective-permute-done((f32[8,2816]{1,0:T(8,128)S(1)}, f32[8,2816]{1,0:T(8,128)S(1)}, u32[]{:S(2)}, u32[]{:S(2)}) %collective-permute-start.4) | collective-permute-done | bytes 90144 | tf_op jit(solution)/shard_map/ppermute | solution.py:126
  217.8 2.5 collective-permute-done.36.refs_2_
  225.2 2.0 collective-permute-start.38
  237.7 2.0 collective-permute-start.49
  241.1 2.3 collective-permute-done.50.refs_4_.refs_12_
  243.4 3.5 %collective-permute-done.48.refs_1_ = bf16[128,512]{1,0:T(8,128)(2,1)S(1)} collective-permute-done((bf16[128,512]{1,0:T(8,128)(2,1)S(1)}, bf16[128,512]{1,0:T(8,128)(2,1)S(1)}, u32[]{:S(2)}, u32[]{:S(2)}) %collective-permute-start.48) | collective-permute-done | bytes 131104 | tf_op jit(solution)/shard_map/ppermute | solution.py:123
  250.6 4.2 %own.1 = (f32[2816,512]{1,0:T(8,128)S(1)}, f32[8,128]{1,0:T(8,128)S(1)}) custom-call(s32[5]{0:T(128)S(1)} %stack.27.flags, f32[2816,128]{1,0:T(8,128)S(1)} %get-tuple-element.224.refs_0_, bf16[2816,512]{1,0:T(8,128)(2,1)S(1)} %get-tuple-element.225.refs_1_.refs_3_, ...), custom_call_target="tpu_custom_call", output_to_operand_aliasing={{1}: (10, {})} | custom-call | tf_op jit(solution)/shard_map/own/pallas_call | solution.py:66
  257.6 6.6 %backward.1 = (f32[2816,512]{1,0:T(8,128)S(1)}, f32[8,512]{1,0:T(8,128)S(1)}, f32[8,128]{1,0:T(8,128)S(1)}) custom-call(s32[5]{0:T(128)S(1)} %stack.27.flags, bf16[2816,512]{1,0:T(8,128)(2,1)S(1)} %copy-done.2, f32[8,512]{1,0:T(8,128)S(1)} %get-tuple-element.140.refs_1_, ...), custom_call_target="tpu_custom_call", output_to_operand_aliasing={{2}: (14, {})} | custom-call | tf_op jit(solution)/shard_map/backward/pallas_call | solution.py:66
  267.0 2.2 collective-permute-done.55
  269.2 3.4 %collective-permute-start.56 = (f32[8,512]{1,0:T(8,128)S(1)}, f32[8,512]{1,0:T(8,128)S(1)}, u32[]{:S(2)}, u32[]{:S(2)}) collective-permute-start(f32[8,512]{1,0:T(8,128)S(1)} %add.32), channel_id=1, source_target_pairs={{0,1},{1,0},{2,3},{3,2},{4,5},{5,4},{6,7},{7,6},{8,9},{9,8},{10,11... | collective-permute-start | bytes 49160 | tf_op jit(solution)/shard_map/ppermute | solution.py:123
  273.1 1.9 collective-permute-start.58
  275.1 2.2 collective-permute-done.57
  278.7 4.0 %final.1 = (f32[2816,512]{1,0:T(8,128)}, f32[5]{0:T(128)}, f32[8,128]{1,0:T(8,128)S(1)}) custom-call(s32[5]{0:T(128)S(1)} %stack.27.flags, bf16[2816,512]{1,0:T(8,128)(2,1)S(1)} %copy-done.2, f32[8,512]{1,0:T(8,128)S(1)} %get-tuple-element.140.refs_1_, f32[2816,512]{1,0:T(8,128)S(1)} %get-tuple-element.255.refs_2_, ...), custom_call_target="tpu_custom_call", output_to_operand_aliasing={{2}: (5, {})} | custom-call | tf_op jit(solution)/shard_map/final/pallas_call | solution.py:66
  (149 shorter events, 77.0 us)
Async XLA Ops:
  3.4 35.7 %collective-permute-start.3 = (bf16[2,2816,128]{2,1,0:T(8,128)(2,1)}, bf16[2,2816,128]{2,1,0:T(8,128)(2,1)}, u32[]{:S(2)}, u32[]{:S(2)}) collective-permute-start(bf16[2,2816,128]{2,1,0:T(8,128)(2,1)} %slice.4), channel_id=1, source_target_pairs={{0,4},{4,0},{1,5},{5,1},{2,6},{6,2},{3,7},{7,3},{8,12},{12,8},{9,1... | collective-permute-start | bytes 4325384 | tf_op jit(solution)/shard_map/ppermute | solution.py:126
  12.4 57.5 %collective-permute-start.9 = (bf16[2,2816,128]{2,1,0:T(8,128)(2,1)}, bf16[2,2816,128]{2,1,0:T(8,128)(2,1)}, u32[]{:S(2)}, u32[]{:S(2)}) collective-permute-start(bf16[2,2816,128]{2,1,0:T(8,128)(2,1)} %get-tuple-element.147), channel_id=1, source_target_pairs={{0,4},{4,0},{1,5},{5,1},{2,6},{6,2},{3,7},{7,3},{8,12},{12,8},{9,1... | collective-permute-start | bytes 4325384 | tf_op jit(solution)/shard_map/ppermute | solution.py:126
  24.1 4.4 %collective-permute-start = (f32[8,512]{1,0:T(8,128)S(1)}, f32[8,512]{1,0:T(8,128)S(1)}, u32[]{:S(2)}, u32[]{:S(2)}) collective-permute-start(f32[8,512]{1,0:T(8,128)S(1)} %psum.7.refs_1_), channel_id=1, source_target_pairs={{0,1},{1,0},{2,3},{3,2},{4,5},{5,4},{6,7},{7,6},{8,9},{9,8},{10,11... | collective-permute-start | bytes 49160 | tf_op jit(solution)/shard_map/ppermute | solution.py:123
  25.7 4.7 %collective-permute-start.1 = (f32[8,512]{1,0:T(8,128)S(1)}, f32[8,512]{1,0:T(8,128)S(1)}, u32[]{:S(2)}, u32[]{:S(2)}) collective-permute-start(f32[8,512]{1,0:T(8,128)S(1)} %psum.7.refs_1_), channel_id=1, source_target_pairs={{0,2},{1,3},{2,0},{3,1},{4,6},{5,7},{6,4},{7,5},{8,10},{9,11},{10,... | collective-permute-start | bytes 49160 | tf_op jit(solution)/shard_map/ppermute | solution.py:123
  28.3 5.5 %collective-permute-start.2 = (f32[8,512]{1,0:T(8,128)S(1)}, f32[8,512]{1,0:T(8,128)S(1)}, u32[]{:S(2)}, u32[]{:S(2)}) collective-permute-start(f32[8,512]{1,0:T(8,128)S(1)} %psum.7.refs_1_), channel_id=1, source_target_pairs={{0,3},{1,2},{2,1},{3,0},{4,7},{5,6},{6,5},{7,4},{8,11},{9,10},{10,... | collective-permute-start | bytes 49160 | tf_op jit(solution)/shard_map/ppermute | solution.py:123
  41.6 34.3 %collective-permute-start.5 = (bf16[2816,128]{1,0:T(8,128)(2,1)S(1)}, bf16[2816,128]{1,0:T(8,128)(2,1)S(1)}, u32[]{:S(2)}, u32[]{:S(2)}) collective-permute-start(bf16[2816,128]{1,0:T(8,128)(2,1)S(1)} %get-tuple-element.143), channel_id=1, source_target_pairs={{0,1},{1,0},{2,3},{3,2},{4,5},{5,4},{6,7},{7,6},{8,9},{9,8},{10,11... | collective-permute-start | bytes 2162696 | tf_op jit(solution)/shard_map/ppermute | solution.py:123
  43.8 57.0 %collective-permute-start.8 = (bf16[2,2816,128]{2,1,0:T(8,128)(2,1)S(1)}, bf16[2,2816,128]{2,1,0:T(8,128)(2,1)S(1)}, u32[]{:S(2)}, u32[]{:S(2)}) collective-permute-start(bf16[2,2816,128]{2,1,0:T(8,128)(2,1)S(1)} %get-tuple-element.146), channel_id=1, source_target_pairs={{0,4},{4,0},{1,5},{5,1},{2,6},{6,2},{3,7},{7,3},{8,12},{12,8},{9,1... | collective-permute-start | bytes 4325384 | tf_op jit(solution)/shard_map/ppermute | solution.py:126
  45.5 27.0 %collective-permute-start.6 = (bf16[1408,128]{1,0:T(8,128)(2,1)S(1)}, bf16[1408,128]{1,0:T(8,128)(2,1)S(1)}, u32[]{:S(2)}, u32[]{:S(2)}) collective-permute-start(bf16[1408,128]{1,0:T(8,128)(2,1)S(1)} %get-tuple-element.144), channel_id=1, source_target_pairs={{0,2},{1,3},{2,0},{3,1},{4,6},{5,7},{6,4},{7,5},{8,10},{9,11},{10,... | collective-permute-start | bytes 1081352 | tf_op jit(solution)/shard_map/ppermute | solution.py:123
  47.9 28.0 %collective-permute-start.7 = (bf16[1408,128]{1,0:T(8,128)(2,1)S(1)}, bf16[1408,128]{1,0:T(8,128)(2,1)S(1)}, u32[]{:S(2)}, u32[]{:S(2)}) collective-permute-start(bf16[1408,128]{1,0:T(8,128)(2,1)S(1)} %get-tuple-element.145), channel_id=1, source_target_pairs={{0,3},{1,2},{2,1},{3,0},{4,7},{5,6},{6,5},{7,4},{8,11},{9,10},{10,... | collective-permute-start | bytes 1081352 | tf_op jit(solution)/shard_map/ppermute | solution.py:123
  77.0 32.5 %collective-permute-start.12 = (bf16[2816,128]{1,0:T(8,128)(2,1)S(1)}, bf16[2816,128]{1,0:T(8,128)(2,1)S(1)}, u32[]{:S(2)}, u32[]{:S(2)}) collective-permute-start(bf16[2816,128]{1,0:T(8,128)(2,1)S(1)} %get-tuple-element.161), channel_id=1, source_target_pairs={{0,1},{1,0},{2,3},{3,2},{4,5},{5,4},{6,7},{7,6},{8,9},{9,8},{10,11... | collective-permute-start | bytes 2162696 | tf_op jit(solution)/shard_map/ppermute | solution.py:123
  78.9 52.7 %collective-permute-start.14 = (bf16[2,2816,128]{2,1,0:T(8,128)(2,1)S(1)}, bf16[2,2816,128]{2,1,0:T(8,128)(2,1)S(1)}, u32[]{:S(2)}, u32[]{:S(2)}) collective-permute-start(bf16[2,2816,128]{2,1,0:T(8,128)(2,1)S(1)} %get-tuple-element.165), channel_id=1, source_target_pairs={{0,4},{4,0},{1,5},{5,1},{2,6},{6,2},{3,7},{7,3},{8,12},{12,8},{9,1... | collective-permute-start | bytes 4325384 | tf_op jit(solution)/shard_map/ppermute | solution.py:126
  79.4 22.4 %collective-permute-start.10 = (bf16[1408,128]{1,0:T(8,128)(2,1)S(1)}, bf16[1408,128]{1,0:T(8,128)(2,1)S(1)}, u32[]{:S(2)}, u32[]{:S(2)}) collective-permute-start(bf16[1408,128]{1,0:T(8,128)(2,1)S(1)} %get-tuple-element.159), channel_id=1, source_target_pairs={{0,2},{1,3},{2,0},{3,1},{4,6},{5,7},{6,4},{7,5},{8,10},{9,11},{10,... | collective-permute-start | bytes 1081352 | tf_op jit(solution)/shard_map/ppermute | solution.py:123
  80.5 28.9 %collective-permute-start.11 = (bf16[1408,128]{1,0:T(8,128)(2,1)S(1)}, bf16[1408,128]{1,0:T(8,128)(2,1)S(1)}, u32[]{:S(2)}, u32[]{:S(2)}) collective-permute-start(bf16[1408,128]{1,0:T(8,128)(2,1)S(1)} %get-tuple-element.160), channel_id=1, source_target_pairs={{0,3},{1,2},{2,1},{3,0},{4,7},{5,6},{6,5},{7,4},{8,11},{9,10},{10,... | collective-permute-start | bytes 1081352 | tf_op jit(solution)/shard_map/ppermute | solution.py:123
  110.6 28.2 %collective-permute-start.17 = (bf16[2816,128]{1,0:T(8,128)(2,1)S(1)}, bf16[2816,128]{1,0:T(8,128)(2,1)S(1)}, u32[]{:S(2)}, u32[]{:S(2)}) collective-permute-start(bf16[2816,128]{1,0:T(8,128)(2,1)S(1)} %get-tuple-element.172), channel_id=1, source_target_pairs={{0,1},{1,0},{2,3},{3,2},{4,5},{5,4},{6,7},{7,6},{8,9},{9,8},{10,11... | collective-permute-start | bytes 2162696 | tf_op jit(solution)/shard_map/ppermute | solution.py:123
  112.6 20.2 %collective-permute-start.15 = (bf16[1408,128]{1,0:T(8,128)(2,1)S(1)}, bf16[1408,128]{1,0:T(8,128)(2,1)S(1)}, u32[]{:S(2)}, u32[]{:S(2)}) collective-permute-start(bf16[1408,128]{1,0:T(8,128)(2,1)S(1)} %get-tuple-element.170), channel_id=1, source_target_pairs={{0,2},{1,3},{2,0},{3,1},{4,6},{5,7},{6,4},{7,5},{8,10},{9,11},{10,... | collective-permute-start | bytes 1081352 | tf_op jit(solution)/shard_map/ppermute | solution.py:123
  113.2 25.6 %collective-permute-start.16 = (bf16[1408,128]{1,0:T(8,128)(2,1)S(1)}, bf16[1408,128]{1,0:T(8,128)(2,1)S(1)}, u32[]{:S(2)}, u32[]{:S(2)}) collective-permute-start(bf16[1408,128]{1,0:T(8,128)(2,1)S(1)} %get-tuple-element.171), channel_id=1, source_target_pairs={{0,3},{1,2},{2,1},{3,0},{4,7},{5,6},{6,5},{7,4},{8,11},{9,10},{10,... | collective-permute-start | bytes 1081352 | tf_op jit(solution)/shard_map/ppermute | solution.py:123
  115.6 31.5 %collective-permute-start.13 = (bf16[2,1408,128]{2,1,0:T(8,128)(2,1)S(1)}, bf16[2,1408,128]{2,1,0:T(8,128)(2,1)S(1)}, u32[]{:S(2)}, u32[]{:S(2)}) collective-permute-start(bf16[2,1408,128]{2,1,0:T(8,128)(2,1)S(1)} %get-tuple-element.164), channel_id=1, source_target_pairs={{0,4},{4,0},{1,5},{5,1},{2,6},{6,2},{3,7},{7,3},{8,12},{12,8},{9,1... | collective-permute-start | bytes 2162696 | tf_op jit(solution)/shard_map/ppermute | solution.py:126
  140.5 22.0 %collective-permute-start.18 = (bf16[2,1408,128]{2,1,0:T(8,128)(2,1)S(1)}, bf16[2,1408,128]{2,1,0:T(8,128)(2,1)S(1)}, u32[]{:S(2)}, u32[]{:S(2)}) collective-permute-start(bf16[2,1408,128]{2,1,0:T(8,128)(2,1)S(1)} %get-tuple-element.175), channel_id=1, source_target_pairs={{0,4},{4,0},{1,5},{5,1},{2,6},{6,2},{3,7},{7,3},{8,12},{12,8},{9,1... | collective-permute-start | bytes 2162696 | tf_op jit(solution)/shard_map/ppermute | solution.py:126
  142.5 28.7 %collective-permute-start.21 = (bf16[2816,128]{1,0:T(8,128)(2,1)S(1)}, bf16[2816,128]{1,0:T(8,128)(2,1)S(1)}, u32[]{:S(2)}, u32[]{:S(2)}) collective-permute-start(bf16[2816,128]{1,0:T(8,128)(2,1)S(1)} %get-tuple-element.183), channel_id=1, source_target_pairs={{0,1},{1,0},{2,3},{3,2},{4,5},{5,4},{6,7},{7,6},{8,9},{9,8},{10,11... | collective-permute-start | bytes 2162696 | tf_op jit(solution)/shard_map/ppermute | solution.py:123
  144.2 23.9 %collective-permute-start.19 = (bf16[1536,128]{1,0:T(8,128)(2,1)S(1)}, bf16[1536,128]{1,0:T(8,128)(2,1)S(1)}, u32[]{:S(2)}, u32[]{:S(2)}) collective-permute-start(bf16[1536,128]{1,0:T(8,128)(2,1)S(1)} %get-tuple-element.181), channel_id=1, source_target_pairs={{0,2},{1,3},{2,0},{3,1},{4,6},{5,7},{6,4},{7,5},{8,10},{9,11},{10,... | collective-permute-start | bytes 1179656 | tf_op jit(solution)/shard_map/ppermute | solution.py:123
  145.0 26.2 %collective-permute-start.20 = (bf16[1536,128]{1,0:T(8,128)(2,1)S(1)}, bf16[1536,128]{1,0:T(8,128)(2,1)S(1)}, u32[]{:S(2)}, u32[]{:S(2)}) collective-permute-start(bf16[1536,128]{1,0:T(8,128)(2,1)S(1)} %get-tuple-element.182), channel_id=1, source_target_pairs={{0,3},{1,2},{2,1},{3,0},{4,7},{5,6},{6,5},{7,4},{8,11},{9,10},{10,... | collective-permute-start | bytes 1179656 | tf_op jit(solution)/shard_map/ppermute | solution.py:123
  148.2 29.7 %collective-permute-start.25 = (bf16[2,1408,128]{2,1,0:T(8,128)(2,1)S(1)}, bf16[2,1408,128]{2,1,0:T(8,128)(2,1)S(1)}, u32[]{:S(2)}, u32[]{:S(2)}) collective-permute-start(bf16[2,1408,128]{2,1,0:T(8,128)(2,1)S(1)} %get-tuple-element.191), channel_id=1, source_target_pairs={{0,4},{4,0},{1,5},{5,1},{2,6},{6,2},{3,7},{7,3},{8,12},{12,8},{9,1... | collective-permute-start | bytes 2162696 | tf_op jit(solution)/shard_map/ppermute | solution.py:126
  173.5 18.2 %collective-permute-start.30 = (bf16[2,1280,128]{2,1,0:T(8,128)(2,1)S(1)}, bf16[2,1280,128]{2,1,0:T(8,128)(2,1)S(1)}, u32[]{:S(2)}, u32[]{:S(2)}) collective-permute-start(bf16[2,1280,128]{2,1,0:T(8,128)(2,1)S(1)} %get-tuple-element.207), channel_id=1, source_target_pairs={{0,4},{4,0},{1,5},{5,1},{2,6},{6,2},{3,7},{7,3},{8,12},{12,8},{9,1... | collective-permute-start | bytes 1966088 | tf_op jit(solution)/shard_map/ppermute | solution.py:126
  176.3 14.8 %collective-permute-start.24 = (f32[128,1024]{1,0:T(8,128)S(1)}, f32[128,1024]{1,0:T(8,128)S(1)}, u32[]{:S(2)}, u32[]{:S(2)}) collective-permute-start(f32[128,1024]{1,0:T(8,128)S(1)} %get-tuple-element.190), channel_id=1, source_target_pairs={{0,16},{8,24},{16,0},{24,8},{1,17},{9,25},{17,1},{25,9},{2,18},{10... | collective-permute-start | bytes 1572872 | tf_op jit(solution)/shard_map/ppermute | solution.py:120
  184.5 15.2 %collective-permute-start.29 = (f32[136,512]{1,0:T(8,128)S(1)}, f32[136,512]{1,0:T(8,128)S(1)}, u32[]{:S(2)}, u32[]{:S(2)}) collective-permute-start(f32[136,512]{1,0:T(8,128)S(1)} %get-tuple-element.206), channel_id=1, source_target_pairs={{0,16},{8,24},{16,0},{24,8},{1,17},{9,25},{17,1},{25,9},{2,18},{10... | collective-permute-start | bytes 835592 | tf_op jit(solution)/shard_map/ppermute | solution.py:120
  193.0 4.6 %collective-permute-start.31 = (f32[128,512]{1,0:T(8,128)S(1)}, f32[128,512]{1,0:T(8,128)S(1)}, u32[]{:S(2)}, u32[]{:S(2)}) collective-permute-start(f32[128,512]{1,0:T(8,128)S(1)} %get-tuple-element.214), channel_id=1, source_target_pairs={{0,8},{8,0},{16,24},{24,16},{1,9},{9,1},{17,25},{25,17},{2,10},{10... | collective-permute-start | bytes 786440 | tf_op jit(solution)/shard_map/ppermute | solution.py:117
  193.1 4.5 %collective-permute-start.32 = (f32[128,512]{1,0:T(8,128)S(1)}, f32[128,512]{1,0:T(8,128)S(1)}, u32[]{:S(2)}, u32[]{:S(2)}) collective-permute-start(f32[128,512]{1,0:T(8,128)S(1)} %get-tuple-element.215), channel_id=1, source_target_pairs={{0,8},{8,0},{16,24},{24,16},{1,9},{9,1},{17,25},{25,17},{2,10},{10... | collective-permute-start | bytes 786440 | tf_op jit(solution)/shard_map/ppermute | solution.py:117
  193.6 17.7 %collective-permute-start.28 = (f32[2,128,256]{2,1,0:T(8,128)S(1)}, f32[2,128,256]{2,1,0:T(8,128)S(1)}, u32[]{:S(2)}, u32[]{:S(2)}) collective-permute-start(f32[2,128,256]{2,1,0:T(8,128)S(1)} %get-tuple-element.204), channel_id=1, source_target_pairs={{0,2},{1,3},{2,0},{3,1},{4,6},{5,7},{6,4},{7,5},{8,10},{9,11},{10,... | collective-permute-start | bytes 786440 | tf_op jit(solution)/shard_map/ppermute | solution.py:123
  198.2 8.1 %collective-permute-start.33 = (f32[128,512]{1,0:T(8,128)S(1)}, f32[128,512]{1,0:T(8,128)S(1)}, u32[]{:S(2)}, u32[]{:S(2)}) collective-permute-start(f32[128,512]{1,0:T(8,128)S(1)} %get-tuple-element.220), channel_id=1, source_target_pairs={{0,16},{8,24},{16,0},{24,8},{1,17},{9,25},{17,1},{25,9},{2,18},{10... | collective-permute-start | bytes 786440 | tf_op jit(solution)/shard_map/ppermute | solution.py:120
  206.9 10.9 %collective-permute-start.35 = (f32[128,256]{1,0:T(8,128)S(1)}, f32[128,256]{1,0:T(8,128)S(1)}, u32[]{:S(2)}, u32[]{:S(2)}) collective-permute-start(f32[128,256]{1,0:T(8,128)S(1)} %get-tuple-element.235), channel_id=1, source_target_pairs={{0,1},{1,0},{2,3},{3,2},{4,5},{5,4},{6,7},{7,6},{8,9},{9,8},{10,11... | collective-permute-start | bytes 393224 | tf_op jit(solution)/shard_map/ppermute | solution.py:123
  208.0 12.2 %collective-permute-start.36 = (f32[128,256]{1,0:T(8,128)S(1)}, f32[128,256]{1,0:T(8,128)S(1)}, u32[]{:S(2)}, u32[]{:S(2)}) collective-permute-start(f32[128,256]{1,0:T(8,128)S(1)} %get-tuple-element.236), channel_id=1, source_target_pairs={{0,2},{1,3},{2,0},{3,1},{4,6},{5,7},{6,4},{7,5},{8,10},{9,11},{10,... | collective-permute-start | bytes 393224 | tf_op jit(solution)/shard_map/ppermute | solution.py:123
  209.2 11.1 %collective-permute-start.37 = (f32[128,256]{1,0:T(8,128)S(1)}, f32[128,256]{1,0:T(8,128)S(1)}, u32[]{:S(2)}, u32[]{:S(2)}) collective-permute-start(f32[128,256]{1,0:T(8,128)S(1)} %get-tuple-element.237), channel_id=1, source_target_pairs={{0,3},{1,2},{2,1},{3,0},{4,7},{5,6},{6,5},{7,4},{8,11},{9,10},{10,... | collective-permute-start | bytes 393224 | tf_op jit(solution)/shard_map/ppermute | solution.py:123
  211.9 9.1 %collective-permute-start.34 = (f32[128,256]{1,0:T(8,128)S(1)}, f32[128,256]{1,0:T(8,128)S(1)}, u32[]{:S(2)}, u32[]{:S(2)}) collective-permute-start(f32[128,256]{1,0:T(8,128)S(1)} %get-tuple-element.233), channel_id=1, source_target_pairs={{0,1},{1,0},{2,3},{3,2},{4,5},{5,4},{6,7},{7,6},{8,9},{9,8},{10,11... | collective-permute-start | bytes 393224 | tf_op jit(solution)/shard_map/ppermute | solution.py:123
  212.2 4.5 %collective-permute-start.4 = (f32[8,2816]{1,0:T(8,128)S(1)}, f32[8,2816]{1,0:T(8,128)S(1)}, u32[]{:S(2)}, u32[]{:S(2)}) collective-permute-start(f32[8,2816]{1,0:T(8,128)S(1)} %get-tuple-element.141.refs_2_), channel_id=1, source_target_pairs={{0,4},{4,0},{1,5},{5,1},{2,6},{6,2},{3,7},{7,3},{8,12},{12,8},{9,1... | collective-permute-start | bytes 270344 | tf_op jit(solution)/shard_map/ppermute | solution.py:126
  223.7 5.9 %collective-permute-start.42 = (f32[16,512]{1,0:T(8,128)S(1)}, f32[16,512]{1,0:T(8,128)S(1)}, u32[]{:S(2)}, u32[]{:S(2)}) collective-permute-start(f32[16,512]{1,0:T(8,128)S(1)} %add.29), channel_id=1, source_target_pairs={{0,16},{8,24},{16,0},{24,8},{1,17},{9,25},{17,1},{25,9},{2,18},{10... | collective-permute-start | bytes 98312 | tf_op jit(solution)/shard_map/ppermute | solution.py:120
  225.2 5.1 %collective-permute-start.38 = (f32[8,128]{1,0:T(8,128)S(1)}, f32[8,128]{1,0:T(8,128)S(1)}, u32[]{:S(2)}, u32[]{:S(2)}) collective-permute-start(f32[8,128]{1,0:T(8,128)S(1)} %get-tuple-element.243.refs_0_.refs_4_), channel_id=1, source_target_pairs={{0,1},{1,0},{2,3},{3,2},{4,5},{5,4},{6,7},{7,6},{8,9},{9,8},{10,11... | collective-permute-start | bytes 12296 | tf_op jit(solution)/shard_map/ppermute | solution.py:123
  227.2 4.5 %collective-permute-start.39 = (f32[8,128]{1,0:T(8,128)S(1)}, f32[8,128]{1,0:T(8,128)S(1)}, u32[]{:S(2)}, u32[]{:S(2)}) collective-permute-start(f32[8,128]{1,0:T(8,128)S(1)} %get-tuple-element.243.refs_0_.refs_4_), channel_id=1, source_target_pairs={{0,2},{1,3},{2,0},{3,1},{4,6},{5,7},{6,4},{7,5},{8,10},{9,11},{10,... | collective-permute-start | bytes 12296 | tf_op jit(solution)/shard_map/ppermute | solution.py:123
  227.8 5.4 %collective-permute-start.40 = (f32[8,128]{1,0:T(8,128)S(1)}, f32[8,128]{1,0:T(8,128)S(1)}, u32[]{:S(2)}, u32[]{:S(2)}) collective-permute-start(f32[8,128]{1,0:T(8,128)S(1)} %get-tuple-element.243.refs_0_.refs_4_), channel_id=1, source_target_pairs={{0,3},{1,2},{2,1},{3,0},{4,7},{5,6},{6,5},{7,4},{8,11},{9,10},{10,... | collective-permute-start | bytes 12296 | tf_op jit(solution)/shard_map/ppermute | solution.py:123
  229.6 4.1 %collective-permute-start.43 = (f32[16,512]{1,0:T(8,128)S(1)}, f32[16,512]{1,0:T(8,128)S(1)}, u32[]{:S(2)}, u32[]{:S(2)}) collective-permute-start(f32[16,512]{1,0:T(8,128)S(1)} %add.30.refs_8_), channel_id=1, source_target_pairs={{0,4},{4,0},{1,5},{5,1},{2,6},{6,2},{3,7},{7,3},{8,12},{12,8},{9,1... | collective-permute-start | bytes 98312 | tf_op jit(solution)/shard_map/ppermute | solution.py:126
  234.7 8.7 %collective-permute-start.45 = (bf16[128,512]{1,0:T(8,128)(2,1)S(1)}, bf16[128,512]{1,0:T(8,128)(2,1)S(1)}, u32[]{:S(2)}, u32[]{:S(2)}) collective-permute-start(bf16[128,512]{1,0:T(8,128)(2,1)S(1)} %get-tuple-element.246.refs_5_), channel_id=1, source_target_pairs={{0,16},{8,24},{16,0},{24,8},{1,17},{9,25},{17,1},{25,9},{2,18},{10... | collective-permute-start | bytes 393224 | tf_op jit(solution)/shard_map/ppermute | solution.py:120
  235.3 8.1 %collective-permute-start.47 = (bf16[128,512]{1,0:T(8,128)(2,1)S(1)}, bf16[128,512]{1,0:T(8,128)(2,1)S(1)}, u32[]{:S(2)}, u32[]{:S(2)}) collective-permute-start(bf16[128,512]{1,0:T(8,128)(2,1)S(1)} %get-tuple-element.246.refs_5_), channel_id=1, source_target_pairs={{0,1},{1,0},{2,3},{3,2},{4,5},{5,4},{6,7},{7,6},{8,9},{9,8},{10,11... | collective-permute-start | bytes 393224 | tf_op jit(solution)/shard_map/ppermute | solution.py:123
  236.2 10.7 %collective-permute-start.48 = (bf16[128,512]{1,0:T(8,128)(2,1)S(1)}, bf16[128,512]{1,0:T(8,128)(2,1)S(1)}, u32[]{:S(2)}, u32[]{:S(2)}) collective-permute-start(bf16[128,512]{1,0:T(8,128)(2,1)S(1)} %get-tuple-element.246.refs_5_), channel_id=1, source_target_pairs={{0,2},{1,3},{2,0},{3,1},{4,6},{5,7},{6,4},{7,5},{8,10},{9,11},{10,... | collective-permute-start | bytes 393224 | tf_op jit(solution)/shard_map/ppermute | solution.py:123
  237.7 9.2 %collective-permute-start.49 = (bf16[128,512]{1,0:T(8,128)(2,1)S(1)}, bf16[128,512]{1,0:T(8,128)(2,1)S(1)}, u32[]{:S(2)}, u32[]{:S(2)}) collective-permute-start(bf16[128,512]{1,0:T(8,128)(2,1)S(1)} %get-tuple-element.246.refs_5_), channel_id=1, source_target_pairs={{0,3},{1,2},{2,1},{3,0},{4,7},{5,6},{6,5},{7,4},{8,11},{9,10},{10,... | collective-permute-start | bytes 393224 | tf_op jit(solution)/shard_map/ppermute | solution.py:123
  247.5 7.8 %collective-permute-start.52 = (bf16[3,128,512]{2,1,0:T(8,128)(2,1)S(1)}, bf16[3,128,512]{2,1,0:T(8,128)(2,1)S(1)}, u32[]{:S(2)}, u32[]{:S(2)}) collective-permute-start(bf16[3,128,512]{2,1,0:T(8,128)(2,1)S(1)} %get-tuple-element.251.refs_7_), channel_id=1, source_target_pairs={{0,16},{8,24},{16,0},{24,8},{1,17},{9,25},{17,1},{25,9},{2,18},{10... | collective-permute-start | bytes 1179656 | tf_op jit(solution)/shard_map/ppermute | solution.py:120
  249.5 6.4 %collective-permute-start.51 = (bf16[3,128,512]{2,1,0:T(8,128)(2,1)S(1)}, bf16[3,128,512]{2,1,0:T(8,128)(2,1)S(1)}, u32[]{:S(2)}, u32[]{:S(2)}) collective-permute-start(bf16[3,128,512]{2,1,0:T(8,128)(2,1)S(1)} %get-tuple-element.251.refs_7_), channel_id=1, source_target_pairs={{0,8},{8,0},{16,24},{24,16},{1,9},{9,1},{17,25},{25,17},{2,10},{10... | collective-permute-start | bytes 1179656 | tf_op jit(solution)/shard_map/ppermute | solution.py:117
  269.2 5.8 %collective-permute-start.56 = (f32[8,512]{1,0:T(8,128)S(1)}, f32[8,512]{1,0:T(8,128)S(1)}, u32[]{:S(2)}, u32[]{:S(2)}) collective-permute-start(f32[8,512]{1,0:T(8,128)S(1)} %add.32), channel_id=1, source_target_pairs={{0,1},{1,0},{2,3},{3,2},{4,5},{5,4},{6,7},{7,6},{8,9},{9,8},{10,11... | collective-permute-start | bytes 49160 | tf_op jit(solution)/shard_map/ppermute | solution.py:123
  272.6 4.6 %collective-permute-start.57 = (f32[8,512]{1,0:T(8,128)S(1)}, f32[8,512]{1,0:T(8,128)S(1)}, u32[]{:S(2)}, u32[]{:S(2)}) collective-permute-start(f32[8,512]{1,0:T(8,128)S(1)} %add.32), channel_id=1, source_target_pairs={{0,2},{1,3},{2,0},{3,1},{4,6},{5,7},{6,4},{7,5},{8,10},{9,11},{10,... | collective-permute-start | bytes 49160 | tf_op jit(solution)/shard_map/ppermute | solution.py:123
  273.1 5.5 %collective-permute-start.58 = (f32[8,512]{1,0:T(8,128)S(1)}, f32[8,512]{1,0:T(8,128)S(1)}, u32[]{:S(2)}, u32[]{:S(2)}) collective-permute-start(f32[8,512]{1,0:T(8,128)S(1)} %add.32), channel_id=1, source_target_pairs={{0,3},{1,2},{2,1},{3,0},{4,7},{5,6},{6,5},{7,4},{8,11},{9,10},{10,... | collective-permute-start | bytes 49160 | tf_op jit(solution)/shard_map/ppermute | solution.py:123
  (20 other events, 134.2 us)
